TPU v7x, 32 devices: a whole 2x2x4 slice. The times are simulated.
32 devices in a mesh: grp: 4 (over y, core), blk: 8 (over z, x).
Axes of the slice: x: 2, y: 2, z: 4, core: 2. Of those that a mesh axis runs over, the one named last changes fastest.
Arguments:
- head_table: bfloat16 [8192, 256], P(('grp', 'blk')), may hold values from -4 to 4
- tail_table: bfloat16 [131072, 256], P(('grp', 'blk')), may hold values from -0.25 to 0.25
- qual_table: bfloat16 [32768, 256], P(('grp', 'blk')), may hold values from -4 to 4
- rel_table: float32 [512, 256], replicated, may hold values from -3 to 3
- proj: float32 [256, 256], replicated, may hold values from -0.375 to 0.375
- head_id: int32 [32768], P(('grp', 'blk')), may hold values from 0 to 2047, as said below
- tail_id: int32 [32768], P(('grp', 'blk')), may hold values from 0 to 4095
- rel_id: int32 [32768], P(('grp', 'blk')), may hold values from 0 to 511
- qual_rel: int32 [32768, 4], P(('grp', 'blk')), may hold values from 0 to 511
- qual_ref: int32 [32768, 4], P(('grp', 'blk')), may hold values from 0 to 255
- qual_req: int32 [8192], P(('grp', 'blk')), may hold values from 0 to 1023
- neg_id: int32 [32768], P(('grp', 'blk')), may hold values from 0 to 4095
- edge_count: int32 [32], P(('grp', 'blk')), may hold values from 128 to 1024
Outputs:
- head_grad: float32 [8192, 256], P(('grp', 'blk'))
- tail_grad: float32 [131072, 256], P(('grp', 'blk'))
- qual_grad: float32 [32768, 256], P(('grp', 'blk'))
- rel_grad: float32 [512, 256], replicated
- proj_grad: float32 [256, 256], replicated
Inputs may be any that keep to these rules, and one draw needn't show every extreme that they name: Among the edges of one device, at most 192 have head rows held by any one device of blk (head_id // 256), and some device of blk is named that often by every device's edges.
All inputs are finite; a program needn't handle non-finite values.
Results may differ from a plain program's by a relative error of at most 0.0046.
Values may be sent and summed in bfloat16 or wider, within the bound.
No kernel may reach another device: no remote copies, remote signals or barrier semaphores. Data moves between devices by JAX's collectives and lax.ppermute only.
A program may use at most 128 MiB of HBM per device.

v0:
```python
import jax
import jax.numpy as jnp
from jax import lax
from jax.sharding import PartitionSpec as P

REL = 512
NQ = 4


HIGHEST = lax.Precision.HIGHEST


def split_three(values):
    upper = values.astype(jnp.bfloat16)
    remain = values - lax.optimization_barrier(upper).astype(jnp.float32)
    middle = remain.astype(jnp.bfloat16)
    lower = (remain - lax.optimization_barrier(middle).astype(jnp.float32)).astype(jnp.bfloat16)
    return jnp.concatenate([upper, middle, lower], axis=-1)


def table_lookup(pieces, row_ids, piece_count, block_rows):
    table_rows = pieces.shape[0]
    width = pieces.shape[1] // piece_count
    columns = jnp.arange(table_rows, dtype=jnp.int32)

    def one_block(block_ids):
        onehot = (block_ids[:, None] == columns[None, :]).astype(jnp.bfloat16)
        picked = jnp.dot(onehot, pieces, preferred_element_type=jnp.float32)
        summed = picked[:, :width]
        for piece_index in range(1, piece_count):
            summed = summed + picked[:, piece_index * width : (piece_index + 1) * width]
        return summed

    return lax.map(one_block, row_ids.reshape(-1, block_rows)).reshape(-1, width)


def table_scatter(row_ids, values, table_rows, block_rows):
    width = values.shape[1]
    columns = jnp.arange(table_rows, dtype=jnp.int32)

    def add_block(running, inputs):
        block_ids, block_values = inputs
        onehot = (block_ids[:, None] == columns[None, :]).astype(jnp.bfloat16)
        pieces = split_three(block_values)
        added = lax.dot_general(
            onehot, pieces, (((0,), (0,)), ((), ())), preferred_element_type=jnp.float32
        )
        return (running + added, None)

    start_sum = jnp.zeros((table_rows, 3 * width), jnp.float32)
    summed, _ = lax.scan(
        add_block,
        start_sum,
        (row_ids.reshape(-1, block_rows), values.reshape(-1, block_rows, width)),
    )
    return summed[:, :width] + summed[:, width : 2 * width] + summed[:, 2 * width :]


def local_backward(
    heads,
    tail_part,
    fetched,
    rel_table,
    proj,
    tail_ids,
    rel_ids,
    qual_rels,
    qual_refs,
    neg_ids,
    count,
):
    edge_total = heads.shape[0]
    width = heads.shape[1]
    block_rows = min(512, edge_total)
    rel_pieces = split_three(rel_table)
    rel_all_ids = jnp.concatenate([rel_ids[None, :], qual_rels.T], axis=0).reshape(-1)
    rel_looked = table_lookup(rel_pieces, rel_all_ids, 3, block_rows).reshape(
        NQ + 1, edge_total, width
    )
    rel_rows = rel_looked[0]
    ref_all_ids = qual_refs.T.reshape(-1)
    fetched_rows = table_lookup(fetched, ref_all_ids, 1, block_rows).reshape(NQ, edge_total, width)
    composed = jnp.zeros(heads.shape, jnp.float32)
    for qual_index in range(NQ):
        composed = composed + rel_looked[qual_index + 1] * fetched_rows[qual_index]
    relation = rel_rows + jnp.dot(composed, proj, precision=HIGHEST)
    query = (heads * relation).astype(jnp.bfloat16)
    tails = tail_part[tail_ids]
    negatives = tail_part[neg_ids]
    positive = jnp.sum(query.astype(jnp.float32) * tails.astype(jnp.float32), axis=1)
    live_mask = (jnp.arange(edge_total, dtype=jnp.int32) < count).astype(jnp.float32)
    block_count = edge_total // block_rows

    def block_step(neg_acc, inputs):
        query_block, tail_block, positive_block, live_block = inputs
        scores = jnp.dot(query_block, negatives.T, preferred_element_type=jnp.float32)
        top_score = jnp.maximum(jnp.max(scores, axis=1), positive_block)
        neg_exp = jnp.exp(scores - top_score[:, None])
        pos_exp = jnp.exp(positive_block - top_score)
        total_exp = jnp.sum(neg_exp, axis=1) + pos_exp
        pos_coef = pos_exp / total_exp * live_block - live_block
        neg_round = (neg_exp / total_exp[:, None] * live_block[:, None]).astype(jnp.bfloat16)
        grad_block = pos_coef[:, None] * tail_block.astype(jnp.float32) + jnp.dot(
            neg_round, negatives, preferred_element_type=jnp.float32
        )
        neg_acc = neg_acc + jnp.dot(neg_round.T, query_block, preferred_element_type=jnp.float32)
        return (neg_acc, (grad_block, pos_coef))

    inputs = (
        query.reshape(block_count, block_rows, width),
        tails.reshape(block_count, block_rows, width),
        positive.reshape(block_count, block_rows),
        live_mask.reshape(block_count, block_rows),
    )
    negative_grad, (grad_blocks, coef_blocks) = lax.scan(
        block_step, jnp.zeros((negatives.shape[0], width), jnp.float32), inputs
    )
    query_grad = grad_blocks.reshape(edge_total, width)
    pos_coef = coef_blocks.reshape(edge_total)
    tail_grad = jax.ops.segment_sum(
        pos_coef[:, None] * query.astype(jnp.float32), tail_ids, tail_part.shape[0]
    )
    tail_grad = tail_grad + jax.ops.segment_sum(negative_grad, neg_ids, tail_part.shape[0])
    head_rows_grad = query_grad * relation
    relation_grad = query_grad * heads
    composed_grad = jnp.dot(relation_grad, proj.T, precision=HIGHEST)
    proj_grad = jnp.dot(composed.T, relation_grad, precision=HIGHEST)
    rel_terms = [relation_grad]
    fetched_terms = []
    for qual_index in range(NQ):
        rel_terms.append(composed_grad * fetched_rows[qual_index])
        fetched_terms.append(composed_grad * rel_looked[qual_index + 1])
    rel_grad = table_scatter(rel_all_ids, jnp.concatenate(rel_terms, axis=0), REL, block_rows)
    fetched_grad = table_scatter(
        ref_all_ids, jnp.concatenate(fetched_terms, axis=0), fetched.shape[0], block_rows
    )
    return (head_rows_grad, tail_grad, fetched_grad, rel_grad, proj_grad)


def fetch_rows(qual_req, qual_table):
    width = qual_table.shape[1]
    group_count = lax.axis_size("grp")
    member_count = lax.axis_size("blk")
    shaped = qual_req.reshape(group_count * member_count, -1)
    arrived = lax.all_to_all(shaped, ("grp", "blk"), split_axis=0, concat_axis=0, tiled=True)
    picked = jnp.take(qual_table, arrived, axis=0)
    fetched = lax.all_to_all(picked, ("grp", "blk"), split_axis=0, concat_axis=0, tiled=True)
    return (fetched.reshape(-1, width), arrived.reshape(-1))


def return_grads(fetched_grad):
    width = fetched_grad.shape[1]
    group_count = lax.axis_size("grp")
    member_count = lax.axis_size("blk")
    shaped = fetched_grad.reshape(group_count * member_count, -1, width)
    returned = lax.all_to_all(shaped, ("grp", "blk"), split_axis=0, concat_axis=0, tiled=True)
    return returned.reshape(-1, width)


def body(
    head_table,
    tail_table,
    qual_table,
    rel_table,
    proj,
    head_id,
    tail_id,
    rel_id,
    qual_rel,
    qual_ref,
    qual_req,
    neg_id,
    edge_count,
):
    head_rows = head_table.shape[0]
    member_count = lax.axis_size("blk")
    group_table = lax.all_gather(head_table, "blk", axis=0, tiled=True)
    heads = jnp.take(group_table, head_id, axis=0).astype(jnp.float32)
    fetched, arrived_ids = fetch_rows(qual_req, qual_table)
    head_rows_grad, tail_grad, fetched_grad, rel_part, proj_part = local_backward(
        heads,
        tail_table,
        fetched,
        rel_table,
        proj,
        tail_id,
        rel_id,
        qual_rel,
        qual_ref,
        neg_id,
        edge_count[0],
    )
    group_grad = jax.ops.segment_sum(head_rows_grad, head_id, head_rows * member_count)
    head_grad = lax.psum_scatter(group_grad, "blk", scatter_dimension=0, tiled=True)
    returned = return_grads(fetched_grad)
    qual_grad = jax.ops.segment_sum(returned, arrived_ids, qual_table.shape[0])
    rel_grad, proj_grad = lax.psum((rel_part, proj_part), ("grp", "blk"))
    return (head_grad, tail_grad, qual_grad, rel_grad, proj_grad)


def solution(mesh):
    in_specs = (
        P(("grp", "blk"), None),
        P(("grp", "blk"), None),
        P(("grp", "blk"), None),
        P(),
        P(),
        P(("grp", "blk")),
        P(("grp", "blk")),
        P(("grp", "blk")),
        P(("grp", "blk"), None),
        P(("grp", "blk"), None),
        P(("grp", "blk")),
        P(("grp", "blk")),
        P(("grp", "blk")),
    )
    out_specs = (
        P(("grp", "blk"), None),
        P(("grp", "blk"), None),
        P(("grp", "blk"), None),
        P(),
        P(),
    )
    return jax.shard_map(body, mesh=mesh, in_specs=in_specs, out_specs=out_specs, check_vma=False)
```

profile of v0, /device:TPU:0, one launch (start us, length us, event | category | flops | bytes accessed | tf_op | source)
XLA Modules:
  0.0 383.8 jit_solution(11954736086325789900)
XLA Ops:
  7.9 1.4 all_to_all.16
  9.3 7.3 %all-to-all-start = ((s32[32,1,8]{2,1,0:T(1,128)}), s32[32,1,8]{2,1,0:T(1,128)S(1)}, u32[]{:S(2)}, u32[]{:S(2)}) async-start(s32[32,1,8]{2,1,0:T(1,128)} %bitcast.5), calls=%async_computation | async-start | bytes 32768 | tf_op jit(solution)/shard_map/all_to_all | solution.py:145
  21.8 15.5 %while.59 = (s32[]{:T(128)}, f32[10,512,256]{2,1,0:T(8,128)}, s32[10,512]{1,0:T(8,128)S(1)}, bf16[512,768]{1,0:T(8,128)(2,1)S(1)}, s32[]{:T(128)}) while((s32[]{:T(128)}, f32[10,512,256]{2,1,0:T(8,128)}, s32[10,512]{1,0:T(8,128)S(1)}, bf16[512,768]{1,0:T(8,128)(2,1)S(1)}, s32[]{:T(128)}) %tuple.120), condition=%wide.region_1.2_spmd.clone, body=%wide.region_0.1_spmd.clone.sunk | while | flops 403177472 | bytes 4462669 | solution.py:34
  37.5 5.0 %gather_fusion.3 = bf16[1024,256]{1,0:T(8,128)(2,1)} fusion(bf16[4096,256]{1,0:T(8,128)(2,1)S(1)} %copy-done, s32[1024]{0:T(1024)S(1)} %get-tuple-element.335), kind=kCustom, calls=%fused_computation.3 | custom fusion | bytes 1052672 | tf_op jit(solution)/shard_map/gather | solution.py:88
  42.6 2.1 gather_fusion.1
  45.4 5.8 %all-to-all-start.1 = ((bf16[32,8,256]{2,1,0:T(8,128)(2,1)}), bf16[32,8,256]{2,1,0:T(8,128)(2,1)S(1)}, u32[]{:S(2)}, u32[]{:S(2)}) async-start(bf16[32,8,256]{2,1,0:T(8,128)(2,1)} %bitcast_select_fusion), calls=%async_computation.1 | async-start | bytes 262144 | tf_op jit(solution)/shard_map/all_to_all | solution.py:147
  51.3 4.9 %fusion.84 = (f32[2,512,256]{2,1,0:T(8,128)}, f32[2,512,256]{2,1,0:T(8,128)}, f32[2,512,256]{2,1,0:T(8,128)}, f32[2,512,256]{2,1,0:T(8,128)}, f32[2,512,256]{2,1,0:T(8,128)}) fusion(f32[10,512,256]{2,1,0:T(8,128)} %get-tuple-element.162), kind=kLoop, calls=%fused_computation.160 | loop fusion | bytes 10485760 | tf_op jit(solution)/shard_map/slice | solution.py:85
  56.2 4.9 %gather_fusion.2 = bf16[1024,256]{1,0:T(8,128)(2,1)} fusion(bf16[4096,256]{1,0:T(8,128)(2,1)S(1)} %copy-done, s32[1024]{0:T(1024)S(1)} %get-tuple-element.333), kind=kCustom, calls=%fused_computation.2 | custom fusion | bytes 1052672 | tf_op jit(solution)/shard_map/gather | solution.py:89
  61.1 8.7 %while.60 = (s32[]{:T(128)}, f32[8,512,256]{2,1,0:T(8,128)}, s32[8,512]{1,0:T(8,128)S(1)}, bf16[256,256]{1,0:T(8,128)(2,1)S(1)}, s32[]{:T(128)}) while((s32[]{:T(128)}, f32[8,512,256]{2,1,0:T(8,128)}, s32[8,512]{1,0:T(8,128)S(1)}, bf16[256,256]{1,0:T(8,128)(2,1)S(1)}, s32[]{:T(128)}) %tuple.147), condition=%wide.region_3.4_spmd.clone, body=%wide.region_2.3_spmd.clone.sunk | while | flops 67239936 | bytes 661581 | solution.py:34
  69.8 2.6 fusion.85
  74.4 1.6 fusion.49
  76.0 4.9 %gather_fusion = bf16[1024,256]{1,0:T(8,128)(2,1)S(1)} fusion(bf16[2048,256]{1,0:T(8,128)(2,1)} %all-gather.2.cloned.1.call-done, s32[1024]{0:T(1024)S(1)} %get-tuple-element.336), kind=kCustom, calls=%fused_computation | custom fusion | bytes 1052672 | tf_op jit(solution)/shard_map/jit(_take)/gather | solution.py:178
  80.9 4.0 %fusion.48 = (f32[1024]{0:T(1024)S(1)}, bf16[1024,256]{1,0:T(8,128)(2,1)S(1)}, f32[1024,256]{1,0:T(8,128)}) fusion(bf16[1024,256]{1,0:T(8,128)(2,1)} %gather_fusion.3, bf16[1024,256]{1,0:T(8,128)(2,1)S(1)} %gather_fusion, pred[1024]{0:T(1024)(128)(4,1)S(1)} %compare_and_fusion.1, f32[1024,256]{1,0:T(8,128)} %bitcast.182, f32[1024,256]{1,0:T(8,128)} %fusion.49, ...), kind=kOutput, calls=%fused_computation.89 | convolution fusion | flops 807664640 | bytes 4985856 | tf_op jit(solution)/shard_map/dot_general | solution.py:86
  84.9 9.7 %while.61 = (s32[]{:T(128)}, f32[1024,256]{1,0:T(8,128)S(1)}, f32[2,512,256]{2,1,0:T(8,128)}, f32[2,512]{1,0:T(2,128)S(1)}, bf16[2,512,256]{2,1,0:T(8,128)(2,1)S...) while((s32[]{:T(128)}, f32[1024,256]{1,0:T(8,128)S(1)}, ...), condition=%wide.region_8.9_spmd.clone, body=%wide.region_5.8_spmd.clone.sunk | while | flops 809899008 | bytes 13947031 | solution.py:115
  86.7 2.2 fusion.125
  91.5 2.2 fusion.125
  94.6 3.0 convert_multiply_fusion.3
  97.7 5.7 %bitcast_multiply_fusion.1 = (f32[1024,256]{1,0:T(8,128)S(1)}, f32[1024,256]{1,0:T(8,128)S(1)}, f32[1024,256]{1,0:T(8,128)S(1)}, f32[1024,256]{1,0:T(8,128)S(1)}...) fusion(f32[2,512,256]{2,1,0:T(8,128)} %copy-done.15, ...), kind=kOutput, calls=%fused_computation.91 | convolution fusion | flops 807403520 | bytes 18087936 | tf_op jit(solution)/shard_map/dot_general | solution.py:126
  103.8 2.3 copy-done.3
  106.0 57.0 %while.63 = (s32[]{:T(128)}, f32[512,768]{1,0:T(8,128)}, s32[10,512]{1,0:T(8,128)S(1)}, f32[10,512,256]{2,1,0:T(8,128)}, s32[]{:T(128)}, /*index=5*/s32[]{:T(128)}) while((s32[]{:T(128)}, f32[512,768]{1,0:T(8,128)}, s32[10,512]{1,0:T(8,128)S(1)}, f32[10,512,256]{2,1,0:T(8,128)}, s32[]{:T(128)}, /*index=5*/s32[]{:T(128)}) %tuple.148), condition=%wide.region_16.17_spmd.clone, body=%wide.region_15.16_spmd.clone.sunk | while | flops 407109632 | bytes 19404960 | solution.py:51
  106.0 1.2 bitcast_convert_fusion.5
  110.6 1.2 copy-done.21
  111.7 1.2 bitcast_convert_fusion.5
  116.3 1.2 copy-done.21
  117.4 1.2 bitcast_convert_fusion.5
  122.0 1.2 copy-done.21
  123.1 1.2 bitcast_convert_fusion.5
  127.7 1.2 copy-done.21
  128.9 1.2 bitcast_convert_fusion.5
  133.4 1.2 copy-done.21
  134.6 1.2 bitcast_convert_fusion.5
  140.3 1.2 bitcast_convert_fusion.5
  146.0 1.2 bitcast_convert_fusion.5
  151.7 1.2 bitcast_convert_fusion.5
  157.4 1.2 bitcast_convert_fusion.5
  163.1 2.4 slice_add_fusion.2
  165.4 6.4 %convolution_bitcast_fusion.1 = f32[256,256]{1,0:T(8,128)} fusion(f32[2,512,256]{2,1,0:T(8,128)S(1)} %copy-done.23, bf16[2,512,256]{2,1,0:T(8,128)(2,1)S(1)} %bitcast.180, pred[2,512]{1,0:T(4,128)(4,1)S(1)} %broadcast_in_dim.111, f32[8,512,256]{2,1,0:T(8,128)} %get-tuple-element.163, f32[10,512,256]{2,1,0:T(8,128)} %get-tuple-element.162), kind=kOutput, calls=%fused_computation.87 | convolution fusion | flops 807927808 | bytes 10224640 | tf_op jit(solution)/shard_map/dot_general | solution.py:127
  172.1 8.0 %scatter_custom_fusion = f32[2048,256]{1,0:T(8,128)} fusion(s32[1024]{0:T(1024)} %param.28, f32[1024,256]{1,0:T(8,128)} %get-tuple-element.331, f32[]{:T(128)} %constant.75.clone.1), kind=kCustom, calls=%fused_computation.115 | custom fusion | flops 262144 | bytes 2097664 | tf_op jit(solution)/shard_map/scatter-add | solution.py:193
  180.2 4.1 %pad_maximum_fusion = f32[4096,256]{1,0:T(8,128)} fusion(f32[1024,256]{1,0:T(8,128)S(1)} %copy-done.19, f32[1024,256]{1,0:T(8,128)} %get-tuple-element.327, f32[1024,256]{1,0:T(8,128)} %get-tuple-element.328, f32[1024,256]{1,0:T(8,128)} %get-tuple-element.329), kind=kLoop, calls=%fused_computation.76 | loop fusion | flops 3145728 | bytes 8388608 | tf_op jit(solution)/shard_map/concatenate | solution.py:135
  184.3 39.2 %while.62 = (s32[]{:T(128)}, f32[256,768]{1,0:T(8,128)}, s32[8,512]{1,0:T(8,128)S(1)}, f32[8,512,256]{2,1,0:T(8,128)}, s32[]{:T(128)}, /*index=5*/s32[]{:T(128)}) while((s32[]{:T(128)}, f32[256,768]{1,0:T(8,128)}, s32[8,512]{1,0:T(8,128)S(1)}, f32[8,512,256]{2,1,0:T(8,128)}, s32[]{:T(128)}, /*index=5*/s32[]{:T(128)}) %tuple.149), condition=%wide.region_13.14_spmd.clone, body=%wide.region_12.13_spmd.clone.sunk | while | flops 205258752 | bytes 11540639 | solution.py:51
  223.5 1.9 add_bitcast_fusion
  225.4 5.9 %all-to-all-start.2 = ((f32[32,8,256]{2,1,0:T(8,128)}), f32[32,8,256]{2,1,0:T(8,128)S(1)}, u32[]{:S(2)}, u32[]{:S(2)}) async-start(f32[32,8,256]{2,1,0:T(8,128)} %add_bitcast_fusion), calls=%async_computation.3 | async-start | bytes 524288 | tf_op jit(solution)/shard_map/all_to_all | solution.py:156
  233.7 14.8 %scatter_custom_fusion.1 = f32[4096,256]{1,0:T(8,128)} fusion(s32[2048]{0:T(1024)S(1)} %bitcast.200, f32[1024,256]{1,0:T(8,128)S(1)} %get-tuple-element.166, f32[]{:T(128)} %constant.110, f32[1024,256]{1,0:T(8,128)} %convert_multiply_fusion.1, f32[]{:T(128)} %constant.75.clone.1), kind=kCustom, calls=%fused_computation.77 | custom fusion | flops 1048576 | bytes 6291464 | tf_op jit(solution)/shard_map/add | solution.py:123
  248.5 2.9 scatter_custom_fusion.2
  251.5 51.1 %all-reduce.3.cloned.1.call-done = (f32[512,256]{1,0:T(8,128)}, f32[256,256]{1,0:T(8,128)}) async-done(((f32[512,256]{1,0:T(8,128)}, f32[256,256]{1,0:T(8,128)}), (f32[512,256]{1,0:T(8,128)}, f32[256,256]{1,0:T(8,128)})) %all-reduce.3.cloned.1.call-update) | async-done | bytes 786448 | tf_op jit(solution)/shard_map/psum | solution.py:197
  302.6 71.2 %reduce-scatter.2.cloned.1.call-done = f32[256,256]{1,0:T(8,128)} async-done(((f32[2048,256]{1,0:T(8,128)}), f32[256,256]{1,0:T(8,128)}) %reduce-scatter.2.cloned.1.call-update) | async-done | bytes 262160 | tf_op jit(solution)/shard_map/reduce_scatter | solution.py:194
  373.8 1.9 copy.71
  375.6 1.7 copy.72
  (305 shorter events, 118.3 us)
Async XLA Ops:
  7.2 30.3 %copy-start = (bf16[4096,256]{1,0:T(8,128)(2,1)S(1)}, bf16[4096,256]{1,0:T(8,128)(2,1)}, u32[]{:S(2)}) copy-start(bf16[4096,256]{1,0:T(8,128)(2,1)} %param.24) | copy-start | bytes 6291460
  7.2 14.5 %copy-start.16 = (f32[512,256]{1,0:T(8,128)S(1)}, f32[512,256]{1,0:T(8,128)}, u32[]{:S(2)}) copy-start(f32[512,256]{1,0:T(8,128)} %param.26) | copy-start | bytes 1572868
  7.2 68.8 %all-gather.2.cloned.1.call-start = ((), (), s32[]{:S(2)}) async-start(), calls=%async_computation.4 | async-start | bytes 1179648 | tf_op jit(solution)/shard_map/all_gather | solution.py:177
  9.3 33.1 %all-to-all-start = ((s32[32,1,8]{2,1,0:T(1,128)}), s32[32,1,8]{2,1,0:T(1,128)S(1)}, u32[]{:S(2)}, u32[]{:S(2)}) async-start(s32[32,1,8]{2,1,0:T(1,128)} %bitcast.5), calls=%async_computation | async-start | bytes 32768 | tf_op jit(solution)/shard_map/all_to_all | solution.py:145
  21.8 15.6 %copy-start.26 = (s32[1024,4]{0,1:T(4,128)S(1)}, s32[1024,4]{0,1:T(4,128)}, u32[]{:S(2)}) copy-start(s32[1024,4]{0,1:T(4,128)} %param.32) | copy-start | bytes 49156
  37.4 5.1 %copy-start.27 = (s32[1024]{0:T(1024)S(1)}, s32[1024]{0:T(1024)}, u32[]{:S(2)}) copy-start(s32[1024]{0:T(1024)} %param.34) | copy-start | bytes 12292
  45.4 15.7 %all-to-all-start.1 = ((bf16[32,8,256]{2,1,0:T(8,128)(2,1)}), bf16[32,8,256]{2,1,0:T(8,128)(2,1)S(1)}, u32[]{:S(2)}, u32[]{:S(2)}) async-start(bf16[32,8,256]{2,1,0:T(8,128)(2,1)} %bitcast_select_fusion), calls=%async_computation.1 | async-start | bytes 262144 | tf_op jit(solution)/shard_map/all_to_all | solution.py:147
  51.3 251.3 %all-reduce.3.cloned.1.call-start = ((), (), s32[]{:S(2)}) async-start(), calls=%async_computation.6 | async-start | bytes 1572864 | tf_op jit(solution)/shard_map/psum | solution.py:197
  69.8 4.6 %copy-start.4 = (f32[2,512,256]{2,1,0:T(8,128)S(1)}, f32[2,512,256]{2,1,0:T(8,128)}, u32[]{:S(2)}) copy-start(f32[2,512,256]{2,1,0:T(8,128)} %get-tuple-element.313) | copy-start | bytes 3145732
  69.8 4.6 %copy-start.6 = (f32[2,512,256]{2,1,0:T(8,128)S(1)}, f32[2,512,256]{2,1,0:T(8,128)}, u32[]{:S(2)}) copy-start(f32[2,512,256]{2,1,0:T(8,128)} %get-tuple-element.314) | copy-start | bytes 3145732
  69.8 4.6 %copy-start.8 = (f32[2,512,256]{2,1,0:T(8,128)S(1)}, f32[2,512,256]{2,1,0:T(8,128)}, u32[]{:S(2)}) copy-start(f32[2,512,256]{2,1,0:T(8,128)} %get-tuple-element.315) | copy-start | bytes 3145732
  69.8 4.6 %copy-start.10 = (f32[2,512,256]{2,1,0:T(8,128)S(1)}, f32[2,512,256]{2,1,0:T(8,128)}, u32[]{:S(2)}) copy-start(f32[2,512,256]{2,1,0:T(8,128)} %get-tuple-element.317) | copy-start | bytes 3145732
  72.4 1.3 copy-start.13
  72.5 1.6 copy-start.14
  72.5 2.0 copy-start.15
  76.0 4.9 %copy-start.22 = (f32[256,256]{1,0:T(8,128)S(1)}, f32[256,256]{1,0:T(8,128)}, u32[]{:S(2)}) copy-start(f32[256,256]{1,0:T(8,128)} %param.27) | copy-start | bytes 786436
  80.9 4.0 %copy-start.17 = (bf16[1024,256]{1,0:T(8,128)(2,1)}, bf16[1024,256]{1,0:T(8,128)(2,1)S(1)}, u32[]{:S(2)}) copy-start(bf16[1024,256]{1,0:T(8,128)(2,1)S(1)} %gather_fusion) | copy-start | bytes 1572868
  80.9 4.0 %copy-start.2 = (bf16[1024,256]{1,0:T(8,128)(2,1)S(1)}, bf16[1024,256]{1,0:T(8,128)(2,1)}, u32[]{:S(2)}) copy-start(bf16[1024,256]{1,0:T(8,128)(2,1)} %gather_fusion.2) | copy-start | bytes 1572868
  94.6 3.1 copy-start.5
  94.6 3.1 copy-start.7
  94.6 3.1 copy-start.9
  94.6 3.1 copy-start.11
  103.8 2.3 copy-start.3
  106.0 3.4 copy-start.20
  111.7 3.4 copy-start.20
  117.4 3.4 copy-start.20
  123.1 3.4 copy-start.20
  128.8 3.4 copy-start.20
  134.5 3.4 copy-start.20
  140.2 3.4 copy-start.20
  145.9 3.4 copy-start.20
  151.6 3.4 copy-start.20
  157.3 3.4 copy-start.20
  163.0 2.4 copy-start.18
  163.0 2.4 copy-start.23
  171.8 201.9 %reduce-scatter.2.cloned.1.call-start = ((), (), s32[]{:S(2)}) async-start(), calls=%async_computation.5 | async-start | bytes 2359296 | tf_op jit(solution)/shard_map/reduce_scatter | solution.py:194
  172.1 8.1 %copy-start.19 = (f32[1024,256]{1,0:T(8,128)S(1)}, f32[1024,256]{1,0:T(8,128)}, u32[]{:S(2)}) copy-start(f32[1024,256]{1,0:T(8,128)} %get-tuple-element.326) | copy-start | bytes 3145732
  184.3 46.9 %copy-start.28 = (s32[1024]{0:T(1024)S(1)}, s32[1024]{0:T(1024)}, u32[]{:S(2)}) copy-start(s32[1024]{0:T(1024)} %param.29) | copy-start | bytes 12292
  184.3 3.4 copy-start.24
  189.2 3.4 copy-start.24
  194.1 3.4 copy-start.24
  199.0 3.4 copy-start.24
  203.9 3.4 copy-start.24
  208.8 3.4 copy-start.24
  213.7 3.4 copy-start.24
  218.6 3.4 copy-start.24
  225.4 23.2 %all-to-all-start.2 = ((f32[32,8,256]{2,1,0:T(8,128)}), f32[32,8,256]{2,1,0:T(8,128)S(1)}, u32[]{:S(2)}, u32[]{:S(2)}) async-start(f32[32,8,256]{2,1,0:T(8,128)} %add_bitcast_fusion), calls=%async_computation.3 | async-start | bytes 524288 | tf_op jit(solution)/shard_map/all_to_all | solution.py:156
  233.7 143.6 %copy-start.1 = (bf16[4096,256]{1,0:T(8,128)(2,1)S(1)}, bf16[4096,256]{1,0:T(8,128)(2,1)}, u32[]{:S(2)}) copy-start(bf16[4096,256]{1,0:T(8,128)(2,1)} %param.24) | copy-start | bytes 6291460
  (19 other events, 19.9 us)
Sparse Core Ops, SparseCore 0:
  10.2 42.8 all-gather.1
  171.9 130.6 all-reduce.2
  307.1 66.5 reduce-scatter.1
where the time goes:
time: 386 us; the launch traced here: 384 us
  waiting for transfers between devices  123 us (32%)
  other arithmetic  97.4 us (25%)
  local copies, waits for them, and re-layouts  74.9 us (19%)
  matrix products  53.5 us (14%)
  starting transfers between devices  19.3 us (5%)
  between operations  14.8 us (4%)
    reduce_scatter x1, waiting for transfers between devices, body(): lax.psum_scatter(group_grad, 'blk', scatter_dimension=0, tiled=True)  71.2 us
    psum x1, waiting for transfers between devices, body(): rel_grad, proj_grad = lax.psum((rel_part, proj_part), ('grp', 'blk'))  51.1 us
    convert_element_type x18, local copies, waits for them, and re-layouts, split_three(): upper = values.astype(jnp.bfloat16)  21.1 us
    convert_element_type x19, other arithmetic, split_three(): middle = remain.astype(jnp.bfloat16)  21 us
    convert_element_type x19, other arithmetic, split_three(): (remain - lax.optimization_barrier(middle).astype(jnp.float32)).astype(jn...  20.4 us
    while x72, local copies, waits for them, and re-layouts  18.8 us
    dot_general x18, matrix products, add_block(): lax.dot_general(onehot, pieces, (((0,), (0,)), ((), ())), preferred_eleme...  15.3 us
    dot_general x18, matrix products, one_block(): picked = jnp.dot(onehot, pieces, preferred_element_type=jnp.float32)  14.9 us
  transfers between devices with their start and end apart: 6, of which 2 were waited for; matrix products, arithmetic and copies ran while one was open for 30% of the time, Pallas kernels for 0%

commit v1 on v0

v1 whole, which is shorter than its diff:
```python
import functools

import jax
import jax.numpy as jnp
from jax import lax
from jax.experimental import pallas as pl
from jax.experimental.pallas import tpu as pltpu
from jax.sharding import PartitionSpec as P

BF = jnp.bfloat16
F32 = jnp.float32
VMEM_BYTES = 56 * 1024 * 1024
BOTH = ("grp", "blk")
BLOCK = 256


def nn(a, b):
    return jnp.dot(a, b, preferred_element_type=F32)


def nt(a, b):
    return lax.dot_general(a, b, (((1,), (1,)), ((), ())), preferred_element_type=F32)


def pieces(values, count):
    out = []
    for _ in range(count):
        part = values.astype(BF)
        out.append(part)
        values = values - part.astype(F32)
    return out


def onehot(ids_row, first, rows):
    iota = lax.broadcasted_iota(jnp.int32, (rows, ids_row.shape[1]), 0)
    return jnp.where(iota == ids_row - first, 1.0, 0.0).astype(BF)


def lookup_kernel(rel_ref, tail_ref, rel_ids, tn_ids, rel_out, tails_out, negt_out, neg_out, rel_t, tail_t):
    width = rel_ref.shape[1]
    rel_rows = rel_ref.shape[0]
    tail_rows = tail_ref.shape[0]
    edges = rel_ids.shape[1]
    for index, part in enumerate(pieces(rel_ref[...].T, 3)):
        rel_t[index * width : (index + 1) * width, :] = part

    @pl.loop(0, tail_rows // BLOCK)
    def _(step):
        start = pl.multiple_of(step * BLOCK, BLOCK)
        tail_t[:, pl.ds(start, BLOCK)] = tail_ref[pl.ds(start, BLOCK), :].T

    for which in range(rel_ids.shape[0]):

        @pl.loop(0, edges // BLOCK)
        def _(step):
            at = pl.ds(pl.multiple_of(step * BLOCK, BLOCK), BLOCK)
            got = nn(rel_t[...], onehot(rel_ids[which : which + 1, at], 0, rel_rows))
            rel_out[which, :, at] = got[:width] + got[width : 2 * width] + got[2 * width :]

    for which, out in ((0, tails_out), (1, negt_out)):

        @pl.loop(0, edges // BLOCK)
        def _(step):
            at = pl.ds(pl.multiple_of(step * BLOCK, BLOCK), BLOCK)
            got = nn(tail_t[...], onehot(tn_ids[which : which + 1, at], 0, tail_rows))
            out[:, at] = got.astype(BF)
            if which == 1:
                neg_out[at, :] = got.T.astype(BF)


def edge_kernel(
    count_ref,
    rel_ref,
    fetched_ref,
    ref_ids,
    head_ref,
    head_ids,
    proj_ref,
    tails_ref,
    negt_ref,
    neg_ref,
    head_out,
    rg_out,
    cg_out,
    comp_out,
    nr_out,
    query_out,
    pq_out,
    fetched_t,
    head_terms,
    proj_n,
    proj_t,
):
    width, edges = tails_ref.shape
    slots = fetched_ref.shape[0]
    owners, _, head_rows = head_ref.shape
    fetched_t[...] = fetched_ref[...].astype(F32).T.astype(BF)
    for index, part in enumerate(pieces(proj_ref[...], 2)):
        proj_n[index] = part
    for index, part in enumerate(pieces(proj_ref[...].T, 2)):
        proj_t[index] = part

    @pl.loop(0, edges // BLOCK)
    def _(step):
        start = pl.multiple_of(step * BLOCK, BLOCK)
        at = pl.ds(start, BLOCK)
        composed = jnp.zeros((width, BLOCK), F32)
        for k in range(ref_ids.shape[0]):
            rows = nn(fetched_t[...], onehot(ref_ids[k : k + 1, at], 0, slots))
            composed = composed + rel_ref[k + 1, :, at] * rows
        comp_hi, comp_lo = pieces(composed, 2)
        comp_out[0, :, at] = comp_hi
        comp_out[1, :, at] = comp_lo
        relation = rel_ref[0, :, at] + (
            nn(proj_t[0], comp_hi) + (nn(proj_t[0], comp_lo) + nn(proj_t[1], comp_hi))
        )
        heads = jnp.zeros((width, BLOCK), F32)
        for owner in range(owners):
            heads = heads + nn(head_ref[owner], onehot(head_ids[:, at], owner * head_rows, head_rows))
        query = (heads * relation).astype(BF)
        query_out[:, at] = query
        query_f = query.astype(F32)
        tails = tails_ref[:, at].astype(F32)
        positive = jnp.sum(query_f * tails, axis=0, keepdims=True)
        scores = nn(neg_ref[...], query)
        top = jnp.maximum(jnp.max(scores, axis=0, keepdims=True), positive)
        neg_exp = jnp.exp(scores - top)
        pos_exp = jnp.exp(positive - top)
        total = jnp.sum(neg_exp, axis=0, keepdims=True) + pos_exp
        slot = lax.broadcasted_iota(jnp.int32, (1, BLOCK), 1) + start
        live = jnp.where(slot < count_ref[0], 1.0, 0.0)
        scale = live / total
        neg_round = (neg_exp * scale).astype(BF)
        nr_out[:, at] = neg_round
        coef = pos_exp * scale - live
        pq_out[:, at] = (coef * query_f).astype(BF)
        query_grad = coef * tails + nn(negt_ref[...], neg_round)
        head_terms[:, at] = (query_grad * relation).astype(BF)
        relation_grad = query_grad * heads
        rg_hi, rg_lo = pieces(relation_grad, 2)
        rg_out[0, :, at] = rg_hi
        rg_out[1, :, at] = rg_lo
        cg_out[:, at] = nn(proj_n[0], rg_hi) + (nn(proj_n[0], rg_lo) + nn(proj_n[1], rg_hi))

    @pl.loop(0, owners)
    def _(owner):
        at = pl.ds(pl.multiple_of(owner * head_rows, head_rows), head_rows)
        head_out[at, :] = nt(onehot(head_ids[...], owner * head_rows, head_rows), head_terms[...]).astype(BF)


def relation_kernel(rel_ref, fetched_ref, ref_ids, rel_ids, rg_ref, cg_ref, comp_ref, sums_out, fetched_out, fetched_t):
    rel_rows = sums_out.shape[0] - rg_ref.shape[1]
    slots = fetched_ref.shape[0]
    fetched_t[...] = fetched_ref[...].astype(F32).T.astype(BF)
    comp_grad = cg_ref[...]
    rel_sum = nt(onehot(rel_ids[0:1, :], 0, rel_rows), rg_ref[0])
    fetched_sum = jnp.zeros(fetched_ref.shape, F32)
    for k in range(ref_ids.shape[0]):
        hot = onehot(ref_ids[k : k + 1, :], 0, slots)
        rows = nn(fetched_t[...], hot)
        rel_sum = rel_sum + nt(onehot(rel_ids[k + 1 : k + 2, :], 0, rel_rows), (comp_grad * rows).astype(BF))
        fetched_sum = fetched_sum + nt(hot, (comp_grad * rel_ref[k + 1]).astype(BF))
    sums_out[:rel_rows, :] = rel_sum.astype(BF)
    fetched_out[...] = fetched_sum.astype(BF)
    proj_sum = nt(comp_ref[0], rg_ref[0]) + (nt(comp_ref[0], rg_ref[1]) + nt(comp_ref[1], rg_ref[0]))
    sums_out[rel_rows:, :] = proj_sum.astype(BF)


def tail_kernel(tn_ids, nr_ref, query_ref, pq_ref, tail_out, terms):
    edges = query_ref.shape[1]
    rows = tail_out.shape[0]
    step = pl.program_id(0)

    @pl.when(step == 0)
    def _():
        terms[:edges, :] = pq_ref[...].astype(F32).T.astype(BF)
        terms[edges:, :] = nt(nr_ref[...], query_ref[...]).astype(BF)

    first = step * rows
    tail_out[...] = nn(onehot(tn_ids[0:1, :], first, rows), terms[:edges, :]) + nn(
        onehot(tn_ids[1:2, :], first, rows), terms[edges:, :]
    )


def call(kernel, outs, scratch, cost, *args, smem=()):
    specs = [
        pl.BlockSpec(memory_space=pltpu.SMEM if index in smem else pltpu.VMEM) for index in range(len(args))
    ]
    return pl.pallas_call(
        kernel,
        out_shape=[jax.ShapeDtypeStruct(shape, dtype) for shape, dtype in outs],
        in_specs=specs,
        out_specs=[pl.BlockSpec(memory_space=pltpu.VMEM)] * len(outs),
        scratch_shapes=[pltpu.VMEM(shape, dtype) for shape, dtype in scratch],
        compiler_params=pltpu.CompilerParams(vmem_limit_bytes=VMEM_BYTES),
        cost_estimate=pl.CostEstimate(flops=cost, bytes_accessed=1 << 22, transcendentals=0),
    )(*args)


def exchange(values, axes):
    return lax.all_to_all(values, axes, split_axis=0, concat_axis=0, tiled=True)


def body(
    head_table,
    tail_table,
    qual_table,
    rel_table,
    proj,
    head_id,
    tail_id,
    rel_id,
    qual_rel,
    qual_ref,
    qual_req,
    neg_id,
    edge_count,
):
    head_rows, width = head_table.shape
    tail_rows = tail_table.shape[0]
    qual_rows = qual_table.shape[0]
    rel_rows = rel_table.shape[0]
    edges = head_id.shape[0]
    negs = neg_id.shape[0]
    slots = qual_req.shape[0]
    members = lax.axis_size("blk")
    devices = lax.axis_size("grp") * members

    arrived = exchange(qual_req.reshape(devices, -1), BOTH)
    picked = jnp.take(qual_table, arrived, axis=0)
    fetched = exchange(picked, BOTH).reshape(slots, width)
    head_all = exchange(jnp.broadcast_to(head_table.T[None], (members, width, head_rows)), "blk")

    rel_ids = jnp.concatenate([rel_id[None, :], qual_rel.T], axis=0)
    ref_ids = qual_ref.T
    tn_ids = jnp.stack([tail_id, neg_id])
    rel_looked, tails, neg_t, neg = call(
        lookup_kernel,
        [((5, width, edges), F32), ((width, edges), BF), ((width, negs), BF), ((negs, width), BF)],
        [((3 * width, rel_rows), BF), ((width, tail_rows), BF)],
        8 << 30,
        rel_table,
        tail_table,
        rel_ids,
        tn_ids,
    )
    head_part, rg, cg, comp, neg_round, query, pq = call(
        edge_kernel,
        [
            ((members * head_rows, width), BF),
            ((2, width, edges), BF),
            ((width, edges), F32),
            ((2, width, edges), BF),
            ((negs, edges), BF),
            ((width, edges), BF),
            ((width, edges), BF),
        ],
        [((width, slots), BF), ((width, edges), BF), ((2, width, width), BF), ((2, width, width), BF)],
        8 << 30,
        edge_count,
        rel_looked,
        fetched,
        ref_ids,
        head_all,
        head_id[None, :],
        proj,
        tails,
        neg_t,
        neg,
        smem=(0,),
    )
    sums_part, fetched_part = call(
        relation_kernel,
        [((rel_rows + width, width), BF), ((slots, width), BF)],
        [((width, slots), BF)],
        4 << 30,
        rel_looked,
        fetched,
        ref_ids,
        rel_ids,
        rg,
        cg,
        comp,
    )
    head_got = exchange(head_part.reshape(members, head_rows, width), "blk")
    sums_got = exchange(sums_part.reshape(devices, -1, width), BOTH)
    sums_own = jnp.sum(sums_got.astype(F32), axis=0).astype(BF)
    sums_all = exchange(jnp.broadcast_to(sums_own[None], (devices,) + sums_own.shape), BOTH)
    returned = exchange(fetched_part.reshape(devices, -1, width), BOTH).reshape(-1, width)

    block = min(512, tail_rows)
    tail_grad = pl.pallas_call(
        tail_kernel,
        out_shape=jax.ShapeDtypeStruct((tail_rows, width), F32),
        grid=(tail_rows // block,),
        in_specs=[pl.BlockSpec(memory_space=pltpu.VMEM)] * 4,
        out_specs=pl.BlockSpec((block, width), lambda i: (i, 0)),
        scratch_shapes=[pltpu.VMEM((edges + negs, width), BF)],
        compiler_params=pltpu.CompilerParams(vmem_limit_bytes=VMEM_BYTES),
        cost_estimate=pl.CostEstimate(flops=8 << 30, bytes_accessed=1 << 22, transcendentals=0),
    )(tn_ids, neg_round, query, pq)

    head_grad = jnp.sum(head_got.astype(F32), axis=0)
    hot = (jnp.arange(qual_rows, dtype=jnp.int32)[:, None] == arrived.reshape(1, -1)).astype(BF)
    qual_grad = jnp.dot(hot, returned, preferred_element_type=F32)
    sums = sums_all.reshape(rel_rows + width, width).astype(F32)
    return (head_grad, tail_grad, qual_grad, sums[:rel_rows], sums[rel_rows:])


def solution(mesh):
    rows = P(BOTH, None)
    ids = P(BOTH)
    in_specs = (rows, rows, rows, P(), P(), ids, ids, ids, rows, rows, ids, ids, ids)
    out_specs = (rows, rows, rows, P(), P())
    return jax.shard_map(body, mesh=mesh, in_specs=in_specs, out_specs=out_specs, check_vma=False)
```

time: 386 us -> 158 us (0.41)
  other arithmetic: 97.4 us -> 3.69 us
  waiting for transfers between devices: 123 us -> 31.8 us
  local copies, waits for them, and re-layouts: 74.9 us -> 7.27 us
  Pallas kernels: 0 us -> 54 us
  matrix products: 53.5 us -> 1.29 us
  blocking collectives: 0 us -> 46.3 us
  between operations: 14.8 us -> 1.43 us
  starting transfers between devices: 19.3 us -> 12.3 us
    reduce_scatter x1 -> x0, waiting for transfers between devices: 71.2 us -> none  [body(): lax.psum_scatter(group_grad, 'blk', scatter_dimension=0, tiled=True)]
    pallas_call x0 -> x4, Pallas kernels: none -> 54 us  [the longest x3 44.6 us: call(): pl.pallas_call(kernel, out_shape=[jax.ShapeDtypeStruct(shape, dtype) for...]
    dot_general x45 -> x1, matrix products: 53.5 us -> 1.29 us  [body(): qual_grad = jnp.dot(hot, returned, preferred_element_type=F32)]
    psum x1 -> x0, waiting for transfers between devices: 51.1 us -> none  [body(): rel_grad, proj_grad = lax.psum((rel_part, proj_part), ('grp', 'blk'))]
    all_to_all x0 -> x3, blocking collectives: none -> 46.3 us  [exchange(): return lax.all_to_all(values, axes, split_axis=0, concat_axis=0, tiled=True)]
    convert_element_type x42 -> x1, other arithmetic: 43.7 us -> 0.08 us  [body(): sums = sums_all.reshape(rel_rows + width, width).astype(F32)]
    all_to_all x3 -> x4, waiting for transfers between devices: 0.01 us -> 31.8 us  [exchange(): return lax.all_to_all(values, axes, split_axis=0, concat_axis=0, tiled=True)]
    convert_element_type x18 -> x0, local copies, waits for them, and re-layouts: 21.1 us -> none  [split_three(): upper = values.astype(jnp.bfloat16)]
  transfers between devices with their start and end apart: 6 -> 4, of which waited for: 2 -> 4; matrix products, arithmetic and copies ran while one was open for 30% -> 4% of each run, Pallas kernels for 0% -> 18%
where the time goes in v1:
time: 158 us
  Pallas kernels  54 us (34%)
  blocking collectives  46.3 us (29%)
  waiting for transfers between devices  31.8 us (20%)
  starting transfers between devices  12.3 us (8%)
  local copies, waits for them, and re-layouts  7.27 us (5%)
  other arithmetic  3.69 us (2%)
    all_to_all x3, blocking collectives, exchange(): return lax.all_to_all(values, axes, split_axis=0, concat_axis=0, tiled=True)  46.3 us
    pallas_call x3, Pallas kernels, call(): pl.pallas_call(kernel, out_shape=[jax.ShapeDtypeStruct(shape, dtype) for...  44.6 us
    all_to_all x4, waiting for transfers between devices, exchange(): return lax.all_to_all(values, axes, split_axis=0, concat_axis=0, tiled=True)  31.8 us
    all_to_all x4, starting transfers between devices, exchange(): return lax.all_to_all(values, axes, split_axis=0, concat_axis=0, tiled=True)  12.3 us
    pallas_call x1, Pallas kernels, body(): pl.pallas_call(tail_kernel, out_shape=jax.ShapeDtypeStruct((tail_rows, wi...  9.36 us
  transfers between devices with their start and end apart: 4, of which 4 were waited for; matrix products, arithmetic and copies ran while one was open for 4% of the time, Pallas kernels for 18%

profile of v1, /device:TPU:0, one launch (start us, length us, event | category | flops | bytes accessed | tf_op | source)
XLA Modules:
  0.0 158.0 jit_solution(5912710266693692482)
XLA Ops:
  0.6 0.0 copy-start
  0.6 0.8 all_to_all.28
  1.5 14.2 %all_to_all.45 = s32[32,1,8]{2,1,0:T(1,128)S(1)} all-to-all(s32[32,1,8]{2,1,0:T(1,128)S(1)} %bitcast.31), channel_id=1, replica_groups=mesh['grp'=4,'blk'=8] {'grp','blk'}, dimensions={0} | all-to-all | bytes 2048 | tf_op jit(solution)/shard_map/all_to_all | solution.py:201
  15.7 0.1 reshape.79
  15.8 0.0 copy-done
  15.8 1.2 gather_fusion
  17.0 0.0 copy-start.4
  17.0 0.0 copy-start.5
  17.0 0.0 copy-start.3
  17.0 0.0 copy-start.6
  17.0 0.8 bitcast_select_fusion
  17.8 2.6 %all-to-all-start.1 = ((bf16[32,8,256]{2,1,0:T(8,128)(2,1)}), bf16[32,8,256]{2,1,0:T(8,128)(2,1)S(1)}, u32[]{:S(2)}, u32[]{:S(2)}) async-start(bf16[32,8,256]{2,1,0:T(8,128)(2,1)} %bitcast_select_fusion), calls=%async_computation.1 | async-start | bytes 262144 | tf_op jit(solution)/shard_map/all_to_all | solution.py:201
  20.4 1.0 copy.21
  21.4 6.7 %all-to-all-done.1 = bf16[32,8,256]{2,1,0:T(8,128)(2,1)S(1)} async-done(((bf16[32,8,256]{2,1,0:T(8,128)(2,1)}), bf16[32,8,256]{2,1,0:T(8,128)(2,1)S(1)}, u32[]{:S(2)}, u32[]{:S(2)}) %all-to-all-start.1) | async-done | bytes 131104 | tf_op jit(solution)/shard_map/all_to_all | solution.py:201
  28.1 0.0 copy-start.2
  28.1 1.0 broadcast_in_dim.32
  29.1 3.6 %all-to-all-start.2 = ((bf16[8,256,256]{2,1,0:T(8,128)(2,1)}), bf16[8,256,256]{2,1,0:T(8,128)(2,1)S(1)}, u32[]{:S(2)}, u32[]{:S(2)}) async-start(bf16[8,256,256]{2,1,0:T(8,128)(2,1)} %broadcast_in_dim.32), calls=%async_computation.2 | async-start | bytes 2097152 | tf_op jit(solution)/shard_map/all_to_all | solution.py:201
  33.4 0.0 copy-done.4
  33.4 0.0 copy-done.5
  33.4 0.6 pad_add_fusion.1.tn_ids
  34.0 0.0 copy-done.3
  34.0 0.0 copy-done.6
  34.0 0.6 pad_add_fusion.rel_ids
  34.6 18.9 %shard_map.164 = (f32[5,256,1024]{2,1,0:T(8,128)}, bf16[256,1024]{1,0:T(8,128)(2,1)}, bf16[256,1024]{1,0:T(8,128)(2,1)}, bf16[1024,256]{1,0:T(8,128)(2,1)}) custom-call(f32[512,256]{1,0:T(8,128)} %rel_ref.1, bf16[4096,256]{1,0:T(8,128)(2,1)} %tail_ref.1, s32[5,1024]{1,0:T(8,128)} %pad_add_fusion.rel_ids, s32[2,1024]{1,0:T(2,128)} %pad_add_fusion.1.tn_ids), custom_call_target="tpu_custom_call" | custom-call | flops 8589934592 | bytes 4194304 | tf_op jit(solution)/shard_map/pallas_call | solution.py:189
  53.5 0.0 copy-done.2
  53.6 5.4 %all-to-all-done.2.head_ref = bf16[8,256,256]{2,1,0:T(8,128)(2,1)S(1)} async-done(((bf16[8,256,256]{2,1,0:T(8,128)(2,1)}), bf16[8,256,256]{2,1,0:T(8,128)(2,1)S(1)}, u32[]{:S(2)}, u32[]{:S(2)}) %all-to-all-start.2) | async-done | bytes 1048608 | tf_op jit(solution)/shard_map/all_to_all | solution.py:201
  58.9 0.0 copy-start.1
  59.0 1.0 copy-done.1
  59.9 18.2 %shard_map.165 = (bf16[2048,256]{1,0:T(8,128)(2,1)}, bf16[2,256,1024]{2,1,0:T(8,128)(2,1)}, f32[256,1024]{1,0:T(8,128)}, bf16[2,256,1024]{2,1,0:T(8,128)(2,1)}, ...) custom-call(s32[1]{0:T(128)S(6)} %copy.22.count_ref, ...), custom_call_target="tpu_custom_call" | custom-call | flops 8589934592 | bytes 4194304 | tf_op jit(solution)/shard_map/pallas_call | solution.py:189
  78.2 7.4 %shard_map.167 = (bf16[768,256]{1,0:T(8,128)(2,1)}, bf16[256,256]{1,0:T(8,128)(2,1)}) custom-call(f32[5,256,1024]{2,1,0:T(8,128)} %get-tuple-element.18.rel_ref, bf16[256,256]{1,0:T(8,128)(2,1)} %bitcast.29, s32[4,1024]{1,0:T(4,128)} %bitcast.37, s32[5,1024]{1,0:T(8,128)} %pad_add_fusion.rel_ids, bf16[2,256,1024]{2,1,0:T(8,128)(2,1)} %get-tuple-element.26.rg_ref, ...), custom_call_target="tpu_custom_call" | custom-call | flops 4294967296 | bytes 4194304 | tf_op jit(solution)/shard_map/pallas_call | solution.py:189
  85.6 16.3 %all_to_all.46 = bf16[32,24,256]{2,1,0:T(8,128)(2,1)S(1)} all-to-all(bf16[32,24,256]{2,1,0:T(8,128)(2,1)} %bitcast.24), channel_id=1, replica_groups=mesh['grp'=4,'blk'=8] {'grp','blk'}, dimensions={0} | all-to-all | bytes 786432 | tf_op jit(solution)/shard_map/all_to_all | solution.py:201
  101.9 2.6 %all-to-all-start.4 = ((bf16[32,8,256]{2,1,0:T(8,128)(2,1)}), bf16[32,8,256]{2,1,0:T(8,128)(2,1)S(1)}, u32[]{:S(2)}, u32[]{:S(2)}) async-start(bf16[32,8,256]{2,1,0:T(8,128)(2,1)} %bitcast.30), calls=%async_computation.4 | async-start | bytes 262144 | tf_op jit(solution)/shard_map/all_to_all | solution.py:201
  104.5 0.1 reduce_sum.22
  104.6 7.7 %all-to-all-done.4 = bf16[32,8,256]{2,1,0:T(8,128)(2,1)S(1)} async-done(((bf16[32,8,256]{2,1,0:T(8,128)(2,1)}), bf16[32,8,256]{2,1,0:T(8,128)(2,1)S(1)}, u32[]{:S(2)}, u32[]{:S(2)}) %all-to-all-start.4) | async-done | bytes 131104 | tf_op jit(solution)/shard_map/all_to_all | solution.py:201
  112.3 15.7 %all_to_all.47 = bf16[32,24,256]{2,1,0:T(8,128)(2,1)S(1)} all-to-all(bf16[32,24,256]{2,1,0:T(8,128)(2,1)S(1)} %broadcast_in_dim.34), channel_id=1, replica_groups=mesh['grp'=4,'blk'=8] {'grp','blk'}, dimensions={0} | all-to-all | bytes 786432 | tf_op jit(solution)/shard_map/all_to_all | solution.py:201
  128.0 3.6 %all-to-all-start.3 = ((bf16[8,256,256]{2,1,0:T(8,128)(2,1)}), bf16[8,256,256]{2,1,0:T(8,128)(2,1)S(1)}, u32[]{:S(2)}, u32[]{:S(2)}) async-start(bf16[8,256,256]{2,1,0:T(8,128)(2,1)} %bitcast.12), calls=%async_computation.3 | async-start | bytes 2097152 | tf_op jit(solution)/shard_map/all_to_all | solution.py:201
  131.5 0.5 broadcast.33
  132.1 0.7 reduce.4
  132.8 0.1 eq.16
  132.8 9.4 %shard_map.166 = f32[4096,256]{1,0:T(8,128)} custom-call(s32[2,1024]{1,0:T(2,128)} %pad_add_fusion.1.tn_ids, bf16[1024,1024]{1,0:T(8,128)(2,1)} %get-tuple-element.23.nr_ref, bf16[256,1024]{1,0:T(8,128)(2,1)} %get-tuple-element.24.query_ref, bf16[256,1024]{1,0:T(8,128)(2,1)} %get-tuple-element.25.pq_ref), custom_call_target="tpu_custom_call" | custom-call | flops 8589934592 | bytes 4194304 | tf_op jit(solution)/shard_map/pallas_call | solution.py:292
  142.2 1.3 fusion
  143.5 0.1 bitcast_convert_fusion
  143.6 0.7 slice.11
  144.3 0.8 slice.10
  145.1 12.0 %all-to-all-done.3 = bf16[8,256,256]{2,1,0:T(8,128)(2,1)S(1)} async-done(((bf16[8,256,256]{2,1,0:T(8,128)(2,1)}), bf16[8,256,256]{2,1,0:T(8,128)(2,1)S(1)}, u32[]{:S(2)}, u32[]{:S(2)}) %all-to-all-start.3) | async-done | bytes 1048608 | tf_op jit(solution)/shard_map/all_to_all | solution.py:201
  157.1 0.8 convert_reduce_fusion
  (4 shorter events, 0.0 us)
Async XLA Ops:
  0.6 15.2 %copy-start = (bf16[1024,256]{1,0:T(8,128)(2,1)S(1)}, bf16[1024,256]{1,0:T(8,128)(2,1)}, u32[]{:S(2)}) copy-start(bf16[1024,256]{1,0:T(8,128)(2,1)} %param.15) | copy-start | bytes 1572868
  17.0 16.4 %copy-start.4 = (s32[1024]{0:T(1024)S(1)}, s32[1024]{0:T(1024)}, u32[]{:S(2)}) copy-start(s32[1024]{0:T(1024)} %param.24) | copy-start | bytes 12292
  17.0 16.4 %copy-start.5 = (s32[1024]{0:T(1024)S(1)}, s32[1024]{0:T(1024)}, u32[]{:S(2)}) copy-start(s32[1024]{0:T(1024)} %param.19) | copy-start | bytes 12292
  17.0 17.0 %copy-start.3 = (s32[1024,4]{0,1:T(4,128)S(1)}, s32[1024,4]{0,1:T(4,128)}, u32[]{:S(2)}) copy-start(s32[1024,4]{0,1:T(4,128)} %param.21) | copy-start | bytes 49156
  17.0 17.0 %copy-start.6 = (s32[1024]{0:T(1024)S(1)}, s32[1024]{0:T(1024)}, u32[]{:S(2)}) copy-start(s32[1024]{0:T(1024)} %param.20) | copy-start | bytes 12292
  17.8 10.3 %all-to-all-start.1 = ((bf16[32,8,256]{2,1,0:T(8,128)(2,1)}), bf16[32,8,256]{2,1,0:T(8,128)(2,1)S(1)}, u32[]{:S(2)}, u32[]{:S(2)}) async-start(bf16[32,8,256]{2,1,0:T(8,128)(2,1)} %bitcast_select_fusion), calls=%async_computation.1 | async-start | bytes 262144 | tf_op jit(solution)/shard_map/all_to_all | solution.py:201
  28.1 25.4 %copy-start.2 = (bf16[32,8,256]{2,1,0:T(8,128)(2,1)}, bf16[32,8,256]{2,1,0:T(8,128)(2,1)S(1)}, u32[]{:S(2)}) copy-start(bf16[32,8,256]{2,1,0:T(8,128)(2,1)S(1)} %all-to-all-done.1) | copy-start | bytes 393220
  29.1 29.8 %all-to-all-start.2 = ((bf16[8,256,256]{2,1,0:T(8,128)(2,1)}), bf16[8,256,256]{2,1,0:T(8,128)(2,1)S(1)}, u32[]{:S(2)}, u32[]{:S(2)}) async-start(bf16[8,256,256]{2,1,0:T(8,128)(2,1)} %broadcast_in_dim.32), calls=%async_computation.2 | async-start | bytes 2097152 | tf_op jit(solution)/shard_map/all_to_all | solution.py:201
  58.9 1.0 copy-start.1
  101.9 10.3 %all-to-all-start.4 = ((bf16[32,8,256]{2,1,0:T(8,128)(2,1)}), bf16[32,8,256]{2,1,0:T(8,128)(2,1)S(1)}, u32[]{:S(2)}, u32[]{:S(2)}) async-start(bf16[32,8,256]{2,1,0:T(8,128)(2,1)} %bitcast.30), calls=%async_computation.4 | async-start | bytes 262144 | tf_op jit(solution)/shard_map/all_to_all | solution.py:201
  128.0 29.1 %all-to-all-start.3 = ((bf16[8,256,256]{2,1,0:T(8,128)(2,1)}), bf16[8,256,256]{2,1,0:T(8,128)(2,1)S(1)}, u32[]{:S(2)}, u32[]{:S(2)}) async-start(bf16[8,256,256]{2,1,0:T(8,128)(2,1)} %bitcast.12), calls=%async_computation.3 | async-start | bytes 2097152 | tf_op jit(solution)/shard_map/all_to_all | solution.py:201

commit v2 on v1

--- a/solution.py
+++ b/solution.py
@@ -36,19 +36,11 @@
     return jnp.where(iota == ids_row - first, 1.0, 0.0).astype(BF)
 
 
-def lookup_kernel(rel_ref, tail_ref, rel_ids, tn_ids, rel_out, tails_out, negt_out, neg_out, rel_t, tail_t):
-    width = rel_ref.shape[1]
-    rel_rows = rel_ref.shape[0]
-    tail_rows = tail_ref.shape[0]
+def relation_lookup_kernel(rel_ref, rel_ids, rel_out, rel_t):
+    rel_rows, width = rel_ref.shape
     edges = rel_ids.shape[1]
     for index, part in enumerate(pieces(rel_ref[...].T, 3)):
         rel_t[index * width : (index + 1) * width, :] = part
-
-    @pl.loop(0, tail_rows // BLOCK)
-    def _(step):
-        start = pl.multiple_of(step * BLOCK, BLOCK)
-        tail_t[:, pl.ds(start, BLOCK)] = tail_ref[pl.ds(start, BLOCK), :].T
-
     for which in range(rel_ids.shape[0]):
 
         @pl.loop(0, edges // BLOCK)
@@ -56,6 +48,16 @@
             at = pl.ds(pl.multiple_of(step * BLOCK, BLOCK), BLOCK)
             got = nn(rel_t[...], onehot(rel_ids[which : which + 1, at], 0, rel_rows))
             rel_out[which, :, at] = got[:width] + got[width : 2 * width] + got[2 * width :]
+
+
+def tail_lookup_kernel(tail_ref, tn_ids, tails_out, negt_out, neg_out, tail_t):
+    tail_rows = tail_ref.shape[0]
+    edges = tn_ids.shape[1]
+
+    @pl.loop(0, tail_rows // BLOCK)
+    def _(step):
+        start = pl.multiple_of(step * BLOCK, BLOCK)
+        tail_t[:, pl.ds(start, BLOCK)] = tail_ref[pl.ds(start, BLOCK), :].T
 
     for which, out in ((0, tails_out), (1, negt_out)):
 
@@ -73,13 +75,15 @@
     rel_ref,
     fetched_ref,
     ref_ids,
-    head_ref,
+    head_near_ref,
+    head_far_ref,
     head_ids,
     proj_ref,
     tails_ref,
     negt_ref,
     neg_ref,
-    head_out,
+    head_near_out,
+    head_far_out,
     rg_out,
     cg_out,
     comp_out,
@@ -93,7 +97,7 @@
 ):
     width, edges = tails_ref.shape
     slots = fetched_ref.shape[0]
-    owners, _, head_rows = head_ref.shape
+    half, _, head_rows = head_near_ref.shape
     fetched_t[...] = fetched_ref[...].astype(F32).T.astype(BF)
     for index, part in enumerate(pieces(proj_ref[...], 2)):
         proj_n[index] = part
@@ -115,8 +119,10 @@
             nn(proj_t[0], comp_hi) + (nn(proj_t[0], comp_lo) + nn(proj_t[1], comp_hi))
         )
         heads = jnp.zeros((width, BLOCK), F32)
-        for owner in range(owners):
-            heads = heads + nn(head_ref[owner], onehot(head_ids[:, at], owner * head_rows, head_rows))
+        for first, table in ((0, head_near_ref), (half, head_far_ref)):
+            for owner in range(half):
+                hot = onehot(head_ids[:, at], (first + owner) * head_rows, head_rows)
+                heads = heads + nn(table[owner], hot)
         query = (heads * relation).astype(BF)
         query_out[:, at] = query
         query_f = query.astype(F32)
@@ -142,14 +148,19 @@
         rg_out[1, :, at] = rg_lo
         cg_out[:, at] = nn(proj_n[0], rg_hi) + (nn(proj_n[0], rg_lo) + nn(proj_n[1], rg_hi))
 
-    @pl.loop(0, owners)
-    def _(owner):
-        at = pl.ds(pl.multiple_of(owner * head_rows, head_rows), head_rows)
-        head_out[at, :] = nt(onehot(head_ids[...], owner * head_rows, head_rows), head_terms[...]).astype(BF)
-
-
-def relation_kernel(rel_ref, fetched_ref, ref_ids, rel_ids, rg_ref, cg_ref, comp_ref, sums_out, fetched_out, fetched_t):
-    rel_rows = sums_out.shape[0] - rg_ref.shape[1]
+    for first, out in ((0, head_near_out), (half, head_far_out)):
+
+        @pl.loop(0, half)
+        def _(owner):
+            hot = onehot(head_ids[...], (first + owner) * head_rows, head_rows)
+            out[owner] = nt(hot, head_terms[...]).astype(BF)
+
+
+def relation_kernel(
+    group_ref, rel_ref, fetched_ref, ref_ids, rel_ids, rg_ref, cg_ref, comp_ref, sums_out, fetched_out, fetched_t, sums
+):
+    groups, share, _ = sums_out.shape
+    rel_rows = sums.shape[0] - rg_ref.shape[1]
     slots = fetched_ref.shape[0]
     fetched_t[...] = fetched_ref[...].astype(F32).T.astype(BF)
     comp_grad = cg_ref[...]
@@ -160,10 +171,23 @@
         rows = nn(fetched_t[...], hot)
         rel_sum = rel_sum + nt(onehot(rel_ids[k + 1 : k + 2, :], 0, rel_rows), (comp_grad * rows).astype(BF))
         fetched_sum = fetched_sum + nt(hot, (comp_grad * rel_ref[k + 1]).astype(BF))
-    sums_out[:rel_rows, :] = rel_sum.astype(BF)
+    sums[:rel_rows, :] = rel_sum
+    sums[rel_rows:, :] = nt(comp_ref[0], rg_ref[0]) + (nt(comp_ref[0], rg_ref[1]) + nt(comp_ref[1], rg_ref[0]))
     fetched_out[...] = fetched_sum.astype(BF)
-    proj_sum = nt(comp_ref[0], rg_ref[0]) + (nt(comp_ref[0], rg_ref[1]) + nt(comp_ref[1], rg_ref[0]))
-    sums_out[rel_rows:, :] = proj_sum.astype(BF)
+    for offset in range(groups):
+        start = pl.multiple_of(jnp.bitwise_xor(group_ref[0], offset) * share, share)
+        sums_out[offset] = sums[pl.ds(start, share), :].astype(BF)
+
+
+def finish_kernel(group_ref, own_ref, other_ref, rel_out, proj_out, sums):
+    pairs, share, _ = own_ref.shape
+    for pair in range(pairs):
+        for bit, table in ((0, own_ref), (1, other_ref)):
+            start = pl.multiple_of(jnp.bitwise_xor(group_ref[0], 2 * pair + bit) * share, share)
+            sums[pl.ds(start, share), :] = table[pair].astype(F32)
+    rel_rows = rel_out.shape[0]
+    rel_out[...] = sums[:rel_rows, :]
+    proj_out[...] = sums[rel_rows:, :]
 
 
 def tail_kernel(tn_ids, nr_ref, query_ref, pq_ref, tail_out, terms):
@@ -199,6 +223,11 @@
 
 def exchange(values, axes):
     return lax.all_to_all(values, axes, split_axis=0, concat_axis=0, tiled=True)
+
+
+def swap(values, axis, offset):
+    count = lax.axis_size(axis)
+    return lax.ppermute(values, axis, [(i, i ^ offset) for i in range(count)])
 
 
 def body(
@@ -226,28 +255,46 @@
     members = lax.axis_size("blk")
     devices = lax.axis_size("grp") * members
 
+    groups = lax.axis_size("grp")
+    half = members // 2
+    me = lax.axis_index("blk")
+    group = lax.axis_index("grp").reshape(1)
+
     arrived = exchange(qual_req.reshape(devices, -1), BOTH)
-    picked = jnp.take(qual_table, arrived, axis=0)
-    fetched = exchange(picked, BOTH).reshape(slots, width)
-    head_all = exchange(jnp.broadcast_to(head_table.T[None], (members, width, head_rows)), "blk")
+    head_t = head_table.T
+    head_near = jnp.stack([head_t] + [swap(head_t, "blk", 2 * m) for m in range(1, half)])
+    head_far = swap(head_near, "blk", 1)
+    offset = jnp.bitwise_xor(head_id // head_rows, me)
+    head_slot = ((offset % 2) * half + offset // 2) * head_rows + head_id % head_rows
+    head_slot = head_slot[None, :]
 
     rel_ids = jnp.concatenate([rel_id[None, :], qual_rel.T], axis=0)
     ref_ids = qual_ref.T
     tn_ids = jnp.stack([tail_id, neg_id])
-    rel_looked, tails, neg_t, neg = call(
-        lookup_kernel,
-        [((5, width, edges), F32), ((width, edges), BF), ((width, negs), BF), ((negs, width), BF)],
-        [((3 * width, rel_rows), BF), ((width, tail_rows), BF)],
+    (rel_looked,) = call(
+        relation_lookup_kernel,
+        [((5, width, edges), F32)],
+        [((3 * width, rel_rows), BF)],
+        5 << 30,
+        rel_table,
+        rel_ids,
+    )
+    arrived, rel_looked = lax.optimization_barrier((arrived, rel_looked))
+    picked = jnp.take(qual_table, arrived, axis=0)
+    fetched = exchange(picked, BOTH).reshape(slots, width)
+    tails, neg_t, neg = call(
+        tail_lookup_kernel,
+        [((width, edges), BF), ((width, negs), BF), ((negs, width), BF)],
+        [((width, tail_rows), BF)],
         8 << 30,
-        rel_table,
         tail_table,
-        rel_ids,
         tn_ids,
     )
-    head_part, rg, cg, comp, neg_round, query, pq = call(
+    near_part, far_part, rg, cg, comp, neg_round, query, pq = call(
         edge_kernel,
         [
-            ((members * head_rows, width), BF),
+            ((half, head_rows, width), BF),
+            ((half, head_rows, width), BF),
             ((2, width, edges), BF),
             ((width, edges), F32),
             ((2, width, edges), BF),
@@ -261,19 +308,23 @@
         rel_looked,
         fetched,
         ref_ids,
-        head_all,
-        head_id[None, :],
+        head_near,
+        head_far,
+        head_slot,
         proj,
         tails,
         neg_t,
         neg,
         smem=(0,),
     )
+    far_got = swap(far_part, "blk", 1)
+    share = (rel_rows + width) // groups
     sums_part, fetched_part = call(
         relation_kernel,
-        [((rel_rows + width, width), BF), ((slots, width), BF)],
-        [((width, slots), BF)],
+        [((groups, share, width), BF), ((slots, width), BF)],
+        [((width, slots), BF), ((rel_rows + width, width), F32)],
         4 << 30,
+        group,
         rel_looked,
         fetched,
         ref_ids,
@@ -281,11 +332,26 @@
         rg,
         cg,
         comp,
-    )
-    head_got = exchange(head_part.reshape(members, head_rows, width), "blk")
-    sums_got = exchange(sums_part.reshape(devices, -1, width), BOTH)
-    sums_own = jnp.sum(sums_got.astype(F32), axis=0).astype(BF)
-    sums_all = exchange(jnp.broadcast_to(sums_own[None], (devices,) + sums_own.shape), BOTH)
+        smem=(0,),
+    )
+    sums_part = sums_part.reshape(groups // 2, 2, share, width)
+    core_got = swap(sums_part[:, 1], "grp", 1)
+    pair_sum = sums_part[:, 0].astype(F32) + core_got.astype(F32)
+    quarter = pair_sum[0]
+    for pair in range(1, groups // 2):
+        quarter = quarter + swap(pair_sum[pair].astype(BF), "grp", 2 * pair).astype(F32)
+    parts = exchange(quarter.astype(BF).reshape(members, -1, width), "blk")
+    own = jnp.sum(parts.astype(F32), axis=0).astype(BF)
+    whole = exchange(jnp.broadcast_to(own[None], (members,) + own.shape), "blk").reshape(share, width)
+    sums_own = jnp.stack([whole] + [swap(whole, "grp", 2 * pair) for pair in range(1, groups // 2)])
+    sums_other = swap(sums_own, "grp", 1)
+
+    near_sum = near_part.astype(F32) + far_got.astype(F32)
+    head_grad = near_sum[0]
+    near_send = near_sum.astype(BF)
+    for m in range(1, half):
+        head_grad = head_grad + swap(near_send[m], "blk", 2 * m).astype(F32)
+
     returned = exchange(fetched_part.reshape(devices, -1, width), BOTH).reshape(-1, width)
 
     block = min(512, tail_rows)
@@ -300,11 +366,19 @@
         cost_estimate=pl.CostEstimate(flops=8 << 30, bytes_accessed=1 << 22, transcendentals=0),
     )(tn_ids, neg_round, query, pq)
 
-    head_grad = jnp.sum(head_got.astype(F32), axis=0)
     hot = (jnp.arange(qual_rows, dtype=jnp.int32)[:, None] == arrived.reshape(1, -1)).astype(BF)
     qual_grad = jnp.dot(hot, returned, preferred_element_type=F32)
-    sums = sums_all.reshape(rel_rows + width, width).astype(F32)
-    return (head_grad, tail_grad, qual_grad, sums[:rel_rows], sums[rel_rows:])
+    rel_grad, proj_grad = call(
+        finish_kernel,
+        [((rel_rows, width), F32), ((width, width), F32)],
+        [((rel_rows + width, width), F32)],
+        1 << 20,
+        group,
+        sums_own,
+        sums_other,
+        smem=(0,),
+    )
+    return (head_grad, tail_grad, qual_grad, rel_grad, proj_grad)
 
 
 def solution(mesh):

time: 158 us -> 140 us (0.89)
  blocking collectives: 46.3 us -> 0 us
  starting transfers between devices: 12.3 us -> 43.4 us
  waiting for transfers between devices: 31.8 us -> 22.2 us
  Pallas kernels: 54 us -> 58.2 us
  other arithmetic: 3.69 us -> 5.98 us
    all_to_all x3 -> x0, blocking collectives: 46.3 us -> none  [exchange(): return lax.all_to_all(values, axes, split_axis=0, concat_axis=0, tiled=True)]
    all_to_all x4 -> x5, waiting for transfers between devices: 31.8 us -> 6.95 us  [exchange(): return lax.all_to_all(values, axes, split_axis=0, concat_axis=0, tiled=True)]
    ppermute x0 -> x12, starting transfers between devices: none -> 17.2 us  [swap(): return lax.ppermute(values, axis, [(i, i ^ offset) for i in range(count)])]
    ppermute x0 -> x12, waiting for transfers between devices: none -> 15.3 us  [swap(): return lax.ppermute(values, axis, [(i, i ^ offset) for i in range(count)])]
    all_to_all x4 -> x5, starting transfers between devices: 12.3 us -> 26.1 us  [exchange(): return lax.all_to_all(values, axes, split_axis=0, concat_axis=0, tiled=True)]
    pallas_call x3 -> x5, Pallas kernels: 44.6 us -> 48.8 us  [call(): pl.pallas_call(kernel, out_shape=[jax.ShapeDtypeStruct(shape, dtype) for...]
    add x0 -> x3, other arithmetic: none -> 2.34 us  [the longest x1 0.97 us: body(): pair_sum = sums_part[:, 0].astype(F32) + core_got.astype(F32)]
  transfers between devices with their start and end apart: 4 -> 17, of which waited for: 4 -> 7; matrix products, arithmetic and copies ran while one was open for 4% -> 5% of each run, Pallas kernels for 18% -> 22%
where the time goes in v2:
time: 140 us
  Pallas kernels  58.2 us (42%)
  starting transfers between devices  43.4 us (31%)
  waiting for transfers between devices  22.2 us (16%)
  local copies, waits for them, and re-layouts  6.91 us (5%)
  other arithmetic  5.98 us (4%)
  between operations  1.54 us (1%)
    pallas_call x5, Pallas kernels, call(): pl.pallas_call(kernel, out_shape=[jax.ShapeDtypeStruct(shape, dtype) for...  48.8 us
    all_to_all x5, starting transfers between devices, exchange(): return lax.all_to_all(values, axes, split_axis=0, concat_axis=0, tiled=True)  26.1 us
    ppermute x12, starting transfers between devices, swap(): return lax.ppermute(values, axis, [(i, i ^ offset) for i in range(count)])  17.2 us
    ppermute x12, waiting for transfers between devices, swap(): return lax.ppermute(values, axis, [(i, i ^ offset) for i in range(count)])  15.3 us
    pallas_call x1, Pallas kernels, body(): pl.pallas_call(tail_kernel, out_shape=jax.ShapeDtypeStruct((tail_rows, wi...  9.42 us
    all_to_all x5, waiting for transfers between devices, exchange(): return lax.all_to_all(values, axes, split_axis=0, concat_axis=0, tiled=True)  6.95 us
  transfers between devices with their start and end apart: 17, of which 7 were waited for; matrix products, arithmetic and copies ran while one was open for 5% of the time, Pallas kernels for 22%

profile of v2, /device:TPU:0, one launch (start us, length us, event | category | flops | bytes accessed | tf_op | source)
XLA Modules:
  0.0 139.5 jit_solution(16833953025934389326)
XLA Ops:
  0.6 1.1 copy.23
  1.7 4.1 %collective-permute-start.1 = (bf16[256,256]{1,0:T(8,128)(2,1)S(1)}, bf16[256,256]{1,0:T(8,128)(2,1)S(1)}, u32[]{:S(2)}, u32[]{:S(2)}) collective-permute-start(bf16[256,256]{1,0:T(8,128)(2,1)S(1)} %bitcast.58), channel_id=1, source_target_pairs={{0,4},{1,5},{2,6},{3,7},{4,0},{5,1},{6,2},{7,3},{8,12},{9,13},{10,... | collective-permute-start | bytes 393224 | tf_op jit(solution)/shard_map/ppermute | solution.py:230
  5.8 1.6 %collective-permute-start = (bf16[256,256]{1,0:T(8,128)(2,1)S(1)}, bf16[256,256]{1,0:T(8,128)(2,1)S(1)}, u32[]{:S(2)}, u32[]{:S(2)}) collective-permute-start(bf16[256,256]{1,0:T(8,128)(2,1)S(1)} %bitcast.59), channel_id=1, source_target_pairs={{0,2},{1,3},{2,0},{3,1},{4,6},{5,7},{6,4},{7,5},{8,10},{9,11},{10,... | collective-permute-start | bytes 393224 | tf_op jit(solution)/shard_map/ppermute | solution.py:230
  7.4 1.4 all_to_all.20
  8.8 6.1 %all-to-all-start = ((s32[32,1,8]{2,1,0:T(1,128)}), s32[32,1,8]{2,1,0:T(1,128)S(1)}, u32[]{:S(2)}, u32[]{:S(2)}) async-start(s32[32,1,8]{2,1,0:T(1,128)} %bitcast), calls=%async_computation | async-start | bytes 32768 | tf_op jit(solution)/shard_map/all_to_all | solution.py:225
  14.8 1.3 pad_add_fusion.rel_ids
  16.2 11.0 %shard_map.164.rel_ref = f32[5,256,1024]{2,1,0:T(8,128)} custom-call(f32[512,256]{1,0:T(8,128)} %rel_ref.1, s32[5,1024]{1,0:T(8,128)} %pad_add_fusion.rel_ids), custom_call_target="tpu_custom_call" | custom-call | flops 5368709120 | bytes 4194304 | tf_op jit(solution)/shard_map/pallas_call | solution.py:213
  27.2 0.6 pad_add_fusion.1.tn_ids
  27.8 0.1 reshape.56
  27.9 1.2 gather_fusion
  29.1 0.8 bitcast_select_fusion
  29.8 5.8 %all-to-all-start.1 = ((bf16[32,8,256]{2,1,0:T(8,128)(2,1)}), bf16[32,8,256]{2,1,0:T(8,128)(2,1)S(1)}, u32[]{:S(2)}, u32[]{:S(2)}) async-start(bf16[32,8,256]{2,1,0:T(8,128)(2,1)} %bitcast_select_fusion), calls=%async_computation.1 | async-start | bytes 262144 | tf_op jit(solution)/shard_map/all_to_all | solution.py:225
  35.7 0.1 pad_maximum_fusion.head_near_ref
  35.8 1.8 %collective-permute-start.3 = (bf16[4,256,256]{2,1,0:T(8,128)(2,1)S(1)}, bf16[4,256,256]{2,1,0:T(8,128)(2,1)S(1)}, u32[]{:S(2)}, u32[]{:S(2)}) collective-permute-start(bf16[4,256,256]{2,1,0:T(8,128)(2,1)S(1)} %pad_maximum_fusion.head_near_ref), channel_id=1, source_target_pairs={{0,1},{1,0},{2,3},{3,2},{4,5},{5,4},{6,7},{7,6},{8,9},{9,8},{10,11... | collective-permute-start | bytes 1572872 | tf_op jit(solution)/shard_map/ppermute | solution.py:230
  37.6 10.1 %shard_map.165 = (bf16[256,1024]{1,0:T(8,128)(2,1)}, bf16[256,1024]{1,0:T(8,128)(2,1)}, bf16[1024,256]{1,0:T(8,128)(2,1)}) custom-call(bf16[4096,256]{1,0:T(8,128)(2,1)} %tail_ref.1, s32[2,1024]{1,0:T(2,128)} %pad_add_fusion.1.tn_ids), custom_call_target="tpu_custom_call" | custom-call | flops 8589934592 | bytes 4194304 | tf_op jit(solution)/shard_map/pallas_call | solution.py:213
  48.4 0.6 fusion.13
  49.1 2.1 %collective-permute-done.3.head_far_ref = bf16[4,256,256]{2,1,0:T(8,128)(2,1)S(1)} collective-permute-done((bf16[4,256,256]{2,1,0:T(8,128)(2,1)S(1)}, bf16[4,256,256]{2,1,0:T(8,128)(2,1)S(1)}, u32[]{:S(2)}, u32[]{:S(2)}) %collective-permute-start.3) | collective-permute-done | bytes 524320 | tf_op jit(solution)/shard_map/ppermute | solution.py:230
  51.2 0.8 copy-done.10
  52.0 18.2 %shard_map.166 = (bf16[4,256,256]{2,1,0:T(8,128)(2,1)}, bf16[4,256,256]{2,1,0:T(8,128)(2,1)}, bf16[2,256,1024]{2,1,0:T(8,128)(2,1)}, f32[256,1024]{1,0:T(8,128)}...) custom-call(s32[1]{0:T(128)S(6)} %copy.26.count_ref, ...), custom_call_target="tpu_custom_call" | custom-call | flops 8589934592 | bytes 4194304 | tf_op jit(solution)/shard_map/pallas_call | solution.py:213
  70.2 7.5 %shard_map.168 = (bf16[4,192,256]{2,1,0:T(8,128)(2,1)}, bf16[256,256]{1,0:T(8,128)(2,1)}) custom-call(s32[1]{0:T(128)} %bitcast.19.group_ref, f32[5,256,1024]{2,1,0:T(8,128)} %shard_map.164.rel_ref, bf16[256,256]{1,0:T(8,128)(2,1)} %bitcast.70, s32[4,1024]{1,0:T(4,128)} %bitcast.81, s32[5,1024]{1,0:T(8,128)} %pad_add_fusion.rel_ids, ...), custom_call_target="tpu_custom_call" | custom-call | flops 4294967296 | bytes 4194304 | tf_op jit(solution)/shard_map/pallas_call | solution.py:213
  77.7 0.9 slice_bitcast_fusion.2
  78.6 0.1 collective-permute-start.8
  78.7 1.4 %collective-permute-done.8 = bf16[2,192,256]{2,1,0:T(8,128)(2,1)S(1)} collective-permute-done((bf16[2,192,256]{2,1,0:T(8,128)(2,1)S(1)}, bf16[2,192,256]{2,1,0:T(8,128)(2,1)S(1)}, u32[]{:S(2)}, u32[]{:S(2)}) %collective-permute-start.8) | collective-permute-done | bytes 196640 | tf_op jit(solution)/shard_map/ppermute | solution.py:230
  80.1 1.0 convert_add_fusion.1
  81.1 1.7 %collective-permute-start.9 = (bf16[192,256]{1,0:T(8,128)(2,1)S(1)}, bf16[192,256]{1,0:T(8,128)(2,1)S(1)}, u32[]{:S(2)}, u32[]{:S(2)}) collective-permute-start(bf16[192,256]{1,0:T(8,128)(2,1)S(1)} %fusion.8), channel_id=1, source_target_pairs={{0,16},{8,24},{16,0},{24,8},{1,17},{9,25},{17,1},{25,9},{2,18},{10... | collective-permute-start | bytes 294920 | tf_op jit(solution)/shard_map/ppermute | solution.py:230
  82.9 3.2 %collective-permute-done.9 = bf16[192,256]{1,0:T(8,128)(2,1)S(1)} collective-permute-done((bf16[192,256]{1,0:T(8,128)(2,1)S(1)}, bf16[192,256]{1,0:T(8,128)(2,1)S(1)}, u32[]{:S(2)}, u32[]{:S(2)}) %collective-permute-start.9) | collective-permute-done | bytes 98336 | tf_op jit(solution)/shard_map/ppermute | solution.py:230
  86.0 0.7 fusion.6
  86.7 4.9 %all-to-all-start.3 = ((bf16[8,24,256]{2,1,0:T(8,128)(2,1)}), bf16[8,24,256]{2,1,0:T(8,128)(2,1)S(1)}, u32[]{:S(2)}, u32[]{:S(2)}) async-start(bf16[8,24,256]{2,1,0:T(8,128)(2,1)} %bitcast.27), calls=%async_computation.3 | async-start | bytes 196608 | tf_op jit(solution)/shard_map/all_to_all | solution.py:225
  91.6 0.1 eq.19
  91.7 2.1 %collective-permute-start.4 = (bf16[4,256,256]{2,1,0:T(8,128)(2,1)S(1)}, bf16[4,256,256]{2,1,0:T(8,128)(2,1)S(1)}, u32[]{:S(2)}, u32[]{:S(2)}) collective-permute-start(bf16[4,256,256]{2,1,0:T(8,128)(2,1)S(1)} %copy-done.9), channel_id=1, source_target_pairs={{0,1},{1,0},{2,3},{3,2},{4,5},{5,4},{6,7},{7,6},{8,9},{9,8},{10,11... | collective-permute-start | bytes 1572872 | tf_op jit(solution)/shard_map/ppermute | solution.py:230
  93.8 5.1 %all-to-all-done.3 = bf16[8,24,256]{2,1,0:T(8,128)(2,1)S(1)} async-done(((bf16[8,24,256]{2,1,0:T(8,128)(2,1)}), bf16[8,24,256]{2,1,0:T(8,128)(2,1)S(1)}, u32[]{:S(2)}, u32[]{:S(2)}) %all-to-all-start.3) | async-done | bytes 98336 | tf_op jit(solution)/shard_map/all_to_all | solution.py:225
  98.8 0.7 broadcast_in_dim.30
  99.5 3.4 %all-to-all-start.4 = ((bf16[8,24,256]{2,1,0:T(8,128)(2,1)}), bf16[8,24,256]{2,1,0:T(8,128)(2,1)S(1)}, u32[]{:S(2)}, u32[]{:S(2)}) async-start(bf16[8,24,256]{2,1,0:T(8,128)(2,1)} %broadcast_in_dim.30), calls=%async_computation.4 | async-start | bytes 196608 | tf_op jit(solution)/shard_map/all_to_all | solution.py:225
  102.9 9.4 %shard_map.167 = f32[4096,256]{1,0:T(8,128)} custom-call(s32[2,1024]{1,0:T(2,128)} %pad_add_fusion.1.tn_ids, bf16[1024,1024]{1,0:T(8,128)(2,1)} %get-tuple-element.29.nr_ref, bf16[256,1024]{1,0:T(8,128)(2,1)} %get-tuple-element.30.query_ref, bf16[256,1024]{1,0:T(8,128)(2,1)} %get-tuple-element.31.pq_ref), custom_call_target="tpu_custom_call" | custom-call | flops 8589934592 | bytes 4194304 | tf_op jit(solution)/shard_map/pallas_call | solution.py:358
  112.3 6.0 %all-to-all-start.2 = ((bf16[32,8,256]{2,1,0:T(8,128)(2,1)}), bf16[32,8,256]{2,1,0:T(8,128)(2,1)S(1)}, u32[]{:S(2)}, u32[]{:S(2)}) async-start(bf16[32,8,256]{2,1,0:T(8,128)(2,1)} %bitcast.20), calls=%async_computation.2 | async-start | bytes 262144 | tf_op jit(solution)/shard_map/all_to_all | solution.py:225
  118.3 0.1 fusion.20
  118.5 1.8 %collective-permute-start.5 = (bf16[256,256]{1,0:T(8,128)(2,1)S(1)}, bf16[256,256]{1,0:T(8,128)(2,1)S(1)}, u32[]{:S(2)}, u32[]{:S(2)}) collective-permute-start(bf16[256,256]{1,0:T(8,128)(2,1)S(1)} %get-tuple-element.41), channel_id=1, source_target_pairs={{0,2},{1,3},{2,0},{3,1},{4,6},{5,7},{6,4},{7,5},{8,10},{9,11},{10,... | collective-permute-start | bytes 393224 | tf_op jit(solution)/shard_map/ppermute | solution.py:230
  120.3 2.4 %collective-permute-start.7 = (bf16[256,256]{1,0:T(8,128)(2,1)S(1)}, bf16[256,256]{1,0:T(8,128)(2,1)S(1)}, u32[]{:S(2)}, u32[]{:S(2)}) collective-permute-start(bf16[256,256]{1,0:T(8,128)(2,1)S(1)} %get-tuple-element.42), channel_id=1, source_target_pairs={{0,6},{1,7},{2,4},{3,5},{4,2},{5,3},{6,0},{7,1},{8,14},{9,15},{10,... | collective-permute-start | bytes 393224 | tf_op jit(solution)/shard_map/ppermute | solution.py:230
  122.7 0.1 collective-permute-start.6
  122.8 1.5 %collective-permute-start.10 = (bf16[192,256]{1,0:T(8,128)(2,1)S(1)}, bf16[192,256]{1,0:T(8,128)(2,1)S(1)}, u32[]{:S(2)}, u32[]{:S(2)}) collective-permute-start(bf16[192,256]{1,0:T(8,128)(2,1)S(1)} %bitcast.64), channel_id=1, source_target_pairs={{0,16},{8,24},{16,0},{24,8},{1,17},{9,25},{17,1},{25,9},{2,18},{10... | collective-permute-start | bytes 294920 | tf_op jit(solution)/shard_map/ppermute | solution.py:230
  124.3 1.9 %all-to-all-done.2 = bf16[32,8,256]{2,1,0:T(8,128)(2,1)S(1)} async-done(((bf16[32,8,256]{2,1,0:T(8,128)(2,1)}), bf16[32,8,256]{2,1,0:T(8,128)(2,1)S(1)}, u32[]{:S(2)}, u32[]{:S(2)}) %all-to-all-start.2) | async-done | bytes 131104 | tf_op jit(solution)/shard_map/all_to_all | solution.py:225
  126.1 1.3 fusion
  127.5 0.1 collective-permute-start.11
  127.6 3.8 %collective-permute-done.7 = bf16[256,256]{1,0:T(8,128)(2,1)S(1)} collective-permute-done((bf16[256,256]{1,0:T(8,128)(2,1)S(1)}, bf16[256,256]{1,0:T(8,128)(2,1)S(1)}, u32[]{:S(2)}, u32[]{:S(2)}) %collective-permute-start.7) | collective-permute-done | bytes 131104 | tf_op jit(solution)/shard_map/ppermute | solution.py:230
  131.3 4.8 %collective-permute-done.6 = bf16[256,256]{1,0:T(8,128)(2,1)S(1)} collective-permute-done((bf16[256,256]{1,0:T(8,128)(2,1)S(1)}, bf16[256,256]{1,0:T(8,128)(2,1)S(1)}, u32[]{:S(2)}, u32[]{:S(2)}) %collective-permute-start.6) | collective-permute-done | bytes 131104 | tf_op jit(solution)/shard_map/ppermute | solution.py:230
  136.1 0.8 fusion.4
  136.9 0.7 copy-done.4
  137.5 2.0 %shard_map.169 = (f32[512,256]{1,0:T(8,128)}, f32[256,256]{1,0:T(8,128)}) custom-call(s32[1]{0:T(128)} %bitcast.19.group_ref, bf16[2,192,256]{2,1,0:T(8,128)(2,1)} %copy-done.1, bf16[2,192,256]{2,1,0:T(8,128)(2,1)} %copy-done.4), custom_call_target="tpu_custom_call" | custom-call | flops 1048576 | bytes 4194304 | tf_op jit(solution)/shard_map/pallas_call | solution.py:213
  (38 shorter events, 0.2 us)
Async XLA Ops:
  0.6 27.3 %copy-start = (bf16[1024,256]{1,0:T(8,128)(2,1)S(1)}, bf16[1024,256]{1,0:T(8,128)(2,1)}, u32[]{:S(2)}) copy-start(bf16[1024,256]{1,0:T(8,128)(2,1)} %param.15) | copy-start | bytes 1572868
  1.7 34.0 %collective-permute-start.1 = (bf16[256,256]{1,0:T(8,128)(2,1)S(1)}, bf16[256,256]{1,0:T(8,128)(2,1)S(1)}, u32[]{:S(2)}, u32[]{:S(2)}) collective-permute-start(bf16[256,256]{1,0:T(8,128)(2,1)S(1)} %bitcast.58), channel_id=1, source_target_pairs={{0,4},{1,5},{2,6},{3,7},{4,0},{5,1},{6,2},{7,3},{8,12},{9,13},{10,... | collective-permute-start | bytes 393224 | tf_op jit(solution)/shard_map/ppermute | solution.py:230
  5.8 29.9 %collective-permute-start = (bf16[256,256]{1,0:T(8,128)(2,1)S(1)}, bf16[256,256]{1,0:T(8,128)(2,1)S(1)}, u32[]{:S(2)}, u32[]{:S(2)}) collective-permute-start(bf16[256,256]{1,0:T(8,128)(2,1)S(1)} %bitcast.59), channel_id=1, source_target_pairs={{0,2},{1,3},{2,0},{3,1},{4,6},{5,7},{6,4},{7,5},{8,10},{9,11},{10,... | collective-permute-start | bytes 393224 | tf_op jit(solution)/shard_map/ppermute | solution.py:230
  7.4 28.3 %collective-permute-start.2 = (bf16[256,256]{1,0:T(8,128)(2,1)S(1)}, bf16[256,256]{1,0:T(8,128)(2,1)S(1)}, u32[]{:S(2)}, u32[]{:S(2)}) collective-permute-start(bf16[256,256]{1,0:T(8,128)(2,1)S(1)} %bitcast.60), channel_id=1, source_target_pairs={{0,6},{1,7},{2,4},{3,5},{4,2},{5,3},{6,0},{7,1},{8,14},{9,15},{10,... | collective-permute-start | bytes 393224 | tf_op jit(solution)/shard_map/ppermute | solution.py:230
  8.8 19.0 %all-to-all-start = ((s32[32,1,8]{2,1,0:T(1,128)}), s32[32,1,8]{2,1,0:T(1,128)S(1)}, u32[]{:S(2)}, u32[]{:S(2)}) async-start(s32[32,1,8]{2,1,0:T(1,128)} %bitcast), calls=%async_computation | async-start | bytes 32768 | tf_op jit(solution)/shard_map/all_to_all | solution.py:225
  16.2 11.0 %copy-start.7 = (s32[1024]{0:T(1024)S(1)}, s32[1024]{0:T(1024)}, u32[]{:S(2)}) copy-start(s32[1024]{0:T(1024)} %param.24) | copy-start | bytes 12292
  16.2 11.0 %copy-start.8 = (s32[1024]{0:T(1024)S(1)}, s32[1024]{0:T(1024)}, u32[]{:S(2)}) copy-start(s32[1024]{0:T(1024)} %param.19) | copy-start | bytes 12292
  29.8 19.2 %all-to-all-start.1 = ((bf16[32,8,256]{2,1,0:T(8,128)(2,1)}), bf16[32,8,256]{2,1,0:T(8,128)(2,1)S(1)}, u32[]{:S(2)}, u32[]{:S(2)}) async-start(bf16[32,8,256]{2,1,0:T(8,128)(2,1)} %bitcast_select_fusion), calls=%async_computation.1 | async-start | bytes 262144 | tf_op jit(solution)/shard_map/all_to_all | solution.py:225
  35.8 12.0 %copy-start.3 = (bf16[4,256,256]{2,1,0:T(8,128)(2,1)}, bf16[4,256,256]{2,1,0:T(8,128)(2,1)S(1)}, u32[]{:S(2)}) copy-start(bf16[4,256,256]{2,1,0:T(8,128)(2,1)S(1)} %pad_maximum_fusion.head_near_ref) | copy-start | bytes 1572868
  35.8 12.6 %copy-start.6 = (s32[1024]{0:T(1024)S(1)}, s32[1024]{0:T(1024)}, u32[]{:S(2)}) copy-start(s32[1024]{0:T(1024)} %param.18) | copy-start | bytes 12292
  35.8 15.4 %collective-permute-start.3 = (bf16[4,256,256]{2,1,0:T(8,128)(2,1)S(1)}, bf16[4,256,256]{2,1,0:T(8,128)(2,1)S(1)}, u32[]{:S(2)}, u32[]{:S(2)}) collective-permute-start(bf16[4,256,256]{2,1,0:T(8,128)(2,1)S(1)} %pad_maximum_fusion.head_near_ref), channel_id=1, source_target_pairs={{0,1},{1,0},{2,3},{3,2},{4,5},{5,4},{6,7},{7,6},{8,9},{9,8},{10,11... | collective-permute-start | bytes 1572872 | tf_op jit(solution)/shard_map/ppermute | solution.py:230
  49.1 2.1 %copy-start.5 = (bf16[32,8,256]{2,1,0:T(8,128)(2,1)}, bf16[32,8,256]{2,1,0:T(8,128)(2,1)S(1)}, u32[]{:S(2)}) copy-start(bf16[32,8,256]{2,1,0:T(8,128)(2,1)S(1)} %all-to-all-done.1) | copy-start | bytes 393220
  51.2 0.8 copy-start.10
  70.2 21.5 %copy-start.9 = (bf16[4,256,256]{2,1,0:T(8,128)(2,1)S(1)}, bf16[4,256,256]{2,1,0:T(8,128)(2,1)}, u32[]{:S(2)}) copy-start(bf16[4,256,256]{2,1,0:T(8,128)(2,1)} %get-tuple-element.28) | copy-start | bytes 1572868
  78.6 1.5 %collective-permute-start.8 = (bf16[2,192,256]{2,1,0:T(8,128)(2,1)S(1)}, bf16[2,192,256]{2,1,0:T(8,128)(2,1)S(1)}, u32[]{:S(2)}, u32[]{:S(2)}) collective-permute-start(bf16[2,192,256]{2,1,0:T(8,128)(2,1)S(1)} %slice_bitcast_fusion.2), channel_id=1, source_target_pairs={{0,8},{8,0},{16,24},{24,16},{1,9},{9,1},{17,25},{25,17},{2,10},{10... | collective-permute-start | bytes 589832 | tf_op jit(solution)/shard_map/ppermute | solution.py:230
  81.1 4.9 %collective-permute-start.9 = (bf16[192,256]{1,0:T(8,128)(2,1)S(1)}, bf16[192,256]{1,0:T(8,128)(2,1)S(1)}, u32[]{:S(2)}, u32[]{:S(2)}) collective-permute-start(bf16[192,256]{1,0:T(8,128)(2,1)S(1)} %fusion.8), channel_id=1, source_target_pairs={{0,16},{8,24},{16,0},{24,8},{1,17},{9,25},{17,1},{25,9},{2,18},{10... | collective-permute-start | bytes 294920 | tf_op jit(solution)/shard_map/ppermute | solution.py:230
  86.7 12.1 %all-to-all-start.3 = ((bf16[8,24,256]{2,1,0:T(8,128)(2,1)}), bf16[8,24,256]{2,1,0:T(8,128)(2,1)S(1)}, u32[]{:S(2)}, u32[]{:S(2)}) async-start(bf16[8,24,256]{2,1,0:T(8,128)(2,1)} %bitcast.27), calls=%async_computation.3 | async-start | bytes 196608 | tf_op jit(solution)/shard_map/all_to_all | solution.py:225
  91.7 26.6 %collective-permute-start.4 = (bf16[4,256,256]{2,1,0:T(8,128)(2,1)S(1)}, bf16[4,256,256]{2,1,0:T(8,128)(2,1)S(1)}, u32[]{:S(2)}, u32[]{:S(2)}) collective-permute-start(bf16[4,256,256]{2,1,0:T(8,128)(2,1)S(1)} %copy-done.9), channel_id=1, source_target_pairs={{0,1},{1,0},{2,3},{3,2},{4,5},{5,4},{6,7},{7,6},{8,9},{9,8},{10,11... | collective-permute-start | bytes 1572872 | tf_op jit(solution)/shard_map/ppermute | solution.py:230
  99.5 12.8 %all-to-all-start.4 = ((bf16[8,24,256]{2,1,0:T(8,128)(2,1)}), bf16[8,24,256]{2,1,0:T(8,128)(2,1)S(1)}, u32[]{:S(2)}, u32[]{:S(2)}) async-start(bf16[8,24,256]{2,1,0:T(8,128)(2,1)} %broadcast_in_dim.30), calls=%async_computation.4 | async-start | bytes 196608 | tf_op jit(solution)/shard_map/all_to_all | solution.py:225
  102.9 15.5 %copy-start.2 = (bf16[4,256,256]{2,1,0:T(8,128)(2,1)S(1)}, bf16[4,256,256]{2,1,0:T(8,128)(2,1)}, u32[]{:S(2)}) copy-start(bf16[4,256,256]{2,1,0:T(8,128)(2,1)} %get-tuple-element.27) | copy-start | bytes 1572868
  112.3 13.9 %all-to-all-start.2 = ((bf16[32,8,256]{2,1,0:T(8,128)(2,1)}), bf16[32,8,256]{2,1,0:T(8,128)(2,1)S(1)}, u32[]{:S(2)}, u32[]{:S(2)}) async-start(bf16[32,8,256]{2,1,0:T(8,128)(2,1)} %bitcast.20), calls=%async_computation.2 | async-start | bytes 262144 | tf_op jit(solution)/shard_map/all_to_all | solution.py:225
  118.5 9.1 %collective-permute-start.5 = (bf16[256,256]{1,0:T(8,128)(2,1)S(1)}, bf16[256,256]{1,0:T(8,128)(2,1)S(1)}, u32[]{:S(2)}, u32[]{:S(2)}) collective-permute-start(bf16[256,256]{1,0:T(8,128)(2,1)S(1)} %get-tuple-element.41), channel_id=1, source_target_pairs={{0,2},{1,3},{2,0},{3,1},{4,6},{5,7},{6,4},{7,5},{8,10},{9,11},{10,... | collective-permute-start | bytes 393224 | tf_op jit(solution)/shard_map/ppermute | solution.py:230
  120.3 11.0 %collective-permute-start.7 = (bf16[256,256]{1,0:T(8,128)(2,1)S(1)}, bf16[256,256]{1,0:T(8,128)(2,1)S(1)}, u32[]{:S(2)}, u32[]{:S(2)}) collective-permute-start(bf16[256,256]{1,0:T(8,128)(2,1)S(1)} %get-tuple-element.42), channel_id=1, source_target_pairs={{0,6},{1,7},{2,4},{3,5},{4,2},{5,3},{6,0},{7,1},{8,14},{9,15},{10,... | collective-permute-start | bytes 393224 | tf_op jit(solution)/shard_map/ppermute | solution.py:230
  122.7 13.4 %collective-permute-start.6 = (bf16[256,256]{1,0:T(8,128)(2,1)S(1)}, bf16[256,256]{1,0:T(8,128)(2,1)S(1)}, u32[]{:S(2)}, u32[]{:S(2)}) collective-permute-start(bf16[256,256]{1,0:T(8,128)(2,1)S(1)} %get-tuple-element.43), channel_id=1, source_target_pairs={{0,4},{1,5},{2,6},{3,7},{4,0},{5,1},{6,2},{7,3},{8,12},{9,13},{10,... | collective-permute-start | bytes 393224 | tf_op jit(solution)/shard_map/ppermute | solution.py:230
  122.8 4.7 %collective-permute-start.10 = (bf16[192,256]{1,0:T(8,128)(2,1)S(1)}, bf16[192,256]{1,0:T(8,128)(2,1)S(1)}, u32[]{:S(2)}, u32[]{:S(2)}) collective-permute-start(bf16[192,256]{1,0:T(8,128)(2,1)S(1)} %bitcast.64), channel_id=1, source_target_pairs={{0,16},{8,24},{16,0},{24,8},{1,17},{9,25},{17,1},{25,9},{2,18},{10... | collective-permute-start | bytes 294920 | tf_op jit(solution)/shard_map/ppermute | solution.py:230
  127.5 9.4 %copy-start.1 = (bf16[2,192,256]{2,1,0:T(8,128)(2,1)}, bf16[2,192,256]{2,1,0:T(8,128)(2,1)S(1)}, u32[]{:S(2)}) copy-start(bf16[2,192,256]{2,1,0:T(8,128)(2,1)S(1)} %pad_maximum_fusion.1.own_ref) | copy-start | bytes 589828
  127.5 9.4 %collective-permute-start.11 = (bf16[2,192,256]{2,1,0:T(8,128)(2,1)S(1)}, bf16[2,192,256]{2,1,0:T(8,128)(2,1)S(1)}, u32[]{:S(2)}, u32[]{:S(2)}) collective-permute-start(bf16[2,192,256]{2,1,0:T(8,128)(2,1)S(1)} %pad_maximum_fusion.1.own_ref), channel_id=1, source_target_pairs={{0,8},{8,0},{16,24},{24,16},{1,9},{9,1},{17,25},{25,17},{2,10},{10... | collective-permute-start | bytes 589832 | tf_op jit(solution)/shard_map/ppermute | solution.py:230
  136.9 0.7 copy-start.4

commit v3 on v1

v3 whole, which is shorter than its diff:
```python
import jax
import jax.numpy as jnp
from jax import lax
from jax.experimental import pallas as pl
from jax.experimental.pallas import tpu as pltpu
from jax.sharding import Mesh, PartitionSpec as P

BF = jnp.bfloat16
F32 = jnp.float32
MIB = 1024 * 1024
AXES = ("pair", "core", "line", "near")
MEMBER = ("line", "near")
BLOCK = 256


def nn(a, b):
    return jnp.dot(a, b, preferred_element_type=F32)


def nt(a, b):
    return lax.dot_general(a, b, (((1,), (1,)), ((), ())), preferred_element_type=F32)


def pieces(values, count):
    out = []
    for _ in range(count):
        part = values.astype(BF)
        out.append(part)
        values = values - part.astype(F32)
    return out


def flip(values):
    return values.astype(F32).T.astype(BF)


def onehot(ids_row, first, rows):
    iota = lax.broadcasted_iota(jnp.int32, (rows, ids_row.shape[1]), 0)
    return jnp.where(iota == ids_row - first, 1.0, 0.0).astype(BF)


def relation_lookup_kernel(rel_ref, rel_id, qual_rel, rel_out, table):
    rel_rows, width = rel_ref.shape
    edges = rel_id.shape[1]
    step = pl.program_id(0)

    @pl.when(step == 0)
    def _():
        for index, part in enumerate(pieces(rel_ref[...].T, 2)):
            table[index * width : (index + 1) * width, :] = part

    def look(ids):
        for start in range(0, edges, BLOCK):
            at = pl.ds(start, BLOCK)
            got = nn(table[...], onehot(ids[:, at], 0, rel_rows))
            rel_out[0, :, at] = got[:width] + got[width:]

    @pl.when(step == 0)
    def _():
        look(rel_id)

    for k in range(qual_rel.shape[0]):

        @pl.when(step == k + 1)
        def _():
            look(qual_rel.at[k : k + 1])


def tail_lookup_kernel(tail_ref, tail_id, neg_id, tails_out, negt_out, neg_out, table):
    tail_rows = tail_ref.shape[0]
    for start in range(0, tail_rows, BLOCK):
        at = pl.ds(start, BLOCK)
        table[:, at] = tail_ref[at, :].T
    for ids, out in ((tail_id, tails_out), (neg_id, negt_out)):
        for start in range(0, ids.shape[1], BLOCK):
            at = pl.ds(start, BLOCK)
            got = nn(table[...], onehot(ids[:, at], 0, tail_rows))
            out[:, at] = got.astype(BF)
            if ids is neg_id:
                neg_out[at, :] = got.T.astype(BF)


def edge_kernel(
    count_ref,
    rel_ref,
    fetched_ref,
    ref_ids,
    rel_id,
    qual_rel,
    near_ref,
    far_ref,
    head_slot,
    proj_ref,
    tails_ref,
    negt_ref,
    neg_ref,
    near_out,
    far_out,
    sums_out,
    nr_out,
    query_out,
    pq_out,
    sums,
    *,
    rel_rows,
):
    width, edges = tails_ref.shape
    slots = fetched_ref.shape[0]
    half, head_rows, _ = near_ref.shape
    devices, sent_rows, _ = sums_out.shape
    share = sums.shape[0] // devices
    quals = ref_ids.shape[0]
    fetched_t = flip(fetched_ref[...])
    proj_hi, proj_lo = pieces(proj_ref[...], 2)
    projt_hi, projt_lo = pieces(proj_ref[...].T, 2)

    composed = jnp.zeros((width, edges), F32)
    rows = []
    for k in range(quals):
        rows.append(nn(fetched_t, onehot(ref_ids[k : k + 1, :], 0, slots)))
        composed = composed + rel_ref[k + 1] * rows[k]
    comp_hi, comp_lo = pieces(composed, 2)
    relation = rel_ref[0] + (nn(projt_hi, comp_hi) + (nn(projt_hi, comp_lo) + nn(projt_lo, comp_hi)))
    heads = jnp.zeros((width, edges), F32)
    for first, table in ((0, near_ref), (half, far_ref)):
        for owner in range(half):
            heads = heads + nn(flip(table[owner]), onehot(head_slot[...], (first + owner) * head_rows, head_rows))
    query = (heads * relation).astype(BF)
    query_out[...] = query
    query_f = query.astype(F32)
    tails = tails_ref[...].astype(F32)
    positive = jnp.sum(query_f * tails, axis=0, keepdims=True)
    scores = nn(neg_ref[...], query)
    top = jnp.maximum(jnp.max(scores, axis=0, keepdims=True), positive)
    neg_exp = jnp.exp(scores - top)
    pos_exp = jnp.exp(positive - top)
    total = jnp.sum(neg_exp, axis=0, keepdims=True) + pos_exp
    slot = lax.broadcasted_iota(jnp.int32, (1, edges), 1)
    live = jnp.where(slot < count_ref[0], 1.0, 0.0)
    scale = live / total
    neg_round = (neg_exp * scale).astype(BF)
    nr_out[...] = neg_round
    coef = pos_exp * scale - live
    pq_out[...] = (coef * query_f).astype(BF)
    query_grad = coef * tails + nn(negt_ref[...], neg_round)

    head_terms = (query_grad * relation).astype(BF)
    for first, out in ((0, near_out), (half, far_out)):
        for owner in range(half):
            hot = onehot(head_slot[...], (first + owner) * head_rows, head_rows)
            out[owner] = nt(hot, head_terms).astype(BF)

    relation_grad = query_grad * heads
    rg_hi, rg_lo = pieces(relation_grad, 2)
    comp_grad = nn(proj_hi, rg_hi) + (nn(proj_hi, rg_lo) + nn(proj_lo, rg_hi))
    rel_sum = nt(onehot(rel_id[...], 0, rel_rows), rg_hi)
    fetched_sum = jnp.zeros((slots, width), F32)
    for k in range(quals):
        hot = onehot(ref_ids[k : k + 1, :], 0, slots)
        rel_sum = rel_sum + nt(onehot(qual_rel[k : k + 1, :], 0, rel_rows), (comp_grad * rows[k]).astype(BF))
        fetched_sum = fetched_sum + nt(hot, (comp_grad * rel_ref[k + 1]).astype(BF))
    sums[:rel_rows, :] = rel_sum
    sums[rel_rows : rel_rows + width, :] = nt(comp_hi, rg_hi) + (nt(comp_hi, rg_lo) + nt(comp_lo, rg_hi))
    if sums.shape[0] > rel_rows + width:
        sums[rel_rows + width :, :] = jnp.zeros((sums.shape[0] - rel_rows - width, width), F32)
    both = [sums[...].reshape(devices, share, width), fetched_sum.reshape(devices, sent_rows - share, width)]
    sums_out[...] = jnp.concatenate(both, axis=1).astype(BF)


def add_kernel(got_ref, out_ref):
    devices, share, _ = out_ref.shape
    total = got_ref[0, :share, :].astype(F32)
    for index in range(1, devices):
        total = total + got_ref[index, :share, :].astype(F32)
    total = total.astype(BF)
    for index in range(devices):
        out_ref[index] = total


def tail_kernel(tail_id, neg_id, nr_ref, query_ref, pq_ref, tail_out, terms):
    edges = query_ref.shape[1]
    rows = tail_out.shape[0]
    step = pl.program_id(0)

    @pl.when(step == 0)
    def _():
        terms[:edges, :] = flip(pq_ref[...])
        terms[edges:, :] = nt(nr_ref[...], query_ref[...]).astype(BF)

    first = step * rows
    tail_out[...] = nn(onehot(tail_id[...], first, rows), terms[:edges, :]) + nn(
        onehot(neg_id[...], first, rows), terms[edges:, :]
    )


WHOLE = pl.BlockSpec(memory_space=pltpu.VMEM)


def call(kernel, outs, scratch, micros, vmem, *args, smem=(), grid=(), out_specs=None):
    shapes = [jax.ShapeDtypeStruct(shape, dtype) for shape, dtype in outs]
    return pl.pallas_call(
        kernel,
        out_shape=shapes,
        grid=grid,
        in_specs=[pl.BlockSpec(memory_space=pltpu.SMEM) if index in smem else WHOLE for index in range(len(args))],
        out_specs=out_specs or [WHOLE] * len(outs),
        scratch_shapes=[pltpu.VMEM(shape, dtype) for shape, dtype in scratch],
        compiler_params=pltpu.CompilerParams(vmem_limit_bytes=vmem * MIB),
        cost_estimate=pl.CostEstimate(flops=micros << 30, bytes_accessed=MIB, transcendentals=0),
    )(*args)


def exchange(values, axes):
    return lax.all_to_all(values, axes, split_axis=0, concat_axis=0, tiled=True)


def swap(values, axis):
    return lax.ppermute(values, axis, [(0, 1), (1, 0)])


def body(
    head_table,
    tail_table,
    qual_table,
    rel_table,
    proj,
    head_id,
    tail_id,
    rel_id,
    qual_rel,
    qual_ref,
    qual_req,
    neg_id,
    edge_count,
):
    head_rows, width = head_table.shape
    tail_rows = tail_table.shape[0]
    qual_rows = qual_table.shape[0]
    rel_rows = rel_table.shape[0]
    edges = head_id.shape[0]
    negs = neg_id.shape[0]
    slots = qual_req.shape[0]
    half = lax.axis_size("line")
    devices = lax.axis_size(AXES)
    quals = qual_ref.shape[1]
    cap = slots // devices
    near = lax.axis_index("near")

    arrived = exchange(qual_req.reshape(devices, cap), AXES)
    head_near = exchange(jnp.broadcast_to(head_table[None], (half, head_rows, width)), "line")
    head_far = swap(head_near, "near")
    owner = head_id // head_rows
    head_slot = ((jnp.bitwise_xor(owner, near) % 2) * half + owner // 2) * head_rows + head_id % head_rows
    head_slot = head_slot[None, :]

    rel_row = rel_id[None, :]
    qual_row = qual_rel.T
    ref_row = qual_ref.T
    tail_row = tail_id[None, :]
    neg_row = neg_id[None, :]
    (rel_looked,) = call(
        relation_lookup_kernel,
        [((quals + 1, width, edges), F32)],
        [((2 * width, rel_rows), BF)],
        5,
        24,
        rel_table,
        rel_row,
        qual_row,
        grid=(quals + 1,),
        out_specs=[pl.BlockSpec((1, width, edges), lambda i: (i, 0, 0))],
    )
    arrived, rel_looked = lax.optimization_barrier((arrived, rel_looked))
    picked = qual_table.at[arrived].get(mode="promise_in_bounds")
    fetched = exchange(picked, AXES).reshape(slots, width)
    tails, neg_t, neg = call(
        tail_lookup_kernel,
        [((width, edges), BF), ((width, negs), BF), ((negs, width), BF)],
        [((width, tail_rows), BF)],
        7,
        32,
        tail_table,
        tail_row,
        neg_row,
    )
    share = -(-(rel_rows + width) // (8 * devices)) * 8

    def edge(*refs):
        edge_kernel(*refs, rel_rows=rel_rows)

    near_part, far_part, sums_part, neg_round, query, pq = call(
        edge,
        [
            ((half, head_rows, width), BF),
            ((half, head_rows, width), BF),
            ((devices, share + cap, width), BF),
            ((negs, edges), BF),
            ((width, edges), BF),
            ((width, edges), BF),
        ],
        [((devices * share, width), F32)],
        15,
        48,
        edge_count,
        rel_looked,
        fetched,
        ref_row,
        rel_row,
        qual_row,
        head_near,
        head_far,
        head_slot,
        proj,
        tails,
        neg_t,
        neg,
        smem=(0,),
    )
    far_got = swap(far_part, "near")
    sums_got = exchange(sums_part, AXES)
    (sums_own,) = call(add_kernel, [((devices, share, width), BF)], [], 1, 16, sums_got)
    sums = exchange(sums_own, AXES).reshape(devices * share, width)

    near_sum = (near_part.astype(F32) + far_got.astype(F32)).astype(BF)
    head_got = exchange(near_sum, "line")
    head_grad = jnp.sum(head_got.astype(F32), axis=0)

    block = min(1024, tail_rows)
    (tail_grad,) = call(
        tail_kernel,
        [((tail_rows, width), F32)],
        [((edges + negs, width), BF)],
        8,
        32,
        tail_row,
        neg_row,
        neg_round,
        query,
        pq,
        grid=(tail_rows // block,),
        out_specs=[pl.BlockSpec((block, width), lambda i: (i, 0))],
    )
    returned = sums_got[:, share:, :].reshape(slots, width)
    hot = (jnp.arange(qual_rows, dtype=jnp.int32)[:, None] == arrived.reshape(1, -1)).astype(BF)
    qual_grad = jnp.dot(hot, returned, preferred_element_type=F32)
    rel_grad = sums[:rel_rows].astype(F32)
    proj_grad = sums[rel_rows : rel_rows + width].astype(F32)
    return (head_grad, tail_grad, qual_grad, rel_grad, proj_grad)


def solution(mesh):
    groups, members = mesh.devices.shape
    view = Mesh(mesh.devices.reshape(groups // 2, 2, members // 2, 2), AXES)
    rows = P(AXES, None)
    ids = P(AXES)
    in_specs = (rows, rows, rows, P(), P(), ids, ids, ids, rows, rows, ids, ids, ids)
    out_specs = (rows, rows, rows, P(), P())
    return jax.shard_map(body, mesh=view, in_specs=in_specs, out_specs=out_specs, check_vma=False)
```

time: 158 us -> 136 us (0.86)
  blocking collectives: 46.3 us -> 14.2 us
  Pallas kernels: 54 us -> 29.9 us
  local copies, waits for them, and re-layouts: 7.27 us -> 19.6 us
  waiting for transfers between devices: 31.8 us -> 43 us
  starting transfers between devices: 12.3 us -> 22.1 us
    all_to_all x3 -> x1, blocking collectives: 46.3 us -> 14.2 us  [exchange(): return lax.all_to_all(values, axes, split_axis=0, concat_axis=0, tiled=True)]
    pallas_call x4 -> x5, Pallas kernels: 54 us -> 29.9 us  [call(): pl.pallas_call(kernel, out_shape=shapes, grid=grid, in_specs=[pl.BlockSpe...]
    ppermute x0 -> x2, waiting for transfers between devices: none -> 22 us  [swap(): return lax.ppermute(values, axis, [(0, 1), (1, 0)])]
    unnamed x14 -> x48, local copies, waits for them, and re-layouts: 1.01 us -> 15.1 us
    all_to_all x4 -> x5, waiting for transfers between devices: 31.8 us -> 21.1 us  [exchange(): return lax.all_to_all(values, axes, split_axis=0, concat_axis=0, tiled=True)]
    all_to_all x4 -> x5, starting transfers between devices: 12.3 us -> 18.5 us  [exchange(): return lax.all_to_all(values, axes, split_axis=0, concat_axis=0, tiled=True)]
    ppermute x0 -> x2, starting transfers between devices: none -> 3.53 us  [swap(): return lax.ppermute(values, axis, [(0, 1), (1, 0)])]
    convert_element_type x1 -> x3, other arithmetic: 0.08 us -> 2.48 us  [the longest x1 0.93 us: body(): near_sum = (near_part.astype(F32) + far_got.astype(F32)).astype(BF)]
  transfers between devices with their start and end apart: 4 -> 7, of which waited for: 4 -> 5; matrix products, arithmetic and copies ran while one was open for 4% -> 4% of each run, Pallas kernels for 18% -> 12%
where the time goes in v3:
time: 136 us; the launch traced here: 135 us
  waiting for transfers between devices  43 us (32%)
  Pallas kernels  29.9 us (22%)
  starting transfers between devices  22.1 us (16%)
  local copies, waits for them, and re-layouts  19.6 us (14%)
  blocking collectives  14.2 us (10%)
  other arithmetic  3.29 us (2%)
  between operations  1.48 us (1%)
    pallas_call x5, Pallas kernels, call(): pl.pallas_call(kernel, out_shape=shapes, grid=grid, in_specs=[pl.BlockSpe...  29.9 us
    ppermute x2, waiting for transfers between devices, swap(): return lax.ppermute(values, axis, [(0, 1), (1, 0)])  22 us
    all_to_all x5, waiting for transfers between devices, exchange(): return lax.all_to_all(values, axes, split_axis=0, concat_axis=0, tiled=True)  21.1 us
    all_to_all x5, starting transfers between devices, exchange(): return lax.all_to_all(values, axes, split_axis=0, concat_axis=0, tiled=True)  18.5 us
    unnamed x48, local copies, waits for them, and re-layouts  15.1 us
    all_to_all x1, blocking collectives, exchange(): return lax.all_to_all(values, axes, split_axis=0, concat_axis=0, tiled=True)  14.2 us
    ppermute x2, starting transfers between devices, swap(): return lax.ppermute(values, axis, [(0, 1), (1, 0)])  3.53 us
  transfers between devices with their start and end apart: 7, of which 5 were waited for; matrix products, arithmetic and copies ran while one was open for 4% of the time, Pallas kernels for 12%

profile of v3, /device:TPU:0, one launch (start us, length us, event | category | flops | bytes accessed | tf_op | source)
XLA Modules:
  0.0 134.9 jit_solution(7843718497055104401)
XLA Ops:
  0.6 0.0 copy-start
  0.6 0.8 all_to_all.23
  1.5 14.2 %all_to_all.37 = s32[32,1,8]{2,1,0:T(1,128)S(1)} all-to-all(s32[32,1,8]{2,1,0:T(1,128)S(1)} %bitcast.29), channel_id=1, replica_groups=mesh['pair'=2,'core'=2,'line'=4,'near'=2] {'pair','core','line','near'}, dimensions={0} | all-to-all | bytes 2048 | tf_op jit(solution)/shard_map/all_to_all | solution.py:214
  15.7 1.7 %broadcast_in_dim.24 = bf16[4,256,256]{2,1,0:T(8,128)(2,1)} broadcast(bf16[256,256]{1,0:T(8,128)(2,1)} %param.13), dimensions={1,2} | broadcast | bytes 655360 | tf_op jit(solution)/shard_map/broadcast_in_dim | solution.py:250
  17.4 3.5 %all-to-all-start.2 = ((bf16[4,256,256]{2,1,0:T(8,128)(2,1)}), bf16[4,256,256]{2,1,0:T(8,128)(2,1)S(1)}, u32[]{:S(2)}, u32[]{:S(2)}) async-start(bf16[4,256,256]{2,1,0:T(8,128)(2,1)} %broadcast_in_dim.24), calls=%async_computation.2 | async-start | bytes 1048576 | tf_op jit(solution)/shard_map/all_to_all | solution.py:214
  20.9 0.0 copy-start.2
  20.9 1.0 copy-done.2
  21.9 0.7 copy-done.4
  22.7 0.7 copy-done.7
  23.3 3.7 %shard_map.164.refs_1_ = f32[5,256,1024]{2,1,0:T(8,128)S(1)} custom-call(f32[512,256]{1,0:T(8,128)S(1)} %copy-done.2, s32[1,1024]{1,0:T(1,128)S(1)} %bitcast.19, s32[4,1024]{1,0:T(4,128)S(1)} %bitcast.16), custom_call_target="tpu_custom_call" | custom-call | flops 5368709120 | bytes 1048576 | tf_op jit(solution)/shard_map/pallas_call | solution.py:201
  27.1 2.3 %copy-done.11 = f32[5,256,1024]{2,1,0:T(8,128)} copy-done((f32[5,256,1024]{2,1,0:T(8,128)}, f32[5,256,1024]{2,1,0:T(8,128)S(1)}, u32[]{:S(2)}) %copy-start.11) | copy-done | bytes 5242904
  29.4 0.1 reshape.31
  29.5 1.8 %gather_fusion = bf16[256,256]{1,0:T(8,128)(2,1)} fusion(bf16[1024,256]{1,0:T(8,128)(2,1)S(1)} %copy-done, s32[1024]{0:T(1024)S(1)} %pad_clamp_fusion), kind=kCustom, calls=%fused_computation | custom fusion | bytes 263168 | tf_op jit(solution)/shard_map/gather | solution.py:274
  31.4 4.3 %all-to-all-done.2.refs_6_ = bf16[4,256,256]{2,1,0:T(8,128)(2,1)S(1)} async-done(((bf16[4,256,256]{2,1,0:T(8,128)(2,1)}), bf16[4,256,256]{2,1,0:T(8,128)(2,1)S(1)}, u32[]{:S(2)}, u32[]{:S(2)}) %all-to-all-start.2) | async-done | bytes 524320 | tf_op jit(solution)/shard_map/all_to_all | solution.py:214
  35.6 2.8 %all-to-all-start.1 = ((bf16[32,8,256]{2,1,0:T(8,128)(2,1)}), bf16[32,8,256]{2,1,0:T(8,128)(2,1)S(1)}, u32[]{:S(2)}, u32[]{:S(2)}) async-start(bf16[32,8,256]{2,1,0:T(8,128)(2,1)} %bitcast.4), calls=%async_computation.1 | async-start | bytes 262144 | tf_op jit(solution)/shard_map/all_to_all | solution.py:214
  38.4 1.7 %collective-permute-start = (bf16[4,256,256]{2,1,0:T(8,128)(2,1)S(1)}, bf16[4,256,256]{2,1,0:T(8,128)(2,1)S(1)}, u32[]{:S(2)}, u32[]{:S(2)}) collective-permute-start(bf16[4,256,256]{2,1,0:T(8,128)(2,1)S(1)} %all-to-all-done.2.refs_6_), channel_id=1, source_target_pairs={{0,1},{1,0},{2,3},{3,2},{4,5},{5,4},{6,7},{7,6},{8,9},{9,8},{10,11... | collective-permute-start | bytes 1572872 | tf_op jit(solution)/shard_map/ppermute | solution.py:218
  40.1 1.6 %copy-done.1 = bf16[4096,256]{1,0:T(8,128)(2,1)S(1)} copy-done((bf16[4096,256]{1,0:T(8,128)(2,1)S(1)}, bf16[4096,256]{1,0:T(8,128)(2,1)}, u32[]{:S(2)}) %copy-start.1) | copy-done | bytes 2097176
  41.7 0.0 copy-start.8
  41.7 4.7 %shard_map.165 = (bf16[256,1024]{1,0:T(8,128)(2,1)S(1)}, bf16[256,1024]{1,0:T(8,128)(2,1)S(1)}, bf16[1024,256]{1,0:T(8,128)(2,1)S(1)}) custom-call(bf16[4096,256]{1,0:T(8,128)(2,1)S(1)} %copy-done.1, s32[1,1024]{1,0:T(1,128)S(1)} %bitcast.21, s32[1,1024]{1,0:T(1,128)S(1)} %bitcast.23), custom_call_target="tpu_custom_call" | custom-call | flops 7516192768 | bytes 1048576 | tf_op jit(solution)/shard_map/pallas_call | solution.py:201
  46.5 0.0 copy-start.17
  46.5 0.8 copy-done.17
  47.3 0.8 copy-done.19
  48.1 0.8 copy-done.21
  49.6 4.1 %collective-permute-done.refs_7_ = bf16[4,256,256]{2,1,0:T(8,128)(2,1)S(1)} collective-permute-done((bf16[4,256,256]{2,1,0:T(8,128)(2,1)S(1)}, bf16[4,256,256]{2,1,0:T(8,128)(2,1)S(1)}, u32[]{:S(2)}, u32[]{:S(2)}) %collective-permute-start) | collective-permute-done | bytes 524320 | tf_op jit(solution)/shard_map/ppermute | solution.py:218
  53.7 0.0 copy-start.18
  53.7 1.0 copy-done.18
  54.7 1.0 copy-done.20
  55.7 1.0 copy-done.22
  56.8 13.9 %shard_map.166 = (bf16[4,256,256]{2,1,0:T(8,128)(2,1)S(1)}, bf16[4,256,256]{2,1,0:T(8,128)(2,1)S(1)}, bf16[32,32,256]{2,1,0:T(8,128)(2,1)}, bf16[1024,1024]{1,0:...) custom-call(s32[1]{0:T(128)S(6)} %copy.19.refs_0_, f32[5,256,1024]{2,1,0:T(8,128)} %copy-done.11, ...), custom_call_target="tpu_custom_call" | custom-call | flops 16106127360 | bytes 1048576 | tf_op jit(solution)/shard_map/pallas_call | solution.py:201
  70.6 0.8 copy-done.13
  71.4 0.8 copy-done.15
  72.2 5.0 %all-to-all-start.4 = ((bf16[32,32,256]{2,1,0:T(8,128)(2,1)}), bf16[32,32,256]{2,1,0:T(8,128)(2,1)S(1)}, u32[]{:S(2)}, u32[]{:S(2)}) async-start(bf16[32,32,256]{2,1,0:T(8,128)(2,1)} %get-tuple-element.26), calls=%async_computation.4 | async-start | bytes 1048576 | tf_op jit(solution)/shard_map/all_to_all | solution.py:214
  77.3 1.8 %collective-permute-start.1 = (bf16[4,256,256]{2,1,0:T(8,128)(2,1)S(1)}, bf16[4,256,256]{2,1,0:T(8,128)(2,1)S(1)}, u32[]{:S(2)}, u32[]{:S(2)}) collective-permute-start(bf16[4,256,256]{2,1,0:T(8,128)(2,1)S(1)} %get-tuple-element.22), channel_id=1, source_target_pairs={{0,1},{1,0},{2,3},{3,2},{4,5},{5,4},{6,7},{7,6},{8,9},{9,8},{10,11... | collective-permute-start | bytes 1572872 | tf_op jit(solution)/shard_map/ppermute | solution.py:218
  79.1 17.9 %collective-permute-done.1 = bf16[4,256,256]{2,1,0:T(8,128)(2,1)S(1)} collective-permute-done((bf16[4,256,256]{2,1,0:T(8,128)(2,1)S(1)}, bf16[4,256,256]{2,1,0:T(8,128)(2,1)S(1)}, u32[]{:S(2)}, u32[]{:S(2)}) %collective-permute-start.1) | collective-permute-done | bytes 524320 | tf_op jit(solution)/shard_map/ppermute | solution.py:218
  97.0 0.9 add_convert_fusion
  97.9 4.5 %all-to-all-start.3 = ((bf16[4,256,256]{2,1,0:T(8,128)(2,1)}), bf16[4,256,256]{2,1,0:T(8,128)(2,1)S(1)}, u32[]{:S(2)}, u32[]{:S(2)}) async-start(bf16[4,256,256]{2,1,0:T(8,128)(2,1)} %add_convert_fusion), calls=%async_computation.3 | async-start | bytes 1048576 | tf_op jit(solution)/shard_map/all_to_all | solution.py:214
  102.5 0.1 eq.19
  102.5 0.8 shard_map.168
  103.4 13.7 %all-to-all-done.3 = bf16[4,256,256]{2,1,0:T(8,128)(2,1)S(1)} async-done(((bf16[4,256,256]{2,1,0:T(8,128)(2,1)}), bf16[4,256,256]{2,1,0:T(8,128)(2,1)S(1)}, u32[]{:S(2)}, u32[]{:S(2)}) %all-to-all-start.3) | async-done | bytes 524320 | tf_op jit(solution)/shard_map/all_to_all | solution.py:214
  117.1 2.7 %all-to-all-start.5 = ((bf16[32,24,256]{2,1,0:T(8,128)(2,1)}), bf16[32,24,256]{2,1,0:T(8,128)(2,1)S(1)}, u32[]{:S(2)}, u32[]{:S(2)}) async-start(bf16[32,24,256]{2,1,0:T(8,128)(2,1)} %shard_map.168), calls=%async_computation.5 | async-start | bytes 786432 | tf_op jit(solution)/shard_map/all_to_all | solution.py:214
  119.8 0.0 copy-start.12
  119.8 1.6 %copy-done.12 = bf16[1024,1024]{1,0:T(8,128)(2,1)S(1)} copy-done((bf16[1024,1024]{1,0:T(8,128)(2,1)S(1)}, bf16[1024,1024]{1,0:T(8,128)(2,1)}, u32[]{:S(2)}) %copy-start.12) | copy-done | bytes 2097176
  121.4 6.8 %shard_map.167 = f32[4096,256]{1,0:T(8,128)} custom-call(s32[1,1024]{1,0:T(1,128)S(1)} %bitcast.22, s32[1,1024]{1,0:T(1,128)S(1)} %bitcast.24, bf16[1024,1024]{1,0:T(8,128)(2,1)S(1)} %copy-done.12, bf16[256,1024]{1,0:T(8,128)(2,1)S(1)} %copy-done.14, bf16[256,1024]{1,0:T(8,128)(2,1)S(1)} %copy-done.16), custom_call_target="tpu_custom_call" | custom-call | flops 8589934592 | bytes 1048576 | tf_op jit(solution)/shard_map/pallas_call | solution.py:201
  128.2 1.3 fusion
  129.5 0.8 convert_reduce_fusion
  130.2 3.1 %all-to-all-done.5 = bf16[32,24,256]{2,1,0:T(8,128)(2,1)S(1)} async-done(((bf16[32,24,256]{2,1,0:T(8,128)(2,1)}), bf16[32,24,256]{2,1,0:T(8,128)(2,1)S(1)}, u32[]{:S(2)}, u32[]{:S(2)}) %all-to-all-start.5) | async-done | bytes 393248 | tf_op jit(solution)/shard_map/all_to_all | solution.py:214
  133.4 0.7 slice_convert_fusion.1
  134.1 0.8 slice_convert_fusion
  (33 shorter events, 0.1 us)
Async XLA Ops:
  0.6 28.9 %copy-start = (bf16[1024,256]{1,0:T(8,128)(2,1)S(1)}, bf16[1024,256]{1,0:T(8,128)(2,1)}, u32[]{:S(2)}) copy-start(bf16[1024,256]{1,0:T(8,128)(2,1)} %param.15) | copy-start | bytes 1572868
  17.4 18.2 %all-to-all-start.2 = ((bf16[4,256,256]{2,1,0:T(8,128)(2,1)}), bf16[4,256,256]{2,1,0:T(8,128)(2,1)S(1)}, u32[]{:S(2)}, u32[]{:S(2)}) async-start(bf16[4,256,256]{2,1,0:T(8,128)(2,1)} %broadcast_in_dim.24), calls=%async_computation.2 | async-start | bytes 1048576 | tf_op jit(solution)/shard_map/all_to_all | solution.py:214
  20.9 1.0 copy-start.2
  21.9 0.7 copy-start.4
  22.7 0.7 copy-start.7
  23.3 16.8 %copy-start.9 = (s32[1024]{0:T(1024)S(1)}, s32[1024]{0:T(1024)}, u32[]{:S(2)}) copy-start(s32[1024]{0:T(1024)} %param.19) | copy-start | bytes 12292
  23.3 16.8 %copy-start.10 = (s32[1024]{0:T(1024)S(1)}, s32[1024]{0:T(1024)}, u32[]{:S(2)}) copy-start(s32[1024]{0:T(1024)} %param.24) | copy-start | bytes 12292
  27.1 2.3 %copy-start.11 = (f32[5,256,1024]{2,1,0:T(8,128)}, f32[5,256,1024]{2,1,0:T(8,128)S(1)}, u32[]{:S(2)}) copy-start(f32[5,256,1024]{2,1,0:T(8,128)S(1)} %shard_map.164.refs_1_) | copy-start | bytes 15728644
  35.6 13.9 %all-to-all-start.1 = ((bf16[32,8,256]{2,1,0:T(8,128)(2,1)}), bf16[32,8,256]{2,1,0:T(8,128)(2,1)S(1)}, u32[]{:S(2)}, u32[]{:S(2)}) async-start(bf16[32,8,256]{2,1,0:T(8,128)(2,1)} %bitcast.4), calls=%async_computation.1 | async-start | bytes 262144 | tf_op jit(solution)/shard_map/all_to_all | solution.py:214
  38.4 15.2 %collective-permute-start = (bf16[4,256,256]{2,1,0:T(8,128)(2,1)S(1)}, bf16[4,256,256]{2,1,0:T(8,128)(2,1)S(1)}, u32[]{:S(2)}, u32[]{:S(2)}) collective-permute-start(bf16[4,256,256]{2,1,0:T(8,128)(2,1)S(1)} %all-to-all-done.2.refs_6_), channel_id=1, source_target_pairs={{0,1},{1,0},{2,3},{3,2},{4,5},{5,4},{6,7},{7,6},{8,9},{9,8},{10,11... | collective-permute-start | bytes 1572872 | tf_op jit(solution)/shard_map/ppermute | solution.py:218
  40.1 1.6 %copy-start.1 = (bf16[4096,256]{1,0:T(8,128)(2,1)S(1)}, bf16[4096,256]{1,0:T(8,128)(2,1)}, u32[]{:S(2)}) copy-start(bf16[4096,256]{1,0:T(8,128)(2,1)} %tail_ref.1) | copy-start | bytes 6291460
  41.7 7.8 %copy-start.23 = (s32[1024]{0:T(1024)S(1)}, s32[1024]{0:T(1024)}, u32[]{:S(2)}) copy-start(s32[1024]{0:T(1024)} %param.18) | copy-start | bytes 12292
  41.7 11.9 %copy-start.3 = (f32[256,256]{1,0:T(8,128)S(1)}, f32[256,256]{1,0:T(8,128)}, u32[]{:S(2)}) copy-start(f32[256,256]{1,0:T(8,128)} %refs_9_.1) | copy-start | bytes 786436
  41.7 11.9 %copy-start.5 = (s32[1024,4]{0,1:T(4,128)S(1)}, s32[1024,4]{0,1:T(4,128)}, u32[]{:S(2)}) copy-start(s32[1024,4]{0,1:T(4,128)} %param.21) | copy-start | bytes 49156
  41.7 11.9 %copy-start.6 = (s32[1024,4]{0,1:T(4,128)S(1)}, s32[1024,4]{0,1:T(4,128)}, u32[]{:S(2)}) copy-start(s32[1024,4]{0,1:T(4,128)} %param.22) | copy-start | bytes 49156
  41.7 11.9 %copy-start.8 = (s32[1024]{0:T(1024)S(1)}, s32[1024]{0:T(1024)}, u32[]{:S(2)}) copy-start(s32[1024]{0:T(1024)} %param.20) | copy-start | bytes 12292
  46.5 0.8 copy-start.17
  47.3 0.8 copy-start.19
  48.1 0.8 copy-start.21
  53.7 1.0 copy-start.18
  54.7 1.0 copy-start.20
  55.7 1.0 copy-start.22
  70.6 0.8 copy-start.13
  71.4 0.8 copy-start.15
  72.2 47.6 %copy-start.14 = (bf16[256,1024]{1,0:T(8,128)(2,1)S(1)}, bf16[256,1024]{1,0:T(8,128)(2,1)}, u32[]{:S(2)}) copy-start(bf16[256,1024]{1,0:T(8,128)(2,1)} %copy-done.13) | copy-start | bytes 1572868
  72.2 25.7 %all-to-all-start.4 = ((bf16[32,32,256]{2,1,0:T(8,128)(2,1)}), bf16[32,32,256]{2,1,0:T(8,128)(2,1)S(1)}, u32[]{:S(2)}, u32[]{:S(2)}) async-start(bf16[32,32,256]{2,1,0:T(8,128)(2,1)} %get-tuple-element.26), calls=%async_computation.4 | async-start | bytes 1048576 | tf_op jit(solution)/shard_map/all_to_all | solution.py:214
  77.3 19.7 %collective-permute-start.1 = (bf16[4,256,256]{2,1,0:T(8,128)(2,1)S(1)}, bf16[4,256,256]{2,1,0:T(8,128)(2,1)S(1)}, u32[]{:S(2)}, u32[]{:S(2)}) collective-permute-start(bf16[4,256,256]{2,1,0:T(8,128)(2,1)S(1)} %get-tuple-element.22), channel_id=1, source_target_pairs={{0,1},{1,0},{2,3},{3,2},{4,5},{5,4},{6,7},{7,6},{8,9},{9,8},{10,11... | collective-permute-start | bytes 1572872 | tf_op jit(solution)/shard_map/ppermute | solution.py:218
  97.0 22.8 %copy-start.16 = (bf16[256,1024]{1,0:T(8,128)(2,1)S(1)}, bf16[256,1024]{1,0:T(8,128)(2,1)}, u32[]{:S(2)}) copy-start(bf16[256,1024]{1,0:T(8,128)(2,1)} %copy-done.15) | copy-start | bytes 1572868
  97.9 19.1 %all-to-all-start.3 = ((bf16[4,256,256]{2,1,0:T(8,128)(2,1)}), bf16[4,256,256]{2,1,0:T(8,128)(2,1)S(1)}, u32[]{:S(2)}, u32[]{:S(2)}) async-start(bf16[4,256,256]{2,1,0:T(8,128)(2,1)} %add_convert_fusion), calls=%async_computation.3 | async-start | bytes 1048576 | tf_op jit(solution)/shard_map/all_to_all | solution.py:214
  117.1 16.3 %all-to-all-start.5 = ((bf16[32,24,256]{2,1,0:T(8,128)(2,1)}), bf16[32,24,256]{2,1,0:T(8,128)(2,1)S(1)}, u32[]{:S(2)}, u32[]{:S(2)}) async-start(bf16[32,24,256]{2,1,0:T(8,128)(2,1)} %shard_map.168), calls=%async_computation.5 | async-start | bytes 786432 | tf_op jit(solution)/shard_map/all_to_all | solution.py:214
  119.8 1.6 %copy-start.12 = (bf16[1024,1024]{1,0:T(8,128)(2,1)S(1)}, bf16[1024,1024]{1,0:T(8,128)(2,1)}, u32[]{:S(2)}) copy-start(bf16[1024,1024]{1,0:T(8,128)(2,1)} %get-tuple-element.23.nr_ref) | copy-start | bytes 6291460

commit v4 on v3

v4 whole, which is shorter than its diff:
```python
import jax
import jax.numpy as jnp
from jax import lax
from jax.experimental import pallas as pl
from jax.experimental.pallas import tpu as pltpu
from jax.sharding import Mesh, PartitionSpec as P

BF = jnp.bfloat16
F32 = jnp.float32
MIB = 1024 * 1024
AXES = ("pair", "core", "line", "near")
MEMBER = ("line", "near")
CHIPS = ("pair", "line", "near")
PAIRS = 2
BLOCK = 256


def nn(a, b):
    return jnp.dot(a, b, preferred_element_type=F32)


def nt(a, b):
    return lax.dot_general(a, b, (((1,), (1,)), ((), ())), preferred_element_type=F32)


def pieces(values, count):
    out = []
    for _ in range(count):
        part = values.astype(BF)
        out.append(part)
        values = values - part.astype(F32)
    return out


def flip(values):
    return values.astype(F32).T.astype(BF)


def onehot(ids_row, first, rows):
    iota = lax.broadcasted_iota(jnp.int32, (rows, ids_row.shape[1]), 0)
    return jnp.where(iota == ids_row - first, 1.0, 0.0).astype(BF)


def relation_lookup_kernel(rel_ref, rel_id, qual_rel, rel_out, table):
    rel_rows, width = rel_ref.shape
    edges = rel_id.shape[1]
    step = pl.program_id(0)

    @pl.when(step == 0)
    def _():
        for index, part in enumerate(pieces(rel_ref[...].T, 2)):
            table[index * width : (index + 1) * width, :] = part

    def look(ids):
        for start in range(0, edges, BLOCK):
            at = pl.ds(start, BLOCK)
            got = nn(table[...], onehot(ids[:, at], 0, rel_rows))
            rel_out[0, :, at] = got[:width] + got[width:]

    @pl.when(step == 0)
    def _():
        look(rel_id)

    for k in range(qual_rel.shape[0]):

        @pl.when(step == k + 1)
        def _():
            look(qual_rel.at[k : k + 1])


def tail_lookup_kernel(
    tail_hbm, tail_id, neg_id, tails_out, negt_out, neg_out, tail_ref, table, tails, negt, neg, in_sems, out_sems
):
    tail_rows = tail_ref.shape[0]
    chunks = in_sems.shape[0]
    size = tail_rows // chunks
    loads = []
    for index in range(chunks):
        at = pl.ds(index * size, size)
        loads.append(pltpu.make_async_copy(tail_hbm.at[at, :], tail_ref.at[at, :], in_sems.at[index]))
        loads[index].start()
    for index in range(chunks):
        loads[index].wait()
        for start in range(index * size, (index + 1) * size, BLOCK):
            at = pl.ds(start, BLOCK)
            table[:, at] = tail_ref[at, :].T
    stores = []

    def store(source, target):
        stores.append(pltpu.make_async_copy(source, target, out_sems.at[len(stores)]))
        stores[-1].start()

    for ids, out in ((neg_id, negt), (tail_id, tails)):
        for start in range(0, ids.shape[1], BLOCK):
            at = pl.ds(start, BLOCK)
            got = nn(table[...], onehot(ids[:, at], 0, tail_rows))
            out[:, at] = got.astype(BF)
            if ids is neg_id:
                neg[at, :] = got.T.astype(BF)
        if ids is neg_id:
            store(negt, negt_out)
            store(neg, neg_out)
    store(tails, tails_out)
    for copy in stores:
        copy.wait()


def edge_kernel(
    count_ref,
    place_ref,
    rel_hbm,
    near_hbm,
    far_hbm,
    tails_hbm,
    neg_hbm,
    negt_hbm,
    fetched_ref,
    ref_ids,
    rel_id,
    qual_rel,
    head_id,
    proj_ref,
    far_out,
    near_out,
    own_out,
    other_out,
    terms_out,
    rel_ref,
    near_ref,
    far_ref,
    tails_ref,
    neg_ref,
    negt_ref,
    sums,
    packed,
    terms,
    in_sems,
    out_sems,
    *,
    rel_rows,
):
    width, edges = tails_ref.shape
    slots = fetched_ref.shape[0]
    half, head_rows, _ = near_ref.shape
    cores, chips, _, lanes = packed.shape
    share = sums.shape[0] // chips
    quals = ref_ids.shape[0]
    cap = slots // (cores * chips)

    loads = []
    for index, (source, target) in enumerate(
        (
            (rel_hbm, rel_ref),
            (near_hbm, near_ref),
            (far_hbm, far_ref),
            (tails_hbm, tails_ref),
            (neg_hbm, neg_ref),
            (negt_hbm, negt_ref),
        )
    ):
        loads.append(pltpu.make_async_copy(source, target, in_sems.at[index]))
        loads[index].start()

    fetched_t = flip(fetched_ref[...])
    proj_hi, proj_lo = pieces(proj_ref[...], 2)
    projt_hi, projt_lo = pieces(proj_ref[...].T, 2)
    rows = [nn(fetched_t, onehot(ref_ids[k : k + 1, :], 0, slots)) for k in range(quals)]
    loads[0].wait()
    composed = rel_ref[1] * rows[0]
    for k in range(1, quals):
        composed = composed + rel_ref[k + 1] * rows[k]
    comp_hi, comp_lo = pieces(composed, 2)
    relation = rel_ref[0] + (nn(projt_hi, comp_hi) + (nn(projt_hi, comp_lo) + nn(projt_lo, comp_hi)))
    loads[1].wait()
    loads[2].wait()
    offset = jnp.bitwise_xor(head_id[...] // head_rows, place_ref[1])
    head_slot = ((offset % 2) * half + offset // 2) * head_rows + head_id[...] % head_rows
    heads = jnp.zeros((width, edges), F32)
    for first, table in ((0, near_ref), (half, far_ref)):
        for owner in range(half):
            heads = heads + nn(flip(table[owner]), onehot(head_slot, (first + owner) * head_rows, head_rows))
    query = (heads * relation).astype(BF)
    query_f = query.astype(F32)
    loads[3].wait()
    tails = tails_ref[...].astype(F32)
    positive = jnp.sum(query_f * tails, axis=0, keepdims=True)
    loads[4].wait()
    scores = nn(neg_ref[...], query)
    top = jnp.maximum(jnp.max(scores, axis=0, keepdims=True), positive)
    neg_exp = jnp.exp(scores - top)
    pos_exp = jnp.exp(positive - top)
    total = jnp.sum(neg_exp, axis=0, keepdims=True) + pos_exp
    slot = lax.broadcasted_iota(jnp.int32, (1, edges), 1)
    live = jnp.where(slot < count_ref[0], 1.0, 0.0)
    scale = live / total
    neg_round = (neg_exp * scale).astype(BF)
    coef = pos_exp * scale - live
    loads[5].wait()
    query_grad = coef * tails + nn(negt_ref[...], neg_round)

    stores = []

    def store(source, target):
        stores.append(pltpu.make_async_copy(source, target, out_sems.at[len(stores)]))
        stores[-1].start()

    head_terms = (query_grad * relation).astype(BF)
    for first, part, out in ((half, far_ref, far_out), (0, near_ref, near_out)):
        for owner in range(half):
            hot = onehot(head_slot, (first + owner) * head_rows, head_rows)
            part[owner] = nt(hot, head_terms).astype(BF)
        store(part, out)

    relation_grad = query_grad * heads
    rg_hi, rg_lo = pieces(relation_grad, 2)
    comp_grad = nn(proj_hi, rg_hi) + (nn(proj_hi, rg_lo) + nn(proj_lo, rg_hi))
    rel_sum = nt(onehot(rel_id[...], 0, rel_rows), rg_hi)
    fetched_sum = jnp.zeros((slots, width), F32)
    for k in range(quals):
        hot = onehot(ref_ids[k : k + 1, :], 0, slots)
        rel_sum = rel_sum + nt(onehot(qual_rel[k : k + 1, :], 0, rel_rows), (comp_grad * rows[k]).astype(BF))
        fetched_sum = fetched_sum + nt(hot, (comp_grad * rel_ref[k + 1]).astype(BF))
    sums[:rel_rows, :] = rel_sum
    sums[rel_rows : rel_rows + width, :] = nt(comp_hi, rg_hi) + (nt(comp_hi, rg_lo) + nt(comp_lo, rg_hi))
    if sums.shape[0] > rel_rows + width:
        sums[rel_rows + width :, :] = jnp.zeros((sums.shape[0] - rel_rows - width, width), F32)
    pairs = fetched_sum.reshape(-1, cores, chips // PAIRS, cap, width)
    for core in range(cores):
        mine = pairs[:, core].reshape(chips, cap, width)
        parts = [sums[:, core * lanes : (core + 1) * lanes].reshape(chips, share, lanes)]
        parts += [mine[:, :, start : start + lanes] for start in range(0, width, lanes)]
        packed[core] = jnp.concatenate(parts, axis=1).astype(BF)
    store(packed.at[place_ref[0]], own_out)
    store(packed.at[1 - place_ref[0]], other_out)

    terms[:edges, :] = flip((coef * query_f).astype(BF))
    terms[edges:, :] = nt(neg_round, query).astype(BF)
    store(terms, terms_out)
    for copy in stores:
        copy.wait()


def combine_kernel(own_ref, got_ref, out_ref):
    chips, sent, lanes = own_ref.shape
    passed = out_ref.shape[1] - sent
    share = sent - passed
    summed = own_ref[:, :share, :].astype(F32) + got_ref[:, :share, :].astype(F32)
    out_ref[:, :share, :] = summed.astype(BF)
    out_ref[:, share:sent, :] = own_ref[:, share:, :]
    out_ref[:, sent:, :] = got_ref[:, share:, :]


def add_kernel(got_ref, out_ref):
    chips, share, _ = out_ref.shape
    total = got_ref[0, :share, :].astype(F32)
    for index in range(1, chips):
        total = total + got_ref[index, :share, :].astype(F32)
    total = total.astype(BF)
    for index in range(chips):
        out_ref[index] = total


def finish_kernel(place_ref, own_ref, got_ref, rel_out, proj_out):
    rel_rows = rel_out.shape[0]
    proj_rows = proj_out.shape[0]
    lanes = own_ref.shape[1]
    for ref, core in ((own_ref, place_ref[0]), (got_ref, 1 - place_ref[0])):
        at = pl.ds(pl.multiple_of(core * lanes, lanes), lanes)
        rel_out[:, at] = ref[:rel_rows, :].astype(F32)
        proj_out[:, at] = ref[rel_rows : rel_rows + proj_rows, :].astype(F32)


def qual_kernel(place_ref, got_ref, asked, qual_out):
    qual_rows, width = qual_out.shape
    chips, rows, lanes = got_ref.shape
    cores = asked.shape[0]
    cap = asked.shape[1] // chips
    parts = width // lanes
    first = rows - cores * parts * cap
    passed = got_ref[:, first:, :].astype(F32)
    hots = [
        onehot(asked[pl.ds(place_ref[0], 1), :], 0, qual_rows),
        onehot(asked[pl.ds(1 - place_ref[0], 1), :], 0, qual_rows),
    ]
    for part in range(parts):
        total = jnp.zeros((qual_rows, lanes), F32)
        for core in range(cores):
            start = (core * parts + part) * cap
            sent = passed[:, start : start + cap, :].reshape(chips * cap, lanes).astype(BF)
            total = total + nn(hots[core], sent)
        qual_out[:, part * lanes : (part + 1) * lanes] = total


def tail_kernel(tail_id, neg_id, terms, *refs, skip):
    tail_out = refs[-1]
    edges = tail_id.shape[1]
    rows = tail_out.shape[0]
    first = (pl.program_id(0) + skip) * rows
    tail_out[...] = nn(onehot(tail_id[...], first, rows), terms[:edges, :]) + nn(
        onehot(neg_id[...], first, rows), terms[edges:, :]
    )


WHOLE = pl.BlockSpec(memory_space=pltpu.VMEM)


def call(kernel, outs, scratch, micros, vmem, *args, smem=(), away=(), aliases={}, grid=(), out_specs=None):
    shapes = [jax.ShapeDtypeStruct(shape, dtype) for shape, dtype in outs]
    places = {**{index: pltpu.SMEM for index in smem}, **{index: pl.ANY for index in away}}
    return pl.pallas_call(
        kernel,
        out_shape=shapes,
        grid=grid,
        in_specs=[pl.BlockSpec(memory_space=places.get(index, pltpu.VMEM)) for index in range(len(args))],
        out_specs=out_specs or [WHOLE] * len(outs),
        scratch_shapes=scratch,
        input_output_aliases=aliases,
        compiler_params=pltpu.CompilerParams(vmem_limit_bytes=vmem * MIB),
        cost_estimate=pl.CostEstimate(flops=micros << 30, bytes_accessed=MIB, transcendentals=0),
    )(*args)


def exchange(values, axes):
    return lax.all_to_all(values, axes, split_axis=0, concat_axis=0, tiled=True)


def swap(values, axis, offset=1):
    return lax.ppermute(values, axis, [(i, i ^ offset) for i in range(lax.axis_size(axis))])


def body(
    head_table,
    tail_table,
    qual_table,
    rel_table,
    proj,
    head_id,
    tail_id,
    rel_id,
    qual_rel,
    qual_ref,
    qual_req,
    neg_id,
    edge_count,
):
    head_rows, width = head_table.shape
    tail_rows = tail_table.shape[0]
    qual_rows = qual_table.shape[0]
    rel_rows = rel_table.shape[0]
    edges = head_id.shape[0]
    negs = neg_id.shape[0]
    slots = qual_req.shape[0]
    half = lax.axis_size("line")
    cores = lax.axis_size("core")
    chips = lax.axis_size(CHIPS)
    devices = cores * chips
    quals = qual_ref.shape[1]
    cap = slots // devices
    lanes = width // cores

    arrived = exchange(qual_req.reshape(devices, cap), AXES)
    head_near = jnp.stack([head_table] + [swap(head_table, "line", offset) for offset in range(1, half)])
    place = jnp.stack([lax.axis_index("core"), lax.axis_index(MEMBER)]).astype(jnp.int32)

    rel_row = rel_id[None, :]
    qual_row = qual_rel.T
    ref_row = qual_ref.T
    tail_row = tail_id[None, :]
    neg_row = neg_id[None, :]
    (rel_looked,) = call(
        relation_lookup_kernel,
        [((quals + 1, width, edges), F32)],
        [pltpu.VMEM((2 * width, rel_rows), BF)],
        5,
        58,
        rel_table,
        rel_row,
        qual_row,
        grid=(quals + 1,),
        out_specs=[pl.BlockSpec((1, width, edges), lambda i: (i, 0, 0))],
    )
    arrived, rel_looked, head_near = lax.optimization_barrier((arrived, rel_looked, head_near))
    head_far = swap(head_near, "near")
    picked = qual_table.at[arrived].get(mode="promise_in_bounds")
    fetched = exchange(picked, AXES).reshape(slots, width)
    chunks = 4
    tails, neg_t, neg = call(
        tail_lookup_kernel,
        [((width, edges), BF), ((width, negs), BF), ((negs, width), BF)],
        [
            pltpu.VMEM((tail_rows, width), BF),
            pltpu.VMEM((width, tail_rows), BF),
            pltpu.VMEM((width, edges), BF),
            pltpu.VMEM((width, negs), BF),
            pltpu.VMEM((negs, width), BF),
            pltpu.SemaphoreType.DMA((chunks,)),
            pltpu.SemaphoreType.DMA((3,)),
        ],
        7,
        58,
        tail_table,
        tail_row,
        neg_row,
        away=(0,),
        out_specs=[pl.BlockSpec(memory_space=pl.ANY)] * 3,
    )
    share = -(-(rel_rows + width) // (16 * chips)) * 16
    passed = cap * cores
    sent = share + passed

    def edge(*refs):
        edge_kernel(*refs, rel_rows=rel_rows)

    far_part, near_part, own_part, other_part, terms = call(
        edge,
        [
            ((half, head_rows, width), BF),
            ((half, head_rows, width), BF),
            ((chips, sent, lanes), BF),
            ((chips, sent, lanes), BF),
            ((edges + negs, width), BF),
        ],
        [
            pltpu.VMEM((quals + 1, width, edges), F32),
            pltpu.VMEM((half, head_rows, width), BF),
            pltpu.VMEM((half, head_rows, width), BF),
            pltpu.VMEM((width, edges), BF),
            pltpu.VMEM((negs, width), BF),
            pltpu.VMEM((width, negs), BF),
            pltpu.VMEM((chips * share, width), F32),
            pltpu.VMEM((cores, chips, sent, lanes), BF),
            pltpu.VMEM((edges + negs, width), BF),
            pltpu.SemaphoreType.DMA((6,)),
            pltpu.SemaphoreType.DMA((5,)),
        ],
        14,
        58,
        edge_count,
        place,
        rel_looked,
        head_near,
        head_far,
        tails,
        neg,
        neg_t,
        fetched,
        ref_row,
        rel_row,
        qual_row,
        head_id[None, :],
        proj,
        smem=(0, 1),
        away=range(2, 8),
        out_specs=[pl.BlockSpec(memory_space=pl.ANY)] * 5,
    )
    other_got = swap(other_part, "core")
    far_got = swap(far_part, "near")
    (chip_part,) = call(combine_kernel, [((chips, sent + passed, lanes), BF)], [], 1, 16, own_part, other_got)
    chip_got = exchange(chip_part, CHIPS)

    block = min(1024, tail_rows)
    steps = tail_rows // block

    def tail_rows_of(skip, count, *begun):
        def kernel(*refs):
            tail_kernel(*refs, skip=skip)

        (out,) = call(
            kernel,
            [((tail_rows, width), F32)],
            [],
            3,
            58,
            tail_row,
            neg_row,
            terms,
            *begun,
            away=(3,) if begun else (),
            aliases={3: 0} if begun else {},
            grid=(count,),
            out_specs=[pl.BlockSpec((block, width), lambda i: (i + skip, 0))],
        )
        return out

    tail_grad = tail_rows_of(0, steps // 2)
    chip_got, tail_grad = lax.optimization_barrier((chip_got, tail_grad))
    (sums_own,) = call(add_kernel, [((chips, share, lanes), BF)], [], 1, 16, chip_got)
    sums_own = exchange(sums_own, CHIPS).reshape(chips * share, lanes)
    tail_grad = tail_rows_of(steps // 2, steps - steps // 2, tail_grad)
    sums_own, tail_grad = lax.optimization_barrier((sums_own, tail_grad))
    sums_got = swap(sums_own, "core")
    rel_grad, proj_grad = call(
        finish_kernel,
        [((rel_rows, width), F32), ((width, width), F32)],
        [],
        1,
        16,
        place,
        sums_own,
        sums_got,
        smem=(0,),
    )

    near_sum = near_part.astype(F32) + far_got.astype(F32)
    near_send = near_sum.astype(BF)
    head_grad = near_sum[0]
    for offset in range(1, half):
        head_grad = head_grad + swap(near_send[offset], "line", offset).astype(F32)

    asked = arrived.reshape(PAIRS, cores, chips // PAIRS * cap).transpose(1, 0, 2).reshape(cores, chips * cap)
    (qual_grad,) = call(
        qual_kernel, [((qual_rows, width), F32)], [], 2, 16, place, chip_got, asked, smem=(0,)
    )
    return (head_grad, tail_grad, qual_grad, rel_grad, proj_grad)


def solution(mesh):
    groups, members = mesh.devices.shape
    view = Mesh(mesh.devices.reshape(groups // 2, 2, members // 2, 2), AXES)
    rows = P(AXES, None)
    ids = P(AXES)
    in_specs = (rows, rows, rows, P(), P(), ids, ids, ids, rows, rows, ids, ids, ids)
    out_specs = (rows, rows, rows, P(), P())
    return jax.shard_map(body, mesh=view, in_specs=in_specs, out_specs=out_specs, check_vma=False)
```

time: 136 us -> 103 us (0.76)
  waiting for transfers between devices: 43 us -> 15.3 us
  local copies, waits for them, and re-layouts: 19.6 us -> 5.24 us
  blocking collectives: 14.2 us -> 0 us
  Pallas kernels: 29.9 us -> 44 us
  starting transfers between devices: 22.1 us -> 34.7 us
  other arithmetic: 3.29 us -> 1.58 us
    all_to_all x5 -> x4, waiting for transfers between devices: 21.1 us -> 1.05 us  [exchange(): return lax.all_to_all(values, axes, split_axis=0, concat_axis=0, tiled=True)]
    all_to_all x1 -> x0, blocking collectives: 14.2 us -> none  [exchange(): return lax.all_to_all(values, axes, split_axis=0, concat_axis=0, tiled=True)]
    pallas_call x5 -> x9, Pallas kernels: 29.9 us -> 44 us  [call(): pl.pallas_call(kernel, out_shape=shapes, grid=grid, in_specs=[pl.BlockSpe...]
    unnamed x48 -> x16, local copies, waits for them, and re-layouts: 15.1 us -> 1.77 us
    ppermute x2 -> x10, starting transfers between devices: 3.53 us -> 13.4 us  [swap(): lax.ppermute(values, axis, [(i, i ^ offset) for i in range(lax.axis_size(...]
    ppermute x2 -> x10, waiting for transfers between devices: 22 us -> 14.2 us  [swap(): lax.ppermute(values, axis, [(i, i ^ offset) for i in range(lax.axis_size(...]
    all_to_all x5 -> x4, starting transfers between devices: 18.5 us -> 21.2 us  [exchange(): return lax.all_to_all(values, axes, split_axis=0, concat_axis=0, tiled=True)]
    convert_element_type x3 -> x1, other arithmetic: 2.48 us -> 0.14 us  [body(): near_send = near_sum.astype(BF)]
  transfers between devices with their start and end apart: 7 -> 14, of which waited for: 5 -> 5; matrix products, arithmetic and copies ran while one was open for 4% -> 2% of each run, Pallas kernels for 12% -> 26%
where the time goes in v4:
time: 103 us; the launch traced here: 102 us
  Pallas kernels  44 us (43%)
  starting transfers between devices  34.7 us (34%)
  waiting for transfers between devices  15.3 us (15%)
  local copies, waits for them, and re-layouts  5.24 us (5%)
  other arithmetic  1.58 us (2%)
  between operations  1.46 us (1%)
    pallas_call x9, Pallas kernels, call(): pl.pallas_call(kernel, out_shape=shapes, grid=grid, in_specs=[pl.BlockSpe...  44 us
    all_to_all x4, starting transfers between devices, exchange(): return lax.all_to_all(values, axes, split_axis=0, concat_axis=0, tiled=True)  21.2 us
    ppermute x10, waiting for transfers between devices, swap(): lax.ppermute(values, axis, [(i, i ^ offset) for i in range(lax.axis_size(...  14.2 us
    ppermute x10, starting transfers between devices, swap(): lax.ppermute(values, axis, [(i, i ^ offset) for i in range(lax.axis_size(...  13.4 us
  transfers between devices with their start and end apart: 14, of which 5 were waited for; matrix products, arithmetic and copies ran while one was open for 2% of the time, Pallas kernels for 26%

profile of v4, /device:TPU:0, one launch (start us, length us, event | category | flops | bytes accessed | tf_op | source)
XLA Modules:
  0.0 102.2 jit_solution(10090441161782394290)
XLA Ops:
  0.6 0.0 copy-start
  0.6 3.1 %collective-permute-start = (bf16[256,256]{1,0:T(8,128)(2,1)}, bf16[256,256]{1,0:T(8,128)(2,1)S(1)}, u32[]{:S(2)}, u32[]{:S(2)}) collective-permute-start(bf16[256,256]{1,0:T(8,128)(2,1)} %param.13), channel_id=1, source_target_pairs={{0,2},{2,0},{4,6},{6,4},{1,3},{3,1},{5,7},{7,5},{8,10},{10,8},{12,... | collective-permute-start | bytes 393224 | tf_op jit(solution)/shard_map/ppermute | solution.py:328
  3.7 2.5 %collective-permute-start.2 = (bf16[256,256]{1,0:T(8,128)(2,1)}, bf16[256,256]{1,0:T(8,128)(2,1)S(1)}, u32[]{:S(2)}, u32[]{:S(2)}) collective-permute-start(bf16[256,256]{1,0:T(8,128)(2,1)} %param.13), channel_id=1, source_target_pairs={{0,6},{2,4},{4,2},{6,0},{1,7},{3,5},{5,3},{7,1},{8,14},{10,12},{12... | collective-permute-start | bytes 393224 | tf_op jit(solution)/shard_map/ppermute | solution.py:328
  6.2 0.1 collective-permute-start.1
  6.3 1.4 %all_to_all.17 = s32[32,1,8]{2,0,1:T(8,128)} reshape(s32[256]{0:T(256)} %param.23) | data formatting | bytes 2048 | tf_op jit(solution)/shard_map/all_to_all | solution.py:324
  7.7 5.2 %all-to-all-start = ((s32[32,1,8]{2,1,0:T(1,128)}), s32[32,1,8]{2,1,0:T(1,128)S(1)}, u32[]{:S(2)}, u32[]{:S(2)}) async-start(s32[32,1,8]{2,1,0:T(1,128)} %bitcast.2), calls=%async_computation | async-start | bytes 32768 | tf_op jit(solution)/shard_map/all_to_all | solution.py:324
  12.9 0.0 copy-start.6
  12.9 6.3 %shard_map.164.refs_2_ = f32[5,256,1024]{2,1,0:T(8,128)} custom-call(f32[512,256]{1,0:T(8,128)} %rel_ref.1, s32[1,1024]{1,0:T(1,128)} %bitcast.45, s32[4,1024]{1,0:T(4,128)} %bitcast.42), custom_call_target="tpu_custom_call" | custom-call | flops 5368709120 | bytes 1048576 | tf_op jit(solution)/shard_map/pallas_call | solution.py:310
  19.2 0.0 collective-permute-done
  19.2 0.0 collective-permute-done.2
  19.2 0.0 collective-permute-done.1
  19.2 0.1 pad_maximum_fusion.refs_3_
  19.3 0.0 copy-start.4
  19.3 1.0 %all-to-all-done = s32[32,1,8]{2,1,0:T(1,128)S(1)} async-done(((s32[32,1,8]{2,1,0:T(1,128)}), s32[32,1,8]{2,1,0:T(1,128)S(1)}, u32[]{:S(2)}, u32[]{:S(2)}) %all-to-all-start) | async-done | bytes 1056 | tf_op jit(solution)/shard_map/all_to_all | solution.py:324
  20.3 0.1 reshape.32
  20.5 1.8 %gather_fusion = bf16[256,256]{1,0:T(8,128)(2,1)} fusion(bf16[1024,256]{1,0:T(8,128)(2,1)S(1)} %copy-done, s32[1024]{0:T(1024)S(1)} %pad_clamp_fusion), kind=kCustom, calls=%fused_computation | custom fusion | bytes 263168 | tf_op jit(solution)/shard_map/gather | solution.py:384
  22.3 5.0 %all-to-all-start.1 = ((bf16[32,8,256]{2,1,0:T(8,128)(2,1)}), bf16[32,8,256]{2,1,0:T(8,128)(2,1)S(1)}, u32[]{:S(2)}, u32[]{:S(2)}) async-start(bf16[32,8,256]{2,1,0:T(8,128)(2,1)} %bitcast.12), calls=%async_computation.1 | async-start | bytes 262144 | tf_op jit(solution)/shard_map/all_to_all | solution.py:324
  27.3 1.8 %collective-permute-start.3 = (bf16[4,256,256]{2,1,0:T(8,128)(2,1)S(1)}, bf16[4,256,256]{2,1,0:T(8,128)(2,1)S(1)}, u32[]{:S(2)}, u32[]{:S(2)}) collective-permute-start(bf16[4,256,256]{2,1,0:T(8,128)(2,1)S(1)} %pad_maximum_fusion.refs_3_), channel_id=1, source_target_pairs={{0,1},{1,0},{2,3},{3,2},{4,5},{5,4},{6,7},{7,6},{8,9},{9,8},{10,11... | collective-permute-start | bytes 1572872 | tf_op jit(solution)/shard_map/ppermute | solution.py:328
  29.1 7.8 %shard_map.165 = (bf16[256,1024]{1,0:T(8,128)(2,1)}, bf16[256,1024]{1,0:T(8,128)(2,1)}, bf16[1024,256]{1,0:T(8,128)(2,1)}) custom-call(bf16[4096,256]{1,0:T(8,128)(2,1)} %tail_hbm.1, s32[1,1024]{1,0:T(1,128)} %bitcast.48, s32[1,1024]{1,0:T(1,128)} %bitcast.51), custom_call_target="tpu_custom_call" | custom-call | flops 7516192768 | bytes 1048576 | tf_op jit(solution)/shard_map/pallas_call | solution.py:310
  37.6 0.6 pad_add_fusion.refs_1_.place_ref
  38.2 4.4 %collective-permute-done.3.refs_4_ = bf16[4,256,256]{2,1,0:T(8,128)(2,1)S(1)} collective-permute-done((bf16[4,256,256]{2,1,0:T(8,128)(2,1)S(1)}, bf16[4,256,256]{2,1,0:T(8,128)(2,1)S(1)}, u32[]{:S(2)}, u32[]{:S(2)}) %collective-permute-start.3) | collective-permute-done | bytes 524320 | tf_op jit(solution)/shard_map/ppermute | solution.py:328
  42.6 0.8 copy-done.7
  43.4 15.5 %shard_map.166 = (bf16[4,256,256]{2,1,0:T(8,128)(2,1)}, bf16[4,256,256]{2,1,0:T(8,128)(2,1)}, bf16[16,64,128]{2,1,0:T(8,128)(2,1)}, bf16[16,64,128]{2,1,0:T(8,128)(2,1)}, bf16[2048,256]{1,0:T(8,128)(2,1)}) custom-call(s32[1]{0:T(128)S(6)} %copy.23.refs_0_, s32[2]{0:T(128)} %pad_add_fusion.refs_1_.place_ref, f32[5,256,1024]{2,1,0:T(8,128)} %shard_map.164.refs_2_, ...), custom_call_target="tpu_custom_call" | custom-call | flops 15032385536 | bytes 1048576 | tf_op jit(solution)/shard_map/pallas_call | solution.py:310
  59.0 1.4 %collective-permute-start.4 = (bf16[4,256,256]{2,1,0:T(8,128)(2,1)}, bf16[4,256,256]{2,1,0:T(8,128)(2,1)S(1)}, u32[]{:S(2)}, u32[]{:S(2)}) collective-permute-start(bf16[4,256,256]{2,1,0:T(8,128)(2,1)} %get-tuple-element.29), channel_id=1, source_target_pairs={{0,1},{1,0},{2,3},{3,2},{4,5},{5,4},{6,7},{7,6},{8,9},{9,8},{10,11... | collective-permute-start | bytes 1572872 | tf_op jit(solution)/shard_map/ppermute | solution.py:328
  60.4 0.1 reshape.28
  60.4 0.1 reshape.29.asked
  60.5 1.6 %collective-permute-done.8.got_ref = bf16[16,64,128]{2,1,0:T(8,128)(2,1)S(1)} collective-permute-done((bf16[16,64,128]{2,1,0:T(8,128)(2,1)}, bf16[16,64,128]{2,1,0:T(8,128)(2,1)S(1)}, u32[]{:S(2)}, u32[]{:S(2)}) %collective-permute-start.8) | collective-permute-done | bytes 262176 | tf_op jit(solution)/shard_map/ppermute | solution.py:328
  62.1 0.9 copy-done.2
  63.0 0.8 shard_map.167
  63.8 5.7 %all-to-all-start.2 = ((bf16[16,80,128]{2,1,0:T(8,128)(2,1)}), bf16[16,80,128]{2,1,0:T(8,128)(2,1)S(1)}, u32[]{:S(2)}, u32[]{:S(2)}) async-start(bf16[16,80,128]{2,1,0:T(8,128)(2,1)} %shard_map.167), calls=%async_computation.2 | async-start | bytes 655360 | tf_op jit(solution)/shard_map/all_to_all | solution.py:324
  69.5 3.6 %collective-permute-done.4 = bf16[4,256,256]{2,1,0:T(8,128)(2,1)S(1)} collective-permute-done((bf16[4,256,256]{2,1,0:T(8,128)(2,1)}, bf16[4,256,256]{2,1,0:T(8,128)(2,1)S(1)}, u32[]{:S(2)}, u32[]{:S(2)}) %collective-permute-start.4) | collective-permute-done | bytes 524320 | tf_op jit(solution)/shard_map/ppermute | solution.py:328
  73.1 0.1 fusion.3
  73.3 2.0 %collective-permute-start.5 = (bf16[256,256]{1,0:T(8,128)(2,1)S(1)}, bf16[256,256]{1,0:T(8,128)(2,1)S(1)}, u32[]{:S(2)}, u32[]{:S(2)}) collective-permute-start(bf16[256,256]{1,0:T(8,128)(2,1)S(1)} %get-tuple-element.41), channel_id=1, source_target_pairs={{0,2},{2,0},{4,6},{6,4},{1,3},{3,1},{5,7},{7,5},{8,10},{10,8},{12,... | collective-permute-start | bytes 393224 | tf_op jit(solution)/shard_map/ppermute | solution.py:328
  75.3 2.2 %collective-permute-start.7 = (bf16[256,256]{1,0:T(8,128)(2,1)S(1)}, bf16[256,256]{1,0:T(8,128)(2,1)S(1)}, u32[]{:S(2)}, u32[]{:S(2)}) collective-permute-start(bf16[256,256]{1,0:T(8,128)(2,1)S(1)} %get-tuple-element.42), channel_id=1, source_target_pairs={{0,6},{2,4},{4,2},{6,0},{1,7},{3,5},{5,3},{7,1},{8,14},{10,12},{12... | collective-permute-start | bytes 393224 | tf_op jit(solution)/shard_map/ppermute | solution.py:328
  77.5 0.4 collective-permute-start.6
  77.8 4.7 %shard_map.168.refs_3_ = f32[4096,256]{1,0:T(8,128)} custom-call(s32[1,1024]{1,0:T(1,128)} %bitcast.49, s32[1,1024]{1,0:T(1,128)} %bitcast.52, bf16[2048,256]{1,0:T(8,128)(2,1)} %get-tuple-element.32.refs_2_), custom_call_target="tpu_custom_call" | custom-call | flops 3221225472 | bytes 1048576 | tf_op jit(solution)/shard_map/pallas_call | solution.py:310
  82.6 0.0 all-to-all-done.2.got_ref
  82.6 0.7 shard_map.169
  83.3 5.4 %all-to-all-start.3 = ((bf16[16,48,128]{2,1,0:T(8,128)(2,1)}), bf16[16,48,128]{2,1,0:T(8,128)(2,1)S(1)}, u32[]{:S(2)}, u32[]{:S(2)}) async-start(bf16[16,48,128]{2,1,0:T(8,128)(2,1)} %shard_map.169), calls=%async_computation.3 | async-start | bytes 393216 | tf_op jit(solution)/shard_map/all_to_all | solution.py:324
  88.7 0.0 collective-permute-done.5
  88.7 0.0 collective-permute-done.7
  88.7 4.6 %collective-permute-done.6 = bf16[256,256]{1,0:T(8,128)(2,1)S(1)} collective-permute-done((bf16[256,256]{1,0:T(8,128)(2,1)S(1)}, bf16[256,256]{1,0:T(8,128)(2,1)S(1)}, u32[]{:S(2)}, u32[]{:S(2)}) %collective-permute-start.6) | collective-permute-done | bytes 131104 | tf_op jit(solution)/shard_map/ppermute | solution.py:328
  93.3 0.8 fusion.2
  94.0 4.7 %shard_map.170 = f32[4096,256]{1,0:T(8,128)} custom-call(s32[1,1024]{1,0:T(1,128)} %bitcast.50, s32[1,1024]{1,0:T(1,128)} %bitcast.53, bf16[2048,256]{1,0:T(8,128)(2,1)} %get-tuple-element.32.refs_2_, f32[4096,256]{1,0:T(8,128)} %shard_map.168.refs_3_), custom_call_target="tpu_custom_call", output_to_operand_aliasing={{}: (3, {})} | custom-call | flops 3221225472 | bytes 1048576 | tf_op jit(solution)/shard_map/pallas_call | solution.py:310
  98.8 0.0 all-to-all-done.3
  98.8 1.9 %shard_map.171 = f32[1024,256]{1,0:T(8,128)} custom-call(s32[2]{0:T(128)S(1)} %copy-done.1, bf16[16,80,128]{2,1,0:T(8,128)(2,1)S(1)} %all-to-all-done.2.got_ref, s32[2,128]{1,0:T(2,128)S(1)} %reshape.29.asked), custom_call_target="tpu_custom_call" | custom-call | flops 2147483648 | bytes 1048576 | tf_op jit(solution)/shard_map/pallas_call | solution.py:310
  100.7 0.0 collective-permute-done.9.got_ref
  100.7 1.5 %shard_map.172 = (f32[512,256]{1,0:T(8,128)}, f32[256,256]{1,0:T(8,128)}) custom-call(s32[2]{0:T(128)S(1)} %copy-done.1, bf16[768,128]{1,0:T(8,128)(2,1)S(1)} %bitcast.33, bf16[768,128]{1,0:T(8,128)(2,1)S(1)} %collective-permute-done.9.got_ref), custom_call_target="tpu_custom_call" | custom-call | flops 1073741824 | bytes 1048576 | tf_op jit(solution)/shard_map/pallas_call | solution.py:310
  (18 shorter events, 0.1 us)
Async XLA Ops:
  0.6 19.8 %copy-start = (bf16[1024,256]{1,0:T(8,128)(2,1)S(1)}, bf16[1024,256]{1,0:T(8,128)(2,1)}, u32[]{:S(2)}) copy-start(bf16[1024,256]{1,0:T(8,128)(2,1)} %param.15) | copy-start | bytes 1572868
  0.6 18.5 %collective-permute-start = (bf16[256,256]{1,0:T(8,128)(2,1)}, bf16[256,256]{1,0:T(8,128)(2,1)S(1)}, u32[]{:S(2)}, u32[]{:S(2)}) collective-permute-start(bf16[256,256]{1,0:T(8,128)(2,1)} %param.13), channel_id=1, source_target_pairs={{0,2},{2,0},{4,6},{6,4},{1,3},{3,1},{5,7},{7,5},{8,10},{10,8},{12,... | collective-permute-start | bytes 393224 | tf_op jit(solution)/shard_map/ppermute | solution.py:328
  3.7 15.5 %collective-permute-start.2 = (bf16[256,256]{1,0:T(8,128)(2,1)}, bf16[256,256]{1,0:T(8,128)(2,1)S(1)}, u32[]{:S(2)}, u32[]{:S(2)}) collective-permute-start(bf16[256,256]{1,0:T(8,128)(2,1)} %param.13), channel_id=1, source_target_pairs={{0,6},{2,4},{4,2},{6,0},{1,7},{3,5},{5,3},{7,1},{8,14},{10,12},{12... | collective-permute-start | bytes 393224 | tf_op jit(solution)/shard_map/ppermute | solution.py:328
  6.2 13.0 %collective-permute-start.1 = (bf16[256,256]{1,0:T(8,128)(2,1)}, bf16[256,256]{1,0:T(8,128)(2,1)S(1)}, u32[]{:S(2)}, u32[]{:S(2)}) collective-permute-start(bf16[256,256]{1,0:T(8,128)(2,1)} %param.13), channel_id=1, source_target_pairs={{0,4},{2,6},{4,0},{6,2},{1,5},{3,7},{5,1},{7,3},{8,12},{10,14},{12... | collective-permute-start | bytes 393224 | tf_op jit(solution)/shard_map/ppermute | solution.py:328
  7.7 12.6 %all-to-all-start = ((s32[32,1,8]{2,1,0:T(1,128)}), s32[32,1,8]{2,1,0:T(1,128)S(1)}, u32[]{:S(2)}, u32[]{:S(2)}) async-start(s32[32,1,8]{2,1,0:T(1,128)} %bitcast.2), calls=%async_computation | async-start | bytes 32768 | tf_op jit(solution)/shard_map/all_to_all | solution.py:324
  12.9 6.3 %copy-start.6 = (bf16[256,256]{1,0:T(8,128)(2,1)S(1)}, bf16[256,256]{1,0:T(8,128)(2,1)}, u32[]{:S(2)}) copy-start(bf16[256,256]{1,0:T(8,128)(2,1)} %param.13) | copy-start | bytes 393220
  19.3 17.6 %copy-start.4 = (bf16[4,256,256]{2,1,0:T(8,128)(2,1)}, bf16[4,256,256]{2,1,0:T(8,128)(2,1)S(1)}, u32[]{:S(2)}) copy-start(bf16[4,256,256]{2,1,0:T(8,128)(2,1)S(1)} %pad_maximum_fusion.refs_3_) | copy-start | bytes 1572868
  22.3 15.9 %all-to-all-start.1 = ((bf16[32,8,256]{2,1,0:T(8,128)(2,1)}), bf16[32,8,256]{2,1,0:T(8,128)(2,1)S(1)}, u32[]{:S(2)}, u32[]{:S(2)}) async-start(bf16[32,8,256]{2,1,0:T(8,128)(2,1)} %bitcast.12), calls=%async_computation.1 | async-start | bytes 262144 | tf_op jit(solution)/shard_map/all_to_all | solution.py:324
  27.3 15.4 %collective-permute-start.3 = (bf16[4,256,256]{2,1,0:T(8,128)(2,1)S(1)}, bf16[4,256,256]{2,1,0:T(8,128)(2,1)S(1)}, u32[]{:S(2)}, u32[]{:S(2)}) collective-permute-start(bf16[4,256,256]{2,1,0:T(8,128)(2,1)S(1)} %pad_maximum_fusion.refs_3_), channel_id=1, source_target_pairs={{0,1},{1,0},{2,3},{3,2},{4,5},{5,4},{6,7},{7,6},{8,9},{9,8},{10,11... | collective-permute-start | bytes 1572872 | tf_op jit(solution)/shard_map/ppermute | solution.py:328
  38.2 4.4 %copy-start.5 = (bf16[32,8,256]{2,1,0:T(8,128)(2,1)}, bf16[32,8,256]{2,1,0:T(8,128)(2,1)S(1)}, u32[]{:S(2)}) copy-start(bf16[32,8,256]{2,1,0:T(8,128)(2,1)S(1)} %all-to-all-done.1) | copy-start | bytes 393220
  42.6 0.8 copy-start.7
  59.0 14.2 %collective-permute-start.4 = (bf16[4,256,256]{2,1,0:T(8,128)(2,1)}, bf16[4,256,256]{2,1,0:T(8,128)(2,1)S(1)}, u32[]{:S(2)}, u32[]{:S(2)}) collective-permute-start(bf16[4,256,256]{2,1,0:T(8,128)(2,1)} %get-tuple-element.29), channel_id=1, source_target_pairs={{0,1},{1,0},{2,3},{3,2},{4,5},{5,4},{6,7},{7,6},{8,9},{9,8},{10,11... | collective-permute-start | bytes 1572872 | tf_op jit(solution)/shard_map/ppermute | solution.py:328
  60.3 1.7 %collective-permute-start.8 = (bf16[16,64,128]{2,1,0:T(8,128)(2,1)}, bf16[16,64,128]{2,1,0:T(8,128)(2,1)S(1)}, u32[]{:S(2)}, u32[]{:S(2)}) collective-permute-start(bf16[16,64,128]{2,1,0:T(8,128)(2,1)} %get-tuple-element.31), channel_id=1, source_target_pairs={{0,8},{8,0},{1,9},{9,1},{2,10},{10,2},{3,11},{11,3},{4,12},{12,4},... | collective-permute-start | bytes 786440 | tf_op jit(solution)/shard_map/ppermute | solution.py:328
  62.1 1.0 copy-start.2
  63.0 10.1 %copy-start.3 = (bf16[4,256,256]{2,1,0:T(8,128)(2,1)S(1)}, bf16[4,256,256]{2,1,0:T(8,128)(2,1)}, u32[]{:S(2)}) copy-start(bf16[4,256,256]{2,1,0:T(8,128)(2,1)} %get-tuple-element.28) | copy-start | bytes 1572868
  63.8 18.7 %all-to-all-start.2 = ((bf16[16,80,128]{2,1,0:T(8,128)(2,1)}), bf16[16,80,128]{2,1,0:T(8,128)(2,1)S(1)}, u32[]{:S(2)}, u32[]{:S(2)}) async-start(bf16[16,80,128]{2,1,0:T(8,128)(2,1)} %shard_map.167), calls=%async_computation.2 | async-start | bytes 655360 | tf_op jit(solution)/shard_map/all_to_all | solution.py:324
  73.3 15.4 %collective-permute-start.5 = (bf16[256,256]{1,0:T(8,128)(2,1)S(1)}, bf16[256,256]{1,0:T(8,128)(2,1)S(1)}, u32[]{:S(2)}, u32[]{:S(2)}) collective-permute-start(bf16[256,256]{1,0:T(8,128)(2,1)S(1)} %get-tuple-element.41), channel_id=1, source_target_pairs={{0,2},{2,0},{4,6},{6,4},{1,3},{3,1},{5,7},{7,5},{8,10},{10,8},{12,... | collective-permute-start | bytes 393224 | tf_op jit(solution)/shard_map/ppermute | solution.py:328
  75.3 13.4 %collective-permute-start.7 = (bf16[256,256]{1,0:T(8,128)(2,1)S(1)}, bf16[256,256]{1,0:T(8,128)(2,1)S(1)}, u32[]{:S(2)}, u32[]{:S(2)}) collective-permute-start(bf16[256,256]{1,0:T(8,128)(2,1)S(1)} %get-tuple-element.42), channel_id=1, source_target_pairs={{0,6},{2,4},{4,2},{6,0},{1,7},{3,5},{5,3},{7,1},{8,14},{10,12},{12... | collective-permute-start | bytes 393224 | tf_op jit(solution)/shard_map/ppermute | solution.py:328
  77.5 15.8 %collective-permute-start.6 = (bf16[256,256]{1,0:T(8,128)(2,1)S(1)}, bf16[256,256]{1,0:T(8,128)(2,1)S(1)}, u32[]{:S(2)}, u32[]{:S(2)}) collective-permute-start(bf16[256,256]{1,0:T(8,128)(2,1)S(1)} %get-tuple-element.43), channel_id=1, source_target_pairs={{0,4},{2,6},{4,0},{6,2},{1,5},{3,7},{5,1},{7,3},{8,12},{10,14},{12... | collective-permute-start | bytes 393224 | tf_op jit(solution)/shard_map/ppermute | solution.py:328
  83.3 15.5 %all-to-all-start.3 = ((bf16[16,48,128]{2,1,0:T(8,128)(2,1)}), bf16[16,48,128]{2,1,0:T(8,128)(2,1)S(1)}, u32[]{:S(2)}, u32[]{:S(2)}) async-start(bf16[16,48,128]{2,1,0:T(8,128)(2,1)} %shard_map.169), calls=%async_computation.3 | async-start | bytes 393216 | tf_op jit(solution)/shard_map/all_to_all | solution.py:324
  94.0 4.7 %copy-start.1 = (s32[2]{0:T(128)S(1)}, s32[2]{0:T(128)}, u32[]{:S(2)}) copy-start(s32[2]{0:T(128)} %pad_add_fusion.refs_1_.place_ref) | copy-start | bytes 28
  98.8 1.9 %collective-permute-start.9 = (bf16[768,128]{1,0:T(8,128)(2,1)S(1)}, bf16[768,128]{1,0:T(8,128)(2,1)S(1)}, u32[]{:S(2)}, u32[]{:S(2)}) collective-permute-start(bf16[768,128]{1,0:T(8,128)(2,1)S(1)} %bitcast.32), channel_id=1, source_target_pairs={{0,8},{8,0},{1,9},{9,1},{2,10},{10,2},{3,11},{11,3},{4,12},{12,4},... | collective-permute-start | bytes 589832 | tf_op jit(solution)/shard_map/ppermute | solution.py:328

commit v5 on v4

--- a/solution.py
+++ b/solution.py
@@ -107,7 +107,8 @@
 
 def edge_kernel(
     count_ref,
-    place_ref,
+    core_ref,
+    member_ref,
     rel_hbm,
     near_hbm,
     far_hbm,
@@ -173,7 +174,7 @@
     relation = rel_ref[0] + (nn(projt_hi, comp_hi) + (nn(projt_hi, comp_lo) + nn(projt_lo, comp_hi)))
     loads[1].wait()
     loads[2].wait()
-    offset = jnp.bitwise_xor(head_id[...] // head_rows, place_ref[1])
+    offset = jnp.bitwise_xor(head_id[...] // head_rows, member_ref[0])
     head_slot = ((offset % 2) * half + offset // 2) * head_rows + head_id[...] % head_rows
     heads = jnp.zeros((width, edges), F32)
     for first, table in ((0, near_ref), (half, far_ref)):
@@ -230,8 +231,8 @@
         parts = [sums[:, core * lanes : (core + 1) * lanes].reshape(chips, share, lanes)]
         parts += [mine[:, :, start : start + lanes] for start in range(0, width, lanes)]
         packed[core] = jnp.concatenate(parts, axis=1).astype(BF)
-    store(packed.at[place_ref[0]], own_out)
-    store(packed.at[1 - place_ref[0]], other_out)
+    store(packed.at[core_ref[0]], own_out)
+    store(packed.at[1 - core_ref[0]], other_out)
 
     terms[:edges, :] = flip((coef * query_f).astype(BF))
     terms[edges:, :] = nt(neg_round, query).astype(BF)
@@ -260,17 +261,17 @@
         out_ref[index] = total
 
 
-def finish_kernel(place_ref, own_ref, got_ref, rel_out, proj_out):
+def finish_kernel(core_ref, own_ref, got_ref, rel_out, proj_out):
     rel_rows = rel_out.shape[0]
     proj_rows = proj_out.shape[0]
     lanes = own_ref.shape[1]
-    for ref, core in ((own_ref, place_ref[0]), (got_ref, 1 - place_ref[0])):
+    for ref, core in ((own_ref, core_ref[0]), (got_ref, 1 - core_ref[0])):
         at = pl.ds(pl.multiple_of(core * lanes, lanes), lanes)
         rel_out[:, at] = ref[:rel_rows, :].astype(F32)
         proj_out[:, at] = ref[rel_rows : rel_rows + proj_rows, :].astype(F32)
 
 
-def qual_kernel(place_ref, got_ref, asked, qual_out):
+def qual_kernel(core_ref, got_ref, asked, qual_out):
     qual_rows, width = qual_out.shape
     chips, rows, lanes = got_ref.shape
     cores = asked.shape[0]
@@ -279,8 +280,8 @@
     first = rows - cores * parts * cap
     passed = got_ref[:, first:, :].astype(F32)
     hots = [
-        onehot(asked[pl.ds(place_ref[0], 1), :], 0, qual_rows),
-        onehot(asked[pl.ds(1 - place_ref[0], 1), :], 0, qual_rows),
+        onehot(asked[pl.ds(core_ref[0], 1), :], 0, qual_rows),
+        onehot(asked[pl.ds(1 - core_ref[0], 1), :], 0, qual_rows),
     ]
     for part in range(parts):
         total = jnp.zeros((qual_rows, lanes), F32)
@@ -360,7 +361,8 @@
 
     arrived = exchange(qual_req.reshape(devices, cap), AXES)
     head_near = jnp.stack([head_table] + [swap(head_table, "line", offset) for offset in range(1, half)])
-    place = jnp.stack([lax.axis_index("core"), lax.axis_index(MEMBER)]).astype(jnp.int32)
+    core = lax.axis_index("core").astype(jnp.int32).reshape(1)
+    member = lax.axis_index(MEMBER).astype(jnp.int32).reshape(1)
 
     rel_row = rel_id[None, :]
     qual_row = qual_rel.T
@@ -434,9 +436,10 @@
             pltpu.SemaphoreType.DMA((5,)),
         ],
         14,
-        58,
+        58 if half > 4 else 44,
         edge_count,
-        place,
+        core,
+        member,
         rel_looked,
         head_near,
         head_far,
@@ -449,8 +452,8 @@
         qual_row,
         head_id[None, :],
         proj,
-        smem=(0, 1),
-        away=range(2, 8),
+        smem=(0, 1, 2),
+        away=range(3, 9),
         out_specs=[pl.BlockSpec(memory_space=pl.ANY)] * 5,
     )
     other_got = swap(other_part, "core")
@@ -483,11 +486,14 @@
         return out
 
     tail_grad = tail_rows_of(0, steps // 2)
-    chip_got, tail_grad = lax.optimization_barrier((chip_got, tail_grad))
+    far_got, tail_grad = lax.optimization_barrier((far_got, tail_grad))
+    near_sum = near_part.astype(F32) + far_got.astype(F32)
+    near_send = near_sum.astype(BF)
+    line_got = [swap(near_send[offset], "line", offset) for offset in range(1, half)]
     (sums_own,) = call(add_kernel, [((chips, share, lanes), BF)], [], 1, 16, chip_got)
     sums_own = exchange(sums_own, CHIPS).reshape(chips * share, lanes)
     tail_grad = tail_rows_of(steps // 2, steps - steps // 2, tail_grad)
-    sums_own, tail_grad = lax.optimization_barrier((sums_own, tail_grad))
+    sums_own, tail_grad, line_got = lax.optimization_barrier((sums_own, tail_grad, line_got))
     sums_got = swap(sums_own, "core")
     rel_grad, proj_grad = call(
         finish_kernel,
@@ -495,21 +501,19 @@
         [],
         1,
         16,
-        place,
+        core,
         sums_own,
         sums_got,
         smem=(0,),
     )
 
-    near_sum = near_part.astype(F32) + far_got.astype(F32)
-    near_send = near_sum.astype(BF)
     head_grad = near_sum[0]
-    for offset in range(1, half):
-        head_grad = head_grad + swap(near_send[offset], "line", offset).astype(F32)
+    for got in line_got:
+        head_grad = head_grad + got.astype(F32)
 
     asked = arrived.reshape(PAIRS, cores, chips // PAIRS * cap).transpose(1, 0, 2).reshape(cores, chips * cap)
     (qual_grad,) = call(
-        qual_kernel, [((qual_rows, width), F32)], [], 2, 16, place, chip_got, asked, smem=(0,)
+        qual_kernel, [((qual_rows, width), F32)], [], 2, 16, core, chip_got, asked, smem=(0,)
     )
     return (head_grad, tail_grad, qual_grad, rel_grad, proj_grad)
 

time: 103 us -> 98.4 us (0.955)
  waiting for transfers between devices: 15.3 us -> 3.97 us
  local copies, waits for them, and re-layouts: 5.24 us -> 9.25 us
  starting transfers between devices: 34.7 us -> 38.2 us
  Pallas kernels: 44 us -> 42.6 us
    ppermute x10, waiting for transfers between devices: 14.2 us -> 1.34 us  [swap(): lax.ppermute(values, axis, [(i, i ^ offset) for i in range(lax.axis_size(...]
    unnamed x16 -> x26, local copies, waits for them, and re-layouts: 1.77 us -> 5.79 us
    all_to_all x4, starting transfers between devices: 21.2 us -> 24.6 us  [exchange(): return lax.all_to_all(values, axes, split_axis=0, concat_axis=0, tiled=True)]
    all_to_all x4, waiting for transfers between devices: 1.05 us -> 2.63 us  [exchange(): return lax.all_to_all(values, axes, split_axis=0, concat_axis=0, tiled=True)]
    pallas_call x9, Pallas kernels: 44 us -> 42.6 us  [call(): pl.pallas_call(kernel, out_shape=shapes, grid=grid, in_specs=[pl.BlockSpe...]
    convert_element_type x1, other arithmetic: 0.14 us -> 1.19 us  [body(): near_send = near_sum.astype(BF)]
  transfers between devices with their start and end apart: 14 -> 14, of which waited for: 5 -> 5; matrix products, arithmetic and copies ran while one was open for 2% -> 4% of each run, Pallas kernels for 26% -> 27%
where the time goes in v5:
time: 98.4 us; the launch traced here: 97.6 us
  Pallas kernels  42.6 us (43%)
  starting transfers between devices  38.2 us (39%)
  local copies, waits for them, and re-layouts  9.25 us (9%)
  waiting for transfers between devices  3.97 us (4%)
  other arithmetic  2.03 us (2%)
  between operations  1.53 us (2%)
    pallas_call x9, Pallas kernels, call(): pl.pallas_call(kernel, out_shape=shapes, grid=grid, in_specs=[pl.BlockSpe...  42.6 us
    all_to_all x4, starting transfers between devices, exchange(): return lax.all_to_all(values, axes, split_axis=0, concat_axis=0, tiled=True)  24.6 us
    ppermute x10, starting transfers between devices, swap(): lax.ppermute(values, axis, [(i, i ^ offset) for i in range(lax.axis_size(...  13.6 us
    unnamed x26, local copies, waits for them, and re-layouts  5.79 us
    all_to_all x4, waiting for transfers between devices, exchange(): return lax.all_to_all(values, axes, split_axis=0, concat_axis=0, tiled=True)  2.63 us
  transfers between devices with their start and end apart: 14, of which 5 were waited for; matrix products, arithmetic and copies ran while one was open for 4% of the time, Pallas kernels for 27%

profile of v5, /device:TPU:0, one launch (start us, length us, event | category | flops | bytes accessed | tf_op | source)
XLA Modules:
  0.0 97.6 jit_solution(5432304273820538246)
XLA Ops:
  0.6 0.0 copy-start
  0.6 3.1 %collective-permute-start = (bf16[256,256]{1,0:T(8,128)(2,1)}, bf16[256,256]{1,0:T(8,128)(2,1)S(1)}, u32[]{:S(2)}, u32[]{:S(2)}) collective-permute-start(bf16[256,256]{1,0:T(8,128)(2,1)} %param.13), channel_id=1, source_target_pairs={{0,2},{2,0},{4,6},{6,4},{1,3},{3,1},{5,7},{7,5},{8,10},{10,8},{12,... | collective-permute-start | bytes 393224 | tf_op jit(solution)/shard_map/ppermute | solution.py:329
  3.7 2.6 %collective-permute-start.1 = (bf16[256,256]{1,0:T(8,128)(2,1)}, bf16[256,256]{1,0:T(8,128)(2,1)S(1)}, u32[]{:S(2)}, u32[]{:S(2)}) collective-permute-start(bf16[256,256]{1,0:T(8,128)(2,1)} %param.13), channel_id=1, source_target_pairs={{0,4},{2,6},{4,0},{6,2},{1,5},{3,7},{5,1},{7,3},{8,12},{10,14},{12... | collective-permute-start | bytes 393224 | tf_op jit(solution)/shard_map/ppermute | solution.py:329
  6.3 1.4 %all_to_all.17 = s32[32,1,8]{2,0,1:T(8,128)} reshape(s32[256]{0:T(256)} %param.23) | data formatting | bytes 2048 | tf_op jit(solution)/shard_map/all_to_all | solution.py:325
  7.7 6.1 %all-to-all-start = ((s32[32,1,8]{2,1,0:T(1,128)}), s32[32,1,8]{2,1,0:T(1,128)S(1)}, u32[]{:S(2)}, u32[]{:S(2)}) async-start(s32[32,1,8]{2,1,0:T(1,128)} %bitcast.2), calls=%async_computation | async-start | bytes 32768 | tf_op jit(solution)/shard_map/all_to_all | solution.py:325
  13.8 0.0 copy-start.12
  13.8 6.3 %shard_map.164.refs_3_ = f32[5,256,1024]{2,1,0:T(8,128)} custom-call(f32[512,256]{1,0:T(8,128)} %rel_ref.1, s32[1,1024]{1,0:T(1,128)} %bitcast.38, s32[4,1024]{1,0:T(4,128)} %bitcast.35), custom_call_target="tpu_custom_call" | custom-call | flops 5368709120 | bytes 1048576 | tf_op jit(solution)/shard_map/pallas_call | solution.py:311
  20.1 0.1 pad_maximum_fusion.refs_4_
  20.2 0.6 all-to-all-done
  20.8 1.2 %collective-permute-start.3 = (bf16[4,256,256]{2,1,0:T(8,128)(2,1)S(1)}, bf16[4,256,256]{2,1,0:T(8,128)(2,1)S(1)}, u32[]{:S(2)}, u32[]{:S(2)}) collective-permute-start(bf16[4,256,256]{2,1,0:T(8,128)(2,1)S(1)} %pad_maximum_fusion.refs_4_), channel_id=1, source_target_pairs={{0,1},{1,0},{2,3},{3,2},{4,5},{5,4},{6,7},{7,6},{8,9},{9,8},{10,11... | collective-permute-start | bytes 1572872 | tf_op jit(solution)/shard_map/ppermute | solution.py:329
  22.1 0.1 reshape.40
  22.2 1.8 %gather_fusion = bf16[256,256]{1,0:T(8,128)(2,1)} fusion(bf16[1024,256]{1,0:T(8,128)(2,1)S(1)} %copy-done, s32[1024]{0:T(1024)S(1)} %pad_clamp_fusion), kind=kCustom, calls=%fused_computation | custom fusion | bytes 263168 | tf_op jit(solution)/shard_map/gather | solution.py:386
  24.0 4.8 %all-to-all-start.1 = ((bf16[32,8,256]{2,1,0:T(8,128)(2,1)}), bf16[32,8,256]{2,1,0:T(8,128)(2,1)S(1)}, u32[]{:S(2)}, u32[]{:S(2)}) async-start(bf16[32,8,256]{2,1,0:T(8,128)(2,1)} %bitcast.12), calls=%async_computation.1 | async-start | bytes 262144 | tf_op jit(solution)/shard_map/all_to_all | solution.py:325
  28.8 0.0 copy-start.1
  28.8 0.0 copy-start.2
  28.8 0.0 copy-start.3
  28.8 0.0 copy-start.4
  28.9 0.0 copy-start.5
  28.9 7.9 %shard_map.165 = (bf16[256,1024]{1,0:T(8,128)(2,1)}, bf16[256,1024]{1,0:T(8,128)(2,1)}, bf16[1024,256]{1,0:T(8,128)(2,1)}) custom-call(bf16[4096,256]{1,0:T(8,128)(2,1)} %tail_hbm.1, s32[1,1024]{1,0:T(1,128)} %bitcast.48, s32[1,1024]{1,0:T(1,128)} %bitcast.51), custom_call_target="tpu_custom_call" | custom-call | flops 7516192768 | bytes 1048576 | tf_op jit(solution)/shard_map/pallas_call | solution.py:311
  37.5 0.0 copy-start.9
  37.5 1.0 %copy-done.9 = bf16[256,1024]{1,0:T(8,128)(2,1)S(1)} copy-done((bf16[256,1024]{1,0:T(8,128)(2,1)S(1)}, bf16[256,1024]{1,0:T(8,128)(2,1)}, u32[]{:S(2)}) %copy-start.9) | copy-done | bytes 524312
  38.5 1.0 %copy-done.10 = bf16[256,1024]{1,0:T(8,128)(2,1)S(1)} copy-done((bf16[256,1024]{1,0:T(8,128)(2,1)S(1)}, bf16[256,1024]{1,0:T(8,128)(2,1)}, u32[]{:S(2)}) %copy-start.10) | copy-done | bytes 524312
  39.6 1.0 %copy-done.11 = bf16[1024,256]{1,0:T(8,128)(2,1)S(1)} copy-done((bf16[1024,256]{1,0:T(8,128)(2,1)S(1)}, bf16[1024,256]{1,0:T(8,128)(2,1)}, u32[]{:S(2)}) %copy-start.11) | copy-done | bytes 524312
  40.6 15.0 %shard_map.166 = (bf16[4,256,256]{2,1,0:T(8,128)(2,1)S(1)}, bf16[4,256,256]{2,1,0:T(8,128)(2,1)S(1)}, bf16[16,64,128]{2,1,0:T(8,128)(2,1)S(1)}, bf16[16,64,128]{2,1,0:T(8,128)(2,1)S(1)}, bf16[2048,256]{1,0:T(8,128)(2,1)S(1)}) custom-call(s32[1]{0:T(128)S(6)} %copy.23.refs_0_, s32[1]{0:T(128)} %bitcast.refs_1_.core_ref, s32[1]{0:T(128)} %bitcast.1.refs_2_, ...), custom_call_target="tpu_custom_call" | custom-call | flops 15032385536 | bytes 1048576 | tf_op jit(solution)/shard_map/pallas_call | solution.py:311
  55.7 0.0 copy-start.6
  55.7 1.0 copy-done.6
  56.6 0.7 copy-done.7
  57.3 0.1 collective-permute-start.5
  57.4 1.7 %collective-permute-start.4 = (bf16[4,256,256]{2,1,0:T(8,128)(2,1)S(1)}, bf16[4,256,256]{2,1,0:T(8,128)(2,1)}, u32[]{:S(2)}, u32[]{:S(2)}) collective-permute-start(bf16[4,256,256]{2,1,0:T(8,128)(2,1)S(1)} %get-tuple-element.32), channel_id=1, source_target_pairs={{0,1},{1,0},{2,3},{3,2},{4,5},{5,4},{6,7},{7,6},{8,9},{9,8},{10,11... | collective-permute-start | bytes 1572872 | tf_op jit(solution)/shard_map/ppermute | solution.py:329
  59.1 0.1 reshape.36
  59.2 0.1 reshape.37.asked
  59.3 1.0 copy-done.8
  60.2 0.8 shard_map.168
  61.0 6.3 %all-to-all-start.2 = ((bf16[16,80,128]{2,1,0:T(8,128)(2,1)}), bf16[16,80,128]{2,1,0:T(8,128)(2,1)S(1)}, u32[]{:S(2)}, u32[]{:S(2)}) async-start(bf16[16,80,128]{2,1,0:T(8,128)(2,1)} %shard_map.168), calls=%async_computation.2 | async-start | bytes 655360 | tf_op jit(solution)/shard_map/all_to_all | solution.py:325
  67.3 4.8 %shard_map.167.refs_3_ = f32[4096,256]{1,0:T(8,128)} custom-call(s32[1,1024]{1,0:T(1,128)} %bitcast.49, s32[1,1024]{1,0:T(1,128)} %bitcast.52, bf16[2048,256]{1,0:T(8,128)(2,1)} %copy-done.6), custom_call_target="tpu_custom_call" | custom-call | flops 3221225472 | bytes 1048576 | tf_op jit(solution)/shard_map/pallas_call | solution.py:311
  72.0 0.6 collective-permute-done.4
  72.7 1.2 %fusion.3 = (bf16[4,256,256]{2,1,0:T(8,128)(2,1)S(1)}, f32[4,256,256]{2,1,0:T(8,128)S(1)}) fusion(bf16[4,256,256]{2,1,0:T(8,128)(2,1)} %collective-permute-done.4, bf16[4,256,256]{2,1,0:T(8,128)(2,1)S(1)} %get-tuple-element.31), kind=kLoop, calls=%fused_computation.12 | loop fusion | flops 1048576 | bytes 2621440 | tf_op jit(solution)/shard_map/convert_element_type | solution.py:491
  73.9 1.6 %collective-permute-start.6 = (bf16[256,256]{1,0:T(8,128)(2,1)S(1)}, bf16[256,256]{1,0:T(8,128)(2,1)S(1)}, u32[]{:S(2)}, u32[]{:S(2)}) collective-permute-start(bf16[256,256]{1,0:T(8,128)(2,1)S(1)} %get-tuple-element.49), channel_id=1, source_target_pairs={{0,2},{2,0},{4,6},{6,4},{1,3},{3,1},{5,7},{7,5},{8,10},{10,8},{12,... | collective-permute-start | bytes 393224 | tf_op jit(solution)/shard_map/ppermute | solution.py:329
  75.5 3.3 %collective-permute-start.7 = (bf16[256,256]{1,0:T(8,128)(2,1)S(1)}, bf16[256,256]{1,0:T(8,128)(2,1)S(1)}, u32[]{:S(2)}, u32[]{:S(2)}) collective-permute-start(bf16[256,256]{1,0:T(8,128)(2,1)S(1)} %get-tuple-element.48), channel_id=1, source_target_pairs={{0,4},{2,6},{4,0},{6,2},{1,5},{3,7},{5,1},{7,3},{8,12},{10,14},{12... | collective-permute-start | bytes 393224 | tf_op jit(solution)/shard_map/ppermute | solution.py:329
  78.8 0.1 all-to-all-done.2.got_ref
  79.0 0.7 shard_map.169
  79.7 7.5 %all-to-all-start.3 = ((bf16[16,48,128]{2,1,0:T(8,128)(2,1)}), bf16[16,48,128]{2,1,0:T(8,128)(2,1)S(1)}, u32[]{:S(2)}, u32[]{:S(2)}) async-start(bf16[16,48,128]{2,1,0:T(8,128)(2,1)} %shard_map.169), calls=%async_computation.3 | async-start | bytes 393216 | tf_op jit(solution)/shard_map/all_to_all | solution.py:325
  87.2 4.8 %shard_map.170 = f32[4096,256]{1,0:T(8,128)} custom-call(s32[1,1024]{1,0:T(1,128)} %bitcast.50, s32[1,1024]{1,0:T(1,128)} %bitcast.53, bf16[2048,256]{1,0:T(8,128)(2,1)} %copy-done.6, f32[4096,256]{1,0:T(8,128)} %shard_map.167.refs_3_), custom_call_target="tpu_custom_call", output_to_operand_aliasing={{}: (3, {})} | custom-call | flops 3221225472 | bytes 1048576 | tf_op jit(solution)/shard_map/pallas_call | solution.py:311
  91.9 1.4 %shard_map.171 = f32[1024,256]{1,0:T(8,128)} custom-call(s32[1]{0:T(128)} %bitcast.refs_1_.core_ref, bf16[16,80,128]{2,1,0:T(8,128)(2,1)S(1)} %all-to-all-done.2.got_ref, s32[2,128]{1,0:T(2,128)S(1)} %reshape.37.asked), custom_call_target="tpu_custom_call" | custom-call | flops 2147483648 | bytes 1048576 | tf_op jit(solution)/shard_map/pallas_call | solution.py:311
  93.3 1.9 %all-to-all-done.3 = bf16[16,48,128]{2,1,0:T(8,128)(2,1)S(1)} async-done(((bf16[16,48,128]{2,1,0:T(8,128)(2,1)}), bf16[16,48,128]{2,1,0:T(8,128)(2,1)S(1)}, u32[]{:S(2)}, u32[]{:S(2)}) %all-to-all-start.3) | async-done | bytes 196640 | tf_op jit(solution)/shard_map/all_to_all | solution.py:325
  95.2 0.8 fusion.2
  96.0 0.7 collective-permute-done.9.got_ref
  96.7 0.9 shard_map.172
  (27 shorter events, 0.1 us)
Async XLA Ops:
  0.6 21.5 %copy-start = (bf16[1024,256]{1,0:T(8,128)(2,1)S(1)}, bf16[1024,256]{1,0:T(8,128)(2,1)}, u32[]{:S(2)}) copy-start(bf16[1024,256]{1,0:T(8,128)(2,1)} %param.15) | copy-start | bytes 1572868
  0.6 19.5 %collective-permute-start = (bf16[256,256]{1,0:T(8,128)(2,1)}, bf16[256,256]{1,0:T(8,128)(2,1)S(1)}, u32[]{:S(2)}, u32[]{:S(2)}) collective-permute-start(bf16[256,256]{1,0:T(8,128)(2,1)} %param.13), channel_id=1, source_target_pairs={{0,2},{2,0},{4,6},{6,4},{1,3},{3,1},{5,7},{7,5},{8,10},{10,8},{12,... | collective-permute-start | bytes 393224 | tf_op jit(solution)/shard_map/ppermute | solution.py:329
  3.7 16.4 %collective-permute-start.1 = (bf16[256,256]{1,0:T(8,128)(2,1)}, bf16[256,256]{1,0:T(8,128)(2,1)S(1)}, u32[]{:S(2)}, u32[]{:S(2)}) collective-permute-start(bf16[256,256]{1,0:T(8,128)(2,1)} %param.13), channel_id=1, source_target_pairs={{0,4},{2,6},{4,0},{6,2},{1,5},{3,7},{5,1},{7,3},{8,12},{10,14},{12... | collective-permute-start | bytes 393224 | tf_op jit(solution)/shard_map/ppermute | solution.py:329
  6.3 13.8 %collective-permute-start.2 = (bf16[256,256]{1,0:T(8,128)(2,1)}, bf16[256,256]{1,0:T(8,128)(2,1)S(1)}, u32[]{:S(2)}, u32[]{:S(2)}) collective-permute-start(bf16[256,256]{1,0:T(8,128)(2,1)} %param.13), channel_id=1, source_target_pairs={{0,6},{2,4},{4,2},{6,0},{1,7},{3,5},{5,3},{7,1},{8,14},{10,12},{12... | collective-permute-start | bytes 393224 | tf_op jit(solution)/shard_map/ppermute | solution.py:329
  7.7 13.1 %all-to-all-start = ((s32[32,1,8]{2,1,0:T(1,128)}), s32[32,1,8]{2,1,0:T(1,128)S(1)}, u32[]{:S(2)}, u32[]{:S(2)}) async-start(s32[32,1,8]{2,1,0:T(1,128)} %bitcast.2), calls=%async_computation | async-start | bytes 32768 | tf_op jit(solution)/shard_map/all_to_all | solution.py:325
  13.8 6.4 %copy-start.12 = (bf16[256,256]{1,0:T(8,128)(2,1)S(1)}, bf16[256,256]{1,0:T(8,128)(2,1)}, u32[]{:S(2)}) copy-start(bf16[256,256]{1,0:T(8,128)(2,1)} %param.13) | copy-start | bytes 393220
  20.8 16.6 %collective-permute-start.3 = (bf16[4,256,256]{2,1,0:T(8,128)(2,1)S(1)}, bf16[4,256,256]{2,1,0:T(8,128)(2,1)S(1)}, u32[]{:S(2)}, u32[]{:S(2)}) collective-permute-start(bf16[4,256,256]{2,1,0:T(8,128)(2,1)S(1)} %pad_maximum_fusion.refs_4_), channel_id=1, source_target_pairs={{0,1},{1,0},{2,3},{3,2},{4,5},{5,4},{6,7},{7,6},{8,9},{9,8},{10,11... | collective-permute-start | bytes 1572872 | tf_op jit(solution)/shard_map/ppermute | solution.py:329
  24.0 13.4 %all-to-all-start.1 = ((bf16[32,8,256]{2,1,0:T(8,128)(2,1)}), bf16[32,8,256]{2,1,0:T(8,128)(2,1)S(1)}, u32[]{:S(2)}, u32[]{:S(2)}) async-start(bf16[32,8,256]{2,1,0:T(8,128)(2,1)} %bitcast.12), calls=%async_computation.1 | async-start | bytes 262144 | tf_op jit(solution)/shard_map/all_to_all | solution.py:325
  28.8 8.6 %copy-start.1 = (f32[256,256]{1,0:T(8,128)S(1)}, f32[256,256]{1,0:T(8,128)}, u32[]{:S(2)}) copy-start(f32[256,256]{1,0:T(8,128)} %refs_14_.1) | copy-start | bytes 786436
  28.8 8.6 %copy-start.2 = (s32[1024,4]{0,1:T(4,128)S(1)}, s32[1024,4]{0,1:T(4,128)}, u32[]{:S(2)}) copy-start(s32[1024,4]{0,1:T(4,128)} %param.21) | copy-start | bytes 49156
  28.8 8.6 %copy-start.3 = (s32[1024,4]{0,1:T(4,128)S(1)}, s32[1024,4]{0,1:T(4,128)}, u32[]{:S(2)}) copy-start(s32[1024,4]{0,1:T(4,128)} %param.22) | copy-start | bytes 49156
  28.8 8.6 %copy-start.4 = (s32[1024]{0:T(1024)S(1)}, s32[1024]{0:T(1024)}, u32[]{:S(2)}) copy-start(s32[1024]{0:T(1024)} %param.20) | copy-start | bytes 12292
  28.9 8.6 %copy-start.5 = (s32[1024]{0:T(1024)S(1)}, s32[1024]{0:T(1024)}, u32[]{:S(2)}) copy-start(s32[1024]{0:T(1024)} %param.18) | copy-start | bytes 12292
  37.5 1.0 %copy-start.9 = (bf16[256,1024]{1,0:T(8,128)(2,1)S(1)}, bf16[256,1024]{1,0:T(8,128)(2,1)}, u32[]{:S(2)}) copy-start(bf16[256,1024]{1,0:T(8,128)(2,1)} %get-tuple-element.27.refs_6_) | copy-start | bytes 1572868
  38.5 1.0 %copy-start.10 = (bf16[256,1024]{1,0:T(8,128)(2,1)S(1)}, bf16[256,1024]{1,0:T(8,128)(2,1)}, u32[]{:S(2)}) copy-start(bf16[256,1024]{1,0:T(8,128)(2,1)} %get-tuple-element.29.refs_8_) | copy-start | bytes 1572868
  39.6 1.0 %copy-start.11 = (bf16[1024,256]{1,0:T(8,128)(2,1)S(1)}, bf16[1024,256]{1,0:T(8,128)(2,1)}, u32[]{:S(2)}) copy-start(bf16[1024,256]{1,0:T(8,128)(2,1)} %get-tuple-element.28.refs_7_) | copy-start | bytes 1572868
  55.7 1.0 copy-start.6
  56.6 0.7 copy-start.7
  57.3 1.9 %collective-permute-start.5 = (bf16[16,64,128]{2,1,0:T(8,128)(2,1)S(1)}, bf16[16,64,128]{2,1,0:T(8,128)(2,1)S(1)}, u32[]{:S(2)}, u32[]{:S(2)}) collective-permute-start(bf16[16,64,128]{2,1,0:T(8,128)(2,1)S(1)} %get-tuple-element.36), channel_id=1, source_target_pairs={{0,8},{8,0},{1,9},{9,1},{2,10},{10,2},{3,11},{11,3},{4,12},{12,4},... | collective-permute-start | bytes 786440 | tf_op jit(solution)/shard_map/ppermute | solution.py:329
  57.4 15.3 %collective-permute-start.4 = (bf16[4,256,256]{2,1,0:T(8,128)(2,1)S(1)}, bf16[4,256,256]{2,1,0:T(8,128)(2,1)}, u32[]{:S(2)}, u32[]{:S(2)}) collective-permute-start(bf16[4,256,256]{2,1,0:T(8,128)(2,1)S(1)} %get-tuple-element.32), channel_id=1, source_target_pairs={{0,1},{1,0},{2,3},{3,2},{4,5},{5,4},{6,7},{7,6},{8,9},{9,8},{10,11... | collective-permute-start | bytes 1572872 | tf_op jit(solution)/shard_map/ppermute | solution.py:329
  59.3 1.0 copy-start.8
  61.0 18.0 %all-to-all-start.2 = ((bf16[16,80,128]{2,1,0:T(8,128)(2,1)}), bf16[16,80,128]{2,1,0:T(8,128)(2,1)S(1)}, u32[]{:S(2)}, u32[]{:S(2)}) async-start(bf16[16,80,128]{2,1,0:T(8,128)(2,1)} %shard_map.168), calls=%async_computation.2 | async-start | bytes 655360 | tf_op jit(solution)/shard_map/all_to_all | solution.py:325
  73.9 19.4 %collective-permute-start.6 = (bf16[256,256]{1,0:T(8,128)(2,1)S(1)}, bf16[256,256]{1,0:T(8,128)(2,1)S(1)}, u32[]{:S(2)}, u32[]{:S(2)}) collective-permute-start(bf16[256,256]{1,0:T(8,128)(2,1)S(1)} %get-tuple-element.49), channel_id=1, source_target_pairs={{0,2},{2,0},{4,6},{6,4},{1,3},{3,1},{5,7},{7,5},{8,10},{10,8},{12,... | collective-permute-start | bytes 393224 | tf_op jit(solution)/shard_map/ppermute | solution.py:329
  75.5 17.8 %collective-permute-start.7 = (bf16[256,256]{1,0:T(8,128)(2,1)S(1)}, bf16[256,256]{1,0:T(8,128)(2,1)S(1)}, u32[]{:S(2)}, u32[]{:S(2)}) collective-permute-start(bf16[256,256]{1,0:T(8,128)(2,1)S(1)} %get-tuple-element.48), channel_id=1, source_target_pairs={{0,4},{2,6},{4,0},{6,2},{1,5},{3,7},{5,1},{7,3},{8,12},{10,14},{12... | collective-permute-start | bytes 393224 | tf_op jit(solution)/shard_map/ppermute | solution.py:329
  78.8 14.5 %collective-permute-start.8 = (bf16[256,256]{1,0:T(8,128)(2,1)S(1)}, bf16[256,256]{1,0:T(8,128)(2,1)S(1)}, u32[]{:S(2)}, u32[]{:S(2)}) collective-permute-start(bf16[256,256]{1,0:T(8,128)(2,1)S(1)} %get-tuple-element.47), channel_id=1, source_target_pairs={{0,6},{2,4},{4,2},{6,0},{1,7},{3,5},{5,3},{7,1},{8,14},{10,12},{12... | collective-permute-start | bytes 393224 | tf_op jit(solution)/shard_map/ppermute | solution.py:329
  79.7 15.6 %all-to-all-start.3 = ((bf16[16,48,128]{2,1,0:T(8,128)(2,1)}), bf16[16,48,128]{2,1,0:T(8,128)(2,1)S(1)}, u32[]{:S(2)}, u32[]{:S(2)}) async-start(bf16[16,48,128]{2,1,0:T(8,128)(2,1)} %shard_map.169), calls=%async_computation.3 | async-start | bytes 393216 | tf_op jit(solution)/shard_map/all_to_all | solution.py:325
  95.2 1.4 %collective-permute-start.9 = (bf16[768,128]{1,0:T(8,128)(2,1)S(1)}, bf16[768,128]{1,0:T(8,128)(2,1)S(1)}, u32[]{:S(2)}, u32[]{:S(2)}) collective-permute-start(bf16[768,128]{1,0:T(8,128)(2,1)S(1)} %bitcast.32), channel_id=1, source_target_pairs={{0,8},{8,0},{1,9},{9,1},{2,10},{10,2},{3,11},{11,3},{4,12},{12,4},... | collective-permute-start | bytes 589832 | tf_op jit(solution)/shard_map/ppermute | solution.py:329

commit v6 on v5

--- a/solution.py
+++ b/solution.py
@@ -13,6 +13,7 @@
 CHIPS = ("pair", "line", "near")
 PAIRS = 2
 BLOCK = 256
+UNROLL = 4
 
 
 def nn(a, b):
@@ -41,68 +42,36 @@
     return jnp.where(iota == ids_row - first, 1.0, 0.0).astype(BF)
 
 
-def relation_lookup_kernel(rel_ref, rel_id, qual_rel, rel_out, table):
+def relation_lookup_kernel(rel_ref, rel_id, qual_rel, rel_out, table, looked, sems):
     rel_rows, width = rel_ref.shape
     edges = rel_id.shape[1]
-    step = pl.program_id(0)
-
-    @pl.when(step == 0)
-    def _():
-        for index, part in enumerate(pieces(rel_ref[...].T, 2)):
-            table[index * width : (index + 1) * width, :] = part
-
-    def look(ids):
+    for index, part in enumerate(pieces(rel_ref[...].T, 2)):
+        table[index * width : (index + 1) * width, :] = part
+    stores = []
+    for which in range(1 + qual_rel.shape[0]):
+        ids = qual_rel.at[which - 1 : which] if which else rel_id
         for start in range(0, edges, BLOCK):
             at = pl.ds(start, BLOCK)
             got = nn(table[...], onehot(ids[:, at], 0, rel_rows))
-            rel_out[0, :, at] = got[:width] + got[width:]
-
-    @pl.when(step == 0)
-    def _():
-        look(rel_id)
-
-    for k in range(qual_rel.shape[0]):
-
-        @pl.when(step == k + 1)
-        def _():
-            look(qual_rel.at[k : k + 1])
-
-
-def tail_lookup_kernel(
-    tail_hbm, tail_id, neg_id, tails_out, negt_out, neg_out, tail_ref, table, tails, negt, neg, in_sems, out_sems
-):
+            looked[which, :, at] = got[:width] + got[width:]
+        stores.append(pltpu.make_async_copy(looked.at[which], rel_out.at[which], sems.at[which]))
+        stores[which].start()
+    for copy in stores:
+        copy.wait()
+
+
+def tail_lookup_kernel(tail_ref, tail_id, neg_id, tails_out, negt_out, neg_out, table):
     tail_rows = tail_ref.shape[0]
-    chunks = in_sems.shape[0]
-    size = tail_rows // chunks
-    loads = []
-    for index in range(chunks):
-        at = pl.ds(index * size, size)
-        loads.append(pltpu.make_async_copy(tail_hbm.at[at, :], tail_ref.at[at, :], in_sems.at[index]))
-        loads[index].start()
-    for index in range(chunks):
-        loads[index].wait()
-        for start in range(index * size, (index + 1) * size, BLOCK):
-            at = pl.ds(start, BLOCK)
-            table[:, at] = tail_ref[at, :].T
-    stores = []
-
-    def store(source, target):
-        stores.append(pltpu.make_async_copy(source, target, out_sems.at[len(stores)]))
-        stores[-1].start()
-
-    for ids, out in ((neg_id, negt), (tail_id, tails)):
+    for start in range(0, tail_rows, BLOCK):
+        at = pl.ds(start, BLOCK)
+        table[:, at] = tail_ref[at, :].T
+    for ids, out in ((tail_id, tails_out), (neg_id, negt_out)):
         for start in range(0, ids.shape[1], BLOCK):
             at = pl.ds(start, BLOCK)
             got = nn(table[...], onehot(ids[:, at], 0, tail_rows))
             out[:, at] = got.astype(BF)
             if ids is neg_id:
-                neg[at, :] = got.T.astype(BF)
-        if ids is neg_id:
-            store(negt, negt_out)
-            store(neg, neg_out)
-    store(tails, tails_out)
-    for copy in stores:
-        copy.wait()
+                neg_out[at, :] = got.T.astype(BF)
 
 
 def edge_kernel(
@@ -133,17 +102,15 @@
     neg_ref,
     negt_ref,
     sums,
-    packed,
-    terms,
     in_sems,
-    out_sems,
     *,
     rel_rows,
 ):
     width, edges = tails_ref.shape
     slots = fetched_ref.shape[0]
     half, head_rows, _ = near_ref.shape
-    cores, chips, _, lanes = packed.shape
+    chips, _, lanes = own_out.shape
+    cores = width // lanes
     share = sums.shape[0] // chips
     quals = ref_ids.shape[0]
     cap = slots // (cores * chips)
@@ -199,18 +166,18 @@
     loads[5].wait()
     query_grad = coef * tails + nn(negt_ref[...], neg_round)
 
-    stores = []
-
-    def store(source, target):
-        stores.append(pltpu.make_async_copy(source, target, out_sems.at[len(stores)]))
-        stores[-1].start()
-
     head_terms = (query_grad * relation).astype(BF)
-    for first, part, out in ((half, far_ref, far_out), (0, near_ref, near_out)):
-        for owner in range(half):
+    for first, out in ((half, far_out), (0, near_out)):
+
+        def scatter(owner):
             hot = onehot(head_slot, (first + owner) * head_rows, head_rows)
-            part[owner] = nt(hot, head_terms).astype(BF)
-        store(part, out)
+            out[owner] = nt(hot, head_terms).astype(BF)
+
+        if half > UNROLL:
+            pl.loop(0, half)(scatter)
+        else:
+            for owner in range(half):
+                scatter(owner)
 
     relation_grad = query_grad * heads
     rg_hi, rg_lo = pieces(relation_grad, 2)
@@ -230,15 +197,18 @@
         mine = pairs[:, core].reshape(chips, cap, width)
         parts = [sums[:, core * lanes : (core + 1) * lanes].reshape(chips, share, lanes)]
         parts += [mine[:, :, start : start + lanes] for start in range(0, width, lanes)]
-        packed[core] = jnp.concatenate(parts, axis=1).astype(BF)
-    store(packed.at[core_ref[0]], own_out)
-    store(packed.at[1 - core_ref[0]], other_out)
-
-    terms[:edges, :] = flip((coef * query_f).astype(BF))
-    terms[edges:, :] = nt(neg_round, query).astype(BF)
-    store(terms, terms_out)
-    for copy in stores:
-        copy.wait()
+        both = jnp.concatenate(parts, axis=1).astype(BF)
+
+        @pl.when(core_ref[0] == core)
+        def _():
+            own_out[...] = both
+
+        @pl.when(core_ref[0] != core)
+        def _():
+            other_out[...] = both
+
+    terms_out[:edges, :] = flip((coef * query_f).astype(BF))
+    terms_out[edges:, :] = nt(neg_round, query).astype(BF)
 
 
 def combine_kernel(own_ref, got_ref, out_ref):
@@ -372,39 +342,31 @@
     (rel_looked,) = call(
         relation_lookup_kernel,
         [((quals + 1, width, edges), F32)],
-        [pltpu.VMEM((2 * width, rel_rows), BF)],
+        [
+            pltpu.VMEM((2 * width, rel_rows), BF),
+            pltpu.VMEM((quals + 1, width, edges), F32),
+            pltpu.SemaphoreType.DMA((quals + 1,)),
+        ],
         5,
         58,
         rel_table,
         rel_row,
         qual_row,
-        grid=(quals + 1,),
-        out_specs=[pl.BlockSpec((1, width, edges), lambda i: (i, 0, 0))],
+        out_specs=[pl.BlockSpec(memory_space=pl.ANY)],
     )
     arrived, rel_looked, head_near = lax.optimization_barrier((arrived, rel_looked, head_near))
     head_far = swap(head_near, "near")
     picked = qual_table.at[arrived].get(mode="promise_in_bounds")
     fetched = exchange(picked, AXES).reshape(slots, width)
-    chunks = 4
     tails, neg_t, neg = call(
         tail_lookup_kernel,
         [((width, edges), BF), ((width, negs), BF), ((negs, width), BF)],
-        [
-            pltpu.VMEM((tail_rows, width), BF),
-            pltpu.VMEM((width, tail_rows), BF),
-            pltpu.VMEM((width, edges), BF),
-            pltpu.VMEM((width, negs), BF),
-            pltpu.VMEM((negs, width), BF),
-            pltpu.SemaphoreType.DMA((chunks,)),
-            pltpu.SemaphoreType.DMA((3,)),
-        ],
+        [pltpu.VMEM((width, tail_rows), BF)],
         7,
-        58,
+        32,
         tail_table,
         tail_row,
         neg_row,
-        away=(0,),
-        out_specs=[pl.BlockSpec(memory_space=pl.ANY)] * 3,
     )
     share = -(-(rel_rows + width) // (16 * chips)) * 16
     passed = cap * cores
@@ -430,13 +392,10 @@
             pltpu.VMEM((negs, width), BF),
             pltpu.VMEM((width, negs), BF),
             pltpu.VMEM((chips * share, width), F32),
-            pltpu.VMEM((cores, chips, sent, lanes), BF),
-            pltpu.VMEM((edges + negs, width), BF),
             pltpu.SemaphoreType.DMA((6,)),
-            pltpu.SemaphoreType.DMA((5,)),
         ],
         14,
-        58 if half > 4 else 44,
+        58 if half > UNROLL else 44,
         edge_count,
         core,
         member,
@@ -454,7 +413,6 @@
         proj,
         smem=(0, 1, 2),
         away=range(3, 9),
-        out_specs=[pl.BlockSpec(memory_space=pl.ANY)] * 5,
     )
     other_got = swap(other_part, "core")
     far_got = swap(far_part, "near")
@@ -473,7 +431,7 @@
             [((tail_rows, width), F32)],
             [],
             3,
-            58,
+            24,
             tail_row,
             neg_row,
             terms,

time: 98.4 us -> 98.6 us (level)
  Pallas kernels: 42.6 us -> 34.9 us
  local copies, waits for them, and re-layouts: 9.25 us -> 14.4 us
  other arithmetic: 2.03 us -> 4.04 us
  waiting for transfers between devices: 3.97 us -> 5.5 us
    pallas_call x9, Pallas kernels: 42.6 us -> 34.9 us  [call(): pl.pallas_call(kernel, out_shape=shapes, grid=grid, in_specs=[pl.BlockSpe...]
    unnamed x26 -> x42, local copies, waits for them, and re-layouts: 5.79 us -> 11 us
    all_to_all x4, waiting for transfers between devices: 2.63 us -> 4.95 us  [exchange(): return lax.all_to_all(values, axes, split_axis=0, concat_axis=0, tiled=True)]
    convert_element_type x1, other arithmetic: 1.19 us -> 2.25 us  [body(): near_send = near_sum.astype(BF)]
  transfers between devices with their start and end apart: 14 -> 14, of which waited for: 5 -> 3; matrix products, arithmetic and copies ran while one was open for 4% -> 6% of each run, Pallas kernels for 27% -> 20%
where the time goes in v6:
time: 98.6 us; the launch traced here: 97.8 us
  starting transfers between devices  37.4 us (38%)
  Pallas kernels  34.9 us (35%)
  local copies, waits for them, and re-layouts  14.4 us (15%)
  waiting for transfers between devices  5.5 us (6%)
  other arithmetic  4.04 us (4%)
  between operations  1.59 us (2%)
    pallas_call x9, Pallas kernels, call(): pl.pallas_call(kernel, out_shape=shapes, grid=grid, in_specs=[pl.BlockSpe...  34.9 us
    all_to_all x4, starting transfers between devices, exchange(): return lax.all_to_all(values, axes, split_axis=0, concat_axis=0, tiled=True)  24 us
    ppermute x10, starting transfers between devices, swap(): lax.ppermute(values, axis, [(i, i ^ offset) for i in range(lax.axis_size(...  13.3 us
    unnamed x42, local copies, waits for them, and re-layouts  11 us
    all_to_all x4, waiting for transfers between devices, exchange(): return lax.all_to_all(values, axes, split_axis=0, concat_axis=0, tiled=True)  4.95 us
    convert_element_type x1, other arithmetic, body(): near_send = near_sum.astype(BF)  2.25 us
  transfers between devices with their start and end apart: 14, of which 3 were waited for; matrix products, arithmetic and copies ran while one was open for 6% of the time, Pallas kernels for 20%

profile of v6, /device:TPU:0, one launch (start us, length us, event | category | flops | bytes accessed | tf_op | source)
XLA Modules:
  0.0 97.8 jit_solution(18322885581698370052)
XLA Ops:
  0.6 0.0 copy-start
  0.6 3.1 %collective-permute-start = (bf16[256,256]{1,0:T(8,128)(2,1)}, bf16[256,256]{1,0:T(8,128)(2,1)S(1)}, u32[]{:S(2)}, u32[]{:S(2)}) collective-permute-start(bf16[256,256]{1,0:T(8,128)(2,1)} %param.13), channel_id=1, source_target_pairs={{0,2},{2,0},{4,6},{6,4},{1,3},{3,1},{5,7},{7,5},{8,10},{10,8},{12,... | collective-permute-start | bytes 393224 | tf_op jit(solution)/shard_map/ppermute | solution.py:299
  3.7 2.6 %collective-permute-start.1 = (bf16[256,256]{1,0:T(8,128)(2,1)}, bf16[256,256]{1,0:T(8,128)(2,1)S(1)}, u32[]{:S(2)}, u32[]{:S(2)}) collective-permute-start(bf16[256,256]{1,0:T(8,128)(2,1)} %param.13), channel_id=1, source_target_pairs={{0,4},{2,6},{4,0},{6,2},{1,5},{3,7},{5,1},{7,3},{8,12},{10,14},{12... | collective-permute-start | bytes 393224 | tf_op jit(solution)/shard_map/ppermute | solution.py:299
  6.3 1.4 %all_to_all.17 = s32[32,1,8]{2,0,1:T(8,128)} reshape(s32[256]{0:T(256)} %param.23) | data formatting | bytes 2048 | tf_op jit(solution)/shard_map/all_to_all | solution.py:295
  7.7 6.1 %all-to-all-start = ((s32[32,1,8]{2,1,0:T(1,128)}), s32[32,1,8]{2,1,0:T(1,128)S(1)}, u32[]{:S(2)}, u32[]{:S(2)}) async-start(s32[32,1,8]{2,1,0:T(1,128)} %bitcast.2), calls=%async_computation | async-start | bytes 32768 | tf_op jit(solution)/shard_map/all_to_all | solution.py:295
  13.8 0.0 copy-start.20
  13.8 0.0 copy-start.7
  13.8 0.0 copy-start.8
  13.8 5.1 %shard_map.164.refs_3_ = f32[5,256,1024]{2,1,0:T(8,128)} custom-call(f32[512,256]{1,0:T(8,128)} %rel_ref.1, s32[1,1024]{1,0:T(1,128)} %bitcast.38, s32[4,1024]{1,0:T(4,128)} %bitcast.35), custom_call_target="tpu_custom_call" | custom-call | flops 5368709120 | bytes 1048576 | tf_op jit(solution)/shard_map/pallas_call | solution.py:281
  19.0 0.1 pad_maximum_fusion.refs_4_
  19.0 1.8 %all-to-all-done = s32[32,1,8]{2,1,0:T(1,128)S(1)} async-done(((s32[32,1,8]{2,1,0:T(1,128)}), s32[32,1,8]{2,1,0:T(1,128)S(1)}, u32[]{:S(2)}, u32[]{:S(2)}) %all-to-all-start) | async-done | bytes 1056 | tf_op jit(solution)/shard_map/all_to_all | solution.py:295
  20.8 0.6 collective-permute-start.3
  21.4 0.1 reshape.40
  21.6 1.8 %gather_fusion = bf16[256,256]{1,0:T(8,128)(2,1)} fusion(bf16[1024,256]{1,0:T(8,128)(2,1)S(1)} %copy-done, s32[1024]{0:T(1024)S(1)} %pad_clamp_fusion), kind=kCustom, calls=%fused_computation | custom fusion | bytes 263168 | tf_op jit(solution)/shard_map/gather | solution.py:359
  23.4 4.1 %all-to-all-start.1 = ((bf16[32,8,256]{2,1,0:T(8,128)(2,1)}), bf16[32,8,256]{2,1,0:T(8,128)(2,1)S(1)}, u32[]{:S(2)}, u32[]{:S(2)}) async-start(bf16[32,8,256]{2,1,0:T(8,128)(2,1)} %bitcast.12), calls=%async_computation.1 | async-start | bytes 262144 | tf_op jit(solution)/shard_map/all_to_all | solution.py:295
  27.5 0.0 copy-start.1
  27.5 1.6 %copy-done.1 = bf16[4096,256]{1,0:T(8,128)(2,1)S(1)} copy-done((bf16[4096,256]{1,0:T(8,128)(2,1)S(1)}, bf16[4096,256]{1,0:T(8,128)(2,1)}, u32[]{:S(2)}) %copy-start.1) | copy-done | bytes 2097176
  29.1 4.7 %shard_map.165 = (bf16[256,1024]{1,0:T(8,128)(2,1)S(1)}, bf16[256,1024]{1,0:T(8,128)(2,1)S(1)}, bf16[1024,256]{1,0:T(8,128)(2,1)S(1)}) custom-call(bf16[4096,256]{1,0:T(8,128)(2,1)S(1)} %copy-done.1, s32[1,1024]{1,0:T(1,128)S(1)} %bitcast.41, s32[1,1024]{1,0:T(1,128)S(1)} %bitcast.44), custom_call_target="tpu_custom_call" | custom-call | flops 7516192768 | bytes 1048576 | tf_op jit(solution)/shard_map/pallas_call | solution.py:281
  33.8 0.0 copy-start.14
  33.8 0.8 copy-done.14
  34.6 0.8 copy-done.16
  35.4 0.8 copy-done.18
  36.9 1.0 %copy-done.15 = bf16[256,1024]{1,0:T(8,128)(2,1)S(1)} copy-done((bf16[256,1024]{1,0:T(8,128)(2,1)S(1)}, bf16[256,1024]{1,0:T(8,128)(2,1)}, u32[]{:S(2)}) %copy-start.15) | copy-done | bytes 524312
  38.0 1.0 %copy-done.17 = bf16[256,1024]{1,0:T(8,128)(2,1)S(1)} copy-done((bf16[256,1024]{1,0:T(8,128)(2,1)S(1)}, bf16[256,1024]{1,0:T(8,128)(2,1)}, u32[]{:S(2)}) %copy-start.17) | copy-done | bytes 524312
  39.0 1.0 %copy-done.19 = bf16[1024,256]{1,0:T(8,128)(2,1)S(1)} copy-done((bf16[1024,256]{1,0:T(8,128)(2,1)S(1)}, bf16[1024,256]{1,0:T(8,128)(2,1)}, u32[]{:S(2)}) %copy-start.19) | copy-done | bytes 524312
  40.1 14.3 %shard_map.166 = (bf16[4,256,256]{2,1,0:T(8,128)(2,1)S(1)}, bf16[4,256,256]{2,1,0:T(8,128)(2,1)S(1)}, bf16[16,64,128]{2,1,0:T(8,128)(2,1)S(1)}, bf16[16,64,128]{2,1,0:T(8,128)(2,1)S(1)}, bf16[2048,256]{1,0:T(8,128)(2,1)S(1)}) custom-call(s32[1]{0:T(128)S(6)} %copy.23.refs_0_, s32[1]{0:T(128)} %bitcast.refs_1_.core_ref, s32[1]{0:T(128)} %bitcast.1.refs_2_, ...), custom_call_target="tpu_custom_call" | custom-call | flops 15032385536 | bytes 1048576 | tf_op jit(solution)/shard_map/pallas_call | solution.py:281
  54.4 1.0 copy-done.9
  55.3 0.7 copy-done.12
  56.0 0.3 collective-permute-start.5
  56.3 1.7 %collective-permute-start.4 = (bf16[4,256,256]{2,1,0:T(8,128)(2,1)S(1)}, bf16[4,256,256]{2,1,0:T(8,128)(2,1)}, u32[]{:S(2)}, u32[]{:S(2)}) collective-permute-start(bf16[4,256,256]{2,1,0:T(8,128)(2,1)S(1)} %get-tuple-element.32), channel_id=1, source_target_pairs={{0,1},{1,0},{2,3},{3,2},{4,5},{5,4},{6,7},{7,6},{8,9},{9,8},{10,11... | collective-permute-start | bytes 1572872 | tf_op jit(solution)/shard_map/ppermute | solution.py:299
  57.9 0.1 reshape.36
  58.0 0.1 reshape.37.asked
  58.1 1.0 copy-done.13
  59.1 0.8 shard_map.168
  59.8 6.3 %all-to-all-start.2 = ((bf16[16,80,128]{2,1,0:T(8,128)(2,1)}), bf16[16,80,128]{2,1,0:T(8,128)(2,1)S(1)}, u32[]{:S(2)}, u32[]{:S(2)}) async-start(bf16[16,80,128]{2,1,0:T(8,128)(2,1)} %shard_map.168), calls=%async_computation.2 | async-start | bytes 655360 | tf_op jit(solution)/shard_map/all_to_all | solution.py:295
  66.2 1.2 %copy-done.10 = bf16[2048,256]{1,0:T(8,128)(2,1)S(1)} copy-done((bf16[2048,256]{1,0:T(8,128)(2,1)S(1)}, bf16[2048,256]{1,0:T(8,128)(2,1)}, u32[]{:S(2)}) %copy-start.10) | copy-done | bytes 1048600
  67.4 3.5 %shard_map.167.refs_3_ = f32[4096,256]{1,0:T(8,128)} custom-call(s32[1,1024]{1,0:T(1,128)S(1)} %bitcast.42, s32[1,1024]{1,0:T(1,128)S(1)} %bitcast.45, bf16[2048,256]{1,0:T(8,128)(2,1)S(1)} %copy-done.10), custom_call_target="tpu_custom_call" | custom-call | flops 3221225472 | bytes 1048576 | tf_op jit(solution)/shard_map/pallas_call | solution.py:281
  70.9 0.5 collective-permute-done.4
  71.4 2.2 %fusion.3 = (bf16[4,256,256]{2,1,0:T(8,128)(2,1)S(1)}, f32[4,256,256]{2,1,0:T(8,128)}) fusion(bf16[4,256,256]{2,1,0:T(8,128)(2,1)} %collective-permute-done.4, bf16[4,256,256]{2,1,0:T(8,128)(2,1)S(1)} %get-tuple-element.31), kind=kLoop, calls=%fused_computation.12 | loop fusion | flops 1048576 | bytes 2621440 | tf_op jit(solution)/shard_map/convert_element_type | solution.py:449
  73.7 1.8 %collective-permute-start.6 = (bf16[256,256]{1,0:T(8,128)(2,1)S(1)}, bf16[256,256]{1,0:T(8,128)(2,1)S(1)}, u32[]{:S(2)}, u32[]{:S(2)}) collective-permute-start(bf16[256,256]{1,0:T(8,128)(2,1)S(1)} %get-tuple-element.49), channel_id=1, source_target_pairs={{0,2},{2,0},{4,6},{6,4},{1,3},{3,1},{5,7},{7,5},{8,10},{10,8},{12,... | collective-permute-start | bytes 393224 | tf_op jit(solution)/shard_map/ppermute | solution.py:299
  75.4 3.3 %collective-permute-start.7 = (bf16[256,256]{1,0:T(8,128)(2,1)S(1)}, bf16[256,256]{1,0:T(8,128)(2,1)S(1)}, u32[]{:S(2)}, u32[]{:S(2)}) collective-permute-start(bf16[256,256]{1,0:T(8,128)(2,1)S(1)} %get-tuple-element.48), channel_id=1, source_target_pairs={{0,4},{2,6},{4,0},{6,2},{1,5},{3,7},{5,1},{7,3},{8,12},{10,14},{12... | collective-permute-start | bytes 393224 | tf_op jit(solution)/shard_map/ppermute | solution.py:299
  78.8 0.7 shard_map.169
  79.5 7.6 %all-to-all-start.3 = ((bf16[16,48,128]{2,1,0:T(8,128)(2,1)}), bf16[16,48,128]{2,1,0:T(8,128)(2,1)S(1)}, u32[]{:S(2)}, u32[]{:S(2)}) async-start(bf16[16,48,128]{2,1,0:T(8,128)(2,1)} %shard_map.169), calls=%async_computation.3 | async-start | bytes 393216 | tf_op jit(solution)/shard_map/all_to_all | solution.py:295
  87.1 3.5 %shard_map.170 = f32[4096,256]{1,0:T(8,128)} custom-call(s32[1,1024]{1,0:T(1,128)S(1)} %bitcast.43, s32[1,1024]{1,0:T(1,128)S(1)} %bitcast.46, bf16[2048,256]{1,0:T(8,128)(2,1)S(1)} %copy-done.11, f32[4096,256]{1,0:T(8,128)} %shard_map.167.refs_3_), custom_call_target="tpu_custom_call", output_to_operand_aliasing={{}: (3, {})} | custom-call | flops 3221225472 | bytes 1048576 | tf_op jit(solution)/shard_map/pallas_call | solution.py:281
  90.6 1.4 %shard_map.171 = f32[1024,256]{1,0:T(8,128)} custom-call(s32[1]{0:T(128)} %bitcast.refs_1_.core_ref, bf16[16,80,128]{2,1,0:T(8,128)(2,1)S(1)} %all-to-all-done.2.got_ref, s32[2,128]{1,0:T(2,128)S(1)} %reshape.37.asked), custom_call_target="tpu_custom_call" | custom-call | flops 2147483648 | bytes 1048576 | tf_op jit(solution)/shard_map/pallas_call | solution.py:281
  92.0 3.2 %all-to-all-done.3 = bf16[16,48,128]{2,1,0:T(8,128)(2,1)S(1)} async-done(((bf16[16,48,128]{2,1,0:T(8,128)(2,1)}), bf16[16,48,128]{2,1,0:T(8,128)(2,1)S(1)}, u32[]{:S(2)}, u32[]{:S(2)}) %all-to-all-start.3) | async-done | bytes 196640 | tf_op jit(solution)/shard_map/all_to_all | solution.py:295
  95.2 1.7 %fusion.2 = f32[256,256]{1,0:T(8,128)} fusion(f32[4,256,256]{2,1,0:T(8,128)} %get-tuple-element.46, bf16[256,256]{1,0:T(8,128)(2,1)S(1)} %collective-permute-done.8, bf16[256,256]{1,0:T(8,128)(2,1)S(1)} %collective-permute-done.7, bf16[256,256]{1,0:T(8,128)(2,1)S(1)} %collective-permute-done.6), kind=kLoop, calls=%fused_computation.6 | loop fusion | flops 393216 | bytes 917504 | tf_op jit(solution)/shard_map/add | solution.py:470
  96.9 0.9 shard_map.172
  (43 shorter events, 0.1 us)
Async XLA Ops:
  0.6 20.9 %copy-start = (bf16[1024,256]{1,0:T(8,128)(2,1)S(1)}, bf16[1024,256]{1,0:T(8,128)(2,1)}, u32[]{:S(2)}) copy-start(bf16[1024,256]{1,0:T(8,128)(2,1)} %param.15) | copy-start | bytes 1572868
  0.6 18.3 %collective-permute-start = (bf16[256,256]{1,0:T(8,128)(2,1)}, bf16[256,256]{1,0:T(8,128)(2,1)S(1)}, u32[]{:S(2)}, u32[]{:S(2)}) collective-permute-start(bf16[256,256]{1,0:T(8,128)(2,1)} %param.13), channel_id=1, source_target_pairs={{0,2},{2,0},{4,6},{6,4},{1,3},{3,1},{5,7},{7,5},{8,10},{10,8},{12,... | collective-permute-start | bytes 393224 | tf_op jit(solution)/shard_map/ppermute | solution.py:299
  3.7 15.2 %collective-permute-start.1 = (bf16[256,256]{1,0:T(8,128)(2,1)}, bf16[256,256]{1,0:T(8,128)(2,1)S(1)}, u32[]{:S(2)}, u32[]{:S(2)}) collective-permute-start(bf16[256,256]{1,0:T(8,128)(2,1)} %param.13), channel_id=1, source_target_pairs={{0,4},{2,6},{4,0},{6,2},{1,5},{3,7},{5,1},{7,3},{8,12},{10,14},{12... | collective-permute-start | bytes 393224 | tf_op jit(solution)/shard_map/ppermute | solution.py:299
  6.3 12.6 %collective-permute-start.2 = (bf16[256,256]{1,0:T(8,128)(2,1)}, bf16[256,256]{1,0:T(8,128)(2,1)S(1)}, u32[]{:S(2)}, u32[]{:S(2)}) collective-permute-start(bf16[256,256]{1,0:T(8,128)(2,1)} %param.13), channel_id=1, source_target_pairs={{0,6},{2,4},{4,2},{6,0},{1,7},{3,5},{5,3},{7,1},{8,14},{10,12},{12... | collective-permute-start | bytes 393224 | tf_op jit(solution)/shard_map/ppermute | solution.py:299
  7.7 13.1 %all-to-all-start = ((s32[32,1,8]{2,1,0:T(1,128)}), s32[32,1,8]{2,1,0:T(1,128)S(1)}, u32[]{:S(2)}, u32[]{:S(2)}) async-start(s32[32,1,8]{2,1,0:T(1,128)} %bitcast.2), calls=%async_computation | async-start | bytes 32768 | tf_op jit(solution)/shard_map/all_to_all | solution.py:295
  13.8 5.2 %copy-start.20 = (bf16[256,256]{1,0:T(8,128)(2,1)S(1)}, bf16[256,256]{1,0:T(8,128)(2,1)}, u32[]{:S(2)}) copy-start(bf16[256,256]{1,0:T(8,128)(2,1)} %param.13) | copy-start | bytes 393220
  13.8 13.6 %copy-start.7 = (s32[1024]{0:T(1024)S(1)}, s32[1024]{0:T(1024)}, u32[]{:S(2)}) copy-start(s32[1024]{0:T(1024)} %param.19) | copy-start | bytes 12292
  13.8 13.6 %copy-start.8 = (s32[1024]{0:T(1024)S(1)}, s32[1024]{0:T(1024)}, u32[]{:S(2)}) copy-start(s32[1024]{0:T(1024)} %param.24) | copy-start | bytes 12292
  20.8 16.1 %collective-permute-start.3 = (bf16[4,256,256]{2,1,0:T(8,128)(2,1)S(1)}, bf16[4,256,256]{2,1,0:T(8,128)(2,1)S(1)}, u32[]{:S(2)}, u32[]{:S(2)}) collective-permute-start(bf16[4,256,256]{2,1,0:T(8,128)(2,1)S(1)} %pad_maximum_fusion.refs_4_), channel_id=1, source_target_pairs={{0,1},{1,0},{2,3},{3,2},{4,5},{5,4},{6,7},{7,6},{8,9},{9,8},{10,11... | collective-permute-start | bytes 1572872 | tf_op jit(solution)/shard_map/ppermute | solution.py:299
  23.4 13.5 %all-to-all-start.1 = ((bf16[32,8,256]{2,1,0:T(8,128)(2,1)}), bf16[32,8,256]{2,1,0:T(8,128)(2,1)S(1)}, u32[]{:S(2)}, u32[]{:S(2)}) async-start(bf16[32,8,256]{2,1,0:T(8,128)(2,1)} %bitcast.12), calls=%async_computation.1 | async-start | bytes 262144 | tf_op jit(solution)/shard_map/all_to_all | solution.py:295
  27.5 1.6 %copy-start.1 = (bf16[4096,256]{1,0:T(8,128)(2,1)S(1)}, bf16[4096,256]{1,0:T(8,128)(2,1)}, u32[]{:S(2)}) copy-start(bf16[4096,256]{1,0:T(8,128)(2,1)} %tail_ref.1) | copy-start | bytes 6291460
  29.1 7.8 %copy-start.2 = (f32[256,256]{1,0:T(8,128)S(1)}, f32[256,256]{1,0:T(8,128)}, u32[]{:S(2)}) copy-start(f32[256,256]{1,0:T(8,128)} %refs_14_.1) | copy-start | bytes 786436
  29.1 7.8 %copy-start.3 = (s32[1024,4]{0,1:T(4,128)S(1)}, s32[1024,4]{0,1:T(4,128)}, u32[]{:S(2)}) copy-start(s32[1024,4]{0,1:T(4,128)} %param.21) | copy-start | bytes 49156
  29.1 7.8 %copy-start.4 = (s32[1024,4]{0,1:T(4,128)S(1)}, s32[1024,4]{0,1:T(4,128)}, u32[]{:S(2)}) copy-start(s32[1024,4]{0,1:T(4,128)} %param.22) | copy-start | bytes 49156
  29.1 7.9 %copy-start.5 = (s32[1024]{0:T(1024)S(1)}, s32[1024]{0:T(1024)}, u32[]{:S(2)}) copy-start(s32[1024]{0:T(1024)} %param.20) | copy-start | bytes 12292
  29.1 7.9 %copy-start.6 = (s32[1024]{0:T(1024)S(1)}, s32[1024]{0:T(1024)}, u32[]{:S(2)}) copy-start(s32[1024]{0:T(1024)} %param.18) | copy-start | bytes 12292
  33.8 0.8 copy-start.14
  34.6 0.8 copy-start.16
  35.4 0.8 copy-start.18
  36.9 1.0 %copy-start.15 = (bf16[256,1024]{1,0:T(8,128)(2,1)S(1)}, bf16[256,1024]{1,0:T(8,128)(2,1)}, u32[]{:S(2)}) copy-start(bf16[256,1024]{1,0:T(8,128)(2,1)} %copy-done.14) | copy-start | bytes 1572868
  38.0 1.0 %copy-start.17 = (bf16[256,1024]{1,0:T(8,128)(2,1)S(1)}, bf16[256,1024]{1,0:T(8,128)(2,1)}, u32[]{:S(2)}) copy-start(bf16[256,1024]{1,0:T(8,128)(2,1)} %copy-done.16) | copy-start | bytes 1572868
  39.0 1.0 %copy-start.19 = (bf16[1024,256]{1,0:T(8,128)(2,1)S(1)}, bf16[1024,256]{1,0:T(8,128)(2,1)}, u32[]{:S(2)}) copy-start(bf16[1024,256]{1,0:T(8,128)(2,1)} %copy-done.18) | copy-start | bytes 1572868
  54.3 1.0 copy-start.9
  55.3 0.7 copy-start.12
  56.0 2.1 %collective-permute-start.5 = (bf16[16,64,128]{2,1,0:T(8,128)(2,1)S(1)}, bf16[16,64,128]{2,1,0:T(8,128)(2,1)S(1)}, u32[]{:S(2)}, u32[]{:S(2)}) collective-permute-start(bf16[16,64,128]{2,1,0:T(8,128)(2,1)S(1)} %get-tuple-element.36), channel_id=1, source_target_pairs={{0,8},{8,0},{1,9},{9,1},{2,10},{10,2},{3,11},{11,3},{4,12},{12,4},... | collective-permute-start | bytes 786440 | tf_op jit(solution)/shard_map/ppermute | solution.py:299
  56.3 15.1 %collective-permute-start.4 = (bf16[4,256,256]{2,1,0:T(8,128)(2,1)S(1)}, bf16[4,256,256]{2,1,0:T(8,128)(2,1)}, u32[]{:S(2)}, u32[]{:S(2)}) collective-permute-start(bf16[4,256,256]{2,1,0:T(8,128)(2,1)S(1)} %get-tuple-element.32), channel_id=1, source_target_pairs={{0,1},{1,0},{2,3},{3,2},{4,5},{5,4},{6,7},{7,6},{8,9},{9,8},{10,11... | collective-permute-start | bytes 1572872 | tf_op jit(solution)/shard_map/ppermute | solution.py:299
  58.1 1.0 copy-start.13
  59.8 18.9 %all-to-all-start.2 = ((bf16[16,80,128]{2,1,0:T(8,128)(2,1)}), bf16[16,80,128]{2,1,0:T(8,128)(2,1)S(1)}, u32[]{:S(2)}, u32[]{:S(2)}) async-start(bf16[16,80,128]{2,1,0:T(8,128)(2,1)} %shard_map.168), calls=%async_computation.2 | async-start | bytes 655360 | tf_op jit(solution)/shard_map/all_to_all | solution.py:295
  66.2 1.2 %copy-start.10 = (bf16[2048,256]{1,0:T(8,128)(2,1)S(1)}, bf16[2048,256]{1,0:T(8,128)(2,1)}, u32[]{:S(2)}) copy-start(bf16[2048,256]{1,0:T(8,128)(2,1)} %copy-done.9) | copy-start | bytes 3145732
  71.4 15.7 %copy-start.11 = (bf16[2048,256]{1,0:T(8,128)(2,1)S(1)}, bf16[2048,256]{1,0:T(8,128)(2,1)}, u32[]{:S(2)}) copy-start(bf16[2048,256]{1,0:T(8,128)(2,1)} %copy-done.9) | copy-start | bytes 3145732
  73.7 18.3 %collective-permute-start.6 = (bf16[256,256]{1,0:T(8,128)(2,1)S(1)}, bf16[256,256]{1,0:T(8,128)(2,1)S(1)}, u32[]{:S(2)}, u32[]{:S(2)}) collective-permute-start(bf16[256,256]{1,0:T(8,128)(2,1)S(1)} %get-tuple-element.49), channel_id=1, source_target_pairs={{0,2},{2,0},{4,6},{6,4},{1,3},{3,1},{5,7},{7,5},{8,10},{10,8},{12,... | collective-permute-start | bytes 393224 | tf_op jit(solution)/shard_map/ppermute | solution.py:299
  75.4 16.6 %collective-permute-start.7 = (bf16[256,256]{1,0:T(8,128)(2,1)S(1)}, bf16[256,256]{1,0:T(8,128)(2,1)S(1)}, u32[]{:S(2)}, u32[]{:S(2)}) collective-permute-start(bf16[256,256]{1,0:T(8,128)(2,1)S(1)} %get-tuple-element.48), channel_id=1, source_target_pairs={{0,4},{2,6},{4,0},{6,2},{1,5},{3,7},{5,1},{7,3},{8,12},{10,14},{12... | collective-permute-start | bytes 393224 | tf_op jit(solution)/shard_map/ppermute | solution.py:299
  78.8 13.2 %collective-permute-start.8 = (bf16[256,256]{1,0:T(8,128)(2,1)S(1)}, bf16[256,256]{1,0:T(8,128)(2,1)S(1)}, u32[]{:S(2)}, u32[]{:S(2)}) collective-permute-start(bf16[256,256]{1,0:T(8,128)(2,1)S(1)} %get-tuple-element.47), channel_id=1, source_target_pairs={{0,6},{2,4},{4,2},{6,0},{1,7},{3,5},{5,3},{7,1},{8,14},{10,12},{12... | collective-permute-start | bytes 393224 | tf_op jit(solution)/shard_map/ppermute | solution.py:299
  79.5 15.7 %all-to-all-start.3 = ((bf16[16,48,128]{2,1,0:T(8,128)(2,1)}), bf16[16,48,128]{2,1,0:T(8,128)(2,1)S(1)}, u32[]{:S(2)}, u32[]{:S(2)}) async-start(bf16[16,48,128]{2,1,0:T(8,128)(2,1)} %shard_map.169), calls=%async_computation.3 | async-start | bytes 393216 | tf_op jit(solution)/shard_map/all_to_all | solution.py:295
  95.2 1.7 %collective-permute-start.9 = (bf16[768,128]{1,0:T(8,128)(2,1)S(1)}, bf16[768,128]{1,0:T(8,128)(2,1)S(1)}, u32[]{:S(2)}, u32[]{:S(2)}) collective-permute-start(bf16[768,128]{1,0:T(8,128)(2,1)S(1)} %bitcast.32), channel_id=1, source_target_pairs={{0,8},{8,0},{1,9},{9,1},{2,10},{10,2},{3,11},{11,3},{4,12},{12,4},... | collective-permute-start | bytes 589832 | tf_op jit(solution)/shard_map/ppermute | solution.py:299

commit v7 on v6

--- a/solution.py
+++ b/solution.py
@@ -102,45 +102,47 @@
     neg_ref,
     negt_ref,
     sums,
+    packed,
+    terms,
     in_sems,
+    out_sems,
     *,
     rel_rows,
 ):
     width, edges = tails_ref.shape
     slots = fetched_ref.shape[0]
     half, head_rows, _ = near_ref.shape
-    chips, _, lanes = own_out.shape
-    cores = width // lanes
+    cores, chips, _, lanes = packed.shape
     share = sums.shape[0] // chips
     quals = ref_ids.shape[0]
     cap = slots // (cores * chips)
 
     loads = []
-    for index, (source, target) in enumerate(
-        (
-            (rel_hbm, rel_ref),
-            (near_hbm, near_ref),
-            (far_hbm, far_ref),
-            (tails_hbm, tails_ref),
-            (neg_hbm, neg_ref),
-            (negt_hbm, negt_ref),
-        )
-    ):
-        loads.append(pltpu.make_async_copy(source, target, in_sems.at[index]))
-        loads[index].start()
+
+    def load(source, target):
+        loads.append(pltpu.make_async_copy(source, target, in_sems.at[len(loads)]))
+        loads[-1].start()
+        return loads[-1]
+
+    rel_loads = [load(rel_hbm.at[which], rel_ref.at[which]) for which in [*range(1, quals + 1), 0]]
+    head_loads = [load(near_hbm, near_ref), load(far_hbm, far_ref)]
+    tails_load = load(tails_hbm, tails_ref)
+    neg_load = load(neg_hbm, neg_ref)
+    negt_load = load(negt_hbm, negt_ref)
 
     fetched_t = flip(fetched_ref[...])
     proj_hi, proj_lo = pieces(proj_ref[...], 2)
     projt_hi, projt_lo = pieces(proj_ref[...].T, 2)
     rows = [nn(fetched_t, onehot(ref_ids[k : k + 1, :], 0, slots)) for k in range(quals)]
-    loads[0].wait()
+    for copy in rel_loads:
+        copy.wait()
     composed = rel_ref[1] * rows[0]
     for k in range(1, quals):
         composed = composed + rel_ref[k + 1] * rows[k]
     comp_hi, comp_lo = pieces(composed, 2)
     relation = rel_ref[0] + (nn(projt_hi, comp_hi) + (nn(projt_hi, comp_lo) + nn(projt_lo, comp_hi)))
-    loads[1].wait()
-    loads[2].wait()
+    for copy in head_loads:
+        copy.wait()
     offset = jnp.bitwise_xor(head_id[...] // head_rows, member_ref[0])
     head_slot = ((offset % 2) * half + offset // 2) * head_rows + head_id[...] % head_rows
     heads = jnp.zeros((width, edges), F32)
@@ -149,10 +151,10 @@
             heads = heads + nn(flip(table[owner]), onehot(head_slot, (first + owner) * head_rows, head_rows))
     query = (heads * relation).astype(BF)
     query_f = query.astype(F32)
-    loads[3].wait()
+    tails_load.wait()
     tails = tails_ref[...].astype(F32)
     positive = jnp.sum(query_f * tails, axis=0, keepdims=True)
-    loads[4].wait()
+    neg_load.wait()
     scores = nn(neg_ref[...], query)
     top = jnp.maximum(jnp.max(scores, axis=0, keepdims=True), positive)
     neg_exp = jnp.exp(scores - top)
@@ -163,21 +165,28 @@
     scale = live / total
     neg_round = (neg_exp * scale).astype(BF)
     coef = pos_exp * scale - live
-    loads[5].wait()
+    negt_load.wait()
     query_grad = coef * tails + nn(negt_ref[...], neg_round)
 
+    stores = []
+
+    def store(source, target):
+        stores.append(pltpu.make_async_copy(source, target, out_sems.at[len(stores)]))
+        stores[-1].start()
+
     head_terms = (query_grad * relation).astype(BF)
-    for first, out in ((half, far_out), (0, near_out)):
+    for first, part, out in ((half, far_ref, far_out), (0, near_ref, near_out)):
 
         def scatter(owner):
             hot = onehot(head_slot, (first + owner) * head_rows, head_rows)
-            out[owner] = nt(hot, head_terms).astype(BF)
+            part[owner] = nt(hot, head_terms).astype(BF)
 
         if half > UNROLL:
             pl.loop(0, half)(scatter)
         else:
             for owner in range(half):
                 scatter(owner)
+        store(part, out)
 
     relation_grad = query_grad * heads
     rg_hi, rg_lo = pieces(relation_grad, 2)
@@ -197,18 +206,15 @@
         mine = pairs[:, core].reshape(chips, cap, width)
         parts = [sums[:, core * lanes : (core + 1) * lanes].reshape(chips, share, lanes)]
         parts += [mine[:, :, start : start + lanes] for start in range(0, width, lanes)]
-        both = jnp.concatenate(parts, axis=1).astype(BF)
-
-        @pl.when(core_ref[0] == core)
-        def _():
-            own_out[...] = both
-
-        @pl.when(core_ref[0] != core)
-        def _():
-            other_out[...] = both
-
-    terms_out[:edges, :] = flip((coef * query_f).astype(BF))
-    terms_out[edges:, :] = nt(neg_round, query).astype(BF)
+        packed[core] = jnp.concatenate(parts, axis=1).astype(BF)
+    store(packed.at[core_ref[0]], own_out)
+    store(packed.at[1 - core_ref[0]], other_out)
+
+    terms[:edges, :] = flip((coef * query_f).astype(BF))
+    terms[edges:, :] = nt(neg_round, query).astype(BF)
+    store(terms, terms_out)
+    for copy in stores:
+        copy.wait()
 
 
 def combine_kernel(own_ref, got_ref, out_ref):
@@ -363,7 +369,7 @@
         [((width, edges), BF), ((width, negs), BF), ((negs, width), BF)],
         [pltpu.VMEM((width, tail_rows), BF)],
         7,
-        32,
+        58,
         tail_table,
         tail_row,
         neg_row,
@@ -392,10 +398,13 @@
             pltpu.VMEM((negs, width), BF),
             pltpu.VMEM((width, negs), BF),
             pltpu.VMEM((chips * share, width), F32),
-            pltpu.SemaphoreType.DMA((6,)),
+            pltpu.VMEM((cores, chips, sent, lanes), BF),
+            pltpu.VMEM((edges + negs, width), BF),
+            pltpu.SemaphoreType.DMA((quals + 6,)),
+            pltpu.SemaphoreType.DMA((5,)),
         ],
         14,
-        58 if half > UNROLL else 44,
+        58,
         edge_count,
         core,
         member,
@@ -413,6 +422,7 @@
         proj,
         smem=(0, 1, 2),
         away=range(3, 9),
+        out_specs=[pl.BlockSpec(memory_space=pl.ANY)] * 5,
     )
     other_got = swap(other_part, "core")
     far_got = swap(far_part, "near")
@@ -445,9 +455,8 @@
 
     tail_grad = tail_rows_of(0, steps // 2)
     far_got, tail_grad = lax.optimization_barrier((far_got, tail_grad))
-    near_sum = near_part.astype(F32) + far_got.astype(F32)
-    near_send = near_sum.astype(BF)
-    line_got = [swap(near_send[offset], "line", offset) for offset in range(1, half)]
+    near_sum = [near_part[offset].astype(F32) + far_got[offset].astype(F32) for offset in range(half)]
+    line_got = [swap(near_sum[offset].astype(BF), "line", offset) for offset in range(1, half)]
     (sums_own,) = call(add_kernel, [((chips, share, lanes), BF)], [], 1, 16, chip_got)
     sums_own = exchange(sums_own, CHIPS).reshape(chips * share, lanes)
     tail_grad = tail_rows_of(steps // 2, steps - steps // 2, tail_grad)

time: 98.6 us -> 92.7 us (0.940)
  local copies, waits for them, and re-layouts: 14.4 us -> 5.26 us
  Pallas kernels: 34.9 us -> 38.8 us
  waiting for transfers between devices: 5.5 us -> 8.93 us
  other arithmetic: 4.04 us -> 1.64 us
  starting transfers between devices: 37.4 us -> 36.1 us
    unnamed x42 -> x20, local copies, waits for them, and re-layouts: 11 us -> 1.83 us
    pallas_call x9, Pallas kernels: 34.9 us -> 38.8 us  [call(): pl.pallas_call(kernel, out_shape=shapes, grid=grid, in_specs=[pl.BlockSpe...]
    ppermute x10, waiting for transfers between devices: 0.54 us -> 2.93 us  [swap(): lax.ppermute(values, axis, [(i, i ^ offset) for i in range(lax.axis_size(...]
    convert_element_type x1, other arithmetic: 2.25 us -> 0.77 us  [body(): near_sum[offset].astype(BF)]
    all_to_all x4, waiting for transfers between devices: 4.95 us -> 6 us  [exchange(): return lax.all_to_all(values, axes, split_axis=0, concat_axis=0, tiled=True)]
  transfers between devices with their start and end apart: 14 -> 14, of which waited for: 3 -> 7; matrix products, arithmetic and copies ran while one was open for 6% -> 4% of each run, Pallas kernels for 20% -> 24%
where the time goes in v7:
time: 92.7 us; the launch traced here: 92.2 us
  Pallas kernels  38.8 us (42%)
  starting transfers between devices  36.1 us (39%)
  waiting for transfers between devices  8.93 us (10%)
  local copies, waits for them, and re-layouts  5.26 us (6%)
  other arithmetic  1.64 us (2%)
  between operations  1.48 us (2%)
    pallas_call x9, Pallas kernels, call(): pl.pallas_call(kernel, out_shape=shapes, grid=grid, in_specs=[pl.BlockSpe...  38.8 us
    all_to_all x4, starting transfers between devices, exchange(): return lax.all_to_all(values, axes, split_axis=0, concat_axis=0, tiled=True)  23.6 us
    ppermute x10, starting transfers between devices, swap(): lax.ppermute(values, axis, [(i, i ^ offset) for i in range(lax.axis_size(...  12.5 us
    all_to_all x4, waiting for transfers between devices, exchange(): return lax.all_to_all(values, axes, split_axis=0, concat_axis=0, tiled=True)  6 us
    ppermute x10, waiting for transfers between devices, swap(): lax.ppermute(values, axis, [(i, i ^ offset) for i in range(lax.axis_size(...  2.93 us
  transfers between devices with their start and end apart: 14, of which 7 were waited for; matrix products, arithmetic and copies ran while one was open for 4% of the time, Pallas kernels for 24%

profile of v7, /device:TPU:0, one launch (start us, length us, event | category | flops | bytes accessed | tf_op | source)
XLA Modules:
  0.0 92.2 jit_solution(257308077038843969)
XLA Ops:
  0.6 0.0 copy-start
  0.6 5.1 %collective-permute-start.2 = (bf16[256,256]{1,0:T(8,128)(2,1)}, bf16[256,256]{1,0:T(8,128)(2,1)S(1)}, u32[]{:S(2)}, u32[]{:S(2)}) collective-permute-start(bf16[256,256]{1,0:T(8,128)(2,1)} %param.13), channel_id=1, source_target_pairs={{0,6},{2,4},{4,2},{6,0},{1,7},{3,5},{5,3},{7,1},{8,14},{10,12},{12... | collective-permute-start | bytes 393224 | tf_op jit(solution)/shard_map/ppermute | solution.py:305
  5.8 0.6 collective-permute-start
  6.4 1.4 %all_to_all.17 = s32[32,1,8]{2,0,1:T(8,128)} reshape(s32[256]{0:T(256)} %param.23) | data formatting | bytes 2048 | tf_op jit(solution)/shard_map/all_to_all | solution.py:301
  7.8 6.0 %all-to-all-start = ((s32[32,1,8]{2,1,0:T(1,128)}), s32[32,1,8]{2,1,0:T(1,128)S(1)}, u32[]{:S(2)}, u32[]{:S(2)}) async-start(s32[32,1,8]{2,1,0:T(1,128)} %bitcast.2), calls=%async_computation | async-start | bytes 32768 | tf_op jit(solution)/shard_map/all_to_all | solution.py:301
  13.8 0.0 copy-start.8
  13.8 5.1 %shard_map.164.refs_3_ = f32[5,256,1024]{2,1,0:T(8,128)} custom-call(f32[512,256]{1,0:T(8,128)} %rel_ref.1, s32[1,1024]{1,0:T(1,128)} %bitcast.49, s32[4,1024]{1,0:T(4,128)} %bitcast.46), custom_call_target="tpu_custom_call" | custom-call | flops 5368709120 | bytes 1048576 | tf_op jit(solution)/shard_map/pallas_call | solution.py:287
  18.9 0.0 collective-permute-done.1
  18.9 0.0 collective-permute-done
  19.0 0.1 pad_maximum_fusion.refs_4_
  19.0 0.0 copy-start.6
  19.0 1.8 %all-to-all-done = s32[32,1,8]{2,1,0:T(1,128)S(1)} async-done(((s32[32,1,8]{2,1,0:T(1,128)}), s32[32,1,8]{2,1,0:T(1,128)S(1)}, u32[]{:S(2)}, u32[]{:S(2)}) %all-to-all-start) | async-done | bytes 1056 | tf_op jit(solution)/shard_map/all_to_all | solution.py:301
  20.8 0.6 collective-permute-start.3
  21.4 0.1 reshape.55
  21.6 1.8 %gather_fusion = bf16[256,256]{1,0:T(8,128)(2,1)} fusion(bf16[1024,256]{1,0:T(8,128)(2,1)S(1)} %copy-done, s32[1024]{0:T(1024)S(1)} %pad_clamp_fusion), kind=kCustom, calls=%fused_computation | custom fusion | bytes 263168 | tf_op jit(solution)/shard_map/gather | solution.py:365
  23.4 4.3 %all-to-all-start.1 = ((bf16[32,8,256]{2,1,0:T(8,128)(2,1)}), bf16[32,8,256]{2,1,0:T(8,128)(2,1)S(1)}, u32[]{:S(2)}, u32[]{:S(2)}) async-start(bf16[32,8,256]{2,1,0:T(8,128)(2,1)} %bitcast.12), calls=%async_computation.1 | async-start | bytes 262144 | tf_op jit(solution)/shard_map/all_to_all | solution.py:301
  27.6 7.3 %shard_map.165 = (bf16[256,1024]{1,0:T(8,128)(2,1)}, bf16[256,1024]{1,0:T(8,128)(2,1)}, bf16[1024,256]{1,0:T(8,128)(2,1)}) custom-call(bf16[4096,256]{1,0:T(8,128)(2,1)} %tail_ref.1, s32[1,1024]{1,0:T(1,128)} %bitcast.32, s32[1,1024]{1,0:T(1,128)} %bitcast.35), custom_call_target="tpu_custom_call" | custom-call | flops 7516192768 | bytes 1048576 | tf_op jit(solution)/shard_map/pallas_call | solution.py:287
  35.6 0.3 all-to-all-done.1
  35.9 0.0 collective-permute-done.3.refs_5_
  35.9 0.6 copy-done.7
  36.5 0.2 copy-done.9
  36.7 15.6 %shard_map.166 = (bf16[4,256,256]{2,1,0:T(8,128)(2,1)}, bf16[4,256,256]{2,1,0:T(8,128)(2,1)}, bf16[16,64,128]{2,1,0:T(8,128)(2,1)}, bf16[16,64,128]{2,1,0:T(8,128)(2,1)}, bf16[2048,256]{1,0:T(8,128)(2,1)}) custom-call(s32[1]{0:T(128)S(6)} %copy.23.refs_0_, s32[1]{0:T(128)} %bitcast.refs_1_.core_ref, s32[1]{0:T(128)} %bitcast.1.refs_2_, ...), custom_call_target="tpu_custom_call" | custom-call | flops 15032385536 | bytes 1048576 | tf_op jit(solution)/shard_map/pallas_call | solution.py:287
  52.3 0.0 copy-start.1
  52.3 0.0 copy-start.2
  52.3 0.0 copy-start.3
  52.3 0.1 collective-permute-start.5
  52.4 1.6 %collective-permute-start.4 = (bf16[4,256,256]{2,1,0:T(8,128)(2,1)}, bf16[4,256,256]{2,1,0:T(8,128)(2,1)S(1)}, u32[]{:S(2)}, u32[]{:S(2)}) collective-permute-start(bf16[4,256,256]{2,1,0:T(8,128)(2,1)} %get-tuple-element.32), channel_id=1, source_target_pairs={{0,1},{1,0},{2,3},{3,2},{4,5},{5,4},{6,7},{7,6},{8,9},{9,8},{10,11... | collective-permute-start | bytes 1572872 | tf_op jit(solution)/shard_map/ppermute | solution.py:305
  54.0 0.1 collective-permute-done.5.got_ref
  54.2 0.9 %copy-done.4 = bf16[16,64,128]{2,1,0:T(8,128)(2,1)S(1)} copy-done((bf16[16,64,128]{2,1,0:T(8,128)(2,1)S(1)}, bf16[16,64,128]{2,1,0:T(8,128)(2,1)}, u32[]{:S(2)}) %copy-start.4) | copy-done | bytes 262168
  55.1 0.8 shard_map.168
  55.9 6.5 %all-to-all-start.2 = ((bf16[16,80,128]{2,1,0:T(8,128)(2,1)}), bf16[16,80,128]{2,1,0:T(8,128)(2,1)S(1)}, u32[]{:S(2)}, u32[]{:S(2)}) async-start(bf16[16,80,128]{2,1,0:T(8,128)(2,1)} %shard_map.168), calls=%async_computation.2 | async-start | bytes 655360 | tf_op jit(solution)/shard_map/all_to_all | solution.py:301
  62.4 0.1 reshape.51
  62.5 0.1 reshape.52.asked
  62.6 3.5 %shard_map.167.refs_3_ = f32[4096,256]{1,0:T(8,128)} custom-call(s32[1,1024]{1,0:T(1,128)S(1)} %bitcast.33, s32[1,1024]{1,0:T(1,128)S(1)} %bitcast.36, bf16[2048,256]{1,0:T(8,128)(2,1)S(1)} %copy-done.3), custom_call_target="tpu_custom_call" | custom-call | flops 3221225472 | bytes 1048576 | tf_op jit(solution)/shard_map/pallas_call | solution.py:287
  66.1 2.1 %collective-permute-done.4 = bf16[4,256,256]{2,1,0:T(8,128)(2,1)S(1)} collective-permute-done((bf16[4,256,256]{2,1,0:T(8,128)(2,1)}, bf16[4,256,256]{2,1,0:T(8,128)(2,1)S(1)}, u32[]{:S(2)}, u32[]{:S(2)}) %collective-permute-start.4) | collective-permute-done | bytes 524320 | tf_op jit(solution)/shard_map/ppermute | solution.py:305
  68.3 0.8 fusion.4
  69.0 1.0 %collective-permute-start.6 = (bf16[256,256]{1,0:T(8,128)(2,1)}, bf16[256,256]{1,0:T(8,128)(2,1)S(1)}, u32[]{:S(2)}, u32[]{:S(2)}) collective-permute-start(bf16[256,256]{1,0:T(8,128)(2,1)} %get-tuple-element.47), channel_id=1, source_target_pairs={{0,2},{2,0},{4,6},{6,4},{1,3},{3,1},{5,7},{7,5},{8,10},{10,8},{12,... | collective-permute-start | bytes 393224 | tf_op jit(solution)/shard_map/ppermute | solution.py:305
  70.0 3.3 %collective-permute-start.7 = (bf16[256,256]{1,0:T(8,128)(2,1)}, bf16[256,256]{1,0:T(8,128)(2,1)S(1)}, u32[]{:S(2)}, u32[]{:S(2)}) collective-permute-start(bf16[256,256]{1,0:T(8,128)(2,1)} %get-tuple-element.46), channel_id=1, source_target_pairs={{0,4},{2,6},{4,0},{6,2},{1,5},{3,7},{5,1},{7,3},{8,12},{10,14},{12... | collective-permute-start | bytes 393224 | tf_op jit(solution)/shard_map/ppermute | solution.py:305
  73.4 0.1 collective-permute-start.8
  73.4 0.7 all-to-all-done.2.got_ref
  74.1 0.7 shard_map.169
  74.8 6.8 %all-to-all-start.3 = ((bf16[16,48,128]{2,1,0:T(8,128)(2,1)}), bf16[16,48,128]{2,1,0:T(8,128)(2,1)S(1)}, u32[]{:S(2)}, u32[]{:S(2)}) async-start(bf16[16,48,128]{2,1,0:T(8,128)(2,1)} %shard_map.169), calls=%async_computation.3 | async-start | bytes 393216 | tf_op jit(solution)/shard_map/all_to_all | solution.py:301
  81.7 3.5 %shard_map.170 = f32[4096,256]{1,0:T(8,128)} custom-call(s32[1,1024]{1,0:T(1,128)S(1)} %bitcast.34, s32[1,1024]{1,0:T(1,128)S(1)} %bitcast.37, bf16[2048,256]{1,0:T(8,128)(2,1)S(1)} %copy-done.3, f32[4096,256]{1,0:T(8,128)} %shard_map.167.refs_3_), custom_call_target="tpu_custom_call", output_to_operand_aliasing={{}: (3, {})} | custom-call | flops 3221225472 | bytes 1048576 | tf_op jit(solution)/shard_map/pallas_call | solution.py:287
  85.2 1.4 %shard_map.171 = f32[1024,256]{1,0:T(8,128)} custom-call(s32[1]{0:T(128)} %bitcast.refs_1_.core_ref, bf16[16,80,128]{2,1,0:T(8,128)(2,1)S(1)} %all-to-all-done.2.got_ref, s32[2,128]{1,0:T(2,128)S(1)} %reshape.52.asked), custom_call_target="tpu_custom_call" | custom-call | flops 2147483648 | bytes 1048576 | tf_op jit(solution)/shard_map/pallas_call | solution.py:287
  86.6 3.2 %all-to-all-done.3 = bf16[16,48,128]{2,1,0:T(8,128)(2,1)S(1)} async-done(((bf16[16,48,128]{2,1,0:T(8,128)(2,1)}), bf16[16,48,128]{2,1,0:T(8,128)(2,1)S(1)}, u32[]{:S(2)}, u32[]{:S(2)}) %all-to-all-start.3) | async-done | bytes 196640 | tf_op jit(solution)/shard_map/all_to_all | solution.py:301
  89.8 0.8 fusion.1
  90.6 0.7 collective-permute-done.9.got_ref
  91.2 0.9 %shard_map.172 = (f32[512,256]{1,0:T(8,128)}, f32[256,256]{1,0:T(8,128)}) custom-call(s32[1]{0:T(128)} %bitcast.refs_1_.core_ref, bf16[768,128]{1,0:T(8,128)(2,1)S(1)} %bitcast.31, bf16[768,128]{1,0:T(8,128)(2,1)S(1)} %collective-permute-done.9.got_ref), custom_call_target="tpu_custom_call" | custom-call | flops 1073741824 | bytes 1048576 | tf_op jit(solution)/shard_map/pallas_call | solution.py:287
  (20 shorter events, 0.1 us)
Async XLA Ops:
  0.6 20.9 %copy-start = (bf16[1024,256]{1,0:T(8,128)(2,1)S(1)}, bf16[1024,256]{1,0:T(8,128)(2,1)}, u32[]{:S(2)}) copy-start(bf16[1024,256]{1,0:T(8,128)(2,1)} %param.15) | copy-start | bytes 1572868
  0.6 18.3 %collective-permute-start.2 = (bf16[256,256]{1,0:T(8,128)(2,1)}, bf16[256,256]{1,0:T(8,128)(2,1)S(1)}, u32[]{:S(2)}, u32[]{:S(2)}) collective-permute-start(bf16[256,256]{1,0:T(8,128)(2,1)} %param.13), channel_id=1, source_target_pairs={{0,6},{2,4},{4,2},{6,0},{1,7},{3,5},{5,3},{7,1},{8,14},{10,12},{12... | collective-permute-start | bytes 393224 | tf_op jit(solution)/shard_map/ppermute | solution.py:305
  5.8 13.2 %collective-permute-start.1 = (bf16[256,256]{1,0:T(8,128)(2,1)}, bf16[256,256]{1,0:T(8,128)(2,1)S(1)}, u32[]{:S(2)}, u32[]{:S(2)}) collective-permute-start(bf16[256,256]{1,0:T(8,128)(2,1)} %param.13), channel_id=1, source_target_pairs={{0,4},{2,6},{4,0},{6,2},{1,5},{3,7},{5,1},{7,3},{8,12},{10,14},{12... | collective-permute-start | bytes 393224 | tf_op jit(solution)/shard_map/ppermute | solution.py:305
  5.8 13.2 %collective-permute-start = (bf16[256,256]{1,0:T(8,128)(2,1)}, bf16[256,256]{1,0:T(8,128)(2,1)S(1)}, u32[]{:S(2)}, u32[]{:S(2)}) collective-permute-start(bf16[256,256]{1,0:T(8,128)(2,1)} %param.13), channel_id=1, source_target_pairs={{0,2},{2,0},{4,6},{6,4},{1,3},{3,1},{5,7},{7,5},{8,10},{10,8},{12,... | collective-permute-start | bytes 393224 | tf_op jit(solution)/shard_map/ppermute | solution.py:305
  7.8 13.0 %all-to-all-start = ((s32[32,1,8]{2,1,0:T(1,128)}), s32[32,1,8]{2,1,0:T(1,128)S(1)}, u32[]{:S(2)}, u32[]{:S(2)}) async-start(s32[32,1,8]{2,1,0:T(1,128)} %bitcast.2), calls=%async_computation | async-start | bytes 32768 | tf_op jit(solution)/shard_map/all_to_all | solution.py:301
  13.8 5.2 %copy-start.8 = (bf16[256,256]{1,0:T(8,128)(2,1)S(1)}, bf16[256,256]{1,0:T(8,128)(2,1)}, u32[]{:S(2)}) copy-start(bf16[256,256]{1,0:T(8,128)(2,1)} %param.13) | copy-start | bytes 393220
  19.0 15.9 %copy-start.6 = (bf16[4,256,256]{2,1,0:T(8,128)(2,1)}, bf16[4,256,256]{2,1,0:T(8,128)(2,1)S(1)}, u32[]{:S(2)}) copy-start(bf16[4,256,256]{2,1,0:T(8,128)(2,1)S(1)} %pad_maximum_fusion.refs_4_) | copy-start | bytes 1572868
  20.8 15.1 %collective-permute-start.3 = (bf16[4,256,256]{2,1,0:T(8,128)(2,1)S(1)}, bf16[4,256,256]{2,1,0:T(8,128)(2,1)S(1)}, u32[]{:S(2)}, u32[]{:S(2)}) collective-permute-start(bf16[4,256,256]{2,1,0:T(8,128)(2,1)S(1)} %pad_maximum_fusion.refs_4_), channel_id=1, source_target_pairs={{0,1},{1,0},{2,3},{3,2},{4,5},{5,4},{6,7},{7,6},{8,9},{9,8},{10,11... | collective-permute-start | bytes 1572872 | tf_op jit(solution)/shard_map/ppermute | solution.py:305
  23.4 12.5 %all-to-all-start.1 = ((bf16[32,8,256]{2,1,0:T(8,128)(2,1)}), bf16[32,8,256]{2,1,0:T(8,128)(2,1)S(1)}, u32[]{:S(2)}, u32[]{:S(2)}) async-start(bf16[32,8,256]{2,1,0:T(8,128)(2,1)} %bitcast.12), calls=%async_computation.1 | async-start | bytes 262144 | tf_op jit(solution)/shard_map/all_to_all | solution.py:301
  35.9 0.7 copy-start.7
  35.9 0.8 copy-start.9
  52.3 10.3 %copy-start.1 = (s32[1024]{0:T(1024)S(1)}, s32[1024]{0:T(1024)}, u32[]{:S(2)}) copy-start(s32[1024]{0:T(1024)} %param.19) | copy-start | bytes 12292
  52.3 10.3 %copy-start.2 = (s32[1024]{0:T(1024)S(1)}, s32[1024]{0:T(1024)}, u32[]{:S(2)}) copy-start(s32[1024]{0:T(1024)} %param.24) | copy-start | bytes 12292
  52.3 10.3 %copy-start.3 = (bf16[2048,256]{1,0:T(8,128)(2,1)S(1)}, bf16[2048,256]{1,0:T(8,128)(2,1)}, u32[]{:S(2)}) copy-start(bf16[2048,256]{1,0:T(8,128)(2,1)} %get-tuple-element.33.refs_2_) | copy-start | bytes 3145732
  52.3 1.8 %collective-permute-start.5 = (bf16[16,64,128]{2,1,0:T(8,128)(2,1)}, bf16[16,64,128]{2,1,0:T(8,128)(2,1)S(1)}, u32[]{:S(2)}, u32[]{:S(2)}) collective-permute-start(bf16[16,64,128]{2,1,0:T(8,128)(2,1)} %get-tuple-element.36), channel_id=1, source_target_pairs={{0,8},{8,0},{1,9},{9,1},{2,10},{10,2},{3,11},{11,3},{4,12},{12,4},... | collective-permute-start | bytes 786440 | tf_op jit(solution)/shard_map/ppermute | solution.py:305
  52.4 15.8 %collective-permute-start.4 = (bf16[4,256,256]{2,1,0:T(8,128)(2,1)}, bf16[4,256,256]{2,1,0:T(8,128)(2,1)S(1)}, u32[]{:S(2)}, u32[]{:S(2)}) collective-permute-start(bf16[4,256,256]{2,1,0:T(8,128)(2,1)} %get-tuple-element.32), channel_id=1, source_target_pairs={{0,1},{1,0},{2,3},{3,2},{4,5},{5,4},{6,7},{7,6},{8,9},{9,8},{10,11... | collective-permute-start | bytes 1572872 | tf_op jit(solution)/shard_map/ppermute | solution.py:305
  54.2 1.0 %copy-start.4 = (bf16[16,64,128]{2,1,0:T(8,128)(2,1)S(1)}, bf16[16,64,128]{2,1,0:T(8,128)(2,1)}, u32[]{:S(2)}) copy-start(bf16[16,64,128]{2,1,0:T(8,128)(2,1)} %get-tuple-element.35.own_ref) | copy-start | bytes 786436
  55.9 18.2 %all-to-all-start.2 = ((bf16[16,80,128]{2,1,0:T(8,128)(2,1)}), bf16[16,80,128]{2,1,0:T(8,128)(2,1)S(1)}, u32[]{:S(2)}, u32[]{:S(2)}) async-start(bf16[16,80,128]{2,1,0:T(8,128)(2,1)} %shard_map.168), calls=%async_computation.2 | async-start | bytes 655360 | tf_op jit(solution)/shard_map/all_to_all | solution.py:301
  62.6 5.6 %copy-start.5 = (bf16[4,256,256]{2,1,0:T(8,128)(2,1)S(1)}, bf16[4,256,256]{2,1,0:T(8,128)(2,1)}, u32[]{:S(2)}) copy-start(bf16[4,256,256]{2,1,0:T(8,128)(2,1)} %get-tuple-element.31) | copy-start | bytes 1572868
  69.0 17.5 %collective-permute-start.6 = (bf16[256,256]{1,0:T(8,128)(2,1)}, bf16[256,256]{1,0:T(8,128)(2,1)S(1)}, u32[]{:S(2)}, u32[]{:S(2)}) collective-permute-start(bf16[256,256]{1,0:T(8,128)(2,1)} %get-tuple-element.47), channel_id=1, source_target_pairs={{0,2},{2,0},{4,6},{6,4},{1,3},{3,1},{5,7},{7,5},{8,10},{10,8},{12,... | collective-permute-start | bytes 393224 | tf_op jit(solution)/shard_map/ppermute | solution.py:305
  70.0 16.5 %collective-permute-start.7 = (bf16[256,256]{1,0:T(8,128)(2,1)}, bf16[256,256]{1,0:T(8,128)(2,1)S(1)}, u32[]{:S(2)}, u32[]{:S(2)}) collective-permute-start(bf16[256,256]{1,0:T(8,128)(2,1)} %get-tuple-element.46), channel_id=1, source_target_pairs={{0,4},{2,6},{4,0},{6,2},{1,5},{3,7},{5,1},{7,3},{8,12},{10,14},{12... | collective-permute-start | bytes 393224 | tf_op jit(solution)/shard_map/ppermute | solution.py:305
  73.4 13.2 %collective-permute-start.8 = (bf16[256,256]{1,0:T(8,128)(2,1)}, bf16[256,256]{1,0:T(8,128)(2,1)S(1)}, u32[]{:S(2)}, u32[]{:S(2)}) collective-permute-start(bf16[256,256]{1,0:T(8,128)(2,1)} %get-tuple-element.45), channel_id=1, source_target_pairs={{0,6},{2,4},{4,2},{6,0},{1,7},{3,5},{5,3},{7,1},{8,14},{10,12},{12... | collective-permute-start | bytes 393224 | tf_op jit(solution)/shard_map/ppermute | solution.py:305
  74.8 15.0 %all-to-all-start.3 = ((bf16[16,48,128]{2,1,0:T(8,128)(2,1)}), bf16[16,48,128]{2,1,0:T(8,128)(2,1)S(1)}, u32[]{:S(2)}, u32[]{:S(2)}) async-start(bf16[16,48,128]{2,1,0:T(8,128)(2,1)} %shard_map.169), calls=%async_computation.3 | async-start | bytes 393216 | tf_op jit(solution)/shard_map/all_to_all | solution.py:301
  89.8 1.4 %collective-permute-start.9 = (bf16[768,128]{1,0:T(8,128)(2,1)S(1)}, bf16[768,128]{1,0:T(8,128)(2,1)S(1)}, u32[]{:S(2)}, u32[]{:S(2)}) collective-permute-start(bf16[768,128]{1,0:T(8,128)(2,1)S(1)} %bitcast.30), channel_id=1, source_target_pairs={{0,8},{8,0},{1,9},{9,1},{2,10},{10,2},{3,11},{11,3},{4,12},{12,4},... | collective-permute-start | bytes 589832 | tf_op jit(solution)/shard_map/ppermute | solution.py:305

commit v8 on v7

--- a/solution.py
+++ b/solution.py
@@ -74,9 +74,19 @@
                 neg_out[at, :] = got.T.astype(BF)
 
 
+def loader(sems):
+    begun = []
+
+    def load(source, target):
+        begun.append(pltpu.make_async_copy(source, target, sems.at[len(begun)]))
+        begun[-1].start()
+        return begun[-1]
+
+    return load, begun
+
+
 def edge_kernel(
     count_ref,
-    core_ref,
     member_ref,
     rel_hbm,
     near_hbm,
@@ -86,14 +96,12 @@
     negt_hbm,
     fetched_ref,
     ref_ids,
-    rel_id,
-    qual_rel,
     head_id,
     proj_ref,
     far_out,
     near_out,
-    own_out,
-    other_out,
+    rg_out,
+    comp_out,
     terms_out,
     rel_ref,
     near_ref,
@@ -101,37 +109,26 @@
     tails_ref,
     neg_ref,
     negt_ref,
-    sums,
-    packed,
+    rg,
+    comp,
     terms,
     in_sems,
     out_sems,
-    *,
-    rel_rows,
 ):
     width, edges = tails_ref.shape
     slots = fetched_ref.shape[0]
     half, head_rows, _ = near_ref.shape
-    cores, chips, _, lanes = packed.shape
-    share = sums.shape[0] // chips
     quals = ref_ids.shape[0]
-    cap = slots // (cores * chips)
-
-    loads = []
-
-    def load(source, target):
-        loads.append(pltpu.make_async_copy(source, target, in_sems.at[len(loads)]))
-        loads[-1].start()
-        return loads[-1]
-
+
+    load, _ = loader(in_sems)
     rel_loads = [load(rel_hbm.at[which], rel_ref.at[which]) for which in [*range(1, quals + 1), 0]]
     head_loads = [load(near_hbm, near_ref), load(far_hbm, far_ref)]
     tails_load = load(tails_hbm, tails_ref)
     neg_load = load(neg_hbm, neg_ref)
     negt_load = load(negt_hbm, negt_ref)
+    store, stores = loader(out_sems)
 
     fetched_t = flip(fetched_ref[...])
-    proj_hi, proj_lo = pieces(proj_ref[...], 2)
     projt_hi, projt_lo = pieces(proj_ref[...].T, 2)
     rows = [nn(fetched_t, onehot(ref_ids[k : k + 1, :], 0, slots)) for k in range(quals)]
     for copy in rel_loads:
@@ -140,7 +137,13 @@
     for k in range(1, quals):
         composed = composed + rel_ref[k + 1] * rows[k]
     comp_hi, comp_lo = pieces(composed, 2)
-    relation = rel_ref[0] + (nn(projt_hi, comp_hi) + (nn(projt_hi, comp_lo) + nn(projt_lo, comp_hi)))
+    comp[0] = comp_hi
+    comp[1] = comp_lo
+    store(comp, comp_out)
+    relation = rel_ref[0] + nn(
+        jnp.concatenate([projt_hi, projt_hi, projt_lo], axis=1),
+        jnp.concatenate([comp_hi, comp_lo, comp_hi], axis=0),
+    )
     for copy in head_loads:
         copy.wait()
     offset = jnp.bitwise_xor(head_id[...] // head_rows, member_ref[0])
@@ -168,12 +171,6 @@
     negt_load.wait()
     query_grad = coef * tails + nn(negt_ref[...], neg_round)
 
-    stores = []
-
-    def store(source, target):
-        stores.append(pltpu.make_async_copy(source, target, out_sems.at[len(stores)]))
-        stores[-1].start()
-
     head_terms = (query_grad * relation).astype(BF)
     for first, part, out in ((half, far_ref, far_out), (0, near_ref, near_out)):
 
@@ -187,18 +184,71 @@
             for owner in range(half):
                 scatter(owner)
         store(part, out)
-
-    relation_grad = query_grad * heads
-    rg_hi, rg_lo = pieces(relation_grad, 2)
-    comp_grad = nn(proj_hi, rg_hi) + (nn(proj_hi, rg_lo) + nn(proj_lo, rg_hi))
-    rel_sum = nt(onehot(rel_id[...], 0, rel_rows), rg_hi)
+    rg_hi, rg_lo = pieces(query_grad * heads, 2)
+    rg[0] = rg_hi
+    rg[1] = rg_lo
+    store(rg, rg_out)
+    terms[:edges, :] = flip((coef * query_f).astype(BF))
+    terms[edges:, :] = nt(neg_round, query).astype(BF)
+    store(terms, terms_out)
+    for copy in stores:
+        copy.wait()
+
+
+def relation_kernel(
+    core_ref,
+    rel_hbm,
+    rg_hbm,
+    comp_hbm,
+    fetched_ref,
+    ref_ids,
+    rel_id,
+    qual_rel,
+    proj_ref,
+    own_out,
+    other_out,
+    rel_ref,
+    rg,
+    comp,
+    sums,
+    packed,
+    in_sems,
+    out_sems,
+    *,
+    rel_rows,
+):
+    slots, width = fetched_ref.shape
+    cores, chips, _, lanes = packed.shape
+    share = sums.shape[0] // chips
+    quals = ref_ids.shape[0]
+    cap = slots // (cores * chips)
+    load, _ = loader(in_sems)
+    rg_load = load(rg_hbm, rg)
+    rel_loads = [load(rel_hbm.at[which + 1], rel_ref.at[which]) for which in range(quals)]
+    comp_load = load(comp_hbm, comp)
+    store, stores = loader(out_sems)
+
+    fetched_t = flip(fetched_ref[...])
+    proj_hi, proj_lo = pieces(proj_ref[...], 2)
+    ref_hots = [onehot(ref_ids[k : k + 1, :], 0, slots) for k in range(quals)]
+    rows = [nn(fetched_t, hot) for hot in ref_hots]
+    rg_load.wait()
+    comp_grad = nn(
+        jnp.concatenate([proj_hi, proj_hi, proj_lo], axis=1), jnp.concatenate([rg[0], rg[1], rg[0]], axis=0)
+    )
+    rel_sum = nt(onehot(rel_id[...], 0, rel_rows), rg[0])
+    for k in range(quals):
+        rel_sum = rel_sum + nt(onehot(qual_rel[k : k + 1, :], 0, rel_rows), (comp_grad * rows[k]).astype(BF))
+    sums[:rel_rows, :] = rel_sum
+    for copy in rel_loads:
+        copy.wait()
+    comp_load.wait()
     fetched_sum = jnp.zeros((slots, width), F32)
     for k in range(quals):
-        hot = onehot(ref_ids[k : k + 1, :], 0, slots)
-        rel_sum = rel_sum + nt(onehot(qual_rel[k : k + 1, :], 0, rel_rows), (comp_grad * rows[k]).astype(BF))
-        fetched_sum = fetched_sum + nt(hot, (comp_grad * rel_ref[k + 1]).astype(BF))
-    sums[:rel_rows, :] = rel_sum
-    sums[rel_rows : rel_rows + width, :] = nt(comp_hi, rg_hi) + (nt(comp_hi, rg_lo) + nt(comp_lo, rg_hi))
+        fetched_sum = fetched_sum + nt(ref_hots[k], (comp_grad * rel_ref[k]).astype(BF))
+    sums[rel_rows : rel_rows + width, :] = nt(
+        jnp.concatenate([comp[0], comp[0], comp[1]], axis=1), jnp.concatenate([rg[0], rg[1], rg[0]], axis=1)
+    )
     if sums.shape[0] > rel_rows + width:
         sums[rel_rows + width :, :] = jnp.zeros((sums.shape[0] - rel_rows - width, width), F32)
     pairs = fetched_sum.reshape(-1, cores, chips // PAIRS, cap, width)
@@ -207,12 +257,8 @@
         parts = [sums[:, core * lanes : (core + 1) * lanes].reshape(chips, share, lanes)]
         parts += [mine[:, :, start : start + lanes] for start in range(0, width, lanes)]
         packed[core] = jnp.concatenate(parts, axis=1).astype(BF)
+    store(packed.at[1 - core_ref[0]], other_out)
     store(packed.at[core_ref[0]], own_out)
-    store(packed.at[1 - core_ref[0]], other_out)
-
-    terms[:edges, :] = flip((coef * query_f).astype(BF))
-    terms[edges:, :] = nt(neg_round, query).astype(BF)
-    store(terms, terms_out)
     for copy in stores:
         copy.wait()
 
@@ -378,16 +424,17 @@
     passed = cap * cores
     sent = share + passed
 
-    def edge(*refs):
-        edge_kernel(*refs, rel_rows=rel_rows)
-
-    far_part, near_part, own_part, other_part, terms = call(
-        edge,
+    def relations(*refs):
+        relation_kernel(*refs, rel_rows=rel_rows)
+
+    anywhere = pl.BlockSpec(memory_space=pl.ANY)
+    far_part, near_part, rg, comp, terms = call(
+        edge_kernel,
         [
             ((half, head_rows, width), BF),
             ((half, head_rows, width), BF),
-            ((chips, sent, lanes), BF),
-            ((chips, sent, lanes), BF),
+            ((2, width, edges), BF),
+            ((2, width, edges), BF),
             ((edges + negs, width), BF),
         ],
         [
@@ -397,16 +444,15 @@
             pltpu.VMEM((width, edges), BF),
             pltpu.VMEM((negs, width), BF),
             pltpu.VMEM((width, negs), BF),
-            pltpu.VMEM((chips * share, width), F32),
-            pltpu.VMEM((cores, chips, sent, lanes), BF),
+            pltpu.VMEM((2, width, edges), BF),
+            pltpu.VMEM((2, width, edges), BF),
             pltpu.VMEM((edges + negs, width), BF),
             pltpu.SemaphoreType.DMA((quals + 6,)),
             pltpu.SemaphoreType.DMA((5,)),
         ],
-        14,
+        11,
         58,
         edge_count,
-        core,
         member,
         rel_looked,
         head_near,
@@ -416,16 +462,41 @@
         neg_t,
         fetched,
         ref_row,
+        head_id[None, :],
+        proj,
+        smem=(0, 1),
+        away=range(2, 8),
+        out_specs=[anywhere] * 5,
+    )
+    far_got = swap(far_part, "near")
+    own_part, other_part = call(
+        relations,
+        [((chips, sent, lanes), BF), ((chips, sent, lanes), BF)],
+        [
+            pltpu.VMEM((quals, width, edges), F32),
+            pltpu.VMEM((2, width, edges), BF),
+            pltpu.VMEM((2, width, edges), BF),
+            pltpu.VMEM((chips * share, width), F32),
+            pltpu.VMEM((cores, chips, sent, lanes), BF),
+            pltpu.SemaphoreType.DMA((quals + 2,)),
+            pltpu.SemaphoreType.DMA((2,)),
+        ],
+        4,
+        58,
+        core,
+        rel_looked,
+        rg,
+        comp,
+        fetched,
+        ref_row,
         rel_row,
         qual_row,
-        head_id[None, :],
         proj,
-        smem=(0, 1, 2),
-        away=range(3, 9),
-        out_specs=[pl.BlockSpec(memory_space=pl.ANY)] * 5,
+        smem=(0,),
+        away=(1, 2, 3),
+        out_specs=[anywhere] * 2,
     )
     other_got = swap(other_part, "core")
-    far_got = swap(far_part, "near")
     (chip_part,) = call(combine_kernel, [((chips, sent + passed, lanes), BF)], [], 1, 16, own_part, other_got)
     chip_got = exchange(chip_part, CHIPS)
 

time: 92.7 us -> 104 us (1.12)
  waiting for transfers between devices: 8.93 us -> 15.2 us
  Pallas kernels: 38.8 us -> 44.6 us
  starting transfers between devices: 36.1 us -> 34.9 us
    ppermute x10, waiting for transfers between devices: 2.93 us -> 10.2 us  [swap(): lax.ppermute(values, axis, [(i, i ^ offset) for i in range(lax.axis_size(...]
    pallas_call x9 -> x10, Pallas kernels: 38.8 us -> 44.6 us  [call(): pl.pallas_call(kernel, out_shape=shapes, grid=grid, in_specs=[pl.BlockSpe...]
    all_to_all x4, starting transfers between devices: 23.6 us -> 21.5 us  [exchange(): return lax.all_to_all(values, axes, split_axis=0, concat_axis=0, tiled=True)]
  transfers between devices with their start and end apart: 14 -> 14, of which waited for: 7 -> 7; matrix products, arithmetic and copies ran while one was open for 4% -> 2% of each run, Pallas kernels for 24% -> 22%
where the time goes in v8:
time: 104 us; the launch traced here: 103 us
  Pallas kernels  44.6 us (43%)
  starting transfers between devices  34.9 us (34%)
  waiting for transfers between devices  15.2 us (15%)
  local copies, waits for them, and re-layouts  5.23 us (5%)
  other arithmetic  1.65 us (2%)
  between operations  1.48 us (1%)
    pallas_call x10, Pallas kernels, call(): pl.pallas_call(kernel, out_shape=shapes, grid=grid, in_specs=[pl.BlockSpe...  44.6 us
    all_to_all x4, starting transfers between devices, exchange(): return lax.all_to_all(values, axes, split_axis=0, concat_axis=0, tiled=True)  21.5 us
    ppermute x10, starting transfers between devices, swap(): lax.ppermute(values, axis, [(i, i ^ offset) for i in range(lax.axis_size(...  13.4 us
    ppermute x10, waiting for transfers between devices, swap(): lax.ppermute(values, axis, [(i, i ^ offset) for i in range(lax.axis_size(...  10.2 us
    all_to_all x4, waiting for transfers between devices, exchange(): return lax.all_to_all(values, axes, split_axis=0, concat_axis=0, tiled=True)  4.97 us
  transfers between devices with their start and end apart: 14, of which 7 were waited for; matrix products, arithmetic and copies ran while one was open for 2% of the time, Pallas kernels for 22%

profile of v8, /device:TPU:0, one launch (start us, length us, event | category | flops | bytes accessed | tf_op | source)
XLA Modules:
  0.0 103.0 jit_solution(4798365275590969523)
XLA Ops:
  0.6 0.0 copy-start
  0.6 3.1 %collective-permute-start = (bf16[256,256]{1,0:T(8,128)(2,1)}, bf16[256,256]{1,0:T(8,128)(2,1)S(1)}, u32[]{:S(2)}, u32[]{:S(2)}) collective-permute-start(bf16[256,256]{1,0:T(8,128)(2,1)} %param.13), channel_id=1, source_target_pairs={{0,2},{2,0},{4,6},{6,4},{1,3},{3,1},{5,7},{7,5},{8,10},{10,8},{12,... | collective-permute-start | bytes 393224 | tf_op jit(solution)/shard_map/ppermute | solution.py:351
  3.7 2.5 %collective-permute-start.2 = (bf16[256,256]{1,0:T(8,128)(2,1)}, bf16[256,256]{1,0:T(8,128)(2,1)S(1)}, u32[]{:S(2)}, u32[]{:S(2)}) collective-permute-start(bf16[256,256]{1,0:T(8,128)(2,1)} %param.13), channel_id=1, source_target_pairs={{0,6},{2,4},{4,2},{6,0},{1,7},{3,5},{5,3},{7,1},{8,14},{10,12},{12... | collective-permute-start | bytes 393224 | tf_op jit(solution)/shard_map/ppermute | solution.py:351
  6.2 0.1 collective-permute-start.1
  6.3 1.4 %all_to_all.17 = s32[32,1,8]{2,0,1:T(8,128)} reshape(s32[256]{0:T(256)} %param.23) | data formatting | bytes 2048 | tf_op jit(solution)/shard_map/all_to_all | solution.py:347
  7.7 5.2 %all-to-all-start = ((s32[32,1,8]{2,1,0:T(1,128)}), s32[32,1,8]{2,1,0:T(1,128)S(1)}, u32[]{:S(2)}, u32[]{:S(2)}) async-start(s32[32,1,8]{2,1,0:T(1,128)} %bitcast.1), calls=%async_computation | async-start | bytes 32768 | tf_op jit(solution)/shard_map/all_to_all | solution.py:347
  12.9 0.0 copy-start.8
  12.9 5.1 %shard_map.164.rel_hbm.refs_1_ = f32[5,256,1024]{2,1,0:T(8,128)} custom-call(f32[512,256]{1,0:T(8,128)} %rel_ref.1, s32[1,1024]{1,0:T(1,128)} %bitcast.52, s32[4,1024]{1,0:T(4,128)} %bitcast.47), custom_call_target="tpu_custom_call" | custom-call | flops 5368709120 | bytes 1048576 | tf_op jit(solution)/shard_map/pallas_call | solution.py:333
  18.0 0.0 collective-permute-done
  18.0 0.4 collective-permute-done.1
  18.5 0.1 pad_maximum_fusion.near_hbm
  18.5 0.0 copy-start.6
  18.6 1.8 %all-to-all-done = s32[32,1,8]{2,1,0:T(1,128)S(1)} async-done(((s32[32,1,8]{2,1,0:T(1,128)}), s32[32,1,8]{2,1,0:T(1,128)S(1)}, u32[]{:S(2)}, u32[]{:S(2)}) %all-to-all-start) | async-done | bytes 1056 | tf_op jit(solution)/shard_map/all_to_all | solution.py:347
  20.3 0.1 reshape.55
  20.5 1.8 %gather_fusion = bf16[256,256]{1,0:T(8,128)(2,1)} fusion(bf16[1024,256]{1,0:T(8,128)(2,1)S(1)} %copy-done, s32[1024]{0:T(1024)S(1)} %pad_clamp_fusion), kind=kCustom, calls=%fused_computation | custom fusion | bytes 263168 | tf_op jit(solution)/shard_map/gather | solution.py:411
  22.3 3.8 %all-to-all-start.1 = ((bf16[32,8,256]{2,1,0:T(8,128)(2,1)}), bf16[32,8,256]{2,1,0:T(8,128)(2,1)S(1)}, u32[]{:S(2)}, u32[]{:S(2)}) async-start(bf16[32,8,256]{2,1,0:T(8,128)(2,1)} %bitcast.11), calls=%async_computation.1 | async-start | bytes 262144 | tf_op jit(solution)/shard_map/all_to_all | solution.py:347
  26.1 1.8 %collective-permute-start.3 = (bf16[4,256,256]{2,1,0:T(8,128)(2,1)S(1)}, bf16[4,256,256]{2,1,0:T(8,128)(2,1)S(1)}, u32[]{:S(2)}, u32[]{:S(2)}) collective-permute-start(bf16[4,256,256]{2,1,0:T(8,128)(2,1)S(1)} %pad_maximum_fusion.near_hbm), channel_id=1, source_target_pairs={{0,1},{1,0},{2,3},{3,2},{4,5},{5,4},{6,7},{7,6},{8,9},{9,8},{10,11... | collective-permute-start | bytes 1572872 | tf_op jit(solution)/shard_map/ppermute | solution.py:351
  27.9 7.3 %shard_map.165 = (bf16[256,1024]{1,0:T(8,128)(2,1)}, bf16[256,1024]{1,0:T(8,128)(2,1)}, bf16[1024,256]{1,0:T(8,128)(2,1)}) custom-call(bf16[4096,256]{1,0:T(8,128)(2,1)} %tail_ref.1, s32[1,1024]{1,0:T(1,128)} %bitcast.32, s32[1,1024]{1,0:T(1,128)} %bitcast.35), custom_call_target="tpu_custom_call" | custom-call | flops 7516192768 | bytes 1048576 | tf_op jit(solution)/shard_map/pallas_call | solution.py:333
  35.9 5.6 %collective-permute-done.3.far_hbm = bf16[4,256,256]{2,1,0:T(8,128)(2,1)S(1)} collective-permute-done((bf16[4,256,256]{2,1,0:T(8,128)(2,1)S(1)}, bf16[4,256,256]{2,1,0:T(8,128)(2,1)S(1)}, u32[]{:S(2)}, u32[]{:S(2)}) %collective-permute-start.3) | collective-permute-done | bytes 524320 | tf_op jit(solution)/shard_map/ppermute | solution.py:351
  41.5 0.8 copy-done.9
  42.3 12.9 %shard_map.166 = (bf16[4,256,256]{2,1,0:T(8,128)(2,1)}, bf16[4,256,256]{2,1,0:T(8,128)(2,1)}, bf16[2,256,1024]{2,1,0:T(8,128)(2,1)}, bf16[2,256,1024]{2,1,0:T(8,128)(2,1)}, bf16[2048,256]{1,0:T(8,128)(2,1)}) custom-call(s32[1]{0:T(128)S(6)} %copy.23.count_ref, s32[1]{0:T(128)} %bitcast.member_ref, f32[5,256,1024]{2,1,0:T(8,128)} %shard_map.164.rel_hbm.refs_1_, ...), custom_call_target="tpu_custom_call" | custom-call | flops 11811160064 | bytes 1048576 | tf_op jit(solution)/shard_map/pallas_call | solution.py:333
  55.2 8.5 %shard_map.168 = (bf16[16,64,128]{2,1,0:T(8,128)(2,1)}, bf16[16,64,128]{2,1,0:T(8,128)(2,1)}) custom-call(s32[1]{0:T(128)} %bitcast.16.refs_0_.core_ref, f32[5,256,1024]{2,1,0:T(8,128)} %shard_map.164.rel_hbm.refs_1_, bf16[2,256,1024]{2,1,0:T(8,128)(2,1)} %get-tuple-element.37.refs_2_, bf16[2,256,1024]{2,1,0:T(8,128)(2,1)} %get-tuple-element.38.refs_3_, ...), custom_call_target="tpu_custom_call" | custom-call | flops 4294967296 | bytes 1048576 | tf_op jit(solution)/shard_map/pallas_call | solution.py:333
  63.7 0.0 copy-start.1
  63.7 0.0 copy-start.2
  63.7 0.1 collective-permute-start.5
  63.8 1.4 %collective-permute-start.4 = (bf16[4,256,256]{2,1,0:T(8,128)(2,1)}, bf16[4,256,256]{2,1,0:T(8,128)(2,1)S(1)}, u32[]{:S(2)}, u32[]{:S(2)}) collective-permute-start(bf16[4,256,256]{2,1,0:T(8,128)(2,1)} %get-tuple-element.34), channel_id=1, source_target_pairs={{0,1},{1,0},{2,3},{3,2},{4,5},{5,4},{6,7},{7,6},{8,9},{9,8},{10,11... | collective-permute-start | bytes 1572872 | tf_op jit(solution)/shard_map/ppermute | solution.py:351
  65.2 0.4 collective-permute-done.5.got_ref
  65.5 0.9 copy-done.4
  66.5 0.8 shard_map.169
  67.2 6.0 %all-to-all-start.2 = ((bf16[16,80,128]{2,1,0:T(8,128)(2,1)}), bf16[16,80,128]{2,1,0:T(8,128)(2,1)S(1)}, u32[]{:S(2)}, u32[]{:S(2)}) async-start(bf16[16,80,128]{2,1,0:T(8,128)(2,1)} %shard_map.169), calls=%async_computation.2 | async-start | bytes 655360 | tf_op jit(solution)/shard_map/all_to_all | solution.py:347
  73.2 0.1 reshape.51
  73.3 0.1 reshape.52.asked
  73.4 3.5 %shard_map.167.refs_3_ = f32[4096,256]{1,0:T(8,128)} custom-call(s32[1,1024]{1,0:T(1,128)S(1)} %bitcast.33, s32[1,1024]{1,0:T(1,128)S(1)} %bitcast.36, bf16[2048,256]{1,0:T(8,128)(2,1)S(1)} %copy-done.3), custom_call_target="tpu_custom_call" | custom-call | flops 3221225472 | bytes 1048576 | tf_op jit(solution)/shard_map/pallas_call | solution.py:333
  76.9 3.2 %collective-permute-done.4 = bf16[4,256,256]{2,1,0:T(8,128)(2,1)S(1)} collective-permute-done((bf16[4,256,256]{2,1,0:T(8,128)(2,1)}, bf16[4,256,256]{2,1,0:T(8,128)(2,1)S(1)}, u32[]{:S(2)}, u32[]{:S(2)}) %collective-permute-start.4) | collective-permute-done | bytes 524320 | tf_op jit(solution)/shard_map/ppermute | solution.py:351
  80.1 0.8 fusion.4
  80.9 3.4 %collective-permute-start.8 = (bf16[256,256]{1,0:T(8,128)(2,1)}, bf16[256,256]{1,0:T(8,128)(2,1)S(1)}, u32[]{:S(2)}, u32[]{:S(2)}) collective-permute-start(bf16[256,256]{1,0:T(8,128)(2,1)} %get-tuple-element.49), channel_id=1, source_target_pairs={{0,6},{2,4},{4,2},{6,0},{1,7},{3,5},{5,3},{7,1},{8,14},{10,12},{12... | collective-permute-start | bytes 393224 | tf_op jit(solution)/shard_map/ppermute | solution.py:351
  84.3 0.0 collective-permute-start.7
  84.3 1.0 collective-permute-start.6
  85.3 0.7 shard_map.170
  86.0 6.6 %all-to-all-start.3 = ((bf16[16,48,128]{2,1,0:T(8,128)(2,1)}), bf16[16,48,128]{2,1,0:T(8,128)(2,1)S(1)}, u32[]{:S(2)}, u32[]{:S(2)}) async-start(bf16[16,48,128]{2,1,0:T(8,128)(2,1)} %shard_map.170), calls=%async_computation.3 | async-start | bytes 393216 | tf_op jit(solution)/shard_map/all_to_all | solution.py:347
  92.6 3.5 %shard_map.171 = f32[4096,256]{1,0:T(8,128)} custom-call(s32[1,1024]{1,0:T(1,128)S(1)} %bitcast.34, s32[1,1024]{1,0:T(1,128)S(1)} %bitcast.37, bf16[2048,256]{1,0:T(8,128)(2,1)S(1)} %copy-done.3, f32[4096,256]{1,0:T(8,128)} %shard_map.167.refs_3_), custom_call_target="tpu_custom_call", output_to_operand_aliasing={{}: (3, {})} | custom-call | flops 3221225472 | bytes 1048576 | tf_op jit(solution)/shard_map/pallas_call | solution.py:333
  96.1 1.4 %shard_map.172 = f32[1024,256]{1,0:T(8,128)} custom-call(s32[1]{0:T(128)} %bitcast.16.refs_0_.core_ref, bf16[16,80,128]{2,1,0:T(8,128)(2,1)S(1)} %all-to-all-done.2.got_ref, s32[2,128]{1,0:T(2,128)S(1)} %reshape.52.asked), custom_call_target="tpu_custom_call" | custom-call | flops 2147483648 | bytes 1048576 | tf_op jit(solution)/shard_map/pallas_call | solution.py:333
  97.4 0.0 collective-permute-done.8
  97.5 0.0 collective-permute-done.7
  97.5 3.2 %all-to-all-done.3 = bf16[16,48,128]{2,1,0:T(8,128)(2,1)S(1)} async-done(((bf16[16,48,128]{2,1,0:T(8,128)(2,1)}), bf16[16,48,128]{2,1,0:T(8,128)(2,1)S(1)}, u32[]{:S(2)}, u32[]{:S(2)}) %all-to-all-start.3) | async-done | bytes 196640 | tf_op jit(solution)/shard_map/all_to_all | solution.py:347
  100.6 0.8 fusion.1
  101.4 0.7 collective-permute-done.9.got_ref
  102.1 0.9 shard_map.173
  (21 shorter events, 0.1 us)
Async XLA Ops:
  0.6 19.8 %copy-start = (bf16[1024,256]{1,0:T(8,128)(2,1)S(1)}, bf16[1024,256]{1,0:T(8,128)(2,1)}, u32[]{:S(2)}) copy-start(bf16[1024,256]{1,0:T(8,128)(2,1)} %param.15) | copy-start | bytes 1572868
  0.6 17.4 %collective-permute-start = (bf16[256,256]{1,0:T(8,128)(2,1)}, bf16[256,256]{1,0:T(8,128)(2,1)S(1)}, u32[]{:S(2)}, u32[]{:S(2)}) collective-permute-start(bf16[256,256]{1,0:T(8,128)(2,1)} %param.13), channel_id=1, source_target_pairs={{0,2},{2,0},{4,6},{6,4},{1,3},{3,1},{5,7},{7,5},{8,10},{10,8},{12,... | collective-permute-start | bytes 393224 | tf_op jit(solution)/shard_map/ppermute | solution.py:351
  3.7 14.3 %collective-permute-start.2 = (bf16[256,256]{1,0:T(8,128)(2,1)}, bf16[256,256]{1,0:T(8,128)(2,1)S(1)}, u32[]{:S(2)}, u32[]{:S(2)}) collective-permute-start(bf16[256,256]{1,0:T(8,128)(2,1)} %param.13), channel_id=1, source_target_pairs={{0,6},{2,4},{4,2},{6,0},{1,7},{3,5},{5,3},{7,1},{8,14},{10,12},{12... | collective-permute-start | bytes 393224 | tf_op jit(solution)/shard_map/ppermute | solution.py:351
  6.2 12.3 %collective-permute-start.1 = (bf16[256,256]{1,0:T(8,128)(2,1)}, bf16[256,256]{1,0:T(8,128)(2,1)S(1)}, u32[]{:S(2)}, u32[]{:S(2)}) collective-permute-start(bf16[256,256]{1,0:T(8,128)(2,1)} %param.13), channel_id=1, source_target_pairs={{0,4},{2,6},{4,0},{6,2},{1,5},{3,7},{5,1},{7,3},{8,12},{10,14},{12... | collective-permute-start | bytes 393224 | tf_op jit(solution)/shard_map/ppermute | solution.py:351
  7.7 12.6 %all-to-all-start = ((s32[32,1,8]{2,1,0:T(1,128)}), s32[32,1,8]{2,1,0:T(1,128)S(1)}, u32[]{:S(2)}, u32[]{:S(2)}) async-start(s32[32,1,8]{2,1,0:T(1,128)} %bitcast.1), calls=%async_computation | async-start | bytes 32768 | tf_op jit(solution)/shard_map/all_to_all | solution.py:347
  12.9 5.6 %copy-start.8 = (bf16[256,256]{1,0:T(8,128)(2,1)S(1)}, bf16[256,256]{1,0:T(8,128)(2,1)}, u32[]{:S(2)}) copy-start(bf16[256,256]{1,0:T(8,128)(2,1)} %param.13) | copy-start | bytes 393220
  18.5 16.7 %copy-start.6 = (bf16[4,256,256]{2,1,0:T(8,128)(2,1)}, bf16[4,256,256]{2,1,0:T(8,128)(2,1)S(1)}, u32[]{:S(2)}) copy-start(bf16[4,256,256]{2,1,0:T(8,128)(2,1)S(1)} %pad_maximum_fusion.near_hbm) | copy-start | bytes 1572868
  22.3 13.6 %all-to-all-start.1 = ((bf16[32,8,256]{2,1,0:T(8,128)(2,1)}), bf16[32,8,256]{2,1,0:T(8,128)(2,1)S(1)}, u32[]{:S(2)}, u32[]{:S(2)}) async-start(bf16[32,8,256]{2,1,0:T(8,128)(2,1)} %bitcast.11), calls=%async_computation.1 | async-start | bytes 262144 | tf_op jit(solution)/shard_map/all_to_all | solution.py:347
  26.1 15.4 %collective-permute-start.3 = (bf16[4,256,256]{2,1,0:T(8,128)(2,1)S(1)}, bf16[4,256,256]{2,1,0:T(8,128)(2,1)S(1)}, u32[]{:S(2)}, u32[]{:S(2)}) collective-permute-start(bf16[4,256,256]{2,1,0:T(8,128)(2,1)S(1)} %pad_maximum_fusion.near_hbm), channel_id=1, source_target_pairs={{0,1},{1,0},{2,3},{3,2},{4,5},{5,4},{6,7},{7,6},{8,9},{9,8},{10,11... | collective-permute-start | bytes 1572872 | tf_op jit(solution)/shard_map/ppermute | solution.py:351
  35.9 5.6 %copy-start.7 = (bf16[32,8,256]{2,1,0:T(8,128)(2,1)}, bf16[32,8,256]{2,1,0:T(8,128)(2,1)S(1)}, u32[]{:S(2)}) copy-start(bf16[32,8,256]{2,1,0:T(8,128)(2,1)S(1)} %all-to-all-done.1) | copy-start | bytes 393220
  41.5 0.8 copy-start.9
  63.7 9.7 %copy-start.1 = (s32[1024]{0:T(1024)S(1)}, s32[1024]{0:T(1024)}, u32[]{:S(2)}) copy-start(s32[1024]{0:T(1024)} %param.19) | copy-start | bytes 12292
  63.7 9.7 %copy-start.2 = (s32[1024]{0:T(1024)S(1)}, s32[1024]{0:T(1024)}, u32[]{:S(2)}) copy-start(s32[1024]{0:T(1024)} %param.24) | copy-start | bytes 12292
  63.7 9.7 %copy-start.3 = (bf16[2048,256]{1,0:T(8,128)(2,1)S(1)}, bf16[2048,256]{1,0:T(8,128)(2,1)}, u32[]{:S(2)}) copy-start(bf16[2048,256]{1,0:T(8,128)(2,1)} %get-tuple-element.35.refs_2_) | copy-start | bytes 3145732
  63.7 1.8 %collective-permute-start.5 = (bf16[16,64,128]{2,1,0:T(8,128)(2,1)}, bf16[16,64,128]{2,1,0:T(8,128)(2,1)S(1)}, u32[]{:S(2)}, u32[]{:S(2)}) collective-permute-start(bf16[16,64,128]{2,1,0:T(8,128)(2,1)} %get-tuple-element.40), channel_id=1, source_target_pairs={{0,8},{8,0},{1,9},{9,1},{2,10},{10,2},{3,11},{11,3},{4,12},{12,4},... | collective-permute-start | bytes 786440 | tf_op jit(solution)/shard_map/ppermute | solution.py:351
  63.8 16.3 %collective-permute-start.4 = (bf16[4,256,256]{2,1,0:T(8,128)(2,1)}, bf16[4,256,256]{2,1,0:T(8,128)(2,1)S(1)}, u32[]{:S(2)}, u32[]{:S(2)}) collective-permute-start(bf16[4,256,256]{2,1,0:T(8,128)(2,1)} %get-tuple-element.34), channel_id=1, source_target_pairs={{0,1},{1,0},{2,3},{3,2},{4,5},{5,4},{6,7},{7,6},{8,9},{9,8},{10,11... | collective-permute-start | bytes 1572872 | tf_op jit(solution)/shard_map/ppermute | solution.py:351
  65.5 1.0 copy-start.4
  67.2 18.0 %all-to-all-start.2 = ((bf16[16,80,128]{2,1,0:T(8,128)(2,1)}), bf16[16,80,128]{2,1,0:T(8,128)(2,1)S(1)}, u32[]{:S(2)}, u32[]{:S(2)}) async-start(bf16[16,80,128]{2,1,0:T(8,128)(2,1)} %shard_map.169), calls=%async_computation.2 | async-start | bytes 655360 | tf_op jit(solution)/shard_map/all_to_all | solution.py:347
  73.4 6.7 %copy-start.5 = (bf16[4,256,256]{2,1,0:T(8,128)(2,1)S(1)}, bf16[4,256,256]{2,1,0:T(8,128)(2,1)}, u32[]{:S(2)}) copy-start(bf16[4,256,256]{2,1,0:T(8,128)(2,1)} %get-tuple-element.33) | copy-start | bytes 1572868
  80.9 16.6 %collective-permute-start.8 = (bf16[256,256]{1,0:T(8,128)(2,1)}, bf16[256,256]{1,0:T(8,128)(2,1)S(1)}, u32[]{:S(2)}, u32[]{:S(2)}) collective-permute-start(bf16[256,256]{1,0:T(8,128)(2,1)} %get-tuple-element.49), channel_id=1, source_target_pairs={{0,6},{2,4},{4,2},{6,0},{1,7},{3,5},{5,3},{7,1},{8,14},{10,12},{12... | collective-permute-start | bytes 393224 | tf_op jit(solution)/shard_map/ppermute | solution.py:351
  84.3 13.1 %collective-permute-start.7 = (bf16[256,256]{1,0:T(8,128)(2,1)}, bf16[256,256]{1,0:T(8,128)(2,1)S(1)}, u32[]{:S(2)}, u32[]{:S(2)}) collective-permute-start(bf16[256,256]{1,0:T(8,128)(2,1)} %get-tuple-element.50), channel_id=1, source_target_pairs={{0,4},{2,6},{4,0},{6,2},{1,5},{3,7},{5,1},{7,3},{8,12},{10,14},{12... | collective-permute-start | bytes 393224 | tf_op jit(solution)/shard_map/ppermute | solution.py:351
  84.3 13.1 %collective-permute-start.6 = (bf16[256,256]{1,0:T(8,128)(2,1)}, bf16[256,256]{1,0:T(8,128)(2,1)S(1)}, u32[]{:S(2)}, u32[]{:S(2)}) collective-permute-start(bf16[256,256]{1,0:T(8,128)(2,1)} %get-tuple-element.51), channel_id=1, source_target_pairs={{0,2},{2,0},{4,6},{6,4},{1,3},{3,1},{5,7},{7,5},{8,10},{10,8},{12,... | collective-permute-start | bytes 393224 | tf_op jit(solution)/shard_map/ppermute | solution.py:351
  86.0 14.7 %all-to-all-start.3 = ((bf16[16,48,128]{2,1,0:T(8,128)(2,1)}), bf16[16,48,128]{2,1,0:T(8,128)(2,1)S(1)}, u32[]{:S(2)}, u32[]{:S(2)}) async-start(bf16[16,48,128]{2,1,0:T(8,128)(2,1)} %shard_map.170), calls=%async_computation.3 | async-start | bytes 393216 | tf_op jit(solution)/shard_map/all_to_all | solution.py:347
  100.6 1.4 %collective-permute-start.9 = (bf16[768,128]{1,0:T(8,128)(2,1)S(1)}, bf16[768,128]{1,0:T(8,128)(2,1)S(1)}, u32[]{:S(2)}, u32[]{:S(2)}) collective-permute-start(bf16[768,128]{1,0:T(8,128)(2,1)S(1)} %bitcast.30), channel_id=1, source_target_pairs={{0,8},{8,0},{1,9},{9,1},{2,10},{10,2},{3,11},{11,3},{4,12},{12,4},... | collective-permute-start | bytes 589832 | tf_op jit(solution)/shard_map/ppermute | solution.py:351

commit v9 on v7

--- a/solution.py
+++ b/solution.py
@@ -22,6 +22,10 @@
 
 def nt(a, b):
     return lax.dot_general(a, b, (((1,), (1,)), ((), ())), preferred_element_type=F32)
+
+
+def tn(a, b):
+    return lax.dot_general(a, b, (((0,), (0,)), ((), ())), preferred_element_type=F32)
 
 
 def pieces(values, count):
@@ -90,7 +94,8 @@
     qual_rel,
     head_id,
     proj_ref,
-    far_out,
+    far_high_out,
+    far_low_out,
     near_out,
     own_out,
     other_out,
@@ -140,7 +145,10 @@
     for k in range(1, quals):
         composed = composed + rel_ref[k + 1] * rows[k]
     comp_hi, comp_lo = pieces(composed, 2)
-    relation = rel_ref[0] + (nn(projt_hi, comp_hi) + (nn(projt_hi, comp_lo) + nn(projt_lo, comp_hi)))
+    relation = rel_ref[0] + nn(
+        jnp.concatenate([projt_hi, projt_hi, projt_lo], axis=1),
+        jnp.concatenate([comp_hi, comp_lo, comp_hi], axis=0),
+    )
     for copy in head_loads:
         copy.wait()
     offset = jnp.bitwise_xor(head_id[...] // head_rows, member_ref[0])
@@ -148,7 +156,7 @@
     heads = jnp.zeros((width, edges), F32)
     for first, table in ((0, near_ref), (half, far_ref)):
         for owner in range(half):
-            heads = heads + nn(flip(table[owner]), onehot(head_slot, (first + owner) * head_rows, head_rows))
+            heads = heads + tn(table[owner], onehot(head_slot, (first + owner) * head_rows, head_rows))
     query = (heads * relation).astype(BF)
     query_f = query.astype(F32)
     tails_load.wait()
@@ -175,7 +183,8 @@
         stores[-1].start()
 
     head_terms = (query_grad * relation).astype(BF)
-    for first, part, out in ((half, far_ref, far_out), (0, near_ref, near_out)):
+    low, high = pl.ds(0, half // 2), pl.ds(half // 2, half - half // 2)
+    for first, part in ((half, far_ref), (0, near_ref)):
 
         def scatter(owner):
             hot = onehot(head_slot, (first + owner) * head_rows, head_rows)
@@ -186,19 +195,30 @@
         else:
             for owner in range(half):
                 scatter(owner)
-        store(part, out)
+        if part is far_ref:
+            store(far_ref.at[high], far_high_out)
+            store(far_ref.at[low], far_low_out)
+        else:
+            store(near_ref, near_out)
 
     relation_grad = query_grad * heads
     rg_hi, rg_lo = pieces(relation_grad, 2)
-    comp_grad = nn(proj_hi, rg_hi) + (nn(proj_hi, rg_lo) + nn(proj_lo, rg_hi))
-    rel_sum = nt(onehot(rel_id[...], 0, rel_rows), rg_hi)
-    fetched_sum = jnp.zeros((slots, width), F32)
+    comp_grad = nn(
+        jnp.concatenate([proj_hi, proj_hi, proj_lo], axis=1), jnp.concatenate([rg_hi, rg_lo, rg_hi], axis=0)
+    )
+    rel_hots, rel_terms = [onehot(rel_id[...], 0, rel_rows)], [rg_hi]
+    ref_hots, ref_terms = [], []
     for k in range(quals):
-        hot = onehot(ref_ids[k : k + 1, :], 0, slots)
-        rel_sum = rel_sum + nt(onehot(qual_rel[k : k + 1, :], 0, rel_rows), (comp_grad * rows[k]).astype(BF))
-        fetched_sum = fetched_sum + nt(hot, (comp_grad * rel_ref[k + 1]).astype(BF))
+        rel_hots.append(onehot(qual_rel[k : k + 1, :], 0, rel_rows))
+        rel_terms.append((comp_grad * rows[k]).astype(BF))
+        ref_hots.append(onehot(ref_ids[k : k + 1, :], 0, slots))
+        ref_terms.append((comp_grad * rel_ref[k + 1]).astype(BF))
+    rel_sum = nt(jnp.concatenate(rel_hots, axis=1), jnp.concatenate(rel_terms, axis=1))
+    fetched_sum = nt(jnp.concatenate(ref_hots, axis=1), jnp.concatenate(ref_terms, axis=1))
     sums[:rel_rows, :] = rel_sum
-    sums[rel_rows : rel_rows + width, :] = nt(comp_hi, rg_hi) + (nt(comp_hi, rg_lo) + nt(comp_lo, rg_hi))
+    sums[rel_rows : rel_rows + width, :] = nt(
+        jnp.concatenate([comp_hi, comp_hi, comp_lo], axis=1), jnp.concatenate([rg_hi, rg_lo, rg_hi], axis=1)
+    )
     if sums.shape[0] > rel_rows + width:
         sums[rel_rows + width :, :] = jnp.zeros((sums.shape[0] - rel_rows - width, width), F32)
     pairs = fetched_sum.reshape(-1, cores, chips // PAIRS, cap, width)
@@ -381,10 +401,11 @@
     def edge(*refs):
         edge_kernel(*refs, rel_rows=rel_rows)
 
-    far_part, near_part, own_part, other_part, terms = call(
+    far_high, far_low, near_part, own_part, other_part, terms = call(
         edge,
         [
-            ((half, head_rows, width), BF),
+            ((half - half // 2, head_rows, width), BF),
+            ((half // 2, head_rows, width), BF),
             ((half, head_rows, width), BF),
             ((chips, sent, lanes), BF),
             ((chips, sent, lanes), BF),
@@ -401,7 +422,7 @@
             pltpu.VMEM((cores, chips, sent, lanes), BF),
             pltpu.VMEM((edges + negs, width), BF),
             pltpu.SemaphoreType.DMA((quals + 6,)),
-            pltpu.SemaphoreType.DMA((5,)),
+            pltpu.SemaphoreType.DMA((6,)),
         ],
         14,
         58,
@@ -422,10 +443,11 @@
         proj,
         smem=(0, 1, 2),
         away=range(3, 9),
-        out_specs=[pl.BlockSpec(memory_space=pl.ANY)] * 5,
+        out_specs=[pl.BlockSpec(memory_space=pl.ANY)] * 6,
     )
     other_got = swap(other_part, "core")
-    far_got = swap(far_part, "near")
+    high_got = swap(far_high, "near")
+    low_got = swap(far_low, "near")
     (chip_part,) = call(combine_kernel, [((chips, sent + passed, lanes), BF)], [], 1, 16, own_part, other_got)
     chip_got = exchange(chip_part, CHIPS)
 
@@ -454,9 +476,13 @@
         return out
 
     tail_grad = tail_rows_of(0, steps // 2)
-    far_got, tail_grad = lax.optimization_barrier((far_got, tail_grad))
-    near_sum = [near_part[offset].astype(F32) + far_got[offset].astype(F32) for offset in range(half)]
-    line_got = [swap(near_sum[offset].astype(BF), "line", offset) for offset in range(1, half)]
+    high_got, tail_grad = lax.optimization_barrier((high_got, tail_grad))
+
+    def near_sum(offset):
+        got = high_got[offset - half // 2] if offset >= half // 2 else low_got[offset]
+        return near_part[offset].astype(F32) + got.astype(F32)
+
+    line_got = [swap(near_sum(offset).astype(BF), "line", offset) for offset in reversed(range(1, half))]
     (sums_own,) = call(add_kernel, [((chips, share, lanes), BF)], [], 1, 16, chip_got)
     sums_own = exchange(sums_own, CHIPS).reshape(chips * share, lanes)
     tail_grad = tail_rows_of(steps // 2, steps - steps // 2, tail_grad)
@@ -474,7 +500,7 @@
         smem=(0,),
     )
 
-    head_grad = near_sum[0]
+    head_grad = near_sum(0)
     for got in line_got:
         head_grad = head_grad + got.astype(F32)
 

time: 92.7 us -> 102 us (1.10)
  waiting for transfers between devices: 8.93 us -> 19.3 us
    ppermute x10 -> x11, waiting for transfers between devices: 2.93 us -> 14 us  [swap(): lax.ppermute(values, axis, [(i, i ^ offset) for i in range(lax.axis_size(...]
    ppermute x10 -> x11, starting transfers between devices: 12.5 us -> 12.9 us  [swap(): lax.ppermute(values, axis, [(i, i ^ offset) for i in range(lax.axis_size(...]
  transfers between devices with their start and end apart: 14 -> 15, of which waited for: 7 -> 7; matrix products, arithmetic and copies ran while one was open for 4% -> 4% of each run, Pallas kernels for 24% -> 21%
where the time goes in v9:
time: 102 us
  Pallas kernels  38.2 us (37%)
  starting transfers between devices  35.7 us (35%)
  waiting for transfers between devices  19.3 us (19%)
  local copies, waits for them, and re-layouts  5.27 us (5%)
  other arithmetic  1.62 us (2%)
  between operations  1.48 us (1%)
    pallas_call x9, Pallas kernels, call(): pl.pallas_call(kernel, out_shape=shapes, grid=grid, in_specs=[pl.BlockSpe...  38.2 us
    all_to_all x4, starting transfers between devices, exchange(): return lax.all_to_all(values, axes, split_axis=0, concat_axis=0, tiled=True)  22.8 us
    ppermute x11, waiting for transfers between devices, swap(): lax.ppermute(values, axis, [(i, i ^ offset) for i in range(lax.axis_size(...  14 us
    ppermute x11, starting transfers between devices, swap(): lax.ppermute(values, axis, [(i, i ^ offset) for i in range(lax.axis_size(...  12.9 us
    all_to_all x4, waiting for transfers between devices, exchange(): return lax.all_to_all(values, axes, split_axis=0, concat_axis=0, tiled=True)  5.34 us
  transfers between devices with their start and end apart: 15, of which 7 were waited for; matrix products, arithmetic and copies ran while one was open for 4% of the time, Pallas kernels for 21%

profile of v9, /device:TPU:0, one launch (start us, length us, event | category | flops | bytes accessed | tf_op | source)
XLA Modules:
  0.0 101.6 jit_solution(13869235852520596442)
XLA Ops:
  0.6 0.0 copy-start
  0.6 5.1 %collective-permute-start.2 = (bf16[256,256]{1,0:T(8,128)(2,1)}, bf16[256,256]{1,0:T(8,128)(2,1)S(1)}, u32[]{:S(2)}, u32[]{:S(2)}) collective-permute-start(bf16[256,256]{1,0:T(8,128)(2,1)} %param.13), channel_id=1, source_target_pairs={{0,6},{2,4},{4,2},{6,0},{1,7},{3,5},{5,3},{7,1},{8,14},{10,12},{12... | collective-permute-start | bytes 393224 | tf_op jit(solution)/shard_map/ppermute | solution.py:325
  5.8 0.6 collective-permute-start
  6.4 1.4 %all_to_all.17 = s32[32,1,8]{2,0,1:T(8,128)} reshape(s32[256]{0:T(256)} %param.23) | data formatting | bytes 2048 | tf_op jit(solution)/shard_map/all_to_all | solution.py:321
  7.8 6.0 %all-to-all-start = ((s32[32,1,8]{2,1,0:T(1,128)}), s32[32,1,8]{2,1,0:T(1,128)S(1)}, u32[]{:S(2)}, u32[]{:S(2)}) async-start(s32[32,1,8]{2,1,0:T(1,128)} %bitcast.2), calls=%async_computation | async-start | bytes 32768 | tf_op jit(solution)/shard_map/all_to_all | solution.py:321
  13.8 0.0 copy-start.8
  13.8 5.1 %shard_map.164.refs_3_ = f32[5,256,1024]{2,1,0:T(8,128)} custom-call(f32[512,256]{1,0:T(8,128)} %rel_ref.1, s32[1,1024]{1,0:T(1,128)} %bitcast.49, s32[4,1024]{1,0:T(4,128)} %bitcast.46), custom_call_target="tpu_custom_call" | custom-call | flops 5368709120 | bytes 1048576 | tf_op jit(solution)/shard_map/pallas_call | solution.py:307
  18.9 0.0 collective-permute-done.1
  19.0 0.1 pad_maximum_fusion.refs_4_
  19.1 0.0 copy-start.6
  19.1 1.8 %all-to-all-done = s32[32,1,8]{2,1,0:T(1,128)S(1)} async-done(((s32[32,1,8]{2,1,0:T(1,128)}), s32[32,1,8]{2,1,0:T(1,128)S(1)}, u32[]{:S(2)}, u32[]{:S(2)}) %all-to-all-start) | async-done | bytes 1056 | tf_op jit(solution)/shard_map/all_to_all | solution.py:321
  20.8 0.6 collective-permute-start.3
  21.4 0.1 reshape.55
  21.6 1.8 %gather_fusion = bf16[256,256]{1,0:T(8,128)(2,1)} fusion(bf16[1024,256]{1,0:T(8,128)(2,1)S(1)} %copy-done, s32[1024]{0:T(1024)S(1)} %pad_clamp_fusion), kind=kCustom, calls=%fused_computation | custom fusion | bytes 263168 | tf_op jit(solution)/shard_map/gather | solution.py:385
  23.4 4.3 %all-to-all-start.1 = ((bf16[32,8,256]{2,1,0:T(8,128)(2,1)}), bf16[32,8,256]{2,1,0:T(8,128)(2,1)S(1)}, u32[]{:S(2)}, u32[]{:S(2)}) async-start(bf16[32,8,256]{2,1,0:T(8,128)(2,1)} %bitcast.12), calls=%async_computation.1 | async-start | bytes 262144 | tf_op jit(solution)/shard_map/all_to_all | solution.py:321
  27.6 7.3 %shard_map.165 = (bf16[256,1024]{1,0:T(8,128)(2,1)}, bf16[256,1024]{1,0:T(8,128)(2,1)}, bf16[1024,256]{1,0:T(8,128)(2,1)}) custom-call(bf16[4096,256]{1,0:T(8,128)(2,1)} %tail_ref.1, s32[1,1024]{1,0:T(1,128)} %bitcast.32, s32[1,1024]{1,0:T(1,128)} %bitcast.35), custom_call_target="tpu_custom_call" | custom-call | flops 7516192768 | bytes 1048576 | tf_op jit(solution)/shard_map/pallas_call | solution.py:307
  35.6 0.3 all-to-all-done.1
  35.9 0.7 copy-done.7
  36.6 0.2 copy-done.9
  36.7 15.0 %shard_map.166 = (bf16[2,256,256]{2,1,0:T(8,128)(2,1)}, bf16[2,256,256]{2,1,0:T(8,128)(2,1)}, bf16[4,256,256]{2,1,0:T(8,128)(2,1)}, bf16[16,64,128]{2,1,0:T(8,12...) custom-call(s32[1]{0:T(128)S(6)} %copy.23.refs_0_, s32[1]{0:T(128)} %bitcast.refs_1_.core_ref, ...), custom_call_target="tpu_custom_call" | custom-call | flops 15032385536 | bytes 1048576 | tf_op jit(solution)/shard_map/pallas_call | solution.py:307
  51.7 0.0 copy-start.1
  51.7 0.0 copy-start.2
  51.7 0.0 copy-start.3
  51.7 0.1 collective-permute-start.5
  51.8 1.7 %collective-permute-done.5.got_ref = bf16[16,64,128]{2,1,0:T(8,128)(2,1)S(1)} collective-permute-done((bf16[16,64,128]{2,1,0:T(8,128)(2,1)}, bf16[16,64,128]{2,1,0:T(8,128)(2,1)S(1)}, u32[]{:S(2)}, u32[]{:S(2)}) %collective-permute-start.5) | collective-permute-done | bytes 262176 | tf_op jit(solution)/shard_map/ppermute | solution.py:325
  53.5 0.9 copy-done.4
  54.5 0.8 shard_map.167
  55.3 6.6 %all-to-all-start.2 = ((bf16[16,80,128]{2,1,0:T(8,128)(2,1)}), bf16[16,80,128]{2,1,0:T(8,128)(2,1)S(1)}, u32[]{:S(2)}, u32[]{:S(2)}) async-start(bf16[16,80,128]{2,1,0:T(8,128)(2,1)} %shard_map.167), calls=%async_computation.2 | async-start | bytes 655360 | tf_op jit(solution)/shard_map/all_to_all | solution.py:321
  61.9 0.1 reshape.51
  61.9 0.1 reshape.52.asked
  62.0 1.9 %collective-permute-start.6 = (bf16[2,256,256]{2,1,0:T(8,128)(2,1)S(1)}, bf16[2,256,256]{2,1,0:T(8,128)(2,1)S(1)}, u32[]{:S(2)}, u32[]{:S(2)}) collective-permute-start(bf16[2,256,256]{2,1,0:T(8,128)(2,1)S(1)} %copy-done.11), channel_id=1, source_target_pairs={{0,1},{1,0},{2,3},{3,2},{4,5},{5,4},{6,7},{7,6},{8,9},{9,8},{10,11... | collective-permute-start | bytes 786440 | tf_op jit(solution)/shard_map/ppermute | solution.py:325
  64.0 0.1 collective-permute-start.4
  64.1 3.5 %shard_map.169.refs_3_ = f32[4096,256]{1,0:T(8,128)} custom-call(s32[1,1024]{1,0:T(1,128)S(1)} %bitcast.33, s32[1,1024]{1,0:T(1,128)S(1)} %bitcast.36, bf16[2048,256]{1,0:T(8,128)(2,1)S(1)} %copy-done.3), custom_call_target="tpu_custom_call" | custom-call | flops 3221225472 | bytes 1048576 | tf_op jit(solution)/shard_map/pallas_call | solution.py:307
  67.6 7.1 %collective-permute-done.6 = bf16[2,256,256]{2,1,0:T(8,128)(2,1)S(1)} collective-permute-done((bf16[2,256,256]{2,1,0:T(8,128)(2,1)S(1)}, bf16[2,256,256]{2,1,0:T(8,128)(2,1)S(1)}, u32[]{:S(2)}, u32[]{:S(2)}) %collective-permute-start.6) | collective-permute-done | bytes 262176 | tf_op jit(solution)/shard_map/ppermute | solution.py:325
  74.7 4.5 %collective-permute-done.4 = bf16[2,256,256]{2,1,0:T(8,128)(2,1)S(1)} collective-permute-done((bf16[2,256,256]{2,1,0:T(8,128)(2,1)S(1)}, bf16[2,256,256]{2,1,0:T(8,128)(2,1)S(1)}, u32[]{:S(2)}, u32[]{:S(2)}) %collective-permute-start.4) | collective-permute-done | bytes 262176 | tf_op jit(solution)/shard_map/ppermute | solution.py:325
  79.2 0.8 fusion.3
  79.9 3.3 %collective-permute-start.7 = (bf16[256,256]{1,0:T(8,128)(2,1)}, bf16[256,256]{1,0:T(8,128)(2,1)S(1)}, u32[]{:S(2)}, u32[]{:S(2)}) collective-permute-start(bf16[256,256]{1,0:T(8,128)(2,1)} %get-tuple-element.48), channel_id=1, source_target_pairs={{0,6},{2,4},{4,2},{6,0},{1,7},{3,5},{5,3},{7,1},{8,14},{10,12},{12... | collective-permute-start | bytes 393224 | tf_op jit(solution)/shard_map/ppermute | solution.py:325
  83.2 0.0 collective-permute-start.8
  83.2 1.1 %collective-permute-start.9 = (bf16[256,256]{1,0:T(8,128)(2,1)S(1)}, bf16[256,256]{1,0:T(8,128)(2,1)S(1)}, u32[]{:S(2)}, u32[]{:S(2)}) collective-permute-start(bf16[256,256]{1,0:T(8,128)(2,1)S(1)} %get-tuple-element.49), channel_id=1, source_target_pairs={{0,2},{2,0},{4,6},{6,4},{1,3},{3,1},{5,7},{7,5},{8,10},{10,8},{12,... | collective-permute-start | bytes 393224 | tf_op jit(solution)/shard_map/ppermute | solution.py:325
  84.3 0.0 all-to-all-done.2.got_ref
  84.3 0.7 shard_map.168
  85.0 6.0 %all-to-all-start.3 = ((bf16[16,48,128]{2,1,0:T(8,128)(2,1)}), bf16[16,48,128]{2,1,0:T(8,128)(2,1)S(1)}, u32[]{:S(2)}, u32[]{:S(2)}) async-start(bf16[16,48,128]{2,1,0:T(8,128)(2,1)} %shard_map.168), calls=%async_computation.3 | async-start | bytes 393216 | tf_op jit(solution)/shard_map/all_to_all | solution.py:321
  91.0 3.5 %shard_map.170 = f32[4096,256]{1,0:T(8,128)} custom-call(s32[1,1024]{1,0:T(1,128)S(1)} %bitcast.34, s32[1,1024]{1,0:T(1,128)S(1)} %bitcast.37, bf16[2048,256]{1,0:T(8,128)(2,1)S(1)} %copy-done.3, f32[4096,256]{1,0:T(8,128)} %shard_map.169.refs_3_), custom_call_target="tpu_custom_call", output_to_operand_aliasing={{}: (3, {})} | custom-call | flops 3221225472 | bytes 1048576 | tf_op jit(solution)/shard_map/pallas_call | solution.py:307
  94.5 1.4 %shard_map.171 = f32[1024,256]{1,0:T(8,128)} custom-call(s32[1]{0:T(128)} %bitcast.refs_1_.core_ref, bf16[16,80,128]{2,1,0:T(8,128)(2,1)S(1)} %all-to-all-done.2.got_ref, s32[2,128]{1,0:T(2,128)S(1)} %reshape.52.asked), custom_call_target="tpu_custom_call" | custom-call | flops 2147483648 | bytes 1048576 | tf_op jit(solution)/shard_map/pallas_call | solution.py:307
  95.9 3.3 %all-to-all-done.3 = bf16[16,48,128]{2,1,0:T(8,128)(2,1)S(1)} async-done(((bf16[16,48,128]{2,1,0:T(8,128)(2,1)}), bf16[16,48,128]{2,1,0:T(8,128)(2,1)S(1)}, u32[]{:S(2)}, u32[]{:S(2)}) %all-to-all-start.3) | async-done | bytes 196640 | tf_op jit(solution)/shard_map/all_to_all | solution.py:321
  99.2 0.8 fusion.1
  100.0 0.7 collective-permute-done.10.got_ref
  100.7 0.9 shard_map.172
  (26 shorter events, 0.1 us)
Async XLA Ops:
  0.6 20.9 %copy-start = (bf16[1024,256]{1,0:T(8,128)(2,1)S(1)}, bf16[1024,256]{1,0:T(8,128)(2,1)}, u32[]{:S(2)}) copy-start(bf16[1024,256]{1,0:T(8,128)(2,1)} %param.15) | copy-start | bytes 1572868
  0.6 18.3 %collective-permute-start.2 = (bf16[256,256]{1,0:T(8,128)(2,1)}, bf16[256,256]{1,0:T(8,128)(2,1)S(1)}, u32[]{:S(2)}, u32[]{:S(2)}) collective-permute-start(bf16[256,256]{1,0:T(8,128)(2,1)} %param.13), channel_id=1, source_target_pairs={{0,6},{2,4},{4,2},{6,0},{1,7},{3,5},{5,3},{7,1},{8,14},{10,12},{12... | collective-permute-start | bytes 393224 | tf_op jit(solution)/shard_map/ppermute | solution.py:325
  5.8 13.2 %collective-permute-start.1 = (bf16[256,256]{1,0:T(8,128)(2,1)}, bf16[256,256]{1,0:T(8,128)(2,1)S(1)}, u32[]{:S(2)}, u32[]{:S(2)}) collective-permute-start(bf16[256,256]{1,0:T(8,128)(2,1)} %param.13), channel_id=1, source_target_pairs={{0,4},{2,6},{4,0},{6,2},{1,5},{3,7},{5,1},{7,3},{8,12},{10,14},{12... | collective-permute-start | bytes 393224 | tf_op jit(solution)/shard_map/ppermute | solution.py:325
  5.8 13.2 %collective-permute-start = (bf16[256,256]{1,0:T(8,128)(2,1)}, bf16[256,256]{1,0:T(8,128)(2,1)S(1)}, u32[]{:S(2)}, u32[]{:S(2)}) collective-permute-start(bf16[256,256]{1,0:T(8,128)(2,1)} %param.13), channel_id=1, source_target_pairs={{0,2},{2,0},{4,6},{6,4},{1,3},{3,1},{5,7},{7,5},{8,10},{10,8},{12,... | collective-permute-start | bytes 393224 | tf_op jit(solution)/shard_map/ppermute | solution.py:325
  7.8 13.0 %all-to-all-start = ((s32[32,1,8]{2,1,0:T(1,128)}), s32[32,1,8]{2,1,0:T(1,128)S(1)}, u32[]{:S(2)}, u32[]{:S(2)}) async-start(s32[32,1,8]{2,1,0:T(1,128)} %bitcast.2), calls=%async_computation | async-start | bytes 32768 | tf_op jit(solution)/shard_map/all_to_all | solution.py:321
  13.8 5.2 %copy-start.8 = (bf16[256,256]{1,0:T(8,128)(2,1)S(1)}, bf16[256,256]{1,0:T(8,128)(2,1)}, u32[]{:S(2)}) copy-start(bf16[256,256]{1,0:T(8,128)(2,1)} %param.13) | copy-start | bytes 393220
  19.1 15.9 %copy-start.6 = (bf16[4,256,256]{2,1,0:T(8,128)(2,1)}, bf16[4,256,256]{2,1,0:T(8,128)(2,1)S(1)}, u32[]{:S(2)}) copy-start(bf16[4,256,256]{2,1,0:T(8,128)(2,1)S(1)} %pad_maximum_fusion.refs_4_) | copy-start | bytes 1572868
  20.8 15.1 %collective-permute-start.3 = (bf16[4,256,256]{2,1,0:T(8,128)(2,1)S(1)}, bf16[4,256,256]{2,1,0:T(8,128)(2,1)S(1)}, u32[]{:S(2)}, u32[]{:S(2)}) collective-permute-start(bf16[4,256,256]{2,1,0:T(8,128)(2,1)S(1)} %pad_maximum_fusion.refs_4_), channel_id=1, source_target_pairs={{0,1},{1,0},{2,3},{3,2},{4,5},{5,4},{6,7},{7,6},{8,9},{9,8},{10,11... | collective-permute-start | bytes 1572872 | tf_op jit(solution)/shard_map/ppermute | solution.py:325
  23.4 12.5 %all-to-all-start.1 = ((bf16[32,8,256]{2,1,0:T(8,128)(2,1)}), bf16[32,8,256]{2,1,0:T(8,128)(2,1)S(1)}, u32[]{:S(2)}, u32[]{:S(2)}) async-start(bf16[32,8,256]{2,1,0:T(8,128)(2,1)} %bitcast.12), calls=%async_computation.1 | async-start | bytes 262144 | tf_op jit(solution)/shard_map/all_to_all | solution.py:321
  35.9 0.7 copy-start.7
  35.9 0.8 copy-start.9
  51.7 12.4 %copy-start.1 = (s32[1024]{0:T(1024)S(1)}, s32[1024]{0:T(1024)}, u32[]{:S(2)}) copy-start(s32[1024]{0:T(1024)} %param.19) | copy-start | bytes 12292
  51.7 12.4 %copy-start.2 = (s32[1024]{0:T(1024)S(1)}, s32[1024]{0:T(1024)}, u32[]{:S(2)}) copy-start(s32[1024]{0:T(1024)} %param.24) | copy-start | bytes 12292
  51.7 12.3 %copy-start.3 = (bf16[2048,256]{1,0:T(8,128)(2,1)S(1)}, bf16[2048,256]{1,0:T(8,128)(2,1)}, u32[]{:S(2)}) copy-start(bf16[2048,256]{1,0:T(8,128)(2,1)} %get-tuple-element.36.refs_2_) | copy-start | bytes 3145732
  51.7 1.8 %collective-permute-start.5 = (bf16[16,64,128]{2,1,0:T(8,128)(2,1)}, bf16[16,64,128]{2,1,0:T(8,128)(2,1)S(1)}, u32[]{:S(2)}, u32[]{:S(2)}) collective-permute-start(bf16[16,64,128]{2,1,0:T(8,128)(2,1)} %get-tuple-element.35), channel_id=1, source_target_pairs={{0,8},{8,0},{1,9},{9,1},{2,10},{10,2},{3,11},{11,3},{4,12},{12,4},... | collective-permute-start | bytes 786440 | tf_op jit(solution)/shard_map/ppermute | solution.py:325
  53.5 1.0 copy-start.4
  54.5 7.5 %copy-start.11 = (bf16[2,256,256]{2,1,0:T(8,128)(2,1)S(1)}, bf16[2,256,256]{2,1,0:T(8,128)(2,1)}, u32[]{:S(2)}) copy-start(bf16[2,256,256]{2,1,0:T(8,128)(2,1)} %get-tuple-element.37) | copy-start | bytes 786436
  54.5 9.5 %copy-start.10 = (bf16[2,256,256]{2,1,0:T(8,128)(2,1)S(1)}, bf16[2,256,256]{2,1,0:T(8,128)(2,1)}, u32[]{:S(2)}) copy-start(bf16[2,256,256]{2,1,0:T(8,128)(2,1)} %get-tuple-element.33) | copy-start | bytes 786436
  55.3 29.0 %all-to-all-start.2 = ((bf16[16,80,128]{2,1,0:T(8,128)(2,1)}), bf16[16,80,128]{2,1,0:T(8,128)(2,1)S(1)}, u32[]{:S(2)}, u32[]{:S(2)}) async-start(bf16[16,80,128]{2,1,0:T(8,128)(2,1)} %shard_map.167), calls=%async_computation.2 | async-start | bytes 655360 | tf_op jit(solution)/shard_map/all_to_all | solution.py:321
  62.0 12.6 %collective-permute-start.6 = (bf16[2,256,256]{2,1,0:T(8,128)(2,1)S(1)}, bf16[2,256,256]{2,1,0:T(8,128)(2,1)S(1)}, u32[]{:S(2)}, u32[]{:S(2)}) collective-permute-start(bf16[2,256,256]{2,1,0:T(8,128)(2,1)S(1)} %copy-done.11), channel_id=1, source_target_pairs={{0,1},{1,0},{2,3},{3,2},{4,5},{5,4},{6,7},{7,6},{8,9},{9,8},{10,11... | collective-permute-start | bytes 786440 | tf_op jit(solution)/shard_map/ppermute | solution.py:325
  64.0 15.2 %collective-permute-start.4 = (bf16[2,256,256]{2,1,0:T(8,128)(2,1)S(1)}, bf16[2,256,256]{2,1,0:T(8,128)(2,1)S(1)}, u32[]{:S(2)}, u32[]{:S(2)}) collective-permute-start(bf16[2,256,256]{2,1,0:T(8,128)(2,1)S(1)} %copy-done.10), channel_id=1, source_target_pairs={{0,1},{1,0},{2,3},{3,2},{4,5},{5,4},{6,7},{7,6},{8,9},{9,8},{10,11... | collective-permute-start | bytes 786440 | tf_op jit(solution)/shard_map/ppermute | solution.py:325
  64.1 15.1 %copy-start.5 = (bf16[4,256,256]{2,1,0:T(8,128)(2,1)S(1)}, bf16[4,256,256]{2,1,0:T(8,128)(2,1)}, u32[]{:S(2)}) copy-start(bf16[4,256,256]{2,1,0:T(8,128)(2,1)} %get-tuple-element.32) | copy-start | bytes 1572868
  79.9 16.0 %collective-permute-start.7 = (bf16[256,256]{1,0:T(8,128)(2,1)}, bf16[256,256]{1,0:T(8,128)(2,1)S(1)}, u32[]{:S(2)}, u32[]{:S(2)}) collective-permute-start(bf16[256,256]{1,0:T(8,128)(2,1)} %get-tuple-element.48), channel_id=1, source_target_pairs={{0,6},{2,4},{4,2},{6,0},{1,7},{3,5},{5,3},{7,1},{8,14},{10,12},{12... | collective-permute-start | bytes 393224 | tf_op jit(solution)/shard_map/ppermute | solution.py:325
  83.2 12.7 %collective-permute-start.8 = (bf16[256,256]{1,0:T(8,128)(2,1)S(1)}, bf16[256,256]{1,0:T(8,128)(2,1)S(1)}, u32[]{:S(2)}, u32[]{:S(2)}) collective-permute-start(bf16[256,256]{1,0:T(8,128)(2,1)S(1)} %get-tuple-element.47), channel_id=1, source_target_pairs={{0,4},{2,6},{4,0},{6,2},{1,5},{3,7},{5,1},{7,3},{8,12},{10,14},{12... | collective-permute-start | bytes 393224 | tf_op jit(solution)/shard_map/ppermute | solution.py:325
  83.2 12.7 %collective-permute-start.9 = (bf16[256,256]{1,0:T(8,128)(2,1)S(1)}, bf16[256,256]{1,0:T(8,128)(2,1)S(1)}, u32[]{:S(2)}, u32[]{:S(2)}) collective-permute-start(bf16[256,256]{1,0:T(8,128)(2,1)S(1)} %get-tuple-element.49), channel_id=1, source_target_pairs={{0,2},{2,0},{4,6},{6,4},{1,3},{3,1},{5,7},{7,5},{8,10},{10,8},{12,... | collective-permute-start | bytes 393224 | tf_op jit(solution)/shard_map/ppermute | solution.py:325
  85.0 14.2 %all-to-all-start.3 = ((bf16[16,48,128]{2,1,0:T(8,128)(2,1)}), bf16[16,48,128]{2,1,0:T(8,128)(2,1)S(1)}, u32[]{:S(2)}, u32[]{:S(2)}) async-start(bf16[16,48,128]{2,1,0:T(8,128)(2,1)} %shard_map.168), calls=%async_computation.3 | async-start | bytes 393216 | tf_op jit(solution)/shard_map/all_to_all | solution.py:321
  99.2 1.4 %collective-permute-start.10 = (bf16[768,128]{1,0:T(8,128)(2,1)S(1)}, bf16[768,128]{1,0:T(8,128)(2,1)S(1)}, u32[]{:S(2)}, u32[]{:S(2)}) collective-permute-start(bf16[768,128]{1,0:T(8,128)(2,1)S(1)} %bitcast.30), channel_id=1, source_target_pairs={{0,8},{8,0},{1,9},{9,1},{2,10},{10,2},{3,11},{11,3},{4,12},{12,4},... | collective-permute-start | bytes 589832 | tf_op jit(solution)/shard_map/ppermute | solution.py:325

commit v10 on v7

--- a/solution.py
+++ b/solution.py
@@ -22,6 +22,10 @@
 
 def nt(a, b):
     return lax.dot_general(a, b, (((1,), (1,)), ((), ())), preferred_element_type=F32)
+
+
+def tn(a, b):
+    return lax.dot_general(a, b, (((0,), (0,)), ((), ())), preferred_element_type=F32)
 
 
 def pieces(values, count):
@@ -72,6 +76,11 @@
             out[:, at] = got.astype(BF)
             if ids is neg_id:
                 neg_out[at, :] = got.T.astype(BF)
+
+
+def pick_kernel(table_ref, ids_ref, out_ref):
+    hot = onehot(ids_ref[...], 0, table_ref.shape[0])
+    out_ref[...] = tn(hot, table_ref[...]).astype(BF)
 
 
 def edge_kernel(
@@ -124,8 +133,8 @@
         loads[-1].start()
         return loads[-1]
 
+    head_loads = [load(near_hbm, near_ref), load(far_hbm, far_ref)]
     rel_loads = [load(rel_hbm.at[which], rel_ref.at[which]) for which in [*range(1, quals + 1), 0]]
-    head_loads = [load(near_hbm, near_ref), load(far_hbm, far_ref)]
     tails_load = load(tails_hbm, tails_ref)
     neg_load = load(neg_hbm, neg_ref)
     negt_load = load(negt_hbm, negt_ref)
@@ -134,13 +143,6 @@
     proj_hi, proj_lo = pieces(proj_ref[...], 2)
     projt_hi, projt_lo = pieces(proj_ref[...].T, 2)
     rows = [nn(fetched_t, onehot(ref_ids[k : k + 1, :], 0, slots)) for k in range(quals)]
-    for copy in rel_loads:
-        copy.wait()
-    composed = rel_ref[1] * rows[0]
-    for k in range(1, quals):
-        composed = composed + rel_ref[k + 1] * rows[k]
-    comp_hi, comp_lo = pieces(composed, 2)
-    relation = rel_ref[0] + (nn(projt_hi, comp_hi) + (nn(projt_hi, comp_lo) + nn(projt_lo, comp_hi)))
     for copy in head_loads:
         copy.wait()
     offset = jnp.bitwise_xor(head_id[...] // head_rows, member_ref[0])
@@ -148,7 +150,17 @@
     heads = jnp.zeros((width, edges), F32)
     for first, table in ((0, near_ref), (half, far_ref)):
         for owner in range(half):
-            heads = heads + nn(flip(table[owner]), onehot(head_slot, (first + owner) * head_rows, head_rows))
+            heads = heads + tn(table[owner], onehot(head_slot, (first + owner) * head_rows, head_rows))
+    for copy in rel_loads:
+        copy.wait()
+    composed = rel_ref[1] * rows[0]
+    for k in range(1, quals):
+        composed = composed + rel_ref[k + 1] * rows[k]
+    comp_hi, comp_lo = pieces(composed, 2)
+    relation = rel_ref[0] + nn(
+        jnp.concatenate([projt_hi, projt_hi, projt_lo], axis=1),
+        jnp.concatenate([comp_hi, comp_lo, comp_hi], axis=0),
+    )
     query = (heads * relation).astype(BF)
     query_f = query.astype(F32)
     tails_load.wait()
@@ -190,15 +202,22 @@
 
     relation_grad = query_grad * heads
     rg_hi, rg_lo = pieces(relation_grad, 2)
-    comp_grad = nn(proj_hi, rg_hi) + (nn(proj_hi, rg_lo) + nn(proj_lo, rg_hi))
-    rel_sum = nt(onehot(rel_id[...], 0, rel_rows), rg_hi)
-    fetched_sum = jnp.zeros((slots, width), F32)
+    comp_grad = nn(
+        jnp.concatenate([proj_hi, proj_hi, proj_lo], axis=1), jnp.concatenate([rg_hi, rg_lo, rg_hi], axis=0)
+    )
+    rel_hots, rel_terms = [onehot(rel_id[...], 0, rel_rows)], [rg_hi]
+    ref_hots, ref_terms = [], []
     for k in range(quals):
-        hot = onehot(ref_ids[k : k + 1, :], 0, slots)
-        rel_sum = rel_sum + nt(onehot(qual_rel[k : k + 1, :], 0, rel_rows), (comp_grad * rows[k]).astype(BF))
-        fetched_sum = fetched_sum + nt(hot, (comp_grad * rel_ref[k + 1]).astype(BF))
+        rel_hots.append(onehot(qual_rel[k : k + 1, :], 0, rel_rows))
+        rel_terms.append((comp_grad * rows[k]).astype(BF))
+        ref_hots.append(onehot(ref_ids[k : k + 1, :], 0, slots))
+        ref_terms.append((comp_grad * rel_ref[k + 1]).astype(BF))
+    rel_sum = nt(jnp.concatenate(rel_hots, axis=1), jnp.concatenate(rel_terms, axis=1))
+    fetched_sum = nt(jnp.concatenate(ref_hots, axis=1), jnp.concatenate(ref_terms, axis=1))
     sums[:rel_rows, :] = rel_sum
-    sums[rel_rows : rel_rows + width, :] = nt(comp_hi, rg_hi) + (nt(comp_hi, rg_lo) + nt(comp_lo, rg_hi))
+    sums[rel_rows : rel_rows + width, :] = nt(
+        jnp.concatenate([comp_hi, comp_hi, comp_lo], axis=1), jnp.concatenate([rg_hi, rg_lo, rg_hi], axis=1)
+    )
     if sums.shape[0] > rel_rows + width:
         sums[rel_rows + width :, :] = jnp.zeros((sums.shape[0] - rel_rows - width, width), F32)
     pairs = fetched_sum.reshape(-1, cores, chips // PAIRS, cap, width)
@@ -362,7 +381,8 @@
     )
     arrived, rel_looked, head_near = lax.optimization_barrier((arrived, rel_looked, head_near))
     head_far = swap(head_near, "near")
-    picked = qual_table.at[arrived].get(mode="promise_in_bounds")
+    (picked,) = call(pick_kernel, [((slots, width), BF)], [], 1, 16, qual_table, arrived.reshape(1, slots))
+    picked = picked.reshape(devices, cap, width)
     fetched = exchange(picked, AXES).reshape(slots, width)
     tails, neg_t, neg = call(
         tail_lookup_kernel,

time: 92.7 us -> 89.9 us (0.970)
  local copies, waits for them, and re-layouts: 5.26 us -> 3.45 us
  waiting for transfers between devices: 8.93 us -> 10.5 us
  starting transfers between devices: 36.1 us -> 35.1 us
    gather x1 -> x0, local copies, waits for them, and re-layouts: 1.81 us -> none  [body(): picked = qual_table.at[arrived].get(mode='promise_in_bounds')]
    ppermute x10, waiting for transfers between devices: 2.93 us -> 4.39 us  [swap(): lax.ppermute(values, axis, [(i, i ^ offset) for i in range(lax.axis_size(...]
    pallas_call x9 -> x10, Pallas kernels: 38.8 us -> 38 us  [call(): pl.pallas_call(kernel, out_shape=shapes, grid=grid, in_specs=[pl.BlockSpe...]
  transfers between devices with their start and end apart: 14 -> 14, of which waited for: 7 -> 7; matrix products, arithmetic and copies ran while one was open for 4% -> 1% of each run, Pallas kernels for 24% -> 26%
where the time goes in v10:
time: 89.9 us; the launch traced here: 89.4 us
  Pallas kernels  38 us (42%)
  starting transfers between devices  35.1 us (39%)
  waiting for transfers between devices  10.5 us (12%)
  local copies, waits for them, and re-layouts  3.45 us (4%)
  between operations  1.47 us (2%)
  other arithmetic  0.95 us (1%)
    pallas_call x10, Pallas kernels, call(): pl.pallas_call(kernel, out_shape=shapes, grid=grid, in_specs=[pl.BlockSpe...  38 us
    all_to_all x4, starting transfers between devices, exchange(): return lax.all_to_all(values, axes, split_axis=0, concat_axis=0, tiled=True)  22.8 us
    ppermute x10, starting transfers between devices, swap(): lax.ppermute(values, axis, [(i, i ^ offset) for i in range(lax.axis_size(...  12.3 us
    all_to_all x4, waiting for transfers between devices, exchange(): return lax.all_to_all(values, axes, split_axis=0, concat_axis=0, tiled=True)  6.07 us
    ppermute x10, waiting for transfers between devices, swap(): lax.ppermute(values, axis, [(i, i ^ offset) for i in range(lax.axis_size(...  4.39 us
    unnamed x20, local copies, waits for them, and re-layouts  1.82 us
  transfers between devices with their start and end apart: 14, of which 7 were waited for; matrix products, arithmetic and copies ran while one was open for 1% of the time, Pallas kernels for 26%

profile of v10, /device:TPU:0, one launch (start us, length us, event | category | flops | bytes accessed | tf_op | source)
XLA Modules:
  0.0 89.4 jit_solution(14439173563487241838)
XLA Ops:
  0.6 5.1 %collective-permute-start.2 = (bf16[256,256]{1,0:T(8,128)(2,1)}, bf16[256,256]{1,0:T(8,128)(2,1)S(1)}, u32[]{:S(2)}, u32[]{:S(2)}) collective-permute-start(bf16[256,256]{1,0:T(8,128)(2,1)} %param.13), channel_id=1, source_target_pairs={{0,6},{2,4},{4,2},{6,0},{1,7},{3,5},{5,3},{7,1},{8,14},{10,12},{12... | collective-permute-start | bytes 393224 | tf_op jit(solution)/shard_map/ppermute | solution.py:324
  5.7 0.0 collective-permute-start.1
  5.7 0.6 collective-permute-start
  6.4 1.4 %all_to_all.17 = s32[32,1,8]{2,0,1:T(8,128)} reshape(s32[256]{0:T(256)} %param.23) | data formatting | bytes 2048 | tf_op jit(solution)/shard_map/all_to_all | solution.py:320
  7.8 6.0 %all-to-all-start = ((s32[32,1,8]{2,1,0:T(1,128)}), s32[32,1,8]{2,1,0:T(1,128)S(1)}, u32[]{:S(2)}, u32[]{:S(2)}) async-start(s32[32,1,8]{2,1,0:T(1,128)} %bitcast.2), calls=%async_computation | async-start | bytes 32768 | tf_op jit(solution)/shard_map/all_to_all | solution.py:320
  13.8 0.0 copy-start.8
  13.8 0.0 copy-start
  13.8 5.1 %shard_map.164.refs_3_ = f32[5,256,1024]{2,1,0:T(8,128)} custom-call(f32[512,256]{1,0:T(8,128)} %rel_ref.1, s32[1,1024]{1,0:T(1,128)} %bitcast.49, s32[4,1024]{1,0:T(4,128)} %bitcast.46), custom_call_target="tpu_custom_call" | custom-call | flops 5368709120 | bytes 1048576 | tf_op jit(solution)/shard_map/pallas_call | solution.py:306
  18.9 0.0 collective-permute-done.1
  19.0 0.0 collective-permute-done
  19.0 0.1 pad_maximum_fusion.refs_4_
  19.1 0.0 copy-start.6
  19.1 1.7 %all-to-all-done = s32[32,1,8]{2,1,0:T(1,128)S(1)} async-done(((s32[32,1,8]{2,1,0:T(1,128)}), s32[32,1,8]{2,1,0:T(1,128)S(1)}, u32[]{:S(2)}, u32[]{:S(2)}) %all-to-all-start) | async-done | bytes 1056 | tf_op jit(solution)/shard_map/all_to_all | solution.py:320
  20.8 0.6 collective-permute-start.3
  21.4 0.1 reshape.55.ids_ref
  21.5 1.0 %shard_map.166 = bf16[256,256]{1,0:T(8,128)(2,1)} custom-call(bf16[1024,256]{1,0:T(8,128)(2,1)S(1)} %copy-done, s32[1,256]{1,0:T(1,128)S(1)} %reshape.55.ids_ref), custom_call_target="tpu_custom_call" | custom-call | flops 1073741824 | bytes 1048576 | tf_op jit(solution)/shard_map/pallas_call | solution.py:306
  22.5 4.3 %all-to-all-start.1 = ((bf16[32,8,256]{2,1,0:T(8,128)(2,1)}), bf16[32,8,256]{2,1,0:T(8,128)(2,1)S(1)}, u32[]{:S(2)}, u32[]{:S(2)}) async-start(bf16[32,8,256]{2,1,0:T(8,128)(2,1)} %bitcast.12), calls=%async_computation.1 | async-start | bytes 262144 | tf_op jit(solution)/shard_map/all_to_all | solution.py:320
  26.8 7.3 %shard_map.165 = (bf16[256,1024]{1,0:T(8,128)(2,1)}, bf16[256,1024]{1,0:T(8,128)(2,1)}, bf16[1024,256]{1,0:T(8,128)(2,1)}) custom-call(bf16[4096,256]{1,0:T(8,128)(2,1)} %tail_ref.1, s32[1,1024]{1,0:T(1,128)} %bitcast.32, s32[1,1024]{1,0:T(1,128)} %bitcast.35), custom_call_target="tpu_custom_call" | custom-call | flops 7516192768 | bytes 1048576 | tf_op jit(solution)/shard_map/pallas_call | solution.py:306
  34.8 1.1 %all-to-all-done.1 = bf16[32,8,256]{2,1,0:T(8,128)(2,1)S(1)} async-done(((bf16[32,8,256]{2,1,0:T(8,128)(2,1)}), bf16[32,8,256]{2,1,0:T(8,128)(2,1)S(1)}, u32[]{:S(2)}, u32[]{:S(2)}) %all-to-all-start.1) | async-done | bytes 131104 | tf_op jit(solution)/shard_map/all_to_all | solution.py:320
  35.9 0.6 copy-done.7
  36.5 0.2 copy-done.9
  36.7 13.7 %shard_map.167 = (bf16[4,256,256]{2,1,0:T(8,128)(2,1)}, bf16[4,256,256]{2,1,0:T(8,128)(2,1)}, bf16[16,64,128]{2,1,0:T(8,128)(2,1)}, bf16[16,64,128]{2,1,0:T(8,128)(2,1)}, bf16[2048,256]{1,0:T(8,128)(2,1)}) custom-call(s32[1]{0:T(128)S(6)} %copy.23.refs_0_, s32[1]{0:T(128)} %bitcast.refs_1_.core_ref, s32[1]{0:T(128)} %bitcast.1.refs_2_, ...), custom_call_target="tpu_custom_call" | custom-call | flops 15032385536 | bytes 1048576 | tf_op jit(solution)/shard_map/pallas_call | solution.py:306
  50.5 0.0 copy-start.1
  50.5 0.0 copy-start.2
  50.5 0.0 copy-start.3
  50.5 0.1 collective-permute-start.5
  50.6 1.4 %collective-permute-start.4 = (bf16[4,256,256]{2,1,0:T(8,128)(2,1)}, bf16[4,256,256]{2,1,0:T(8,128)(2,1)S(1)}, u32[]{:S(2)}, u32[]{:S(2)}) collective-permute-start(bf16[4,256,256]{2,1,0:T(8,128)(2,1)} %get-tuple-element.32), channel_id=1, source_target_pairs={{0,1},{1,0},{2,3},{3,2},{4,5},{5,4},{6,7},{7,6},{8,9},{9,8},{10,11... | collective-permute-start | bytes 1572872 | tf_op jit(solution)/shard_map/ppermute | solution.py:324
  51.9 0.4 collective-permute-done.5.got_ref
  52.3 0.9 %copy-done.4 = bf16[16,64,128]{2,1,0:T(8,128)(2,1)S(1)} copy-done((bf16[16,64,128]{2,1,0:T(8,128)(2,1)S(1)}, bf16[16,64,128]{2,1,0:T(8,128)(2,1)}, u32[]{:S(2)}) %copy-start.4) | copy-done | bytes 262168
  53.3 0.8 shard_map.169
  54.0 5.8 %all-to-all-start.2 = ((bf16[16,80,128]{2,1,0:T(8,128)(2,1)}), bf16[16,80,128]{2,1,0:T(8,128)(2,1)S(1)}, u32[]{:S(2)}, u32[]{:S(2)}) async-start(bf16[16,80,128]{2,1,0:T(8,128)(2,1)} %shard_map.169), calls=%async_computation.2 | async-start | bytes 655360 | tf_op jit(solution)/shard_map/all_to_all | solution.py:320
  59.8 0.1 reshape.59
  59.9 0.1 reshape.60.asked
  60.0 3.5 %shard_map.168.refs_3_ = f32[4096,256]{1,0:T(8,128)} custom-call(s32[1,1024]{1,0:T(1,128)S(1)} %bitcast.33, s32[1,1024]{1,0:T(1,128)S(1)} %bitcast.36, bf16[2048,256]{1,0:T(8,128)(2,1)S(1)} %copy-done.3), custom_call_target="tpu_custom_call" | custom-call | flops 3221225472 | bytes 1048576 | tf_op jit(solution)/shard_map/pallas_call | solution.py:306
  63.5 3.4 %collective-permute-done.4 = bf16[4,256,256]{2,1,0:T(8,128)(2,1)S(1)} collective-permute-done((bf16[4,256,256]{2,1,0:T(8,128)(2,1)}, bf16[4,256,256]{2,1,0:T(8,128)(2,1)S(1)}, u32[]{:S(2)}, u32[]{:S(2)}) %collective-permute-start.4) | collective-permute-done | bytes 524320 | tf_op jit(solution)/shard_map/ppermute | solution.py:324
  66.9 0.1 fusion.4
  67.0 1.1 %collective-permute-start.6 = (bf16[256,256]{1,0:T(8,128)(2,1)S(1)}, bf16[256,256]{1,0:T(8,128)(2,1)S(1)}, u32[]{:S(2)}, u32[]{:S(2)}) collective-permute-start(bf16[256,256]{1,0:T(8,128)(2,1)S(1)} %get-tuple-element.47), channel_id=1, source_target_pairs={{0,2},{2,0},{4,6},{6,4},{1,3},{3,1},{5,7},{7,5},{8,10},{10,8},{12,... | collective-permute-start | bytes 393224 | tf_op jit(solution)/shard_map/ppermute | solution.py:324
  68.1 2.9 %collective-permute-start.7 = (bf16[256,256]{1,0:T(8,128)(2,1)S(1)}, bf16[256,256]{1,0:T(8,128)(2,1)S(1)}, u32[]{:S(2)}, u32[]{:S(2)}) collective-permute-start(bf16[256,256]{1,0:T(8,128)(2,1)S(1)} %get-tuple-element.46), channel_id=1, source_target_pairs={{0,4},{2,6},{4,0},{6,2},{1,5},{3,7},{5,1},{7,3},{8,12},{10,14},{12... | collective-permute-start | bytes 393224 | tf_op jit(solution)/shard_map/ppermute | solution.py:324
  71.0 0.5 collective-permute-start.8
  71.4 0.1 all-to-all-done.2.got_ref
  71.5 0.7 shard_map.170
  72.2 6.7 %all-to-all-start.3 = ((bf16[16,48,128]{2,1,0:T(8,128)(2,1)}), bf16[16,48,128]{2,1,0:T(8,128)(2,1)S(1)}, u32[]{:S(2)}, u32[]{:S(2)}) async-start(bf16[16,48,128]{2,1,0:T(8,128)(2,1)} %shard_map.170), calls=%async_computation.3 | async-start | bytes 393216 | tf_op jit(solution)/shard_map/all_to_all | solution.py:320
  78.9 3.5 %shard_map.171 = f32[4096,256]{1,0:T(8,128)} custom-call(s32[1,1024]{1,0:T(1,128)S(1)} %bitcast.34, s32[1,1024]{1,0:T(1,128)S(1)} %bitcast.37, bf16[2048,256]{1,0:T(8,128)(2,1)S(1)} %copy-done.3, f32[4096,256]{1,0:T(8,128)} %shard_map.168.refs_3_), custom_call_target="tpu_custom_call", output_to_operand_aliasing={{}: (3, {})} | custom-call | flops 3221225472 | bytes 1048576 | tf_op jit(solution)/shard_map/pallas_call | solution.py:306
  82.5 1.4 %shard_map.172 = f32[1024,256]{1,0:T(8,128)} custom-call(s32[1]{0:T(128)} %bitcast.refs_1_.core_ref, bf16[16,80,128]{2,1,0:T(8,128)(2,1)S(1)} %all-to-all-done.2.got_ref, s32[2,128]{1,0:T(2,128)S(1)} %reshape.60.asked), custom_call_target="tpu_custom_call" | custom-call | flops 2147483648 | bytes 1048576 | tf_op jit(solution)/shard_map/pallas_call | solution.py:306
  83.9 3.2 %all-to-all-done.3 = bf16[16,48,128]{2,1,0:T(8,128)(2,1)S(1)} async-done(((bf16[16,48,128]{2,1,0:T(8,128)(2,1)}), bf16[16,48,128]{2,1,0:T(8,128)(2,1)S(1)}, u32[]{:S(2)}, u32[]{:S(2)}) %all-to-all-start.3) | async-done | bytes 196640 | tf_op jit(solution)/shard_map/all_to_all | solution.py:320
  87.1 0.8 fusion.1
  87.9 0.7 collective-permute-done.9.got_ref
  88.5 0.9 %shard_map.173 = (f32[512,256]{1,0:T(8,128)}, f32[256,256]{1,0:T(8,128)}) custom-call(s32[1]{0:T(128)} %bitcast.refs_1_.core_ref, bf16[768,128]{1,0:T(8,128)(2,1)S(1)} %bitcast.31, bf16[768,128]{1,0:T(8,128)(2,1)S(1)} %collective-permute-done.9.got_ref), custom_call_target="tpu_custom_call" | custom-call | flops 1073741824 | bytes 1048576 | tf_op jit(solution)/shard_map/pallas_call | solution.py:306
  (18 shorter events, 0.0 us)
Async XLA Ops:
  0.6 18.3 %collective-permute-start.2 = (bf16[256,256]{1,0:T(8,128)(2,1)}, bf16[256,256]{1,0:T(8,128)(2,1)S(1)}, u32[]{:S(2)}, u32[]{:S(2)}) collective-permute-start(bf16[256,256]{1,0:T(8,128)(2,1)} %param.13), channel_id=1, source_target_pairs={{0,6},{2,4},{4,2},{6,0},{1,7},{3,5},{5,3},{7,1},{8,14},{10,12},{12... | collective-permute-start | bytes 393224 | tf_op jit(solution)/shard_map/ppermute | solution.py:324
  5.7 13.2 %collective-permute-start.1 = (bf16[256,256]{1,0:T(8,128)(2,1)}, bf16[256,256]{1,0:T(8,128)(2,1)S(1)}, u32[]{:S(2)}, u32[]{:S(2)}) collective-permute-start(bf16[256,256]{1,0:T(8,128)(2,1)} %param.13), channel_id=1, source_target_pairs={{0,4},{2,6},{4,0},{6,2},{1,5},{3,7},{5,1},{7,3},{8,12},{10,14},{12... | collective-permute-start | bytes 393224 | tf_op jit(solution)/shard_map/ppermute | solution.py:324
  5.7 13.2 %collective-permute-start = (bf16[256,256]{1,0:T(8,128)(2,1)}, bf16[256,256]{1,0:T(8,128)(2,1)S(1)}, u32[]{:S(2)}, u32[]{:S(2)}) collective-permute-start(bf16[256,256]{1,0:T(8,128)(2,1)} %param.13), channel_id=1, source_target_pairs={{0,2},{2,0},{4,6},{6,4},{1,3},{3,1},{5,7},{7,5},{8,10},{10,8},{12,... | collective-permute-start | bytes 393224 | tf_op jit(solution)/shard_map/ppermute | solution.py:324
  7.8 13.0 %all-to-all-start = ((s32[32,1,8]{2,1,0:T(1,128)}), s32[32,1,8]{2,1,0:T(1,128)S(1)}, u32[]{:S(2)}, u32[]{:S(2)}) async-start(s32[32,1,8]{2,1,0:T(1,128)} %bitcast.2), calls=%async_computation | async-start | bytes 32768 | tf_op jit(solution)/shard_map/all_to_all | solution.py:320
  13.8 5.2 %copy-start.8 = (bf16[256,256]{1,0:T(8,128)(2,1)S(1)}, bf16[256,256]{1,0:T(8,128)(2,1)}, u32[]{:S(2)}) copy-start(bf16[256,256]{1,0:T(8,128)(2,1)} %param.13) | copy-start | bytes 393220
  13.8 7.7 %copy-start = (bf16[1024,256]{1,0:T(8,128)(2,1)S(1)}, bf16[1024,256]{1,0:T(8,128)(2,1)}, u32[]{:S(2)}) copy-start(bf16[1024,256]{1,0:T(8,128)(2,1)} %table_ref.1) | copy-start | bytes 1572868
  19.1 15.1 %copy-start.6 = (bf16[4,256,256]{2,1,0:T(8,128)(2,1)}, bf16[4,256,256]{2,1,0:T(8,128)(2,1)S(1)}, u32[]{:S(2)}) copy-start(bf16[4,256,256]{2,1,0:T(8,128)(2,1)S(1)} %pad_maximum_fusion.refs_4_) | copy-start | bytes 1572868
  20.8 15.1 %collective-permute-start.3 = (bf16[4,256,256]{2,1,0:T(8,128)(2,1)S(1)}, bf16[4,256,256]{2,1,0:T(8,128)(2,1)S(1)}, u32[]{:S(2)}, u32[]{:S(2)}) collective-permute-start(bf16[4,256,256]{2,1,0:T(8,128)(2,1)S(1)} %pad_maximum_fusion.refs_4_), channel_id=1, source_target_pairs={{0,1},{1,0},{2,3},{3,2},{4,5},{5,4},{6,7},{7,6},{8,9},{9,8},{10,11... | collective-permute-start | bytes 1572872 | tf_op jit(solution)/shard_map/ppermute | solution.py:324
  22.5 13.3 %all-to-all-start.1 = ((bf16[32,8,256]{2,1,0:T(8,128)(2,1)}), bf16[32,8,256]{2,1,0:T(8,128)(2,1)S(1)}, u32[]{:S(2)}, u32[]{:S(2)}) async-start(bf16[32,8,256]{2,1,0:T(8,128)(2,1)} %bitcast.12), calls=%async_computation.1 | async-start | bytes 262144 | tf_op jit(solution)/shard_map/all_to_all | solution.py:320
  35.9 0.7 copy-start.7
  35.9 0.8 copy-start.9
  50.5 9.5 %copy-start.1 = (s32[1024]{0:T(1024)S(1)}, s32[1024]{0:T(1024)}, u32[]{:S(2)}) copy-start(s32[1024]{0:T(1024)} %param.19) | copy-start | bytes 12292
  50.5 9.5 %copy-start.2 = (s32[1024]{0:T(1024)S(1)}, s32[1024]{0:T(1024)}, u32[]{:S(2)}) copy-start(s32[1024]{0:T(1024)} %param.24) | copy-start | bytes 12292
  50.5 9.5 %copy-start.3 = (bf16[2048,256]{1,0:T(8,128)(2,1)S(1)}, bf16[2048,256]{1,0:T(8,128)(2,1)}, u32[]{:S(2)}) copy-start(bf16[2048,256]{1,0:T(8,128)(2,1)} %get-tuple-element.33.refs_2_) | copy-start | bytes 3145732
  50.5 1.8 %collective-permute-start.5 = (bf16[16,64,128]{2,1,0:T(8,128)(2,1)}, bf16[16,64,128]{2,1,0:T(8,128)(2,1)S(1)}, u32[]{:S(2)}, u32[]{:S(2)}) collective-permute-start(bf16[16,64,128]{2,1,0:T(8,128)(2,1)} %get-tuple-element.36), channel_id=1, source_target_pairs={{0,8},{8,0},{1,9},{9,1},{2,10},{10,2},{3,11},{11,3},{4,12},{12,4},... | collective-permute-start | bytes 786440 | tf_op jit(solution)/shard_map/ppermute | solution.py:324
  50.6 16.3 %collective-permute-start.4 = (bf16[4,256,256]{2,1,0:T(8,128)(2,1)}, bf16[4,256,256]{2,1,0:T(8,128)(2,1)S(1)}, u32[]{:S(2)}, u32[]{:S(2)}) collective-permute-start(bf16[4,256,256]{2,1,0:T(8,128)(2,1)} %get-tuple-element.32), channel_id=1, source_target_pairs={{0,1},{1,0},{2,3},{3,2},{4,5},{5,4},{6,7},{7,6},{8,9},{9,8},{10,11... | collective-permute-start | bytes 1572872 | tf_op jit(solution)/shard_map/ppermute | solution.py:324
  52.3 1.0 %copy-start.4 = (bf16[16,64,128]{2,1,0:T(8,128)(2,1)S(1)}, bf16[16,64,128]{2,1,0:T(8,128)(2,1)}, u32[]{:S(2)}) copy-start(bf16[16,64,128]{2,1,0:T(8,128)(2,1)} %get-tuple-element.35.own_ref) | copy-start | bytes 786436
  54.0 17.5 %all-to-all-start.2 = ((bf16[16,80,128]{2,1,0:T(8,128)(2,1)}), bf16[16,80,128]{2,1,0:T(8,128)(2,1)S(1)}, u32[]{:S(2)}, u32[]{:S(2)}) async-start(bf16[16,80,128]{2,1,0:T(8,128)(2,1)} %shard_map.169), calls=%async_computation.2 | async-start | bytes 655360 | tf_op jit(solution)/shard_map/all_to_all | solution.py:320
  60.0 6.9 %copy-start.5 = (bf16[4,256,256]{2,1,0:T(8,128)(2,1)S(1)}, bf16[4,256,256]{2,1,0:T(8,128)(2,1)}, u32[]{:S(2)}) copy-start(bf16[4,256,256]{2,1,0:T(8,128)(2,1)} %get-tuple-element.31) | copy-start | bytes 1572868
  67.0 16.9 %collective-permute-start.6 = (bf16[256,256]{1,0:T(8,128)(2,1)S(1)}, bf16[256,256]{1,0:T(8,128)(2,1)S(1)}, u32[]{:S(2)}, u32[]{:S(2)}) collective-permute-start(bf16[256,256]{1,0:T(8,128)(2,1)S(1)} %get-tuple-element.47), channel_id=1, source_target_pairs={{0,2},{2,0},{4,6},{6,4},{1,3},{3,1},{5,7},{7,5},{8,10},{10,8},{12,... | collective-permute-start | bytes 393224 | tf_op jit(solution)/shard_map/ppermute | solution.py:324
  68.1 15.8 %collective-permute-start.7 = (bf16[256,256]{1,0:T(8,128)(2,1)S(1)}, bf16[256,256]{1,0:T(8,128)(2,1)S(1)}, u32[]{:S(2)}, u32[]{:S(2)}) collective-permute-start(bf16[256,256]{1,0:T(8,128)(2,1)S(1)} %get-tuple-element.46), channel_id=1, source_target_pairs={{0,4},{2,6},{4,0},{6,2},{1,5},{3,7},{5,1},{7,3},{8,12},{10,14},{12... | collective-permute-start | bytes 393224 | tf_op jit(solution)/shard_map/ppermute | solution.py:324
  71.0 12.9 %collective-permute-start.8 = (bf16[256,256]{1,0:T(8,128)(2,1)S(1)}, bf16[256,256]{1,0:T(8,128)(2,1)S(1)}, u32[]{:S(2)}, u32[]{:S(2)}) collective-permute-start(bf16[256,256]{1,0:T(8,128)(2,1)S(1)} %get-tuple-element.45), channel_id=1, source_target_pairs={{0,6},{2,4},{4,2},{6,0},{1,7},{3,5},{5,3},{7,1},{8,14},{10,12},{12... | collective-permute-start | bytes 393224 | tf_op jit(solution)/shard_map/ppermute | solution.py:324
  72.2 14.9 %all-to-all-start.3 = ((bf16[16,48,128]{2,1,0:T(8,128)(2,1)}), bf16[16,48,128]{2,1,0:T(8,128)(2,1)S(1)}, u32[]{:S(2)}, u32[]{:S(2)}) async-start(bf16[16,48,128]{2,1,0:T(8,128)(2,1)} %shard_map.170), calls=%async_computation.3 | async-start | bytes 393216 | tf_op jit(solution)/shard_map/all_to_all | solution.py:320
  87.1 1.4 %collective-permute-start.9 = (bf16[768,128]{1,0:T(8,128)(2,1)S(1)}, bf16[768,128]{1,0:T(8,128)(2,1)S(1)}, u32[]{:S(2)}, u32[]{:S(2)}) collective-permute-start(bf16[768,128]{1,0:T(8,128)(2,1)S(1)} %bitcast.30), channel_id=1, source_target_pairs={{0,8},{8,0},{1,9},{9,1},{2,10},{10,2},{3,11},{11,3},{4,12},{12,4},... | collective-permute-start | bytes 589832 | tf_op jit(solution)/shard_map/ppermute | solution.py:324

commit v11 on v10

--- a/solution.py
+++ b/solution.py
@@ -289,12 +289,10 @@
 
 def tail_kernel(tail_id, neg_id, terms, *refs, skip):
     tail_out = refs[-1]
-    edges = tail_id.shape[1]
     rows = tail_out.shape[0]
     first = (pl.program_id(0) + skip) * rows
-    tail_out[...] = nn(onehot(tail_id[...], first, rows), terms[:edges, :]) + nn(
-        onehot(neg_id[...], first, rows), terms[edges:, :]
-    )
+    hots = [onehot(tail_id[...], first, rows), onehot(neg_id[...], first, rows)]
+    tail_out[...] = nn(jnp.concatenate(hots, axis=1), terms[...])
 
 
 WHOLE = pl.BlockSpec(memory_space=pltpu.VMEM)

time: 89.9 us -> 89.9 us (level)
  no operation moved by 1% of the time
where the time goes in v11:
time: 89.9 us; the launch traced here: 89.4 us
  Pallas kernels  38 us (42%)
  starting transfers between devices  35.1 us (39%)
  waiting for transfers between devices  10.5 us (12%)
  local copies, waits for them, and re-layouts  3.45 us (4%)
  between operations  1.47 us (2%)
  other arithmetic  0.95 us (1%)
    pallas_call x10, Pallas kernels, call(): pl.pallas_call(kernel, out_shape=shapes, grid=grid, in_specs=[pl.BlockSpe...  38 us
    all_to_all x4, starting transfers between devices, exchange(): return lax.all_to_all(values, axes, split_axis=0, concat_axis=0, tiled=True)  22.8 us
    ppermute x10, starting transfers between devices, swap(): lax.ppermute(values, axis, [(i, i ^ offset) for i in range(lax.axis_size(...  12.3 us
    all_to_all x4, waiting for transfers between devices, exchange(): return lax.all_to_all(values, axes, split_axis=0, concat_axis=0, tiled=True)  6.07 us
    ppermute x10, waiting for transfers between devices, swap(): lax.ppermute(values, axis, [(i, i ^ offset) for i in range(lax.axis_size(...  4.39 us
    unnamed x20, local copies, waits for them, and re-layouts  1.82 us
  transfers between devices with their start and end apart: 14, of which 7 were waited for; matrix products, arithmetic and copies ran while one was open for 1% of the time, Pallas kernels for 26%

profile of v11, /device:TPU:0, one launch (start us, length us, event | category | flops | bytes accessed | tf_op | source)
XLA Modules:
  0.0 89.4 jit_solution(8337113553263095727)
XLA Ops:
  0.6 5.1 %collective-permute-start.2 = (bf16[256,256]{1,0:T(8,128)(2,1)}, bf16[256,256]{1,0:T(8,128)(2,1)S(1)}, u32[]{:S(2)}, u32[]{:S(2)}) collective-permute-start(bf16[256,256]{1,0:T(8,128)(2,1)} %param.13), channel_id=1, source_target_pairs={{0,6},{2,4},{4,2},{6,0},{1,7},{3,5},{5,3},{7,1},{8,14},{10,12},{12... | collective-permute-start | bytes 393224 | tf_op jit(solution)/shard_map/ppermute | solution.py:322
  5.7 0.0 collective-permute-start.1
  5.7 0.6 collective-permute-start
  6.4 1.4 %all_to_all.17 = s32[32,1,8]{2,0,1:T(8,128)} reshape(s32[256]{0:T(256)} %param.23) | data formatting | bytes 2048 | tf_op jit(solution)/shard_map/all_to_all | solution.py:318
  7.8 6.0 %all-to-all-start = ((s32[32,1,8]{2,1,0:T(1,128)}), s32[32,1,8]{2,1,0:T(1,128)S(1)}, u32[]{:S(2)}, u32[]{:S(2)}) async-start(s32[32,1,8]{2,1,0:T(1,128)} %bitcast.2), calls=%async_computation | async-start | bytes 32768 | tf_op jit(solution)/shard_map/all_to_all | solution.py:318
  13.8 0.0 copy-start.8
  13.8 0.0 copy-start
  13.8 5.1 %shard_map.164.refs_3_ = f32[5,256,1024]{2,1,0:T(8,128)} custom-call(f32[512,256]{1,0:T(8,128)} %rel_ref.1, s32[1,1024]{1,0:T(1,128)} %bitcast.49, s32[4,1024]{1,0:T(4,128)} %bitcast.46), custom_call_target="tpu_custom_call" | custom-call | flops 5368709120 | bytes 1048576 | tf_op jit(solution)/shard_map/pallas_call | solution.py:304
  18.9 0.0 collective-permute-done.1
  19.0 0.0 collective-permute-done
  19.0 0.1 pad_maximum_fusion.refs_4_
  19.1 0.0 copy-start.6
  19.1 1.7 %all-to-all-done = s32[32,1,8]{2,1,0:T(1,128)S(1)} async-done(((s32[32,1,8]{2,1,0:T(1,128)}), s32[32,1,8]{2,1,0:T(1,128)S(1)}, u32[]{:S(2)}, u32[]{:S(2)}) %all-to-all-start) | async-done | bytes 1056 | tf_op jit(solution)/shard_map/all_to_all | solution.py:318
  20.8 0.6 collective-permute-start.3
  21.4 0.1 reshape.55.ids_ref
  21.5 1.0 %shard_map.166 = bf16[256,256]{1,0:T(8,128)(2,1)} custom-call(bf16[1024,256]{1,0:T(8,128)(2,1)S(1)} %copy-done, s32[1,256]{1,0:T(1,128)S(1)} %reshape.55.ids_ref), custom_call_target="tpu_custom_call" | custom-call | flops 1073741824 | bytes 1048576 | tf_op jit(solution)/shard_map/pallas_call | solution.py:304
  22.5 4.3 %all-to-all-start.1 = ((bf16[32,8,256]{2,1,0:T(8,128)(2,1)}), bf16[32,8,256]{2,1,0:T(8,128)(2,1)S(1)}, u32[]{:S(2)}, u32[]{:S(2)}) async-start(bf16[32,8,256]{2,1,0:T(8,128)(2,1)} %bitcast.12), calls=%async_computation.1 | async-start | bytes 262144 | tf_op jit(solution)/shard_map/all_to_all | solution.py:318
  26.8 7.3 %shard_map.165 = (bf16[256,1024]{1,0:T(8,128)(2,1)}, bf16[256,1024]{1,0:T(8,128)(2,1)}, bf16[1024,256]{1,0:T(8,128)(2,1)}) custom-call(bf16[4096,256]{1,0:T(8,128)(2,1)} %tail_ref.1, s32[1,1024]{1,0:T(1,128)} %bitcast.32, s32[1,1024]{1,0:T(1,128)} %bitcast.35), custom_call_target="tpu_custom_call" | custom-call | flops 7516192768 | bytes 1048576 | tf_op jit(solution)/shard_map/pallas_call | solution.py:304
  34.8 1.1 %all-to-all-done.1 = bf16[32,8,256]{2,1,0:T(8,128)(2,1)S(1)} async-done(((bf16[32,8,256]{2,1,0:T(8,128)(2,1)}), bf16[32,8,256]{2,1,0:T(8,128)(2,1)S(1)}, u32[]{:S(2)}, u32[]{:S(2)}) %all-to-all-start.1) | async-done | bytes 131104 | tf_op jit(solution)/shard_map/all_to_all | solution.py:318
  35.9 0.6 copy-done.7
  36.5 0.2 copy-done.9
  36.7 13.7 %shard_map.167 = (bf16[4,256,256]{2,1,0:T(8,128)(2,1)}, bf16[4,256,256]{2,1,0:T(8,128)(2,1)}, bf16[16,64,128]{2,1,0:T(8,128)(2,1)}, bf16[16,64,128]{2,1,0:T(8,128)(2,1)}, bf16[2048,256]{1,0:T(8,128)(2,1)}) custom-call(s32[1]{0:T(128)S(6)} %copy.23.refs_0_, s32[1]{0:T(128)} %bitcast.refs_1_.core_ref, s32[1]{0:T(128)} %bitcast.1.refs_2_, ...), custom_call_target="tpu_custom_call" | custom-call | flops 15032385536 | bytes 1048576 | tf_op jit(solution)/shard_map/pallas_call | solution.py:304
  50.5 0.0 copy-start.1
  50.5 0.0 copy-start.2
  50.5 0.0 copy-start.3
  50.5 0.1 collective-permute-start.5
  50.6 1.4 %collective-permute-start.4 = (bf16[4,256,256]{2,1,0:T(8,128)(2,1)}, bf16[4,256,256]{2,1,0:T(8,128)(2,1)S(1)}, u32[]{:S(2)}, u32[]{:S(2)}) collective-permute-start(bf16[4,256,256]{2,1,0:T(8,128)(2,1)} %get-tuple-element.32), channel_id=1, source_target_pairs={{0,1},{1,0},{2,3},{3,2},{4,5},{5,4},{6,7},{7,6},{8,9},{9,8},{10,11... | collective-permute-start | bytes 1572872 | tf_op jit(solution)/shard_map/ppermute | solution.py:322
  51.9 0.4 collective-permute-done.5.got_ref
  52.3 0.9 %copy-done.4 = bf16[16,64,128]{2,1,0:T(8,128)(2,1)S(1)} copy-done((bf16[16,64,128]{2,1,0:T(8,128)(2,1)S(1)}, bf16[16,64,128]{2,1,0:T(8,128)(2,1)}, u32[]{:S(2)}) %copy-start.4) | copy-done | bytes 262168
  53.3 0.8 shard_map.169
  54.0 5.8 %all-to-all-start.2 = ((bf16[16,80,128]{2,1,0:T(8,128)(2,1)}), bf16[16,80,128]{2,1,0:T(8,128)(2,1)S(1)}, u32[]{:S(2)}, u32[]{:S(2)}) async-start(bf16[16,80,128]{2,1,0:T(8,128)(2,1)} %shard_map.169), calls=%async_computation.2 | async-start | bytes 655360 | tf_op jit(solution)/shard_map/all_to_all | solution.py:318
  59.8 0.1 reshape.59
  59.9 0.1 reshape.60.asked
  60.0 3.5 %shard_map.168.refs_3_ = f32[4096,256]{1,0:T(8,128)} custom-call(s32[1,1024]{1,0:T(1,128)S(1)} %bitcast.33, s32[1,1024]{1,0:T(1,128)S(1)} %bitcast.36, bf16[2048,256]{1,0:T(8,128)(2,1)S(1)} %copy-done.3), custom_call_target="tpu_custom_call" | custom-call | flops 3221225472 | bytes 1048576 | tf_op jit(solution)/shard_map/pallas_call | solution.py:304
  63.5 3.4 %collective-permute-done.4 = bf16[4,256,256]{2,1,0:T(8,128)(2,1)S(1)} collective-permute-done((bf16[4,256,256]{2,1,0:T(8,128)(2,1)}, bf16[4,256,256]{2,1,0:T(8,128)(2,1)S(1)}, u32[]{:S(2)}, u32[]{:S(2)}) %collective-permute-start.4) | collective-permute-done | bytes 524320 | tf_op jit(solution)/shard_map/ppermute | solution.py:322
  66.9 0.1 fusion.4
  67.0 1.1 %collective-permute-start.6 = (bf16[256,256]{1,0:T(8,128)(2,1)S(1)}, bf16[256,256]{1,0:T(8,128)(2,1)S(1)}, u32[]{:S(2)}, u32[]{:S(2)}) collective-permute-start(bf16[256,256]{1,0:T(8,128)(2,1)S(1)} %get-tuple-element.47), channel_id=1, source_target_pairs={{0,2},{2,0},{4,6},{6,4},{1,3},{3,1},{5,7},{7,5},{8,10},{10,8},{12,... | collective-permute-start | bytes 393224 | tf_op jit(solution)/shard_map/ppermute | solution.py:322
  68.1 2.9 %collective-permute-start.7 = (bf16[256,256]{1,0:T(8,128)(2,1)S(1)}, bf16[256,256]{1,0:T(8,128)(2,1)S(1)}, u32[]{:S(2)}, u32[]{:S(2)}) collective-permute-start(bf16[256,256]{1,0:T(8,128)(2,1)S(1)} %get-tuple-element.46), channel_id=1, source_target_pairs={{0,4},{2,6},{4,0},{6,2},{1,5},{3,7},{5,1},{7,3},{8,12},{10,14},{12... | collective-permute-start | bytes 393224 | tf_op jit(solution)/shard_map/ppermute | solution.py:322
  71.0 0.5 collective-permute-start.8
  71.4 0.1 all-to-all-done.2.got_ref
  71.5 0.7 shard_map.170
  72.2 6.7 %all-to-all-start.3 = ((bf16[16,48,128]{2,1,0:T(8,128)(2,1)}), bf16[16,48,128]{2,1,0:T(8,128)(2,1)S(1)}, u32[]{:S(2)}, u32[]{:S(2)}) async-start(bf16[16,48,128]{2,1,0:T(8,128)(2,1)} %shard_map.170), calls=%async_computation.3 | async-start | bytes 393216 | tf_op jit(solution)/shard_map/all_to_all | solution.py:318
  78.9 3.5 %shard_map.171 = f32[4096,256]{1,0:T(8,128)} custom-call(s32[1,1024]{1,0:T(1,128)S(1)} %bitcast.34, s32[1,1024]{1,0:T(1,128)S(1)} %bitcast.37, bf16[2048,256]{1,0:T(8,128)(2,1)S(1)} %copy-done.3, f32[4096,256]{1,0:T(8,128)} %shard_map.168.refs_3_), custom_call_target="tpu_custom_call", output_to_operand_aliasing={{}: (3, {})} | custom-call | flops 3221225472 | bytes 1048576 | tf_op jit(solution)/shard_map/pallas_call | solution.py:304
  82.5 1.4 %shard_map.172 = f32[1024,256]{1,0:T(8,128)} custom-call(s32[1]{0:T(128)} %bitcast.refs_1_.core_ref, bf16[16,80,128]{2,1,0:T(8,128)(2,1)S(1)} %all-to-all-done.2.got_ref, s32[2,128]{1,0:T(2,128)S(1)} %reshape.60.asked), custom_call_target="tpu_custom_call" | custom-call | flops 2147483648 | bytes 1048576 | tf_op jit(solution)/shard_map/pallas_call | solution.py:304
  83.9 3.2 %all-to-all-done.3 = bf16[16,48,128]{2,1,0:T(8,128)(2,1)S(1)} async-done(((bf16[16,48,128]{2,1,0:T(8,128)(2,1)}), bf16[16,48,128]{2,1,0:T(8,128)(2,1)S(1)}, u32[]{:S(2)}, u32[]{:S(2)}) %all-to-all-start.3) | async-done | bytes 196640 | tf_op jit(solution)/shard_map/all_to_all | solution.py:318
  87.1 0.8 fusion.1
  87.9 0.7 collective-permute-done.9.got_ref
  88.5 0.9 %shard_map.173 = (f32[512,256]{1,0:T(8,128)}, f32[256,256]{1,0:T(8,128)}) custom-call(s32[1]{0:T(128)} %bitcast.refs_1_.core_ref, bf16[768,128]{1,0:T(8,128)(2,1)S(1)} %bitcast.31, bf16[768,128]{1,0:T(8,128)(2,1)S(1)} %collective-permute-done.9.got_ref), custom_call_target="tpu_custom_call" | custom-call | flops 1073741824 | bytes 1048576 | tf_op jit(solution)/shard_map/pallas_call | solution.py:304
  (18 shorter events, 0.0 us)
Async XLA Ops:
  0.6 18.3 %collective-permute-start.2 = (bf16[256,256]{1,0:T(8,128)(2,1)}, bf16[256,256]{1,0:T(8,128)(2,1)S(1)}, u32[]{:S(2)}, u32[]{:S(2)}) collective-permute-start(bf16[256,256]{1,0:T(8,128)(2,1)} %param.13), channel_id=1, source_target_pairs={{0,6},{2,4},{4,2},{6,0},{1,7},{3,5},{5,3},{7,1},{8,14},{10,12},{12... | collective-permute-start | bytes 393224 | tf_op jit(solution)/shard_map/ppermute | solution.py:322
  5.7 13.2 %collective-permute-start.1 = (bf16[256,256]{1,0:T(8,128)(2,1)}, bf16[256,256]{1,0:T(8,128)(2,1)S(1)}, u32[]{:S(2)}, u32[]{:S(2)}) collective-permute-start(bf16[256,256]{1,0:T(8,128)(2,1)} %param.13), channel_id=1, source_target_pairs={{0,4},{2,6},{4,0},{6,2},{1,5},{3,7},{5,1},{7,3},{8,12},{10,14},{12... | collective-permute-start | bytes 393224 | tf_op jit(solution)/shard_map/ppermute | solution.py:322
  5.7 13.2 %collective-permute-start = (bf16[256,256]{1,0:T(8,128)(2,1)}, bf16[256,256]{1,0:T(8,128)(2,1)S(1)}, u32[]{:S(2)}, u32[]{:S(2)}) collective-permute-start(bf16[256,256]{1,0:T(8,128)(2,1)} %param.13), channel_id=1, source_target_pairs={{0,2},{2,0},{4,6},{6,4},{1,3},{3,1},{5,7},{7,5},{8,10},{10,8},{12,... | collective-permute-start | bytes 393224 | tf_op jit(solution)/shard_map/ppermute | solution.py:322
  7.8 13.0 %all-to-all-start = ((s32[32,1,8]{2,1,0:T(1,128)}), s32[32,1,8]{2,1,0:T(1,128)S(1)}, u32[]{:S(2)}, u32[]{:S(2)}) async-start(s32[32,1,8]{2,1,0:T(1,128)} %bitcast.2), calls=%async_computation | async-start | bytes 32768 | tf_op jit(solution)/shard_map/all_to_all | solution.py:318
  13.8 5.2 %copy-start.8 = (bf16[256,256]{1,0:T(8,128)(2,1)S(1)}, bf16[256,256]{1,0:T(8,128)(2,1)}, u32[]{:S(2)}) copy-start(bf16[256,256]{1,0:T(8,128)(2,1)} %param.13) | copy-start | bytes 393220
  13.8 7.7 %copy-start = (bf16[1024,256]{1,0:T(8,128)(2,1)S(1)}, bf16[1024,256]{1,0:T(8,128)(2,1)}, u32[]{:S(2)}) copy-start(bf16[1024,256]{1,0:T(8,128)(2,1)} %table_ref.1) | copy-start | bytes 1572868
  19.1 15.1 %copy-start.6 = (bf16[4,256,256]{2,1,0:T(8,128)(2,1)}, bf16[4,256,256]{2,1,0:T(8,128)(2,1)S(1)}, u32[]{:S(2)}) copy-start(bf16[4,256,256]{2,1,0:T(8,128)(2,1)S(1)} %pad_maximum_fusion.refs_4_) | copy-start | bytes 1572868
  20.8 15.1 %collective-permute-start.3 = (bf16[4,256,256]{2,1,0:T(8,128)(2,1)S(1)}, bf16[4,256,256]{2,1,0:T(8,128)(2,1)S(1)}, u32[]{:S(2)}, u32[]{:S(2)}) collective-permute-start(bf16[4,256,256]{2,1,0:T(8,128)(2,1)S(1)} %pad_maximum_fusion.refs_4_), channel_id=1, source_target_pairs={{0,1},{1,0},{2,3},{3,2},{4,5},{5,4},{6,7},{7,6},{8,9},{9,8},{10,11... | collective-permute-start | bytes 1572872 | tf_op jit(solution)/shard_map/ppermute | solution.py:322
  22.5 13.3 %all-to-all-start.1 = ((bf16[32,8,256]{2,1,0:T(8,128)(2,1)}), bf16[32,8,256]{2,1,0:T(8,128)(2,1)S(1)}, u32[]{:S(2)}, u32[]{:S(2)}) async-start(bf16[32,8,256]{2,1,0:T(8,128)(2,1)} %bitcast.12), calls=%async_computation.1 | async-start | bytes 262144 | tf_op jit(solution)/shard_map/all_to_all | solution.py:318
  35.9 0.7 copy-start.7
  35.9 0.8 copy-start.9
  50.5 9.5 %copy-start.1 = (s32[1024]{0:T(1024)S(1)}, s32[1024]{0:T(1024)}, u32[]{:S(2)}) copy-start(s32[1024]{0:T(1024)} %param.19) | copy-start | bytes 12292
  50.5 9.5 %copy-start.2 = (s32[1024]{0:T(1024)S(1)}, s32[1024]{0:T(1024)}, u32[]{:S(2)}) copy-start(s32[1024]{0:T(1024)} %param.24) | copy-start | bytes 12292
  50.5 9.5 %copy-start.3 = (bf16[2048,256]{1,0:T(8,128)(2,1)S(1)}, bf16[2048,256]{1,0:T(8,128)(2,1)}, u32[]{:S(2)}) copy-start(bf16[2048,256]{1,0:T(8,128)(2,1)} %get-tuple-element.33.refs_2_) | copy-start | bytes 3145732
  50.5 1.8 %collective-permute-start.5 = (bf16[16,64,128]{2,1,0:T(8,128)(2,1)}, bf16[16,64,128]{2,1,0:T(8,128)(2,1)S(1)}, u32[]{:S(2)}, u32[]{:S(2)}) collective-permute-start(bf16[16,64,128]{2,1,0:T(8,128)(2,1)} %get-tuple-element.36), channel_id=1, source_target_pairs={{0,8},{8,0},{1,9},{9,1},{2,10},{10,2},{3,11},{11,3},{4,12},{12,4},... | collective-permute-start | bytes 786440 | tf_op jit(solution)/shard_map/ppermute | solution.py:322
  50.6 16.3 %collective-permute-start.4 = (bf16[4,256,256]{2,1,0:T(8,128)(2,1)}, bf16[4,256,256]{2,1,0:T(8,128)(2,1)S(1)}, u32[]{:S(2)}, u32[]{:S(2)}) collective-permute-start(bf16[4,256,256]{2,1,0:T(8,128)(2,1)} %get-tuple-element.32), channel_id=1, source_target_pairs={{0,1},{1,0},{2,3},{3,2},{4,5},{5,4},{6,7},{7,6},{8,9},{9,8},{10,11... | collective-permute-start | bytes 1572872 | tf_op jit(solution)/shard_map/ppermute | solution.py:322
  52.3 1.0 %copy-start.4 = (bf16[16,64,128]{2,1,0:T(8,128)(2,1)S(1)}, bf16[16,64,128]{2,1,0:T(8,128)(2,1)}, u32[]{:S(2)}) copy-start(bf16[16,64,128]{2,1,0:T(8,128)(2,1)} %get-tuple-element.35.own_ref) | copy-start | bytes 786436
  54.0 17.5 %all-to-all-start.2 = ((bf16[16,80,128]{2,1,0:T(8,128)(2,1)}), bf16[16,80,128]{2,1,0:T(8,128)(2,1)S(1)}, u32[]{:S(2)}, u32[]{:S(2)}) async-start(bf16[16,80,128]{2,1,0:T(8,128)(2,1)} %shard_map.169), calls=%async_computation.2 | async-start | bytes 655360 | tf_op jit(solution)/shard_map/all_to_all | solution.py:318
  60.0 6.9 %copy-start.5 = (bf16[4,256,256]{2,1,0:T(8,128)(2,1)S(1)}, bf16[4,256,256]{2,1,0:T(8,128)(2,1)}, u32[]{:S(2)}) copy-start(bf16[4,256,256]{2,1,0:T(8,128)(2,1)} %get-tuple-element.31) | copy-start | bytes 1572868
  67.0 16.9 %collective-permute-start.6 = (bf16[256,256]{1,0:T(8,128)(2,1)S(1)}, bf16[256,256]{1,0:T(8,128)(2,1)S(1)}, u32[]{:S(2)}, u32[]{:S(2)}) collective-permute-start(bf16[256,256]{1,0:T(8,128)(2,1)S(1)} %get-tuple-element.47), channel_id=1, source_target_pairs={{0,2},{2,0},{4,6},{6,4},{1,3},{3,1},{5,7},{7,5},{8,10},{10,8},{12,... | collective-permute-start | bytes 393224 | tf_op jit(solution)/shard_map/ppermute | solution.py:322
  68.1 15.8 %collective-permute-start.7 = (bf16[256,256]{1,0:T(8,128)(2,1)S(1)}, bf16[256,256]{1,0:T(8,128)(2,1)S(1)}, u32[]{:S(2)}, u32[]{:S(2)}) collective-permute-start(bf16[256,256]{1,0:T(8,128)(2,1)S(1)} %get-tuple-element.46), channel_id=1, source_target_pairs={{0,4},{2,6},{4,0},{6,2},{1,5},{3,7},{5,1},{7,3},{8,12},{10,14},{12... | collective-permute-start | bytes 393224 | tf_op jit(solution)/shard_map/ppermute | solution.py:322
  71.0 12.9 %collective-permute-start.8 = (bf16[256,256]{1,0:T(8,128)(2,1)S(1)}, bf16[256,256]{1,0:T(8,128)(2,1)S(1)}, u32[]{:S(2)}, u32[]{:S(2)}) collective-permute-start(bf16[256,256]{1,0:T(8,128)(2,1)S(1)} %get-tuple-element.45), channel_id=1, source_target_pairs={{0,6},{2,4},{4,2},{6,0},{1,7},{3,5},{5,3},{7,1},{8,14},{10,12},{12... | collective-permute-start | bytes 393224 | tf_op jit(solution)/shard_map/ppermute | solution.py:322
  72.2 14.9 %all-to-all-start.3 = ((bf16[16,48,128]{2,1,0:T(8,128)(2,1)}), bf16[16,48,128]{2,1,0:T(8,128)(2,1)S(1)}, u32[]{:S(2)}, u32[]{:S(2)}) async-start(bf16[16,48,128]{2,1,0:T(8,128)(2,1)} %shard_map.170), calls=%async_computation.3 | async-start | bytes 393216 | tf_op jit(solution)/shard_map/all_to_all | solution.py:318
  87.1 1.4 %collective-permute-start.9 = (bf16[768,128]{1,0:T(8,128)(2,1)S(1)}, bf16[768,128]{1,0:T(8,128)(2,1)S(1)}, u32[]{:S(2)}, u32[]{:S(2)}) collective-permute-start(bf16[768,128]{1,0:T(8,128)(2,1)S(1)} %bitcast.30), channel_id=1, source_target_pairs={{0,8},{8,0},{1,9},{9,1},{2,10},{10,2},{3,11},{11,3},{4,12},{12,4},... | collective-permute-start | bytes 589832 | tf_op jit(solution)/shard_map/ppermute | solution.py:322
